TPU v7x, 32 devices: a whole 2x2x4 slice. The times are simulated.
32 devices in a mesh: row: 4 (over y, x), col: 8 (over z, core).
Axes of the slice: x: 2, y: 2, z: 4, core: 2. Of those that a mesh axis runs over, the one named last changes fastest.
Arguments:
- flexibility: float32 [4, 8, 5, 1024, 1024], P('row', 'col'), as said below
- coupling: float32 [4, 8, 5, 24, 1024], P('row', 'col'), may hold values from -0.75 to 0.75
- coarse_inverse: float32 [1536, 1536], P(('row', 'col')), as said below
- precon_weight: float32 [4, 8, 5, 4, 128], P('row', 'col'), may hold values from 0.25 to 2
- right_side: float32 [4, 8, 5, 16, 4, 128], P('row', 'col'), may hold values from -6 to 6
- counts: int32 [4, 8], P('row', 'col'), may hold values from 2 to 5, as said below
- partner: int32 [4, 8, 4, 5], P('row', 'col'), may hold values from 0 to 4, each once within a row
- dof_index: int32 [4, 8, 5, 4, 128], P('row', 'col'), may hold values from 0 to 127, each once within a row
- corner_map: int32 [4, 8, 5, 24], P('row', 'col'), may hold values from 0 to 1535
Outputs:
- solution: float32 [4, 8, 5, 16, 4, 128], P('row', 'col')
- residual: float32 [4, 8, 5, 16, 4, 128], P('row', 'col')
Inputs may be any that keep to these rules, and one draw needn't show every extreme that they name: A device's live subdomains are its first counts slots; some device has 5 and some device has 2 in every draw. `partner`: for each device and each link block separately, the 5 entries are a permutation of the slots; the same values recur on other devices, link blocks and device rows. `dof_index`: for each device, slot and link block separately, the 128 entries are a permutation of the block's unknowns; the same values recur on other slots, link blocks, devices and device rows. `flexibility`: symmetric positive definite. `coarse_inverse`: symmetric positive definite.
All inputs are finite; a program needn't handle non-finite values.
Results may differ from a plain program's by a relative error of at most 0.00029.
Values sent between devices are 32-bit elements; how exact they have to be, the bound alone decides.
No kernel may reach another device: no remote copies, remote signals or barrier semaphores. Data moves between devices by JAX's collectives and lax.ppermute only.
A program may use at most 128 MiB of HBM per device.

v0:
```python
import jax
import jax.numpy as jnp
from jax import lax
from jax.sharding import PartitionSpec as P

ITERS = 3


HIGH = lax.Precision.HIGHEST


def shifted(x, axis, by):
    devices = lax.axis_size(axis)
    return lax.ppermute(x, axis, [(i, (i + by) % devices) for i in range(devices)])


def local(
    flexibility,
    coupling,
    coarse_inverse,
    precon_weight,
    right_side,
    counts,
    partner,
    dof_index,
    corner_map,
):
    flex_local = flexibility[0, 0]
    coupling_local = coupling[0, 0]
    slots = flex_local.shape[0]
    iface = flex_local.shape[1]
    links = partner.shape[2]
    width = dof_index.shape[-1]
    loads = right_side.shape[3]
    corners = corner_map.shape[-1]
    coarse_size = coarse_inverse.shape[1]
    slot_ids = jnp.arange(slots, dtype=jnp.int32)
    counts_prev = shifted(counts, "col", 1)
    partner_next = shifted(partner, "col", -1)
    live = (slot_ids < counts[0, 0]).astype(jnp.float32)
    live_prev = (slot_ids < counts_prev[0, 0]).astype(jnp.float32)
    chosen_own = (partner[0, 0][..., None] == slot_ids).astype(jnp.float32)
    chosen_next = (partner_next[0, 0][..., None] == slot_ids).astype(jnp.float32)
    link_live = jnp.einsum("kjp,p->jk", chosen_own, live_prev, precision=HIGH)
    mask_links = (live[:, None] * link_live)[:, None, :, None]
    permuter = (dof_index[0, 0][..., None] == jnp.arange(width, dtype=jnp.int32)).astype(
        jnp.float32
    )
    corner_table = (
        corner_map[0, 0].reshape(-1)[:, None] == jnp.arange(coarse_size, dtype=jnp.int32)
    ).astype(jnp.float32)

    def coarse_solve(local_load):
        total_load = lax.psum(local_load, ("row", "col"))
        own_rows = lax.dot_general(
            total_load,
            coarse_inverse,
            (((1,), (1,)), ((), ())),
            precision=HIGH,
            preferred_element_type=jnp.float32,
        )
        return lax.all_gather(own_rows, ("row", "col"), axis=1, tiled=True)

    def apply_operator(values):
        forces = jnp.einsum("jkmi,jqkm->jqki", permuter, values, precision=HIGH)
        forces_next = shifted(forces, "col", -1)
        facing = -jnp.einsum("kjp,jqkw->pqkw", chosen_next, forces_next, precision=HIGH)
        force_full = jnp.concatenate([values, facing], axis=2).reshape(slots, loads, iface)
        answer = jnp.einsum("sab,sqb->sqa", flex_local, force_full, precision=HIGH)
        corner_terms = jnp.einsum(
            "snb,sqb->qsn", coupling_local, force_full, precision=HIGH
        ).reshape(loads, slots * corners)
        local_load = jnp.dot(
            corner_terms, corner_table, precision=HIGH, preferred_element_type=jnp.float32
        )
        corner_answer = coarse_solve(local_load)
        picked = lax.dot_general(
            corner_answer,
            corner_table,
            (((1,), (1,)), ((), ())),
            precision=HIGH,
            preferred_element_type=jnp.float32,
        )
        picked = picked.reshape(loads, slots, corners)
        answer = answer + jnp.einsum("snb,qsn->sqb", coupling_local, picked, precision=HIGH)
        split = answer.reshape(slots, loads, 2 * links, width)
        link_part = split[:, :, :links, :]
        facing_prev = shifted(split[:, :, links:, :], "col", 1)
        selected = jnp.einsum("kjp,pqkw->jqkw", chosen_own, facing_prev, precision=HIGH)
        selected = jnp.einsum("jkmi,jqki->jqkm", permuter, selected, precision=HIGH)
        return (link_part - selected) * mask_links

    def local_inner(first, second):
        return jnp.sum(first * second, axis=(0, 2, 3))

    def broadcast_loads(scalars):
        return scalars[None, :, None, None]

    weight = precon_weight[0, 0][:, None]
    residual = right_side[0, 0] * mask_links
    solution = jnp.zeros_like(residual)

    def both_sums(resid_now, precond_now, image_now):
        return lax.psum(
            (local_inner(resid_now, precond_now), local_inner(precond_now, image_now)),
            ("row", "col"),
        )

    precond = weight * residual
    image = apply_operator(precond)
    norm_now, product = both_sums(residual, precond, image)
    alpha_vec = norm_now / product
    direction = precond
    along = image
    for iteration in range(ITERS):
        alpha = broadcast_loads(alpha_vec)
        solution = solution + alpha * direction
        residual = residual - alpha * along
        if iteration + 1 < ITERS:
            precond = weight * residual
            image = apply_operator(precond)
            norm_next, product = both_sums(residual, precond, image)
            ratio = norm_next / norm_now
            alpha_vec = norm_next / (product - ratio * norm_next / alpha_vec)
            direction = precond + broadcast_loads(ratio) * direction
            along = image + broadcast_loads(ratio) * along
            norm_now = norm_next
    return (solution[None, None], residual[None, None])


def solution(mesh):
    in_specs = (
        P("row", "col", None, None, None),
        P("row", "col", None, None, None),
        P(("row", "col"), None),
        P("row", "col", None, None, None),
        P("row", "col", None, None, None, None),
        P("row", "col"),
        P("row", "col", None, None),
        P("row", "col", None, None, None),
        P("row", "col", None, None),
    )
    out_specs = (P("row", "col", None, None, None, None), P("row", "col", None, None, None, None))
    return jax.shard_map(local, mesh=mesh, in_specs=in_specs, out_specs=out_specs, check_vma=False)
```

profile of v0, /device:TPU:0, one launch (start us, length us, event | category | flops | bytes accessed | tf_op | source)
XLA Modules:
  0.0 690.0 jit_solution(7387207770579165841)
XLA Ops:
  7.2 0.5 collective-permute-start
  8.4 0.7 copy.44
  9.1 4.0 collective-permute-done
  13.1 1.6 fusion.62
  14.7 1.0 fusion.50
  15.7 1.8 fusion.15
  17.7 2.3 collective-permute-start.2
  20.0 0.7 reduce
  20.7 0.7 collective-permute-done.2
  22.2 0.5 convolution_bitcast_fusion.5
  22.8 1.0 fusion.23
  24.0 20.1 %fusion.4 = f32[5,16,1024]{2,1,0:T(8,128)S(1)} fusion(f32[5,16,1024]{2,1,0:T(8,128)S(1)} %reshape.56, f32[1,1,5,1024,1024]{4,3,2,1,0:T(8,128)} %param.9), kind=kOutput, calls=%fused_computation.4 | convolution fusion | flops 1006632960 | bytes 21626880 | tf_op jit(solution)/shard_map/sab,sqb->sqa/dot_general | solution.py:69
  44.0 101.9 %all-reduce.7.cloned.1.call-done = f32[16,1536]{1,0:T(8,128)} async-done(((f32[16,1536]{1,0:T(8,128)}), f32[16,1536]{1,0:T(8,128)}) %all-reduce.7.cloned.1.call-update) | async-done | bytes 98320 | tf_op jit(solution)/shard_map/psum | solution.py:54
  145.9 1.2 convolution_bitcast_fusion.8
  147.1 42.4 %all-gather = f32[32,48,16]{1,2,0:T(8,128)S(1)} all-gather(f32[1,48,16]{1,2,0:T(8,128)S(1)} %convolution_bitcast_fusion.8), channel_id=1, replica_groups=mesh['row'=4,'col'=8] {'row','col'}, dimensions={0}, use_global_device_ids=true | all-gather | bytes 101376 | tf_op jit(solution)/shard_map/all_gather | solution.py:62
  189.8 0.5 fusion.22
  191.5 7.3 %collective-permute-done.3 = f32[5,16,4,128]{3,0,1,2:T(8,128)S(1)} collective-permute-done((f32[5,16,4,128]{3,0,1,2:T(8,128)S(1)}, f32[5,16,4,128]{3,0,1,2:T(8,128)S(1)}, u32[]{:S(2)}, u32[]{:S(2)}) %collective-permute-start.3) | collective-permute-done | bytes 163872 | tf_op jit(solution)/shard_map/ppermute | solution.py:14
  199.1 1.4 fusion.10
  201.0 36.9 %all-reduce.2 = (f32[16]{0:T(128)S(1)}, f32[16]{0:T(128)S(1)}) all-reduce(f32[16]{0:T(128)S(1)} %get-tuple-element.13, f32[16]{0:T(128)S(1)} %get-tuple-element.12), channel_id=1, replica_groups=mesh['row'=4,'col'=8] {'row','col'}, use_global_device_ids=true, to_apply=%region_1.0 | all-reduce | flops 32 | bytes 256 | tf_op jit(solution)/shard_map/psum | solution.py:104
  238.2 1.1 fusion.16
  239.2 1.1 collective-permute-start.4
  240.4 2.8 collective-permute-done.4
  243.9 0.5 convolution_bitcast_fusion.4
  244.5 1.0 fusion.21
  245.7 20.0 %fusion.2 = f32[5,16,1024]{2,1,0:T(8,128)S(1)} fusion(f32[5,16,1024]{2,1,0:T(8,128)S(1)} %reshape.60, f32[1,1,5,1024,1024]{4,3,2,1,0:T(8,128)} %param.9), kind=kOutput, calls=%fused_computation.2 | convolution fusion | flops 1006632960 | bytes 21626880 | tf_op jit(solution)/shard_map/sab,sqb->sqa/dot_general | solution.py:69
  265.7 101.9 %all-reduce.9.cloned.1.call-done = f32[16,1536]{1,0:T(8,128)} async-done(((f32[16,1536]{1,0:T(8,128)}), f32[16,1536]{1,0:T(8,128)}) %all-reduce.9.cloned.1.call-update) | async-done | bytes 98320 | tf_op jit(solution)/shard_map/psum | solution.py:54
  367.7 1.2 convolution_bitcast_fusion.7
  368.8 42.4 %all-gather.1 = f32[32,48,16]{1,2,0:T(8,128)S(1)} all-gather(f32[1,48,16]{1,2,0:T(8,128)S(1)} %convolution_bitcast_fusion.7), channel_id=1, replica_groups=mesh['row'=4,'col'=8] {'row','col'}, dimensions={0}, use_global_device_ids=true | all-gather | bytes 101376 | tf_op jit(solution)/shard_map/all_gather | solution.py:62
  411.5 0.5 fusion.20
  413.2 7.3 %collective-permute-done.5 = f32[5,16,4,128]{3,0,1,2:T(8,128)S(1)} collective-permute-done((f32[5,16,4,128]{3,0,1,2:T(8,128)S(1)}, f32[5,16,4,128]{3,0,1,2:T(8,128)S(1)}, u32[]{:S(2)}, u32[]{:S(2)}) %collective-permute-start.5) | collective-permute-done | bytes 163872 | tf_op jit(solution)/shard_map/ppermute | solution.py:14
  420.8 1.4 fusion.8
  422.6 36.9 %all-reduce.1 = (f32[16]{0:T(128)S(1)}, f32[16]{0:T(128)S(1)}) all-reduce(f32[16]{0:T(128)S(1)} %get-tuple-element.11, f32[16]{0:T(128)S(1)} %get-tuple-element.10), channel_id=1, replica_groups=mesh['row'=4,'col'=8] {'row','col'}, use_global_device_ids=true, to_apply=%region_6.0 | all-reduce | flops 32 | bytes 256 | tf_op jit(solution)/shard_map/psum | solution.py:104
  459.9 1.1 fusion.17
  461.0 1.2 collective-permute-start.6
  462.2 2.8 collective-permute-done.6
  465.7 0.5 convolution_bitcast_fusion.3
  466.3 1.0 fusion.19
  467.4 20.0 %fusion = f32[5,16,1024]{2,1,0:T(8,128)S(1)} fusion(f32[5,16,1024]{2,1,0:T(8,128)S(1)} %reshape.64, f32[1,1,5,1024,1024]{4,3,2,1,0:T(8,128)} %param.9), kind=kOutput, calls=%fused_computation | convolution fusion | flops 1006632960 | bytes 21626880 | tf_op jit(solution)/shard_map/sab,sqb->sqa/dot_general | solution.py:69
  487.4 101.9 %all-reduce.11.cloned.1.call-done = f32[16,1536]{1,0:T(8,128)} async-done(((f32[16,1536]{1,0:T(8,128)}), f32[16,1536]{1,0:T(8,128)}) %all-reduce.11.cloned.1.call-update) | async-done | bytes 98320 | tf_op jit(solution)/shard_map/psum | solution.py:54
  589.4 1.2 convolution_bitcast_fusion.6
  590.6 42.4 %all-gather.2 = f32[32,48,16]{1,2,0:T(8,128)S(1)} all-gather(f32[1,48,16]{1,2,0:T(8,128)S(1)} %convolution_bitcast_fusion.6), channel_id=1, replica_groups=mesh['row'=4,'col'=8] {'row','col'}, dimensions={0}, use_global_device_ids=true | all-gather | bytes 101376 | tf_op jit(solution)/shard_map/all_gather | solution.py:62
  633.3 0.5 fusion.18
  634.9 7.3 %collective-permute-done.7 = f32[5,16,4,128]{3,0,1,2:T(8,128)S(1)} collective-permute-done((f32[5,16,4,128]{3,0,1,2:T(8,128)S(1)}, f32[5,16,4,128]{3,0,1,2:T(8,128)S(1)}, u32[]{:S(2)}, u32[]{:S(2)}) %collective-permute-start.7) | collective-permute-done | bytes 163872 | tf_op jit(solution)/shard_map/ppermute | solution.py:14
  642.5 1.4 fusion.6
  644.3 36.9 %all-reduce = (f32[16]{0:T(128)S(1)}, f32[16]{0:T(128)S(1)}) all-reduce(f32[16]{0:T(128)S(1)} %get-tuple-element.9, f32[16]{0:T(128)S(1)} %get-tuple-element.8), channel_id=1, replica_groups=mesh['row'=4,'col'=8] {'row','col'}, use_global_device_ids=true, to_apply=%region_11.0 | all-reduce | flops 32 | bytes 256 | tf_op jit(solution)/shard_map/psum | solution.py:104
  681.2 0.7 subtract_bitcast_fusion
  681.9 0.8 copy.76
  682.7 0.8 copy.75
  (74 shorter events, 9.7 us)
Async XLA Ops:
  7.2 15.0 %copy-start = (f32[1,1,5,24,1024]{4,3,2,1,0:T(8,128)S(1)}, f32[1,1,5,24,1024]{4,3,2,1,0:T(8,128)}, u32[]{:S(2)}) copy-start(f32[1,1,5,24,1024]{4,3,2,1,0:T(8,128)} %param.10) | copy-start | bytes 1474564
  7.2 138.8 %all-reduce.7.cloned.1.call-start = ((), (), s32[]{:S(2)}) async-start(), calls=%async_computation | async-start | bytes 196608 | tf_op jit(solution)/shard_map/psum | solution.py:54
  7.2 5.9 collective-permute-start
  17.5 4.0 collective-permute-start.1
  17.7 3.8 collective-permute-start.2
  23.9 122.1 %copy-start.1 = (f32[48,1536]{1,0:T(8,128)S(1)}, f32[48,1536]{1,0:T(8,128)}, u32[]{:S(2)}) copy-start(f32[48,1536]{1,0:T(8,128)} %param.11) | copy-start | bytes 884740
  23.9 343.7 %all-reduce.9.cloned.1.call-start = ((), (), s32[]{:S(2)}) async-start(), calls=%async_computation.1 | async-start | bytes 196608 | tf_op jit(solution)/shard_map/psum | solution.py:54
  190.4 8.4 %copy-start.3 = (s32[1,1,4,5]{3,2,1,0:T(4,128)S(1)}, s32[1,1,4,5]{3,2,1,0:T(4,128)}, u32[]{:S(2)}) copy-start(s32[1,1,4,5]{3,2,1,0:T(4,128)} %param.15) | copy-start | bytes 244
  190.9 8.2 %copy-start.4 = (s32[1,1,5,4,128]{4,3,2,1,0:T(4,128)S(1)}, s32[1,1,5,4,128]{4,3,2,1,0:T(4,128)}, u32[]{:S(2)}) copy-start(s32[1,1,5,4,128]{4,3,2,1,0:T(4,128)} %param.16) | copy-start | bytes 30724
  190.9 9.6 %copy-start.2 = (f32[1,1,5,16,4,128]{5,4,3,2,1,0:T(4,128)S(1)}, f32[1,1,5,16,4,128]{5,4,3,2,1,0:T(4,128)}, u32[]{:S(2)}) copy-start(f32[1,1,5,16,4,128]{5,4,3,2,1,0:T(4,128)} %param.13) | copy-start | bytes 491524
  191.1 7.6 %collective-permute-start.3 = (f32[5,16,4,128]{3,0,1,2:T(8,128)S(1)}, f32[5,16,4,128]{3,0,1,2:T(8,128)S(1)}, u32[]{:S(2)}, u32[]{:S(2)}) collective-permute-start(f32[5,16,4,128]{3,0,1,2:T(8,128)S(1)} %copy.81), channel_id=1, source_target_pairs={{0,1},{1,2},{2,3},{3,4},{4,5},{5,6},{6,7},{7,0},{8,9},{9,10},{10,1... | collective-permute-start | bytes 491528 | tf_op jit(solution)/shard_map/ppermute | solution.py:14
  239.2 4.0 collective-permute-start.4
  245.6 343.8 %all-reduce.11.cloned.1.call-start = ((), (), s32[]{:S(2)}) async-start(), calls=%async_computation.2 | async-start | bytes 196608 | tf_op jit(solution)/shard_map/psum | solution.py:54
  412.8 7.6 %collective-permute-start.5 = (f32[5,16,4,128]{3,0,1,2:T(8,128)S(1)}, f32[5,16,4,128]{3,0,1,2:T(8,128)S(1)}, u32[]{:S(2)}, u32[]{:S(2)}) collective-permute-start(f32[5,16,4,128]{3,0,1,2:T(8,128)S(1)} %copy.83), channel_id=1, source_target_pairs={{0,1},{1,2},{2,3},{3,4},{4,5},{5,6},{6,7},{7,0},{8,9},{9,10},{10,1... | collective-permute-start | bytes 491528 | tf_op jit(solution)/shard_map/ppermute | solution.py:14
  461.0 4.0 collective-permute-start.6
  634.5 7.6 %collective-permute-start.7 = (f32[5,16,4,128]{3,0,1,2:T(8,128)S(1)}, f32[5,16,4,128]{3,0,1,2:T(8,128)S(1)}, u32[]{:S(2)}, u32[]{:S(2)}) collective-permute-start(f32[5,16,4,128]{3,0,1,2:T(8,128)S(1)} %copy.85), channel_id=1, source_target_pairs={{0,1},{1,2},{2,3},{3,4},{4,5},{5,6},{6,7},{7,0},{8,9},{9,10},{10,1... | collective-permute-start | bytes 491528 | tf_op jit(solution)/shard_map/ppermute | solution.py:14
Sparse Core Ops, SparseCore 0:
  24.0 121.8 all-reduce.6
  245.7 121.8 all-reduce.8
  467.5 121.8 all-reduce.10
where the time goes:
time: 691 us; the launch traced here: 690 us
  waiting for transfers between devices  338 us (49%)
  blocking collectives  238 us (34%)
  matrix products  83 us (12%)
  between operations  14.8 us (2%)
    psum x3, waiting for transfers between devices, coarse_solve(): total_load = lax.psum(local_load, ('row', 'col'))  306 us
    all_gather x3, blocking collectives, coarse_solve(): return lax.all_gather(own_rows, ('row', 'col'), axis=1, tiled=True)  127 us
    psum x3, blocking collectives, both_sums(): lax.psum((local_inner(resid_now, precond_now), local_inner(precond_now, i...  111 us
    dot_general x3, matrix products, apply_operator(): answer = jnp.einsum('sab,sqb->sqa', flex_local, force_full, precision=HIGH)  60.1 us
    ppermute x8, waiting for transfers between devices, shifted(): lax.ppermute(x, axis, [(i, (i + by) % devices) for i in range(devices)])  32.2 us
  transfers between devices with their start and end apart: 11, of which 10 were waited for; matrix products, arithmetic and copies ran while one was open for 9% of the time, Pallas kernels for 0%

commit v1 on v0

v1 whole, which is shorter than its diff:
```python
import functools
import jax
import jax.numpy as jnp
from jax import lax
from jax.experimental import pallas as pl
from jax.experimental.pallas import tpu as pltpu
from jax.sharding import PartitionSpec as P

ITERS = 3
BOTH = ("row", "col")
LANES = 128


def shifted(x, axis, by):
    devices = lax.axis_size(axis)
    return lax.ppermute(x, axis, [(i, (i + by) % devices) for i in range(devices)])


def swapped(x, bit):
    devices = lax.axis_size(BOTH)
    return lax.ppermute(x, BOTH, [(i, i ^ bit) for i in range(devices)])


def pieces(x, count):
    out = []
    for step in range(count):
        part = x.astype(jnp.bfloat16)
        out.append(part)
        if step + 1 < count:
            x = x - part.astype(jnp.float32)
    return out


def dot_pieces(a, b_parts, a_count=3):
    rows = a.shape[0]
    a_parts = pieces(a, a_count)
    terms = []
    for level, b in enumerate(b_parts):
        used = max(1, a_count - level)
        stacked = jnp.concatenate(a_parts[:used], axis=0) if used > 1 else a_parts[0]
        full = jnp.dot(stacked, b, preferred_element_type=jnp.float32)
        for i in range(used):
            terms.append((i + level, full[i * rows : (i + 1) * rows]))
    terms.sort(key=lambda item: -item[0])
    total = terms[0][1]
    for _, term in terms[1:]:
        total = total + term
    return total


def slot_mask(slots, loads, corners, width):
    row = lax.broadcasted_iota(jnp.int32, (slots * loads, width), 0) // loads
    lane = lax.broadcasted_iota(jnp.int32, (slots * loads, width), 1) // corners
    return row == lane


def to_corners(values, matrix_parts, corners):
    slots, loads, n = values.shape
    full = dot_pieces(values.reshape(slots * loads, n), matrix_parts)
    width = full.shape[1]
    kept = jnp.where(slot_mask(slots, loads, corners, width), full, 0.0)
    return jnp.sum(kept.reshape(slots, loads, width), axis=0)


def from_corners(answer, matrix_parts, slots, corners):
    loads, width = answer.shape
    spread = jnp.broadcast_to(answer[None], (slots, loads, width)).reshape(slots * loads, width)
    spread = jnp.where(slot_mask(slots, loads, corners, width), spread, 0.0)
    out = dot_pieces(spread, matrix_parts)
    return out.reshape(slots, loads, out.shape[1])


def column(x):
    return x[:, :1]


def start_exchange(
    z, partner_ref, inverse_ref, link_t_ref, prev_t_ref, map_ref, parity, corners, coarse_size, send_ref, mine_ref, other_ref
):
    slots, loads, width = z.shape
    links = width // LANES
    for j in range(slots):
        for k in range(links):
            block = z[j, :, k * LANES : (k + 1) * LANES]
            index = jnp.broadcast_to(inverse_ref[j * links + k][None], (loads, LANES))
            send_ref[partner_ref[k, j], :, k * LANES : (k + 1) * LANES] = -jnp.take_along_axis(block, index, axis=1)
    own = to_corners(z, pieces(link_t_ref[...], 3), corners)
    prev = to_corners(send_ref[...], pieces(prev_t_ref[...], 3), corners)
    terms = jnp.concatenate([own, prev], axis=1)
    table = map_ref[...] == lax.broadcasted_iota(jnp.int32, (terms.shape[1], coarse_size), 1)
    load = dot_pieces(terms, [table.astype(jnp.bfloat16)])
    half = coarse_size // 2
    low, high = load[:, :half], load[:, half:]
    mine_ref[...] = jnp.where(parity == 0, low, high)
    other_ref[...] = jnp.where(parity == 0, high, low)


def local_norm(r, z):
    slots, loads, width = r.shape
    return jnp.broadcast_to(jnp.sum(jnp.sum(r * z, axis=0), axis=1, keepdims=True), (loads, LANES))


def first_kernel(
    corners, coarse_size, info_ref, partner_ref, right_ref, weight_ref, dof_ref, link_t_ref, prev_t_ref, map_ref,
    inverse_ref, mask_ref, r_ref, z_ref, norm_ref, send_ref, mine_ref, other_ref,
):
    slots, loads, width = right_ref.shape
    links = width // LANES
    for j in range(slots):
        for k in range(links):
            met = dof_ref[j * links + k : j * links + k + 1, :]
            hit = jnp.broadcast_to(met, (LANES, LANES)) == lax.broadcasted_iota(jnp.int32, (LANES, LANES), 0)
            place = jnp.where(hit, lax.broadcasted_iota(jnp.int32, (LANES, LANES), 1), 0).astype(jnp.float32)
            found = jnp.sum(place.T, axis=0, keepdims=True)
            inverse_ref[j * links + k : j * links + k + 1, :] = found.astype(jnp.int32)
            alive = (j < info_ref[0]) & (partner_ref[k, j] < info_ref[1])
            mask_ref[j : j + 1, k * LANES : (k + 1) * LANES] = jnp.full((1, LANES), jnp.where(alive, 1.0, 0.0), jnp.float32)
    mask = mask_ref[...][:, None, :]
    r = right_ref[...] * mask
    z = weight_ref[...][:, None, :] * r
    r_ref[...] = r
    z_ref[...] = z
    norm_ref[...] = local_norm(r, z)
    start_exchange(
        z, partner_ref, inverse_ref, link_t_ref, prev_t_ref, map_ref, info_ref[2], corners, coarse_size,
        send_ref, mine_ref, other_ref,
    )


def gathered_scalars(blocks_ref, rows):
    total = jnp.sum(blocks_ref[...], axis=0)
    at = 2 * rows
    norm = jnp.concatenate([total[:, at : at + 1], total[:, at + 1 : at + 2]], axis=0)
    product = jnp.concatenate([total[:, at + 2 : at + 3], total[:, at + 3 : at + 4]], axis=0)
    return norm, product


def image_of(
    blocks_ref, rows, partner_ref, own_ref, facing_ref, dof_ref, mask_ref, link_ref, prev_ref, place_ref, corners
):
    slots, loads, width = own_ref.shape
    links = width // LANES
    devices, half, block = blocks_ref.shape
    flat = jnp.concatenate([blocks_ref[e] for e in range(devices)], axis=1)
    turned = jnp.concatenate([pltpu.roll(blocks_ref[e], block - rows, 1) for e in range(devices)], axis=1)
    everything = jnp.concatenate([flat, turned], axis=0)
    table = lax.broadcasted_iota(jnp.int32, (devices * block, place_ref.shape[1]), 0) == place_ref[...]
    picked = dot_pieces(everything, [table.astype(jnp.bfloat16)])
    near = own_ref[...] + from_corners(picked[:, :LANES], pieces(link_ref[...], 3), slots, corners)
    far_ref = from_corners(picked[:, LANES:], pieces(prev_ref[...], 3), slots, corners) + facing_ref[...]
    return near, far_ref


def next_kernel(
    corners, coarse_size, rows, first, last, info_ref, partner_ref, blocks_ref, own_ref, facing_ref, weight_ref, dof_ref,
    inverse_ref, mask_ref, link_ref, prev_ref, link_t_ref, prev_t_ref, map_ref, place_ref, r_ref, z_ref, *refs,
):
    refs = list(refs)
    if not first:
        x_ref, p_ref, s_ref, past_ref = refs[:4]
        refs = refs[4:]
    x_out, r_out = refs[:2]
    far_ref = refs[-1]
    slots, loads, width = own_ref.shape
    links = width // LANES
    norm, product = gathered_scalars(blocks_ref, rows)
    near, far = image_of(
        blocks_ref, rows, partner_ref, own_ref, facing_ref, dof_ref, mask_ref, link_ref, prev_ref, place_ref, corners
    )
    far_ref[...] = far
    jumps = []
    for j in range(slots):
        parts = []
        for k in range(links):
            block = far_ref[partner_ref[k, j], :, k * LANES : (k + 1) * LANES]
            index = jnp.broadcast_to(dof_ref[j * links + k][None], (loads, LANES))
            parts.append(jnp.take_along_axis(block, index, axis=1))
        jumps.append(jnp.concatenate(parts, axis=1)[None])
    mask = mask_ref[...][:, None, :]
    image = (near - jnp.concatenate(jumps, axis=0)) * mask
    if first:
        alpha = norm / product
        p, s = z_ref[...], image
        x = alpha[None] * p
    else:
        ratio = norm / past_ref[:, :1]
        alpha = norm / (product - ratio * norm / past_ref[:, 1:2])
        p = z_ref[...] + ratio[None] * p_ref[...]
        s = image + ratio[None] * s_ref[...]
        x = x_ref[...] + alpha[None] * p
    r = r_ref[...] - alpha[None] * s
    x_out[...] = x
    r_out[...] = r
    if last:
        return
    z_out, p_out, s_out, past_out, norm_out, send_ref, mine_ref, other_ref = refs[2:10]
    z = weight_ref[...][:, None, :] * r
    z_out[...] = z
    p_out[...] = p
    s_out[...] = s
    lane = lax.broadcasted_iota(jnp.int32, past_out.shape, 1)
    past_out[...] = jnp.where(lane == 0, norm, alpha)
    norm_out[...] = local_norm(r, z)
    start_exchange(
        z, partner_ref, inverse_ref, link_t_ref, prev_t_ref, map_ref, info_ref[2], corners, coarse_size,
        send_ref, mine_ref, other_ref,
    )


def flex_near_kernel(values_ref, flex_ref, out_ref):
    out_ref[0] = dot_pieces(values_ref[0], pieces(flex_ref[0], 2))


def flex_far_kernel(values_ref, forces_ref, begun_ref, flex_ref, own_ref, facing_ref, energy_ref):
    width = values_ref.shape[2]
    answer = begun_ref[0] + dot_pieces(forces_ref[0], pieces(flex_ref[0], 2))
    own, facing = answer[:, :width], answer[:, width:]
    own_ref[0] = own
    facing_ref[0] = facing
    work = jnp.sum(values_ref[0] * own + forces_ref[0] * facing, axis=1, keepdims=True)

    @pl.when(pl.program_id(0) == 0)
    def _():
        energy_ref[...] = jnp.zeros_like(energy_ref)

    energy_ref[...] += jnp.broadcast_to(work, energy_ref.shape)


def coarse_kernel(info_ref, mine_ref, other_ref, inverse_ref, energy_ref, norm_ref, out_ref):
    parity = info_ref[2]
    mine, other = mine_ref[...], other_ref[...]
    low, high = jnp.where(parity == 0, mine, other), jnp.where(parity == 0, other, mine)
    load = jnp.concatenate([low, high], axis=1)
    size, rows = inverse_ref.shape
    loads = load.shape[0]
    answer = dot_pieces(load, pieces(inverse_ref[...], 3))
    place = lax.broadcasted_iota(jnp.int32, (size, rows), 0) - info_ref[3] * rows
    chosen = (place == lax.broadcasted_iota(jnp.int32, (size, rows), 1)).astype(jnp.bfloat16)
    own = dot_pieces(load, [chosen])
    product = jnp.sum(answer * own, axis=1, keepdims=True) + energy_ref[:, :1]
    norm = norm_ref[:, :1]
    half = loads // 2
    tail = out_ref.shape[2] - 2 * rows - 4
    block = jnp.concatenate(
        [answer[:half], answer[half:], norm[:half], norm[half:], product[:half], product[half:], jnp.zeros((half, tail), jnp.float32)],
        axis=1,
    )
    out_ref[...] = jnp.broadcast_to(block[None], out_ref.shape)


VMEM = pl.BlockSpec(memory_space=pltpu.VMEM)
SMEM = pl.BlockSpec(memory_space=pltpu.SMEM)
LIMIT = 32 * 1024 * 1024


def shape_of(*dims, dtype=jnp.float32):
    return jax.ShapeDtypeStruct(dims, dtype)


def cost(flops, bytes_accessed):
    return pl.CostEstimate(flops=flops, bytes_accessed=bytes_accessed, transcendentals=0)


def local(
    flexibility,
    coupling,
    coarse_inverse,
    precon_weight,
    right_side,
    counts,
    partner,
    dof_index,
    corner_map,
):
    devices = lax.axis_size(BOTH)
    flex = flexibility[0, 0]
    slots, iface = flex.shape[:2]
    links, width = dof_index.shape[-2:]
    loads = right_side.shape[3]
    corners = corner_map.shape[-1]
    rows, coarse_size = coarse_inverse.shape
    span = links * width
    block = -(-(2 * rows + 4) // LANES) * LANES
    me = lax.axis_index("row") * lax.axis_size("col") + lax.axis_index("col")

    def padded(table):
        return jnp.pad(table.reshape(slots * corners, span), ((0, LANES - slots * corners), (0, 0)))

    own_map = corner_map[0, 0].reshape(1, -1)
    counts_prev = shifted(counts, "col", 1)
    map_prev = shifted(own_map, "col", 1)
    prev = shifted(padded(coupling[0, 0, :, :, span:]), "col", 1)
    link = padded(coupling[0, 0, :, :, :span])
    link_t, prev_t = link.T, prev.T
    pad = jnp.full((1, LANES - slots * corners), -1, jnp.int32)
    maps = jnp.concatenate([own_map, pad, map_prev, pad], axis=1)
    place = jnp.where(maps >= 0, (maps // rows) * block + maps % rows, -1)
    map_column = maps.reshape(-1, 1)
    info = jnp.stack([counts[0, 0], counts_prev[0, 0], lax.axis_index("col") % 2, me]).astype(jnp.int32)
    partners = partner[0, 0]
    dof = dof_index[0, 0].reshape(slots * links, width)
    weight = precon_weight[0, 0].reshape(slots, span)
    right = right_side[0, 0].reshape(slots, loads, span)
    inverse_t = coarse_inverse.T

    state = shape_of(slots, loads, span)
    small = shape_of(loads, LANES)
    half_load = shape_of(loads, coarse_size // 2)
    params = pltpu.CompilerParams(vmem_limit_bytes=LIMIT)

    dof_inverse, mask, r, z, norm, send, mine, other = pl.pallas_call(
        functools.partial(first_kernel, corners, coarse_size),
        out_shape=(shape_of(slots * links, width, dtype=jnp.int32), shape_of(slots, span), state, state, small, state, half_load, half_load),
        in_specs=[SMEM, SMEM] + [VMEM] * 6,
        out_specs=[VMEM] * 8,
        compiler_params=params,
        name="first",
    )(info, partners, right, weight, dof, link_t, prev_t, map_column)

    kept = ()
    for iteration in range(ITERS):
        first, last = iteration == 0, iteration + 1 == ITERS
        forces = shifted(send, "col", -1)
        begun = pl.pallas_call(
            flex_near_kernel,
            grid=(slots,),
            out_shape=shape_of(slots, loads, iface),
            in_specs=[
                pl.BlockSpec((1, loads, span), lambda s: (s, 0, 0)),
                pl.BlockSpec((1, span, iface), lambda s: (s, 0, 0)),
            ],
            out_specs=pl.BlockSpec((1, loads, iface), lambda s: (s, 0, 0)),
            compiler_params=params,
            cost_estimate=cost(2 * slots * loads * span * iface * 6, slots * span * iface * 4),
            name="flex_near",
        )(z, flex)
        total = mine + swapped(other, 1)
        bit = 2
        order = []
        while bit < devices:
            order.append(bit)
            bit *= 2
        columns = lax.axis_size("col")
        order = [b for b in order if b >= columns] + [b for b in order if b < columns]
        for b in order:
            total = total + swapped(total, b)
        rest = swapped(total, 1)
        own, facing, energy = pl.pallas_call(
            flex_far_kernel,
            grid=(slots,),
            out_shape=(state, state, small),
            in_specs=[
                pl.BlockSpec((1, loads, span), lambda s: (s, 0, 0)),
                pl.BlockSpec((1, loads, span), lambda s: (s, 0, 0)),
                pl.BlockSpec((1, loads, iface), lambda s: (s, 0, 0)),
                pl.BlockSpec((1, span, iface), lambda s: (s, 1, 0)),
            ],
            out_specs=[
                pl.BlockSpec((1, loads, span), lambda s: (s, 0, 0)),
                pl.BlockSpec((1, loads, span), lambda s: (s, 0, 0)),
                pl.BlockSpec((loads, LANES), lambda s: (0, 0)),
            ],
            compiler_params=params,
            cost_estimate=cost(2 * slots * loads * span * iface * 6, slots * span * iface * 4),
            name="flex_far",
        )(z, forces, begun, flex)
        facing_prev = shifted(facing, "col", 1)
        blocks = pl.pallas_call(
            coarse_kernel,
            out_shape=shape_of(devices, loads // 2, block),
            in_specs=[SMEM] + [VMEM] * 5,
            out_specs=VMEM,
            compiler_params=params,
            name="coarse",
        )(info, total, rest, inverse_t, energy, norm)
        blocks = lax.all_to_all(blocks, BOTH, 0, 0, tiled=True)
        outs = (state, state)
        if not last:
            outs = outs + (state, state, state, small, small, state, half_load, half_load)
        results = pl.pallas_call(
            functools.partial(next_kernel, corners, coarse_size, rows, first, last),
            out_shape=outs,
            in_specs=[SMEM, SMEM] + [VMEM] * (15 + len(kept)),
            out_specs=[VMEM] * len(outs),
            scratch_shapes=[pltpu.VMEM((slots, loads, span), jnp.float32)],
            compiler_params=params,
            name="step",
        )(
            info, partners, blocks, own, facing_prev, weight, dof, dof_inverse, mask, link, prev, link_t, prev_t,
            map_column, place, r, z, *kept,
        )
        if last:
            x, r = results
        else:
            x, r, z, p, s, past, norm, send, mine, other = results
            kept = (x, p, s, past)
    shape = right_side.shape
    return (x.reshape(shape), r.reshape(shape))


def solution(mesh):
    in_specs = (
        P("row", "col", None, None, None),
        P("row", "col", None, None, None),
        P(("row", "col"), None),
        P("row", "col", None, None, None),
        P("row", "col", None, None, None, None),
        P("row", "col"),
        P("row", "col", None, None),
        P("row", "col", None, None, None),
        P("row", "col", None, None),
    )
    out_specs = (P("row", "col", None, None, None, None), P("row", "col", None, None, None, None))
    return jax.shard_map(local, mesh=mesh, in_specs=in_specs, out_specs=out_specs, check_vma=False)
```

time: 691 us -> 164 us (0.24)
  waiting for transfers between devices: 338 us -> 71.7 us
  blocking collectives: 238 us -> 0 us
  matrix products: 83 us -> 0 us
  Pallas kernels: 0 us -> 30.1 us
  local copies, waits for them, and re-layouts: 5.06 us -> 32.9 us
  starting transfers between devices: 6.6 us -> 25.7 us
  between operations: 14.8 us -> 1.6 us
    psum x3 -> x0, waiting for transfers between devices: 306 us -> none  [coarse_solve(): total_load = lax.psum(local_load, ('row', 'col'))]
    all_gather x3 -> x0, blocking collectives: 127 us -> none  [coarse_solve(): return lax.all_gather(own_rows, ('row', 'col'), axis=1, tiled=True)]
    psum x3 -> x0, blocking collectives: 111 us -> none  [both_sums(): lax.psum((local_inner(resid_now, precond_now), local_inner(precond_now, i...]
    dot_general x31 -> x0, matrix products: 83 us -> none  [the longest x3 60.1 us: apply_operator(): answer = jnp.einsum('sab,sqb->sqa', flex_local, force_full, precision=HIGH)]
    ppermute x0 -> x18, waiting for transfers between devices: none -> 43.8 us  [swapped(): return lax.ppermute(x, BOTH, [(i, i ^ bit) for i in range(devices)])]
    pallas_call x0 -> x13, Pallas kernels: none -> 30.1 us  [the longest x3 8.42 us: local(): pl.pallas_call(flex_far_kernel, grid=(slots,), out_shape=(state, state, s...]
    unnamed x21 -> x29, local copies, waits for them, and re-layouts: 2.54 us -> 28 us
    ppermute x0 -> x18, starting transfers between devices: none -> 11.6 us  [swapped(): return lax.ppermute(x, BOTH, [(i, i ^ bit) for i in range(devices)])]
  transfers between devices with their start and end apart: 11 -> 30, of which waited for: 10 -> 19; matrix products, arithmetic and copies ran while one was open for 9% -> 4% of each run, Pallas kernels for 0% -> 10%
where the time goes in v1:
time: 164 us
  waiting for transfers between devices  71.7 us (44%)
  local copies, waits for them, and re-layouts  32.9 us (20%)
  Pallas kernels  30.1 us (18%)
  starting transfers between devices  25.7 us (16%)
    ppermute x18, waiting for transfers between devices, swapped(): return lax.ppermute(x, BOTH, [(i, i ^ bit) for i in range(devices)])  43.8 us
    unnamed x29, local copies, waits for them, and re-layouts  28 us
    ppermute x9, waiting for transfers between devices, shifted(): lax.ppermute(x, axis, [(i, (i + by) % devices) for i in range(devices)])  27.9 us
    ppermute x18, starting transfers between devices, swapped(): return lax.ppermute(x, BOTH, [(i, i ^ bit) for i in range(devices)])  11.6 us
    all_to_all x3, starting transfers between devices, local(): blocks = lax.all_to_all(blocks, BOTH, 0, 0, tiled=True)  9.94 us
    pallas_call x3, Pallas kernels, local(): pl.pallas_call(flex_far_kernel, grid=(slots,), out_shape=(state, state, s...  8.42 us
    pallas_call x3, Pallas kernels, local(): pl.pallas_call(functools.partial(next_kernel, corners, coarse_size, rows,...  7.42 us
    pallas_call x3, Pallas kernels, local(): pl.pallas_call(flex_near_kernel, grid=(slots,), out_shape=shape_of(slots,...  7.16 us
  transfers between devices with their start and end apart: 30, of which 19 were waited for; matrix products, arithmetic and copies ran while one was open for 4% of the time, Pallas kernels for 10%

profile of v1, /device:TPU:0, one launch (start us, length us, event | category | flops | bytes accessed | tf_op | source)
XLA Modules:
  0.0 163.6 jit_solution(10741425946141906584)
XLA Ops:
  1.9 2.7 %collective-permute-start = (s32[1,1]{1,0:T(1,128)}, s32[1,1]{1,0:T(1,128)}, u32[]{:S(2)}, u32[]{:S(2)}) collective-permute-start(s32[1,1]{1,0:T(1,128)} %param.14), channel_id=1, source_target_pairs={{0,1},{1,2},{2,3},{3,4},{4,5},{5,6},{6,7},{7,0},{8,9},{9,10},{10,1... | collective-permute-start | bytes 20 | tf_op jit(solution)/shard_map/ppermute | solution.py:16
  4.5 1.1 fusion.1
  8.1 1.0 reshape_squeeze.18.right_ref
  10.1 3.4 %collective-permute-done.1 = f32[128,512]{0,1:T(8,128)S(1)} collective-permute-done((f32[128,512]{0,1:T(8,128)S(1)}, f32[128,512]{0,1:T(8,128)S(1)}, u32[]{:S(2)}, u32[]{:S(2)}) %collective-permute-start.1) | collective-permute-done | bytes 262176 | tf_op jit(solution)/shard_map/ppermute | solution.py:16
  14.1 1.7 %first.1 = (s32[20,128]{1,0:T(8,128)S(1)}, f32[5,512]{1,0:T(8,128)S(1)}, f32[5,16,512]{2,1,0:T(8,128)S(1)}, f32[5,16,512]{2,1,0:T(8,128)S(1)}, f32[16,128]{1,0:T...) custom-call(s32[4]{0:T(128)S(1)} %pad_add_fusion.1.info_ref, ...), custom_call_target="tpu_custom_call" | custom-call | tf_op jit(solution)/shard_map/first/pallas_call | solution.py:311
  15.9 1.2 collective-permute-done.3
  17.1 1.6 collective-permute-start.4
  18.7 2.6 %collective-permute-done.4 = f32[16,768]{1,0:T(8,128)S(1)} collective-permute-done((f32[16,768]{1,0:T(8,128)S(1)}, f32[16,768]{1,0:T(8,128)S(1)}, u32[]{:S(2)}, u32[]{:S(2)}) %collective-permute-start.4) | collective-permute-done | bytes 49184 | tf_op jit(solution)/shard_map/ppermute | solution.py:21
  21.3 1.6 collective-permute-start.5
  22.9 2.6 %collective-permute-done.5 = f32[16,768]{1,0:T(8,128)S(1)} collective-permute-done((f32[16,768]{1,0:T(8,128)S(1)}, f32[16,768]{1,0:T(8,128)S(1)}, u32[]{:S(2)}, u32[]{:S(2)}) %collective-permute-start.5) | collective-permute-done | bytes 49184 | tf_op jit(solution)/shard_map/ppermute | solution.py:21
  25.5 4.1 %collective-permute-done.6 = f32[16,768]{1,0:T(8,128)S(1)} collective-permute-done((f32[16,768]{1,0:T(8,128)S(1)}, f32[16,768]{1,0:T(8,128)S(1)}, u32[]{:S(2)}, u32[]{:S(2)}) %collective-permute-start.6) | collective-permute-done | bytes 49184 | tf_op jit(solution)/shard_map/ppermute | solution.py:21
  30.4 1.2 copy.23
  31.7 3.0 %collective-permute-done.7 = f32[16,768]{1,0:T(8,128)S(1)} collective-permute-done((f32[16,768]{1,0:T(8,128)S(1)}, f32[16,768]{1,0:T(8,128)S(1)}, u32[]{:S(2)}, u32[]{:S(2)}) %collective-permute-start.7) | collective-permute-done | bytes 49184 | tf_op jit(solution)/shard_map/ppermute | solution.py:21
  34.7 7.0 %copy-done = f32[1,1,5,1024,1024]{4,3,2,1,0:T(8,128)S(1)} copy-done((f32[1,1,5,1024,1024]{4,3,2,1,0:T(8,128)S(1)}, f32[1,1,5,1024,1024]{4,3,2,1,0:T(8,128)}, u32[]{:S(2)}) %copy-start) | copy-done | bytes 20971544
  41.7 2.4 %flex_near.3.begun_ref = f32[5,16,1024]{2,1,0:T(8,128)S(1)} custom-call(f32[5,16,512]{2,1,0:T(8,128)S(1)} %get-tuple-element.43.values_ref.z_ref, f32[5,1024,1024]{2,1,0:T(8,128)S(1)} %bitcast.19), custom_call_target="tpu_custom_call" | custom-call | flops 503316480 | bytes 10485760 | tf_op jit(solution)/shard_map/flex_near/pallas_call | solution.py:324
  44.1 2.8 %flex_far.3 = (f32[5,16,512]{2,1,0:T(8,128)S(1)}, f32[5,16,512]{2,1,0:T(8,128)S(1)}, f32[16,128]{1,0:T(8,128)S(1)}) custom-call(f32[5,16,512]{2,1,0:T(8,128)S(1)} %get-tuple-element.43.values_ref.z_ref, f32[5,16,512]{2,1,0:T(8,128)S(1)} %collective-permute-done.9.forces_ref, f32[5,16,1024]{2,1,0:T(8,128)S(1)} %flex_near.3.begun_ref, ...), custom_call_target="tpu_custom_call" | custom-call | flops 503316480 | bytes 10485760 | tf_op jit(solution)/shard_map/flex_far/pallas_call | solution.py:348
  46.9 1.8 %coarse.3 = f32[32,8,128]{2,1,0:T(8,128)} custom-call(s32[4]{0:T(128)S(1)} %pad_add_fusion.1.info_ref, f32[16,768]{1,0:T(8,128)S(1)} %add.96.mine_ref, f32[16,768]{1,0:T(8,128)S(1)} %collective-permute-done.8.other_ref, f32[1536,48]{1,0:T(8,128)S(1)} %bitcast.25, f32[16,128]{1,0:T(8,128)S(1)} %get-tuple-element.45.energy_ref, ...), custom_call_target="tpu_custom_call" | custom-call | tf_op jit(solution)/shard_map/coarse/pallas_call | solution.py:368
  48.7 3.6 %all-to-all-start = ((f32[32,8,128]{2,1,0:T(8,128)}), f32[32,8,128]{2,1,0:T(8,128)S(1)}, u32[]{:S(2)}, u32[]{:S(2)}) async-start(f32[32,8,128]{2,1,0:T(8,128)} %coarse.3), calls=%async_computation | async-start | bytes 262144 | tf_op jit(solution)/shard_map/all_to_all | solution.py:376
  52.9 8.0 %collective-permute-done.10.facing_ref = f32[5,16,512]{2,1,0:T(8,128)S(1)} collective-permute-done((f32[5,16,512]{2,1,0:T(8,128)S(1)}, f32[5,16,512]{2,1,0:T(8,128)S(1)}, u32[]{:S(2)}, u32[]{:S(2)}) %collective-permute-start.10) | collective-permute-done | bytes 163872 | tf_op jit(solution)/shard_map/ppermute | solution.py:16
  60.9 2.6 %step.3 = (f32[5,16,512]{2,1,0:T(8,128)S(1)}, f32[5,16,512]{2,1,0:T(8,128)S(1)}, f32[5,16,512]{2,1,0:T(8,128)S(1)}, f32[5,16,512]{2,1,0:T(8,128)S(1)}, f32[5,16,...) custom-call(s32[4]{0:T(128)S(1)} %pad_add_fusion.1.info_ref, ...), custom_call_target="tpu_custom_call" | custom-call | tf_op jit(solution)/shard_map/step/pallas_call | solution.py:380
  65.0 1.5 collective-permute-start.12
  66.5 2.6 %collective-permute-done.12 = f32[16,768]{1,0:T(8,128)S(1)} collective-permute-done((f32[16,768]{1,0:T(8,128)S(1)}, f32[16,768]{1,0:T(8,128)S(1)}, u32[]{:S(2)}, u32[]{:S(2)}) %collective-permute-start.12) | collective-permute-done | bytes 49184 | tf_op jit(solution)/shard_map/ppermute | solution.py:21
  69.1 1.5 collective-permute-start.13
  70.6 2.6 %collective-permute-done.13 = f32[16,768]{1,0:T(8,128)S(1)} collective-permute-done((f32[16,768]{1,0:T(8,128)S(1)}, f32[16,768]{1,0:T(8,128)S(1)}, u32[]{:S(2)}, u32[]{:S(2)}) %collective-permute-start.13) | collective-permute-done | bytes 49184 | tf_op jit(solution)/shard_map/ppermute | solution.py:21
  73.5 3.9 %collective-permute-done.14 = f32[16,768]{1,0:T(8,128)S(1)} collective-permute-done((f32[16,768]{1,0:T(8,128)S(1)}, f32[16,768]{1,0:T(8,128)S(1)}, u32[]{:S(2)}, u32[]{:S(2)}) %collective-permute-start.14) | collective-permute-done | bytes 49184 | tf_op jit(solution)/shard_map/ppermute | solution.py:21
  77.6 5.0 %collective-permute-done.15 = f32[16,768]{1,0:T(8,128)S(1)} collective-permute-done((f32[16,768]{1,0:T(8,128)S(1)}, f32[16,768]{1,0:T(8,128)S(1)}, u32[]{:S(2)}, u32[]{:S(2)}) %collective-permute-start.15) | collective-permute-done | bytes 49184 | tf_op jit(solution)/shard_map/ppermute | solution.py:21
  82.7 7.0 %copy-done.1 = f32[1,1,5,1024,1024]{4,3,2,1,0:T(8,128)S(1)} copy-done((f32[1,1,5,1024,1024]{4,3,2,1,0:T(8,128)S(1)}, f32[1,1,5,1024,1024]{4,3,2,1,0:T(8,128)}, u32[]{:S(2)}) %copy-start.1) | copy-done | bytes 20971544
  89.7 2.4 %flex_near.4.begun_ref = f32[5,16,1024]{2,1,0:T(8,128)S(1)} custom-call(f32[5,16,512]{2,1,0:T(8,128)S(1)} %get-tuple-element.54.values_ref.z_ref, f32[5,1024,1024]{2,1,0:T(8,128)S(1)} %bitcast.21), custom_call_target="tpu_custom_call" | custom-call | flops 503316480 | bytes 10485760 | tf_op jit(solution)/shard_map/flex_near/pallas_call | solution.py:324
  92.0 2.8 %flex_far.4 = (f32[5,16,512]{2,1,0:T(8,128)S(1)}, f32[5,16,512]{2,1,0:T(8,128)S(1)}, f32[16,128]{1,0:T(8,128)S(1)}) custom-call(f32[5,16,512]{2,1,0:T(8,128)S(1)} %get-tuple-element.54.values_ref.z_ref, f32[5,16,512]{2,1,0:T(8,128)S(1)} %collective-permute-done.17.forces_ref, f32[5,16,1024]{2,1,0:T(8,128)S(1)} %flex_near.4.begun_ref, ...), custom_call_target="tpu_custom_call" | custom-call | flops 503316480 | bytes 10485760 | tf_op jit(solution)/shard_map/flex_far/pallas_call | solution.py:348
  94.9 1.8 %coarse.4 = f32[32,8,128]{2,1,0:T(8,128)} custom-call(s32[4]{0:T(128)S(1)} %pad_add_fusion.1.info_ref, f32[16,768]{1,0:T(8,128)S(1)} %add.103.mine_ref, f32[16,768]{1,0:T(8,128)S(1)} %collective-permute-done.16.other_ref, f32[1536,48]{1,0:T(8,128)S(1)} %bitcast.26, f32[16,128]{1,0:T(8,128)S(1)} %get-tuple-element.56.energy_ref, ...), custom_call_target="tpu_custom_call" | custom-call | tf_op jit(solution)/shard_map/coarse/pallas_call | solution.py:368
  96.7 3.1 %all-to-all-start.1 = ((f32[32,8,128]{2,1,0:T(8,128)}), f32[32,8,128]{2,1,0:T(8,128)S(1)}, u32[]{:S(2)}, u32[]{:S(2)}) async-start(f32[32,8,128]{2,1,0:T(8,128)} %coarse.4), calls=%async_computation.1 | async-start | bytes 262144 | tf_op jit(solution)/shard_map/all_to_all | solution.py:376
  100.1 8.3 %collective-permute-done.18.facing_ref = f32[5,16,512]{2,1,0:T(8,128)S(1)} collective-permute-done((f32[5,16,512]{2,1,0:T(8,128)S(1)}, f32[5,16,512]{2,1,0:T(8,128)S(1)}, u32[]{:S(2)}, u32[]{:S(2)}) %collective-permute-start.18) | collective-permute-done | bytes 163872 | tf_op jit(solution)/shard_map/ppermute | solution.py:16
  109.0 0.9 copy-done.4
  112.7 2.6 %step.4 = (f32[5,16,512]{2,1,0:T(8,128)S(1)}, f32[5,16,512]{2,1,0:T(8,128)S(1)}, f32[5,16,512]{2,1,0:T(8,128)S(1)}, f32[5,16,512]{2,1,0:T(8,128)S(1)}, f32[5,16,...) custom-call(s32[4]{0:T(128)S(1)} %pad_add_fusion.1.info_ref, ...), custom_call_target="tpu_custom_call" | custom-call | tf_op jit(solution)/shard_map/step/pallas_call | solution.py:380
  115.4 1.2 collective-permute-done.19
  116.6 1.5 collective-permute-start.20
  118.2 2.6 %collective-permute-done.20 = f32[16,768]{1,0:T(8,128)S(1)} collective-permute-done((f32[16,768]{1,0:T(8,128)S(1)}, f32[16,768]{1,0:T(8,128)S(1)}, u32[]{:S(2)}, u32[]{:S(2)}) %collective-permute-start.20) | collective-permute-done | bytes 49184 | tf_op jit(solution)/shard_map/ppermute | solution.py:21
  120.8 1.6 collective-permute-start.21
  122.4 2.6 %collective-permute-done.21 = f32[16,768]{1,0:T(8,128)S(1)} collective-permute-done((f32[16,768]{1,0:T(8,128)S(1)}, f32[16,768]{1,0:T(8,128)S(1)}, u32[]{:S(2)}, u32[]{:S(2)}) %collective-permute-start.21) | collective-permute-done | bytes 49184 | tf_op jit(solution)/shard_map/ppermute | solution.py:21
  125.0 4.1 %collective-permute-done.22 = f32[16,768]{1,0:T(8,128)S(1)} collective-permute-done((f32[16,768]{1,0:T(8,128)S(1)}, f32[16,768]{1,0:T(8,128)S(1)}, u32[]{:S(2)}, u32[]{:S(2)}) %collective-permute-start.22) | collective-permute-done | bytes 49184 | tf_op jit(solution)/shard_map/ppermute | solution.py:21
  129.3 4.8 %collective-permute-done.23 = f32[16,768]{1,0:T(8,128)S(1)} collective-permute-done((f32[16,768]{1,0:T(8,128)S(1)}, f32[16,768]{1,0:T(8,128)S(1)}, u32[]{:S(2)}, u32[]{:S(2)}) %collective-permute-start.23) | collective-permute-done | bytes 49184 | tf_op jit(solution)/shard_map/ppermute | solution.py:21
  134.3 7.0 %copy-done.2 = f32[1,1,5,1024,1024]{4,3,2,1,0:T(8,128)S(1)} copy-done((f32[1,1,5,1024,1024]{4,3,2,1,0:T(8,128)S(1)}, f32[1,1,5,1024,1024]{4,3,2,1,0:T(8,128)}, u32[]{:S(2)}) %copy-start.2) | copy-done | bytes 20971544
  141.2 2.4 %flex_near.5.begun_ref = f32[5,16,1024]{2,1,0:T(8,128)S(1)} custom-call(f32[5,16,512]{2,1,0:T(8,128)S(1)} %get-tuple-element.67.values_ref.z_ref, f32[5,1024,1024]{2,1,0:T(8,128)S(1)} %bitcast.23), custom_call_target="tpu_custom_call" | custom-call | flops 503316480 | bytes 10485760 | tf_op jit(solution)/shard_map/flex_near/pallas_call | solution.py:324
  143.6 2.8 %flex_far.5 = (f32[5,16,512]{2,1,0:T(8,128)S(1)}, f32[5,16,512]{2,1,0:T(8,128)S(1)}, f32[16,128]{1,0:T(8,128)S(1)}) custom-call(f32[5,16,512]{2,1,0:T(8,128)S(1)} %get-tuple-element.67.values_ref.z_ref, f32[5,16,512]{2,1,0:T(8,128)S(1)} %collective-permute-done.25.forces_ref, f32[5,16,1024]{2,1,0:T(8,128)S(1)} %flex_near.5.begun_ref, ...), custom_call_target="tpu_custom_call" | custom-call | flops 503316480 | bytes 10485760 | tf_op jit(solution)/shard_map/flex_far/pallas_call | solution.py:348
  146.4 1.8 %coarse.5 = f32[32,8,128]{2,1,0:T(8,128)} custom-call(s32[4]{0:T(128)S(1)} %pad_add_fusion.1.info_ref, f32[16,768]{1,0:T(8,128)S(1)} %add.108.mine_ref, f32[16,768]{1,0:T(8,128)S(1)} %collective-permute-done.24.other_ref, f32[1536,48]{1,0:T(8,128)S(1)} %bitcast.27, f32[16,128]{1,0:T(8,128)S(1)} %get-tuple-element.69.energy_ref, ...), custom_call_target="tpu_custom_call" | custom-call | tf_op jit(solution)/shard_map/coarse/pallas_call | solution.py:368
  148.2 3.2 %all-to-all-start.2 = ((f32[32,8,128]{2,1,0:T(8,128)}), f32[32,8,128]{2,1,0:T(8,128)S(1)}, u32[]{:S(2)}, u32[]{:S(2)}) async-start(f32[32,8,128]{2,1,0:T(8,128)} %coarse.5), calls=%async_computation.2 | async-start | bytes 262144 | tf_op jit(solution)/shard_map/all_to_all | solution.py:376
  151.8 8.3 %collective-permute-done.26.facing_ref = f32[5,16,512]{2,1,0:T(8,128)S(1)} collective-permute-done((f32[5,16,512]{2,1,0:T(8,128)S(1)}, f32[5,16,512]{2,1,0:T(8,128)S(1)}, u32[]{:S(2)}, u32[]{:S(2)}) %collective-permute-start.26) | collective-permute-done | bytes 163872 | tf_op jit(solution)/shard_map/ppermute | solution.py:16
  160.0 2.1 %step.5 = (f32[5,16,512]{2,1,0:T(8,128)S(1)}, f32[5,16,512]{2,1,0:T(8,128)S(1)}) custom-call(s32[4]{0:T(128)S(1)} %pad_add_fusion.1.info_ref, s32[4,5]{1,0:T(4,128)S(1)} %bitcast.39, f32[32,8,128]{2,1,0:T(8,128)S(1)} %all-to-all-done.2.blocks_ref, f32[5,16,512]{2,1,0:T(8,128)S(1)} %get-tuple-element.71.own_ref, ...), custom_call_target="tpu_custom_call" | custom-call | tf_op jit(solution)/shard_map/step/pallas_call | solution.py:380
  (86 shorter events, 14.1 us)
Async XLA Ops:
  1.4 8.4 %collective-permute-start.2 = (s32[1,120]{1,0:T(1,128)S(1)}, s32[1,120]{1,0:T(1,128)S(1)}, u32[]{:S(2)}, u32[]{:S(2)}) collective-permute-start(s32[1,120]{1,0:T(1,128)S(1)} %reshape_squeeze.23), channel_id=1, source_target_pairs={{0,1},{1,2},{2,3},{3,4},{4,5},{5,6},{6,7},{7,0},{8,9},{9,10},{10,1... | collective-permute-start | bytes 1448 | tf_op jit(solution)/shard_map/ppermute | solution.py:16
  1.9 7.3 %collective-permute-start = (s32[1,1]{1,0:T(1,128)}, s32[1,1]{1,0:T(1,128)}, u32[]{:S(2)}, u32[]{:S(2)}) collective-permute-start(s32[1,1]{1,0:T(1,128)} %param.14), channel_id=1, source_target_pairs={{0,1},{1,2},{2,3},{3,4},{4,5},{5,6},{6,7},{7,0},{8,9},{9,10},{10,1... | collective-permute-start | bytes 20 | tf_op jit(solution)/shard_map/ppermute | solution.py:16
  5.8 7.6 %collective-permute-start.1 = (f32[128,512]{0,1:T(8,128)S(1)}, f32[128,512]{0,1:T(8,128)S(1)}, u32[]{:S(2)}, u32[]{:S(2)}) collective-permute-start(f32[128,512]{0,1:T(8,128)S(1)} %pad.8), channel_id=1, source_target_pairs={{0,1},{1,2},{2,3},{3,4},{4,5},{5,6},{6,7},{7,0},{8,9},{9,10},{10,1... | collective-permute-start | bytes 786440 | tf_op jit(solution)/shard_map/ppermute | solution.py:16
  13.5 0.7 copy-start.11
  15.8 1.3 collective-permute-start.3
  17.1 4.2 %collective-permute-start.4 = (f32[16,768]{1,0:T(8,128)S(1)}, f32[16,768]{1,0:T(8,128)S(1)}, u32[]{:S(2)}, u32[]{:S(2)}) collective-permute-start(f32[16,768]{1,0:T(8,128)S(1)} %add.92), channel_id=1, source_target_pairs={{0,8},{1,9},{2,10},{3,11},{4,12},{5,13},{6,14},{7,15},{8,0},{9,1},... | collective-permute-start | bytes 147464 | tf_op jit(solution)/shard_map/ppermute | solution.py:21
  21.3 4.1 %collective-permute-start.5 = (f32[16,768]{1,0:T(8,128)S(1)}, f32[16,768]{1,0:T(8,128)S(1)}, u32[]{:S(2)}, u32[]{:S(2)}) collective-permute-start(f32[16,768]{1,0:T(8,128)S(1)} %add.93), channel_id=1, source_target_pairs={{0,16},{1,17},{2,18},{3,19},{4,20},{5,21},{6,22},{7,23},{8,24},{9,... | collective-permute-start | bytes 147464 | tf_op jit(solution)/shard_map/ppermute | solution.py:21
  22.8 21.2 %collective-permute-start.9 = (f32[5,16,512]{2,1,0:T(8,128)S(1)}, f32[5,16,512]{2,1,0:T(8,128)S(1)}, u32[]{:S(2)}, u32[]{:S(2)}) collective-permute-start(f32[5,16,512]{2,1,0:T(8,128)S(1)} %get-tuple-element.44), channel_id=1, source_target_pairs={{0,7},{1,0},{2,1},{3,2},{4,3},{5,4},{6,5},{7,6},{8,15},{9,8},{10,9... | collective-permute-start | bytes 491528 | tf_op jit(solution)/shard_map/ppermute | solution.py:16
  25.4 4.1 %collective-permute-start.6 = (f32[16,768]{1,0:T(8,128)S(1)}, f32[16,768]{1,0:T(8,128)S(1)}, u32[]{:S(2)}, u32[]{:S(2)}) collective-permute-start(f32[16,768]{1,0:T(8,128)S(1)} %add.94), channel_id=1, source_target_pairs={{0,2},{1,3},{2,0},{3,1},{4,6},{5,7},{6,4},{7,5},{8,10},{9,11},{10,... | collective-permute-start | bytes 147464 | tf_op jit(solution)/shard_map/ppermute | solution.py:21
  29.6 5.0 %collective-permute-start.7 = (f32[16,768]{1,0:T(8,128)S(1)}, f32[16,768]{1,0:T(8,128)S(1)}, u32[]{:S(2)}, u32[]{:S(2)}) collective-permute-start(f32[16,768]{1,0:T(8,128)S(1)} %add.95), channel_id=1, source_target_pairs={{0,4},{1,5},{2,6},{3,7},{4,0},{5,1},{6,2},{7,3},{8,12},{9,13},{10,... | collective-permute-start | bytes 147464 | tf_op jit(solution)/shard_map/ppermute | solution.py:21
  34.6 12.2 %collective-permute-start.8 = (f32[16,768]{1,0:T(8,128)S(1)}, f32[16,768]{1,0:T(8,128)S(1)}, u32[]{:S(2)}, u32[]{:S(2)}) collective-permute-start(f32[16,768]{1,0:T(8,128)S(1)} %add.96.mine_ref), channel_id=1, source_target_pairs={{0,1},{1,0},{2,3},{3,2},{4,5},{5,4},{6,7},{7,6},{8,9},{9,8},{10,11... | collective-permute-start | bytes 147464 | tf_op jit(solution)/shard_map/ppermute | solution.py:21
  34.7 7.0 %copy-start = (f32[1,1,5,1024,1024]{4,3,2,1,0:T(8,128)S(1)}, f32[1,1,5,1024,1024]{4,3,2,1,0:T(8,128)}, u32[]{:S(2)}) copy-start(f32[1,1,5,1024,1024]{4,3,2,1,0:T(8,128)} %param.9) | copy-start | bytes 62914564
  41.7 19.2 %copy-start.12 = (s32[1,1,4,5]{3,2,1,0:T(4,128)S(1)}, s32[1,1,4,5]{3,2,1,0:T(4,128)}, u32[]{:S(2)}) copy-start(s32[1,1,4,5]{3,2,1,0:T(4,128)} %param.15) | copy-start | bytes 244
  48.7 12.2 %all-to-all-start = ((f32[32,8,128]{2,1,0:T(8,128)}), f32[32,8,128]{2,1,0:T(8,128)S(1)}, u32[]{:S(2)}, u32[]{:S(2)}) async-start(f32[32,8,128]{2,1,0:T(8,128)} %coarse.3), calls=%async_computation | async-start | bytes 262144 | tf_op jit(solution)/shard_map/all_to_all | solution.py:376
  52.3 8.6 %collective-permute-start.10 = (f32[5,16,512]{2,1,0:T(8,128)S(1)}, f32[5,16,512]{2,1,0:T(8,128)S(1)}, u32[]{:S(2)}, u32[]{:S(2)}) collective-permute-start(f32[5,16,512]{2,1,0:T(8,128)S(1)} %get-tuple-element.48), channel_id=1, source_target_pairs={{0,1},{1,2},{2,3},{3,4},{4,5},{5,6},{6,7},{7,0},{8,9},{9,10},{10,1... | collective-permute-start | bytes 491528 | tf_op jit(solution)/shard_map/ppermute | solution.py:16
  63.6 19.1 %copy-start.3 = (f32[5,16,512]{2,1,0:T(8,128)}, f32[5,16,512]{2,1,0:T(8,128)S(1)}, u32[]{:S(2)}) copy-start(f32[5,16,512]{2,1,0:T(8,128)S(1)} %get-tuple-element.62.refs_1_) | copy-start | bytes 491524
  63.6 19.1 %copy-start.5 = (f32[5,16,512]{2,1,0:T(8,128)}, f32[5,16,512]{2,1,0:T(8,128)S(1)}, u32[]{:S(2)}) copy-start(f32[5,16,512]{2,1,0:T(8,128)S(1)} %get-tuple-element.63.refs_2_) | copy-start | bytes 491524
  63.6 1.3 collective-permute-start.11
  65.0 4.1 %collective-permute-start.12 = (f32[16,768]{1,0:T(8,128)S(1)}, f32[16,768]{1,0:T(8,128)S(1)}, u32[]{:S(2)}, u32[]{:S(2)}) collective-permute-start(f32[16,768]{1,0:T(8,128)S(1)} %add.99), channel_id=1, source_target_pairs={{0,8},{1,9},{2,10},{3,11},{4,12},{5,13},{6,14},{7,15},{8,0},{9,1},... | collective-permute-start | bytes 147464 | tf_op jit(solution)/shard_map/ppermute | solution.py:21
  69.1 4.2 %collective-permute-start.13 = (f32[16,768]{1,0:T(8,128)S(1)}, f32[16,768]{1,0:T(8,128)S(1)}, u32[]{:S(2)}, u32[]{:S(2)}) collective-permute-start(f32[16,768]{1,0:T(8,128)S(1)} %add.100), channel_id=1, source_target_pairs={{0,16},{1,17},{2,18},{3,19},{4,20},{5,21},{6,22},{7,23},{8,24},{9,... | collective-permute-start | bytes 147464 | tf_op jit(solution)/shard_map/ppermute | solution.py:21
  70.6 21.4 %collective-permute-start.17 = (f32[5,16,512]{2,1,0:T(8,128)S(1)}, f32[5,16,512]{2,1,0:T(8,128)S(1)}, u32[]{:S(2)}, u32[]{:S(2)}) collective-permute-start(f32[5,16,512]{2,1,0:T(8,128)S(1)} %get-tuple-element.55), channel_id=1, source_target_pairs={{0,7},{1,0},{2,1},{3,2},{4,3},{5,4},{6,5},{7,6},{8,15},{9,8},{10,9... | collective-permute-start | bytes 491528 | tf_op jit(solution)/shard_map/ppermute | solution.py:16
  73.3 4.2 %collective-permute-start.14 = (f32[16,768]{1,0:T(8,128)S(1)}, f32[16,768]{1,0:T(8,128)S(1)}, u32[]{:S(2)}, u32[]{:S(2)}) collective-permute-start(f32[16,768]{1,0:T(8,128)S(1)} %add.101), channel_id=1, source_target_pairs={{0,2},{1,3},{2,0},{3,1},{4,6},{5,7},{6,4},{7,5},{8,10},{9,11},{10,... | collective-permute-start | bytes 147464 | tf_op jit(solution)/shard_map/ppermute | solution.py:21
  77.4 5.2 %collective-permute-start.15 = (f32[16,768]{1,0:T(8,128)S(1)}, f32[16,768]{1,0:T(8,128)S(1)}, u32[]{:S(2)}, u32[]{:S(2)}) collective-permute-start(f32[16,768]{1,0:T(8,128)S(1)} %add.102), channel_id=1, source_target_pairs={{0,4},{1,5},{2,6},{3,7},{4,0},{5,1},{6,2},{7,3},{8,12},{9,13},{10,... | collective-permute-start | bytes 147464 | tf_op jit(solution)/shard_map/ppermute | solution.py:21
  82.6 12.3 %collective-permute-start.16 = (f32[16,768]{1,0:T(8,128)S(1)}, f32[16,768]{1,0:T(8,128)S(1)}, u32[]{:S(2)}, u32[]{:S(2)}) collective-permute-start(f32[16,768]{1,0:T(8,128)S(1)} %add.103.mine_ref), channel_id=1, source_target_pairs={{0,1},{1,0},{2,3},{3,2},{4,5},{5,4},{6,7},{7,6},{8,9},{9,8},{10,11... | collective-permute-start | bytes 147464 | tf_op jit(solution)/shard_map/ppermute | solution.py:21
  82.7 7.0 %copy-start.1 = (f32[1,1,5,1024,1024]{4,3,2,1,0:T(8,128)S(1)}, f32[1,1,5,1024,1024]{4,3,2,1,0:T(8,128)}, u32[]{:S(2)}) copy-start(f32[1,1,5,1024,1024]{4,3,2,1,0:T(8,128)} %param.9) | copy-start | bytes 62914564
  94.9 14.1 %copy-start.7 = (f32[5,16,512]{2,1,0:T(8,128)}, f32[5,16,512]{2,1,0:T(8,128)S(1)}, u32[]{:S(2)}) copy-start(f32[5,16,512]{2,1,0:T(8,128)S(1)} %get-tuple-element.58.own_ref) | copy-start | bytes 491524
  96.7 12.3 %all-to-all-start.1 = ((f32[32,8,128]{2,1,0:T(8,128)}), f32[32,8,128]{2,1,0:T(8,128)S(1)}, u32[]{:S(2)}, u32[]{:S(2)}) async-start(f32[32,8,128]{2,1,0:T(8,128)} %coarse.4), calls=%async_computation.1 | async-start | bytes 262144 | tf_op jit(solution)/shard_map/all_to_all | solution.py:376
  99.8 8.6 %collective-permute-start.18 = (f32[5,16,512]{2,1,0:T(8,128)S(1)}, f32[5,16,512]{2,1,0:T(8,128)S(1)}, u32[]{:S(2)}, u32[]{:S(2)}) collective-permute-start(f32[5,16,512]{2,1,0:T(8,128)S(1)} %get-tuple-element.59), channel_id=1, source_target_pairs={{0,1},{1,2},{2,3},{3,4},{4,5},{5,6},{6,7},{7,0},{8,9},{9,10},{10,1... | collective-permute-start | bytes 491528 | tf_op jit(solution)/shard_map/ppermute | solution.py:16
  108.3 0.7 copy-start.9
  109.0 0.9 copy-start.4
  109.9 0.9 copy-start.6
  110.8 0.9 copy-start.8
  111.8 0.9 copy-start.10
  115.3 1.3 collective-permute-start.19
  116.6 4.1 %collective-permute-start.20 = (f32[16,768]{1,0:T(8,128)S(1)}, f32[16,768]{1,0:T(8,128)S(1)}, u32[]{:S(2)}, u32[]{:S(2)}) collective-permute-start(f32[16,768]{1,0:T(8,128)S(1)} %add.104), channel_id=1, source_target_pairs={{0,8},{1,9},{2,10},{3,11},{4,12},{5,13},{6,14},{7,15},{8,0},{9,1},... | collective-permute-start | bytes 147464 | tf_op jit(solution)/shard_map/ppermute | solution.py:21
  120.8 4.2 %collective-permute-start.21 = (f32[16,768]{1,0:T(8,128)S(1)}, f32[16,768]{1,0:T(8,128)S(1)}, u32[]{:S(2)}, u32[]{:S(2)}) collective-permute-start(f32[16,768]{1,0:T(8,128)S(1)} %add.105), channel_id=1, source_target_pairs={{0,16},{1,17},{2,18},{3,19},{4,20},{5,21},{6,22},{7,23},{8,24},{9,... | collective-permute-start | bytes 147464 | tf_op jit(solution)/shard_map/ppermute | solution.py:21
  122.4 21.2 %collective-permute-start.25 = (f32[5,16,512]{2,1,0:T(8,128)S(1)}, f32[5,16,512]{2,1,0:T(8,128)S(1)}, u32[]{:S(2)}, u32[]{:S(2)}) collective-permute-start(f32[5,16,512]{2,1,0:T(8,128)S(1)} %get-tuple-element.68), channel_id=1, source_target_pairs={{0,7},{1,0},{2,1},{3,2},{4,3},{5,4},{6,5},{7,6},{8,15},{9,8},{10,9... | collective-permute-start | bytes 491528 | tf_op jit(solution)/shard_map/ppermute | solution.py:16
  125.0 4.1 %collective-permute-start.22 = (f32[16,768]{1,0:T(8,128)S(1)}, f32[16,768]{1,0:T(8,128)S(1)}, u32[]{:S(2)}, u32[]{:S(2)}) collective-permute-start(f32[16,768]{1,0:T(8,128)S(1)} %add.106), channel_id=1, source_target_pairs={{0,2},{1,3},{2,0},{3,1},{4,6},{5,7},{6,4},{7,5},{8,10},{9,11},{10,... | collective-permute-start | bytes 147464 | tf_op jit(solution)/shard_map/ppermute | solution.py:21
  129.1 5.0 %collective-permute-start.23 = (f32[16,768]{1,0:T(8,128)S(1)}, f32[16,768]{1,0:T(8,128)S(1)}, u32[]{:S(2)}, u32[]{:S(2)}) collective-permute-start(f32[16,768]{1,0:T(8,128)S(1)} %add.107), channel_id=1, source_target_pairs={{0,4},{1,5},{2,6},{3,7},{4,0},{5,1},{6,2},{7,3},{8,12},{9,13},{10,... | collective-permute-start | bytes 147464 | tf_op jit(solution)/shard_map/ppermute | solution.py:21
  134.2 12.3 %collective-permute-start.24 = (f32[16,768]{1,0:T(8,128)S(1)}, f32[16,768]{1,0:T(8,128)S(1)}, u32[]{:S(2)}, u32[]{:S(2)}) collective-permute-start(f32[16,768]{1,0:T(8,128)S(1)} %add.108.mine_ref), channel_id=1, source_target_pairs={{0,1},{1,0},{2,3},{3,2},{4,5},{5,4},{6,7},{7,6},{8,9},{9,8},{10,11... | collective-permute-start | bytes 147464 | tf_op jit(solution)/shard_map/ppermute | solution.py:21
  134.2 7.0 %copy-start.2 = (f32[1,1,5,1024,1024]{4,3,2,1,0:T(8,128)S(1)}, f32[1,1,5,1024,1024]{4,3,2,1,0:T(8,128)}, u32[]{:S(2)}) copy-start(f32[1,1,5,1024,1024]{4,3,2,1,0:T(8,128)} %param.9) | copy-start | bytes 62914564
  148.2 11.8 %all-to-all-start.2 = ((f32[32,8,128]{2,1,0:T(8,128)}), f32[32,8,128]{2,1,0:T(8,128)S(1)}, u32[]{:S(2)}, u32[]{:S(2)}) async-start(f32[32,8,128]{2,1,0:T(8,128)} %coarse.5), calls=%async_computation.2 | async-start | bytes 262144 | tf_op jit(solution)/shard_map/all_to_all | solution.py:376
  151.5 8.6 %collective-permute-start.26 = (f32[5,16,512]{2,1,0:T(8,128)S(1)}, f32[5,16,512]{2,1,0:T(8,128)S(1)}, u32[]{:S(2)}, u32[]{:S(2)}) collective-permute-start(f32[5,16,512]{2,1,0:T(8,128)S(1)} %get-tuple-element.72), channel_id=1, source_target_pairs={{0,1},{1,2},{2,3},{3,4},{4,5},{5,6},{6,7},{7,0},{8,9},{9,10},{10,1... | collective-permute-start | bytes 491528 | tf_op jit(solution)/shard_map/ppermute | solution.py:16

commit v2 on v0

v2 whole, which is shorter than its diff:
```python
import functools
import jax
import jax.numpy as jnp
from jax import lax
from jax.experimental import pallas as pl
from jax.experimental.pallas import tpu as pltpu
from jax.sharding import PartitionSpec as P

ITERS = 3
BOTH = ("row", "col")
LANES = 128
HALF_TILE = 64


def shifted(x, axis, by):
    devices = lax.axis_size(axis)
    return lax.ppermute(x, axis, [(i, (i + by) % devices) for i in range(devices)])


def swapped(x, bits):
    devices = lax.axis_size(BOTH)
    return lax.ppermute(x, BOTH, [(i, i ^ bits) for i in range(devices)])


def pieces(x, count):
    out = []
    for step in range(count):
        part = x.astype(jnp.bfloat16)
        out.append(part)
        if step + 1 < count:
            x = x - part.astype(jnp.float32)
    return out


def stacked(x, count):
    return jnp.concatenate(pieces(x, count), axis=0)


def matmul(a, b):
    return jnp.dot(a, b, preferred_element_type=jnp.float32)


def through_table(x, table):
    rows = x.shape[0]
    full = matmul(stacked(x, 3), table)
    return full[2 * rows :] + full[rows : 2 * rows] + full[:rows]


def slot_mask(slots, loads, corners):
    row = lax.broadcasted_iota(jnp.int32, (slots * loads, LANES), 0) // loads
    lane = lax.broadcasted_iota(jnp.int32, (slots * loads, LANES), 1) // corners
    return row == lane


def to_corners(values, columns, corners):
    slots, loads, n = values.shape
    rows = slots * loads
    full = matmul(stacked(values.reshape(rows, n), 2), columns)
    full = (full[rows:, :LANES] + full[:rows, LANES:]) + full[:rows, :LANES]
    kept = jnp.where(slot_mask(slots, loads, corners), full, 0.0)
    return jnp.sum(kept.reshape(slots, loads, LANES), axis=0)


def from_corners(answer, matrix, slots, corners):
    loads = answer.shape[0]
    rows = slots * loads
    spread = jnp.broadcast_to(answer[None], (slots, loads, LANES)).reshape(rows, LANES)
    spread = jnp.where(slot_mask(slots, loads, corners), spread, 0.0)
    both = stacked(spread, 2)
    full = matmul(jnp.concatenate([both, both], axis=1), matrix)
    return (full[rows:] + full[:rows]).reshape(slots, loads, full.shape[1])


def corner_rows(coupling, start, width):
    slots, corners, _ = coupling.shape
    parts = [coupling[s, :, start : start + width] for s in range(slots)]
    if slots * corners < LANES:
        parts.append(jnp.zeros((LANES - slots * corners, width), jnp.float32))
    return jnp.concatenate(parts, axis=0)


def prepare_kernel(info_ref, dof_ref, coupling_ref, coarse_ref, inverse_ref, link_ref, link_t_ref, coarse_table_ref):
    slots, links, width = dof_ref.shape[2:]
    span = links * width
    for j in range(slots):
        for k in range(links):
            met = dof_ref[0, 0, j, k : k + 1, :]
            hit = jnp.broadcast_to(met, (width, width)) == lax.broadcasted_iota(jnp.int32, (width, width), 0)
            place = jnp.where(hit, lax.broadcasted_iota(jnp.int32, (width, width), 1), 0).astype(jnp.float32)
            found = jnp.sum(place.T, axis=0, keepdims=True)
            inverse_ref[j * links + k : j * links + k + 1, :] = found.astype(jnp.int32)
    link = corner_rows(coupling_ref[0, 0], 0, span)
    link_ref[...] = stacked(link, 2)
    link_t_ref[...] = jnp.concatenate(pieces(link.T, 2), axis=1)
    rows, size = coarse_ref.shape
    wide = coarse_table_ref.shape[1] // 4
    filled = jnp.concatenate([coarse_ref[...], jnp.zeros((LANES * (-(-wide // LANES)) - rows, size), jnp.float32)], axis=0)
    turned = filled.T[:, :wide]
    place = lax.broadcasted_iota(jnp.int32, (size, wide), 0) - info_ref[0] * rows
    lane = lax.broadcasted_iota(jnp.int32, (size, wide), 1)
    chosen = ((place == lane) & (lane < rows)).astype(jnp.bfloat16)
    coarse_table_ref[...] = jnp.concatenate(pieces(turned, 3) + [chosen], axis=1)


def start_exchange(
    z, partner_ref, inverse_ref, link_t_ref, prev_t_ref, scatter_ref, parity, corners, send_ref, mine_ref, other_ref
):
    slots, loads, span = z.shape
    links = span // LANES
    for j in range(slots):
        for k in range(links):
            block = z[j, :, k * LANES : (k + 1) * LANES]
            index = jnp.broadcast_to(inverse_ref[j * links + k][None], (loads, LANES))
            send_ref[partner_ref[0, 0, k, j], :, k * LANES : (k + 1) * LANES] = -jnp.take_along_axis(block, index, axis=1)
    own = to_corners(z, link_t_ref[...], corners)
    prev = to_corners(send_ref[...], prev_t_ref[...], corners)
    load = through_table(jnp.concatenate([own, prev], axis=1), scatter_ref[...])
    half = load.shape[1] // 2
    low, high = load[:, :half], load[:, half:]
    mine_ref[...] = jnp.where(parity == 0, low, high)
    other_ref[...] = jnp.where(parity == 0, high, low)


def local_norm(r, z):
    slots, loads, span = r.shape
    return jnp.broadcast_to(jnp.sum(jnp.sum(r * z, axis=0), axis=1, keepdims=True), (loads, LANES))


def first_kernel(
    corners, info_ref, partner_ref, counts_ref, prev_info_ref, right_ref, weight_ref, inverse_ref, link_t_ref, prev_coupling_ref,
    map_ref, mask_ref, r_ref, z_ref, norm_ref, send_ref, mine_ref, other_ref, prev_t_ref, scatter_ref,
):
    slots, loads, span = r_ref.shape
    links = span // LANES
    for j in range(slots):
        for k in range(links):
            lanes = slice(k * LANES, (k + 1) * LANES)
            alive = (j < counts_ref[0, 0]) & (partner_ref[0, 0, k, j] < prev_info_ref[0, slots * corners])
            kept = jnp.where(alive, 1.0, 0.0)
            mask_ref[j : j + 1, lanes] = jnp.full((1, LANES), kept, jnp.float32)
            r = right_ref[0, 0, j, :, k, :] * kept
            r_ref[j, :, lanes] = r
            z_ref[j, :, lanes] = weight_ref[0, 0, j, k : k + 1, :] * r
    prev = corner_rows(prev_coupling_ref[...], 0, span)
    prev_t_ref[...] = jnp.concatenate(pieces(prev.T, 2), axis=1)
    scatter_ref[...] = (map_ref[...] == lax.broadcasted_iota(jnp.int32, scatter_ref.shape, 1)).astype(jnp.bfloat16)
    z = z_ref[...]
    norm_ref[...] = local_norm(r_ref[...], z)
    start_exchange(
        z, partner_ref, inverse_ref, link_t_ref, prev_t_ref, scatter_ref, info_ref[1], corners, send_ref, mine_ref, other_ref
    )


def table_kernel(prev_coupling_ref, place_ref, prev_ref, pick_ref):
    prev_ref[...] = stacked(corner_rows(prev_coupling_ref[...], 0, prev_coupling_ref.shape[2]), 2)
    pick_ref[...] = (place_ref[...] == lax.broadcasted_iota(jnp.int32, pick_ref.shape, 0)).astype(jnp.bfloat16)


def gathered_scalars(near_blocks_ref, far_blocks_ref, rows):
    total = jnp.sum(near_blocks_ref[...] + far_blocks_ref[...], axis=0)
    at = 2 * rows
    norm = jnp.concatenate([total[:, at : at + 1], total[:, at + 1 : at + 2]], axis=0)
    product = jnp.concatenate([total[:, at + 2 : at + 3], total[:, at + 3 : at + 4]], axis=0)
    return norm, product


def picked_corners(near_blocks_ref, far_blocks_ref, rows, pick_ref):
    count, half, block = near_blocks_ref.shape
    blocks = [ref[e] for ref in (near_blocks_ref, far_blocks_ref) for e in range(count)]
    low = jnp.concatenate(blocks, axis=1)
    high = jnp.concatenate([pltpu.roll(b, block - rows, 1) for b in blocks], axis=1)
    return through_table(jnp.concatenate([low, high], axis=0), pick_ref[...])


def step_kernel(
    corners, rows, first, last, info_ref, partner_ref, near_blocks_ref, far_blocks_ref, own_ref, facing_ref, weight_ref, dof_ref,
    inverse_ref, mask_ref, link_ref, prev_ref, link_t_ref, prev_t_ref, scatter_ref, pick_ref, r_ref, z_ref, *refs,
):
    refs = list(refs)
    if not first:
        x_ref, p_ref, s_ref, past_ref = refs[:4]
        refs = refs[4:]
    x_out, r_out = refs[:2]
    far_ref = refs[-1]
    slots, loads, span = own_ref.shape
    links = span // LANES
    norm, product = gathered_scalars(near_blocks_ref, far_blocks_ref, rows)
    picked = picked_corners(near_blocks_ref, far_blocks_ref, rows, pick_ref)
    near = own_ref[...] + from_corners(picked[:, :LANES], link_ref[...], slots, corners)
    far_ref[...] = facing_ref[...] + from_corners(picked[:, LANES:], prev_ref[...], slots, corners)
    jumps = []
    for j in range(slots):
        parts = []
        for k in range(links):
            block = far_ref[partner_ref[0, 0, k, j], :, k * LANES : (k + 1) * LANES]
            index = jnp.broadcast_to(dof_ref[0, 0, j, k : k + 1, :], (loads, LANES))
            parts.append(jnp.take_along_axis(block, index, axis=1))
        jumps.append(jnp.concatenate(parts, axis=1)[None])
    image = (near - jnp.concatenate(jumps, axis=0)) * mask_ref[...][:, None, :]
    if first:
        alpha = norm / product
        p, s = z_ref[...], image
        x = alpha[None] * p
    else:
        ratio = norm / past_ref[:, :1]
        alpha = norm / (product - ratio * norm / past_ref[:, 1:2])
        p = z_ref[...] + ratio[None] * p_ref[...]
        s = image + ratio[None] * s_ref[...]
        x = x_ref[...] + alpha[None] * p
    r = r_ref[...] - alpha[None] * s
    if last:
        for j in range(slots):
            for k in range(links):
                x_out[0, 0, j, :, k, :] = x[j, :, k * LANES : (k + 1) * LANES]
                r_out[0, 0, j, :, k, :] = r[j, :, k * LANES : (k + 1) * LANES]
        return
    z_out, p_out, s_out, past_out, norm_out, send_ref, mine_ref, other_ref = refs[2:10]
    x_out[...] = x
    r_out[...] = r
    weight = jnp.concatenate([weight_ref[0, 0, :, k, :] for k in range(links)], axis=1)
    z = weight[:, None, :] * r
    z_out[...] = z
    p_out[...] = p
    s_out[...] = s
    lane = lax.broadcasted_iota(jnp.int32, past_out.shape, 1)
    past_out[...] = jnp.where(lane == 0, norm, alpha)
    norm_out[...] = local_norm(r, z)
    start_exchange(
        z, partner_ref, inverse_ref, link_t_ref, prev_t_ref, scatter_ref, info_ref[1], corners, send_ref, mine_ref, other_ref
    )


def split_kernel(flex_ref, large_ref, small_ref):
    large, small = pieces(flex_ref[0, 0, 0], 2)
    large_ref[0] = large
    small_ref[0] = small


def flex_product(values, large, small):
    loads = values.shape[0]
    full = matmul(stacked(values, 2), large)
    rest = matmul(values.astype(jnp.bfloat16), small)
    return (full[loads:] + rest) + full[:loads]


def flex_near_kernel(values_ref, large_ref, small_ref, out_ref):
    slots, _, width = values_ref.shape
    for s in range(slots):
        out_ref[s] = flex_product(values_ref[s], large_ref[s, :width], small_ref[s, :width])


def flex_far_kernel(values_ref, forces_ref, begun_ref, large_ref, small_ref, own_ref, facing_ref, energy_ref):
    slots, loads, width = values_ref.shape
    work = jnp.zeros((loads, 1), jnp.float32)
    for s in range(slots):
        answer = begun_ref[s] + flex_product(forces_ref[s], large_ref[s, width:], small_ref[s, width:])
        own, facing = answer[:, :width], answer[:, width:]
        own_ref[s] = own
        facing_ref[s] = facing
        work += jnp.sum(values_ref[s] * own + forces_ref[s] * facing, axis=1, keepdims=True)
    energy_ref[...] = jnp.broadcast_to(work, energy_ref.shape)


def coarse_kernel(rows, info_ref, mine_ref, other_ref, table_ref, energy_ref, norm_ref, out_ref):
    parity = info_ref[1]
    mine, other = mine_ref[...], other_ref[...]
    low, high = jnp.where(parity == 0, mine, other), jnp.where(parity == 0, other, mine)
    load = jnp.concatenate([low, high], axis=1)
    loads = load.shape[0]
    wide = table_ref.shape[1] // 4
    full = matmul(stacked(load, 3), table_ref[...])

    def part(i, j):
        return full[i * loads : (i + 1) * loads, j * wide : j * wide + rows]

    answer = ((part(2, 0) + part(1, 1)) + part(0, 2)) + (part(1, 0) + part(0, 1)) + part(0, 0)
    own = (part(2, 3) + part(1, 3)) + part(0, 3)
    product = jnp.sum(answer * own, axis=1, keepdims=True) + energy_ref[:, :1]
    norm = norm_ref[:, :1]
    half = loads // 2
    tail = out_ref.shape[2] - 2 * rows - 4
    out_ref[0] = jnp.concatenate(
        [answer[:half], answer[half:], norm[:half], norm[half:], product[:half], product[half:], jnp.zeros((half, tail), jnp.float32)],
        axis=1,
    )

VMEM = pl.BlockSpec(memory_space=pltpu.VMEM)
SMEM = pl.BlockSpec(memory_space=pltpu.SMEM)
SMALL = pltpu.CompilerParams(vmem_limit_bytes=12 * 1024 * 1024)


def shape_of(*dims, dtype=jnp.float32):
    return pltpu.VMEM(dims, dtype)


def cost(flops, bytes_accessed):
    return pl.CostEstimate(flops=flops, bytes_accessed=bytes_accessed, transcendentals=0)


def gathered(block):
    devices, columns = lax.axis_size(BOTH), lax.axis_size("col")
    for start, stop in ((2, columns), (columns, devices)):
        if stop == 4 * start:
            parts = [block] + [swapped(block, b * start) for b in (1, 2, 3)]
            block = jnp.concatenate(parts, axis=0)
        else:
            while start < stop:
                block = jnp.concatenate([block, swapped(block, start)], axis=0)
                start *= 2
    return block, swapped(block, 1)


def summed(mine, other, between, after):
    devices, columns = lax.axis_size(BOTH), lax.axis_size("col")
    along_rows = [b for b in range(columns, devices, columns)]
    along_columns = [b for b in range(2, columns, 2)]
    total = mine + swapped(other, 1)
    total = between(total)
    for group, hook in ((along_rows, after[0]), (along_columns, after[1])):
        if len(group) <= 3:
            total = sum([swapped(total, b) for b in group], total)
        else:
            for b in [g for g in group if g & (g - 1) == 0]:
                total = total + swapped(total, b)
        total = hook(total)
    return total


def local(
    flexibility,
    coupling,
    coarse_inverse,
    precon_weight,
    right_side,
    counts,
    partner,
    dof_index,
    corner_map,
):
    devices = lax.axis_size(BOTH)
    slots, iface = flexibility.shape[2:4]
    links, width = dof_index.shape[-2:]
    loads = right_side.shape[3]
    corners = corner_map.shape[-1]
    rows, coarse_size = coarse_inverse.shape
    span = links * width
    block = -(-(2 * rows + 4) // LANES) * LANES
    wide = -(-rows // HALF_TILE) * HALF_TILE
    me = lax.axis_index("row") * lax.axis_size("col") + lax.axis_index("col")

    coupling_prev = shifted(coupling[0, 0, :, :, span:], "col", 1)
    spare = jnp.full((1, LANES - slots * corners - 1), -1, jnp.int32)
    own_info = jnp.concatenate([corner_map[0, 0].reshape(1, -1), counts, spare], axis=1)
    prev_info = shifted(own_info, "col", 1)
    unknown = jnp.arange(2 * LANES, dtype=jnp.int32)[None] % LANES < slots * corners
    maps = jnp.where(unknown, jnp.concatenate([own_info, prev_info], axis=1), -1)
    away = jnp.bitwise_xor(maps // rows, me)
    place = jnp.where(unknown, ((away % 2) * (devices // 2) + away // 2) * block + maps % rows, -1)
    map_column = maps.reshape(-1, 1)
    info = jnp.stack([me, lax.axis_index("col") % 2]).astype(jnp.int32)

    state = shape_of(slots, loads, span)
    small = shape_of(loads, LANES)
    half_load = shape_of(loads, coarse_size // 2)
    out_state = jax.ShapeDtypeStruct(right_side.shape, jnp.float32)

    def table(*dims):
        return shape_of(*dims, dtype=jnp.bfloat16)

    inverse, link, link_t, coarse_table = pl.pallas_call(
        prepare_kernel,
        out_shape=(
            shape_of(slots * links, width, dtype=jnp.int32), table(2 * LANES, span), table(span, 2 * LANES),
            table(coarse_size, 4 * wide),
        ),
        in_specs=[SMEM] + [VMEM] * 3,
        out_specs=[VMEM] * 4,
        compiler_params=SMALL,
        name="prepare",
    )(info, dof_index, coupling, coarse_inverse)
    mask, r, z, norm, send, mine, other, prev_t, scatter = pl.pallas_call(
        functools.partial(first_kernel, corners),
        out_shape=(
            shape_of(slots, span), state, state, small, state, half_load, half_load, table(span, 2 * LANES),
            table(2 * LANES, coarse_size),
        ),
        in_specs=[SMEM] * 4 + [VMEM] * 6,
        out_specs=[VMEM] * 9,
        compiler_params=SMALL,
        name="first",
    )(info, partner, counts, prev_info, right_side, precon_weight, inverse, link_t, coupling_prev, map_column)
    prev, pick = pl.pallas_call(
        table_kernel,
        out_shape=(table(2 * LANES, span), table(devices * block, 2 * LANES)),
        in_specs=[VMEM] * 2,
        out_specs=[VMEM] * 2,
        compiler_params=SMALL,
        name="tables",
    )(coupling_prev, place)

    half = pl.BlockSpec((1, span, iface), lambda s, h: (s, h, 0))
    streaming = pltpu.CompilerParams(vmem_limit_bytes=30 * 1024 * 1024)
    large, small_part = pl.pallas_call(
        split_kernel,
        grid=(slots, iface // span),
        out_shape=(table(slots, iface, iface), table(slots, iface, iface)),
        in_specs=[pl.BlockSpec((1, 1, 1, span, iface), lambda s, h: (0, 0, s, h, 0))],
        out_specs=[half, half],
        compiler_params=streaming,
        cost_estimate=cost(0, slots * iface * iface * 8),
        name="split",
    )(flexibility)
    work = cost(2 * slots * loads * span * iface * 6, slots * span * iface * 4)

    def near_call(z):
        return pl.pallas_call(
            flex_near_kernel,
            out_shape=shape_of(slots, loads, iface),
            in_specs=[VMEM] * 3,
            out_specs=VMEM,
            compiler_params=SMALL,
            cost_estimate=work,
            name="flex_near",
        )(z, large, small_part)

    def far_call(z, forces, begun):
        return pl.pallas_call(
            flex_far_kernel,
            out_shape=(state, state, small),
            in_specs=[VMEM] * 5,
            out_specs=[VMEM] * 3,
            compiler_params=SMALL,
            cost_estimate=work,
            name="flex_far",
        )(z, forces, begun, large, small_part)

    kept = ()
    for iteration in range(ITERS):
        first, last = iteration == 0, iteration + 1 == ITERS
        held = {}

        def begin(total):
            total, held["z"] = lax.optimization_barrier((total, z))
            held["begun"] = near_call(held["z"])
            return total

        def after_rows(total):
            total, held["begun"], arrived = lax.optimization_barrier((total, held["begun"], forces))
            held["out"] = far_call(held["z"], arrived, held["begun"])
            return total

        def after_columns(total):
            total, *held["out"] = lax.optimization_barrier((total, *held["out"]))
            return total

        forces = shifted(send, "col", -1)
        total = summed(mine, other, begin, (after_rows, after_columns))
        rest = swapped(total, 1)
        own, facing, energy = held["out"]
        facing_prev = shifted(facing, "col", 1)
        blocks = pl.pallas_call(
            functools.partial(coarse_kernel, rows),
            out_shape=shape_of(1, loads // 2, block),
            in_specs=[SMEM] + [VMEM] * 5,
            out_specs=VMEM,
            compiler_params=SMALL,
            name="coarse",
        )(info, total, rest, coarse_table, energy, norm)
        near_blocks, far_blocks = gathered(blocks)
        outs = (out_state, out_state) if last else (state,) * 5 + (small, small, state, half_load, half_load)
        results = pl.pallas_call(
            functools.partial(step_kernel, corners, rows, first, last),
            out_shape=outs,
            in_specs=[SMEM, SMEM] + [VMEM] * (16 + len(kept)),
            out_specs=[VMEM] * len(outs),
            scratch_shapes=[pltpu.VMEM((slots, loads, span), jnp.float32)],
            compiler_params=SMALL,
            name="step",
        )(
            info, partner, near_blocks, far_blocks, own, facing_prev, precon_weight, dof_index, inverse, mask, link, prev, link_t, prev_t,
            scatter, pick, r, z, *kept,
        )
        if last:
            return results
        x, r, z, p, s, past, norm, send, mine, other = results
        kept = (x, p, s, past)


def solution(mesh):
    in_specs = (
        P("row", "col", None, None, None),
        P("row", "col", None, None, None),
        P(("row", "col"), None),
        P("row", "col", None, None, None),
        P("row", "col", None, None, None, None),
        P("row", "col"),
        P("row", "col", None, None),
        P("row", "col", None, None, None),
        P("row", "col", None, None),
    )
    out_specs = (P("row", "col", None, None, None, None), P("row", "col", None, None, None, None))
    return jax.shard_map(local, mesh=mesh, in_specs=in_specs, out_specs=out_specs, check_vma=False)
```

time: 691 us -> 134 us (0.19)
  waiting for transfers between devices: 338 us -> 34.8 us
  blocking collectives: 238 us -> 0 us
  matrix products: 83 us -> 0 us
  starting transfers between devices: 6.6 us -> 55.2 us
  Pallas kernels: 0 us -> 34.1 us
  between operations: 14.8 us -> 1.57 us
    psum x3 -> x0, waiting for transfers between devices: 306 us -> none  [coarse_solve(): total_load = lax.psum(local_load, ('row', 'col'))]
    all_gather x3 -> x0, blocking collectives: 127 us -> none  [coarse_solve(): return lax.all_gather(own_rows, ('row', 'col'), axis=1, tiled=True)]
    psum x3 -> x0, blocking collectives: 111 us -> none  [both_sums(): lax.psum((local_inner(resid_now, precond_now), local_inner(precond_now, i...]
    dot_general x31 -> x0, matrix products: 83 us -> none  [the longest x3 60.1 us: apply_operator(): answer = jnp.einsum('sab,sqb->sqa', flex_local, force_full, precision=HIGH)]
    ppermute x0 -> x45, starting transfers between devices: none -> 48.7 us  [swapped(): return lax.ppermute(x, BOTH, [(i, i ^ bits) for i in range(devices)])]
    pallas_call x0 -> x16, Pallas kernels: none -> 34.1 us  [the longest x1 10.7 us: local(): pl.pallas_call(split_kernel, grid=(slots, iface // span), out_shape=(tabl...]
    ppermute x0 -> x45, waiting for transfers between devices: none -> 32.6 us  [swapped(): return lax.ppermute(x, BOTH, [(i, i ^ bits) for i in range(devices)])]
    ppermute x8, waiting for transfers between devices: 32.2 us -> 2.15 us  [shifted(): lax.ppermute(x, axis, [(i, (i + by) % devices) for i in range(devices)])]
  transfers between devices with their start and end apart: 11 -> 53, of which waited for: 10 -> 31; matrix products, arithmetic and copies ran while one was open for 9% -> 1% of each run, Pallas kernels for 0% -> 19%
where the time goes in v2:
time: 134 us; the launch traced here: 133 us
  starting transfers between devices  55.2 us (41%)
  waiting for transfers between devices  34.8 us (26%)
  Pallas kernels  34.1 us (25%)
  local copies, waits for them, and re-layouts  6.36 us (5%)
  between operations  1.57 us (1%)
    ppermute x45, starting transfers between devices, swapped(): return lax.ppermute(x, BOTH, [(i, i ^ bits) for i in range(devices)])  48.7 us
    ppermute x45, waiting for transfers between devices, swapped(): return lax.ppermute(x, BOTH, [(i, i ^ bits) for i in range(devices)])  32.6 us
    pallas_call x1, Pallas kernels, local(): pl.pallas_call(split_kernel, grid=(slots, iface // span), out_shape=(tabl...  10.7 us
    pallas_call x3, Pallas kernels, local(): pl.pallas_call(functools.partial(step_kernel, corners, rows, first, last)...  7.27 us
    ppermute x8, starting transfers between devices, shifted(): lax.ppermute(x, axis, [(i, (i + by) % devices) for i in range(devices)])  6.45 us
    pallas_call x3, Pallas kernels, far_call(): pl.pallas_call(flex_far_kernel, out_shape=(state, state, small), in_specs...  5.15 us
    unnamed x34, local copies, waits for them, and re-layouts  5.03 us
    pallas_call x3, Pallas kernels, near_call(): pl.pallas_call(flex_near_kernel, out_shape=shape_of(slots, loads, iface),...  4.84 us
  transfers between devices with their start and end apart: 53, of which 31 were waited for; matrix products, arithmetic and copies ran while one was open for 1% of the time, Pallas kernels for 19%

profile of v2, /device:TPU:0, one launch (start us, length us, event | category | flops | bytes accessed | tf_op | source)
XLA Modules:
  0.0 133.2 jit_solution(13564378049618183471)
XLA Ops:
  3.6 2.7 %collective-permute-start = (s32[1,128]{1,0:T(1,128)S(1)}, s32[1,128]{1,0:T(1,128)S(1)}, u32[]{:S(2)}, u32[]{:S(2)}) collective-permute-start(s32[1,128]{1,0:T(1,128)S(1)} %pad_add_fusion.1), channel_id=1, source_target_pairs={{0,1},{1,2},{2,3},{3,4},{4,5},{5,6},{6,7},{7,0},{8,9},{9,10},{10,1... | collective-permute-start | bytes 1544 | tf_op jit(solution)/shard_map/ppermute | solution.py:17
  9.3 1.4 %prepare.1 = (s32[20,128]{1,0:T(8,128)S(1)}, bf16[256,512]{1,0:T(8,128)(2,1)S(1)}, bf16[512,256]{1,0:T(8,128)(2,1)S(1)}, bf16[1536,256]{1,0:T(8,128)(2,1)S(1)}) custom-call(s32[2]{0:T(128)S(1)} %pad_add_fusion.info_ref, s32[1,1,5,4,128]{4,3,2,1,0:T(4,128)S(1)} %copy-done.3, f32[1,1,5,24,1024]{4,3,2,1,0:T(8,128)S(1)} %copy-done, f32[48,1536]{1,0:T(8,128)S(1)} %copy-done.1), custom_call_target="tpu_custom_call" | custom-call | tf_op jit(solution)/shard_map/prepare/pallas_call | solution.py:370
  13.2 1.3 first.1
  14.6 1.2 collective-permute-done.2
  15.9 2.5 %collective-permute-start.5 = (f32[16,768]{1,0:T(8,128)S(1)}, f32[16,768]{1,0:T(8,128)S(1)}, u32[]{:S(2)}, u32[]{:S(2)}) collective-permute-start(f32[16,768]{1,0:T(8,128)S(1)} %add.163), channel_id=1, source_target_pairs={{0,24},{1,25},{2,26},{3,27},{4,28},{5,29},{6,30},{7,31},{8,16},{9,... | collective-permute-start | bytes 147464 | tf_op jit(solution)/shard_map/ppermute | solution.py:22
  19.4 10.7 %split.1 = (bf16[5,1024,1024]{2,1,0:T(8,128)(2,1)S(1)}, bf16[5,1024,1024]{2,1,0:T(8,128)(2,1)S(1)}) custom-call(f32[1,1,5,1024,1024]{4,3,2,1,0:T(8,128)} %flex_ref.1), custom_call_target="tpu_custom_call" | custom-call | bytes 41943040 | tf_op jit(solution)/shard_map/split/pallas_call | solution.py:403
  30.1 1.0 collective-permute-start.6
  31.2 1.6 %flex_near.3.begun_ref = f32[5,16,1024]{2,1,0:T(8,128)S(1)} custom-call(f32[5,16,512]{2,1,0:T(8,128)S(1)} %get-tuple-element.81.values_ref.z_ref, bf16[5,1024,1024]{2,1,0:T(8,128)(2,1)S(1)} %get-tuple-element.82.large_ref, bf16[5,1024,1024]{2,1,0:T(8,128)(2,1)S(1)} %get-tuple-element.83.small_ref), custom_call_target="tpu_custom_call" | custom-call | flops 503316480 | bytes 10485760 | tf_op jit(solution)/shard_map/flex_near/pallas_call | solution.py:416
  32.9 1.2 collective-permute-done.6.forces_ref
  34.0 1.9 %collective-permute-start.9 = (f32[16,768]{1,0:T(8,128)S(1)}, f32[16,768]{1,0:T(8,128)S(1)}, u32[]{:S(2)}, u32[]{:S(2)}) collective-permute-start(f32[16,768]{1,0:T(8,128)S(1)} %add_add_fusion.5), channel_id=1, source_target_pairs={{0,6},{1,7},{2,4},{3,5},{4,2},{5,3},{6,0},{7,1},{8,14},{9,15},{10,... | collective-permute-start | bytes 147464 | tf_op jit(solution)/shard_map/ppermute | solution.py:22
  36.1 2.3 %collective-permute-start.7 = (f32[16,768]{1,0:T(8,128)S(1)}, f32[16,768]{1,0:T(8,128)S(1)}, u32[]{:S(2)}, u32[]{:S(2)}) collective-permute-start(f32[16,768]{1,0:T(8,128)S(1)} %add_add_fusion.5), channel_id=1, source_target_pairs={{0,2},{1,3},{2,0},{3,1},{4,6},{5,7},{6,4},{7,5},{8,10},{9,11},{10,... | collective-permute-start | bytes 147464 | tf_op jit(solution)/shard_map/ppermute | solution.py:22
  38.4 1.7 %flex_far.3 = (f32[5,16,512]{2,1,0:T(8,128)S(1)}, f32[5,16,512]{2,1,0:T(8,128)S(1)}, f32[16,128]{1,0:T(8,128)S(1)}) custom-call(f32[5,16,512]{2,1,0:T(8,128)S(1)} %get-tuple-element.81.values_ref.z_ref, f32[5,16,512]{2,1,0:T(8,128)S(1)} %collective-permute-done.6.forces_ref, f32[5,16,1024]{2,1,0:T(8,128)S(1)} %flex_near.3.begun_ref, ...), custom_call_target="tpu_custom_call" | custom-call | flops 503316480 | bytes 10485760 | tf_op jit(solution)/shard_map/flex_far/pallas_call | solution.py:427
  40.4 1.9 %collective-permute-done.8 = f32[16,768]{1,0:T(8,128)S(1)} collective-permute-done((f32[16,768]{1,0:T(8,128)S(1)}, f32[16,768]{1,0:T(8,128)S(1)}, u32[]{:S(2)}, u32[]{:S(2)}) %collective-permute-start.8) | collective-permute-done | bytes 49184 | tf_op jit(solution)/shard_map/ppermute | solution.py:22
  44.6 2.2 %collective-permute-start.13 = (f32[1,8,128]{2,1,0:T(8,128)S(1)}, f32[1,8,128]{2,1,0:T(8,128)S(1)}, u32[]{:S(2)}, u32[]{:S(2)}) collective-permute-start(f32[1,8,128]{2,1,0:T(8,128)S(1)} %coarse.3), channel_id=1, source_target_pairs={{0,6},{1,7},{2,4},{3,5},{4,2},{5,3},{6,0},{7,1},{8,14},{9,15},{10,... | collective-permute-start | bytes 12296 | tf_op jit(solution)/shard_map/ppermute | solution.py:22
  46.8 2.2 %collective-permute-start.11 = (f32[1,8,128]{2,1,0:T(8,128)S(1)}, f32[1,8,128]{2,1,0:T(8,128)S(1)}, u32[]{:S(2)}, u32[]{:S(2)}) collective-permute-start(f32[1,8,128]{2,1,0:T(8,128)S(1)} %coarse.3), channel_id=1, source_target_pairs={{0,2},{1,3},{2,0},{3,1},{4,6},{5,7},{6,4},{7,5},{8,10},{9,11},{10,... | collective-permute-start | bytes 12296 | tf_op jit(solution)/shard_map/ppermute | solution.py:22
  50.1 1.3 collective-permute-done.12
  51.4 2.4 %collective-permute-start.16 = (f32[4,8,128]{2,1,0:T(8,128)S(1)}, f32[4,8,128]{2,1,0:T(8,128)S(1)}, u32[]{:S(2)}, u32[]{:S(2)}) collective-permute-start(f32[4,8,128]{2,1,0:T(8,128)S(1)} %pad_maximum_fusion), channel_id=1, source_target_pairs={{0,24},{1,25},{2,26},{3,27},{4,28},{5,29},{6,30},{7,31},{8,16},{9,... | collective-permute-start | bytes 49160 | tf_op jit(solution)/shard_map/ppermute | solution.py:22
  54.9 3.2 %collective-permute-done.14 = f32[4,8,128]{2,1,0:T(8,128)S(1)} collective-permute-done((f32[4,8,128]{2,1,0:T(8,128)S(1)}, f32[4,8,128]{2,1,0:T(8,128)S(1)}, u32[]{:S(2)}, u32[]{:S(2)}) %collective-permute-start.14) | collective-permute-done | bytes 16416 | tf_op jit(solution)/shard_map/ppermute | solution.py:22
  59.4 2.4 %step.3 = (f32[5,16,512]{2,1,0:T(8,128)S(1)}, f32[5,16,512]{2,1,0:T(8,128)S(1)}, f32[5,16,512]{2,1,0:T(8,128)S(1)}, f32[5,16,512]{2,1,0:T(8,128)S(1)}, f32[5,16,...) custom-call(s32[2]{0:T(128)S(1)} %pad_add_fusion.info_ref, ...), custom_call_target="tpu_custom_call" | custom-call | tf_op jit(solution)/shard_map/step/pallas_call | solution.py:471
  62.0 1.1 collective-permute-done.19
  63.1 1.6 %collective-permute-start.22 = (f32[16,768]{1,0:T(8,128)S(1)}, f32[16,768]{1,0:T(8,128)S(1)}, u32[]{:S(2)}, u32[]{:S(2)}) collective-permute-start(f32[16,768]{1,0:T(8,128)S(1)} %add.175), channel_id=1, source_target_pairs={{0,24},{1,25},{2,26},{3,27},{4,28},{5,29},{6,30},{7,31},{8,16},{9,... | collective-permute-start | bytes 147464 | tf_op jit(solution)/shard_map/ppermute | solution.py:22
  65.1 1.5 %collective-permute-start.20 = (f32[16,768]{1,0:T(8,128)S(1)}, f32[16,768]{1,0:T(8,128)S(1)}, u32[]{:S(2)}, u32[]{:S(2)}) collective-permute-start(f32[16,768]{1,0:T(8,128)S(1)} %add.175), channel_id=1, source_target_pairs={{0,8},{1,9},{2,10},{3,11},{4,12},{5,13},{6,14},{7,15},{8,0},{9,1},... | collective-permute-start | bytes 147464 | tf_op jit(solution)/shard_map/ppermute | solution.py:22
  67.2 1.6 %flex_near.4.begun_ref = f32[5,16,1024]{2,1,0:T(8,128)S(1)} custom-call(f32[5,16,512]{2,1,0:T(8,128)S(1)} %get-tuple-element.108.values_ref.z_ref, bf16[5,1024,1024]{2,1,0:T(8,128)(2,1)S(1)} %get-tuple-element.82.large_ref, bf16[5,1024,1024]{2,1,0:T(8,128)(2,1)S(1)} %get-tuple-element.83.small_ref), custom_call_target="tpu_custom_call" | custom-call | flops 503316480 | bytes 10485760 | tf_op jit(solution)/shard_map/flex_near/pallas_call | solution.py:416
  70.0 1.9 %collective-permute-start.26 = (f32[16,768]{1,0:T(8,128)S(1)}, f32[16,768]{1,0:T(8,128)S(1)}, u32[]{:S(2)}, u32[]{:S(2)}) collective-permute-start(f32[16,768]{1,0:T(8,128)S(1)} %add_add_fusion.3), channel_id=1, source_target_pairs={{0,6},{1,7},{2,4},{3,5},{4,2},{5,3},{6,0},{7,1},{8,14},{9,15},{10,... | collective-permute-start | bytes 147464 | tf_op jit(solution)/shard_map/ppermute | solution.py:22
  72.2 2.2 %collective-permute-start.24 = (f32[16,768]{1,0:T(8,128)S(1)}, f32[16,768]{1,0:T(8,128)S(1)}, u32[]{:S(2)}, u32[]{:S(2)}) collective-permute-start(f32[16,768]{1,0:T(8,128)S(1)} %add_add_fusion.3), channel_id=1, source_target_pairs={{0,2},{1,3},{2,0},{3,1},{4,6},{5,7},{6,4},{7,5},{8,10},{9,11},{10,... | collective-permute-start | bytes 147464 | tf_op jit(solution)/shard_map/ppermute | solution.py:22
  74.4 1.7 %flex_far.4 = (f32[5,16,512]{2,1,0:T(8,128)S(1)}, f32[5,16,512]{2,1,0:T(8,128)S(1)}, f32[16,128]{1,0:T(8,128)S(1)}) custom-call(f32[5,16,512]{2,1,0:T(8,128)S(1)} %get-tuple-element.108.values_ref.z_ref, f32[5,16,512]{2,1,0:T(8,128)S(1)} %collective-permute-done.23.forces_ref, f32[5,16,1024]{2,1,0:T(8,128)S(1)} %flex_near.4.begun_ref, ...), custom_call_target="tpu_custom_call" | custom-call | flops 503316480 | bytes 10485760 | tf_op jit(solution)/shard_map/flex_far/pallas_call | solution.py:427
  76.4 2.0 %collective-permute-done.25 = f32[16,768]{1,0:T(8,128)S(1)} collective-permute-done((f32[16,768]{1,0:T(8,128)S(1)}, f32[16,768]{1,0:T(8,128)S(1)}, u32[]{:S(2)}, u32[]{:S(2)}) %collective-permute-start.25) | collective-permute-done | bytes 49184 | tf_op jit(solution)/shard_map/ppermute | solution.py:22
  80.7 2.0 %collective-permute-start.30 = (f32[1,8,128]{2,1,0:T(8,128)S(1)}, f32[1,8,128]{2,1,0:T(8,128)S(1)}, u32[]{:S(2)}, u32[]{:S(2)}) collective-permute-start(f32[1,8,128]{2,1,0:T(8,128)S(1)} %coarse.4), channel_id=1, source_target_pairs={{0,6},{1,7},{2,4},{3,5},{4,2},{5,3},{6,0},{7,1},{8,14},{9,15},{10,... | collective-permute-start | bytes 12296 | tf_op jit(solution)/shard_map/ppermute | solution.py:22
  82.8 2.4 %collective-permute-start.28 = (f32[1,8,128]{2,1,0:T(8,128)S(1)}, f32[1,8,128]{2,1,0:T(8,128)S(1)}, u32[]{:S(2)}, u32[]{:S(2)}) collective-permute-start(f32[1,8,128]{2,1,0:T(8,128)S(1)} %coarse.4), channel_id=1, source_target_pairs={{0,2},{1,3},{2,0},{3,1},{4,6},{5,7},{6,4},{7,5},{8,10},{9,11},{10,... | collective-permute-start | bytes 12296 | tf_op jit(solution)/shard_map/ppermute | solution.py:22
  86.2 1.1 collective-permute-done.29
  87.3 1.9 %collective-permute-start.33 = (f32[4,8,128]{2,1,0:T(8,128)S(1)}, f32[4,8,128]{2,1,0:T(8,128)S(1)}, u32[]{:S(2)}, u32[]{:S(2)}) collective-permute-start(f32[4,8,128]{2,1,0:T(8,128)S(1)} %pad_maximum_fusion.1), channel_id=1, source_target_pairs={{0,24},{1,25},{2,26},{3,27},{4,28},{5,29},{6,30},{7,31},{8,16},{9,... | collective-permute-start | bytes 49160 | tf_op jit(solution)/shard_map/ppermute | solution.py:22
  90.8 2.7 %collective-permute-done.31 = f32[4,8,128]{2,1,0:T(8,128)S(1)} collective-permute-done((f32[4,8,128]{2,1,0:T(8,128)S(1)}, f32[4,8,128]{2,1,0:T(8,128)S(1)}, u32[]{:S(2)}, u32[]{:S(2)}) %collective-permute-start.31) | collective-permute-done | bytes 16416 | tf_op jit(solution)/shard_map/ppermute | solution.py:22
  93.6 1.2 collective-permute-done.34.far_blocks_ref
  94.9 2.4 %step.4 = (f32[5,16,512]{2,1,0:T(8,128)S(1)}, f32[5,16,512]{2,1,0:T(8,128)S(1)}, f32[5,16,512]{2,1,0:T(8,128)S(1)}, f32[5,16,512]{2,1,0:T(8,128)S(1)}, f32[5,16,...) custom-call(s32[2]{0:T(128)S(1)} %pad_add_fusion.info_ref, ...), custom_call_target="tpu_custom_call" | custom-call | tf_op jit(solution)/shard_map/step/pallas_call | solution.py:471
  97.4 1.1 collective-permute-done.36
  98.5 2.0 %collective-permute-start.39 = (f32[16,768]{1,0:T(8,128)S(1)}, f32[16,768]{1,0:T(8,128)S(1)}, u32[]{:S(2)}, u32[]{:S(2)}) collective-permute-start(f32[16,768]{1,0:T(8,128)S(1)} %add.182), channel_id=1, source_target_pairs={{0,24},{1,25},{2,26},{3,27},{4,28},{5,29},{6,30},{7,31},{8,16},{9,... | collective-permute-start | bytes 147464 | tf_op jit(solution)/shard_map/ppermute | solution.py:22
  102.5 1.6 %flex_near.5.begun_ref = f32[5,16,1024]{2,1,0:T(8,128)S(1)} custom-call(f32[5,16,512]{2,1,0:T(8,128)S(1)} %get-tuple-element.130.values_ref.z_ref, bf16[5,1024,1024]{2,1,0:T(8,128)(2,1)S(1)} %get-tuple-element.82.large_ref, bf16[5,1024,1024]{2,1,0:T(8,128)(2,1)S(1)} %get-tuple-element.83.small_ref), custom_call_target="tpu_custom_call" | custom-call | flops 503316480 | bytes 10485760 | tf_op jit(solution)/shard_map/flex_near/pallas_call | solution.py:416
  105.4 1.9 %collective-permute-start.43 = (f32[16,768]{1,0:T(8,128)S(1)}, f32[16,768]{1,0:T(8,128)S(1)}, u32[]{:S(2)}, u32[]{:S(2)}) collective-permute-start(f32[16,768]{1,0:T(8,128)S(1)} %add_add_fusion.1), channel_id=1, source_target_pairs={{0,6},{1,7},{2,4},{3,5},{4,2},{5,3},{6,0},{7,1},{8,14},{9,15},{10,... | collective-permute-start | bytes 147464 | tf_op jit(solution)/shard_map/ppermute | solution.py:22
  108.2 1.6 %collective-permute-start.41 = (f32[16,768]{1,0:T(8,128)S(1)}, f32[16,768]{1,0:T(8,128)S(1)}, u32[]{:S(2)}, u32[]{:S(2)}) collective-permute-start(f32[16,768]{1,0:T(8,128)S(1)} %add_add_fusion.1), channel_id=1, source_target_pairs={{0,2},{1,3},{2,0},{3,1},{4,6},{5,7},{6,4},{7,5},{8,10},{9,11},{10,... | collective-permute-start | bytes 147464 | tf_op jit(solution)/shard_map/ppermute | solution.py:22
  109.8 1.7 %flex_far.5 = (f32[5,16,512]{2,1,0:T(8,128)S(1)}, f32[5,16,512]{2,1,0:T(8,128)S(1)}, f32[16,128]{1,0:T(8,128)S(1)}) custom-call(f32[5,16,512]{2,1,0:T(8,128)S(1)} %get-tuple-element.130.values_ref.z_ref, f32[5,16,512]{2,1,0:T(8,128)S(1)} %collective-permute-done.40.forces_ref, f32[5,16,1024]{2,1,0:T(8,128)S(1)} %flex_near.5.begun_ref, ...), custom_call_target="tpu_custom_call" | custom-call | flops 503316480 | bytes 10485760 | tf_op jit(solution)/shard_map/flex_far/pallas_call | solution.py:427
  111.8 2.1 %collective-permute-done.42 = f32[16,768]{1,0:T(8,128)S(1)} collective-permute-done((f32[16,768]{1,0:T(8,128)S(1)}, f32[16,768]{1,0:T(8,128)S(1)}, u32[]{:S(2)}, u32[]{:S(2)}) %collective-permute-start.42) | collective-permute-done | bytes 49184 | tf_op jit(solution)/shard_map/ppermute | solution.py:22
  116.1 2.4 %collective-permute-start.47 = (f32[1,8,128]{2,1,0:T(8,128)S(1)}, f32[1,8,128]{2,1,0:T(8,128)S(1)}, u32[]{:S(2)}, u32[]{:S(2)}) collective-permute-start(f32[1,8,128]{2,1,0:T(8,128)S(1)} %coarse.5), channel_id=1, source_target_pairs={{0,6},{1,7},{2,4},{3,5},{4,2},{5,3},{6,0},{7,1},{8,14},{9,15},{10,... | collective-permute-start | bytes 12296 | tf_op jit(solution)/shard_map/ppermute | solution.py:22
  118.5 2.0 %collective-permute-start.45 = (f32[1,8,128]{2,1,0:T(8,128)S(1)}, f32[1,8,128]{2,1,0:T(8,128)S(1)}, u32[]{:S(2)}, u32[]{:S(2)}) collective-permute-start(f32[1,8,128]{2,1,0:T(8,128)S(1)} %coarse.5), channel_id=1, source_target_pairs={{0,2},{1,3},{2,0},{3,1},{4,6},{5,7},{6,4},{7,5},{8,10},{9,11},{10,... | collective-permute-start | bytes 12296 | tf_op jit(solution)/shard_map/ppermute | solution.py:22
  121.6 1.5 %collective-permute-done.46 = f32[1,8,128]{2,1,0:T(8,128)S(1)} collective-permute-done((f32[1,8,128]{2,1,0:T(8,128)S(1)}, f32[1,8,128]{2,1,0:T(8,128)S(1)}, u32[]{:S(2)}, u32[]{:S(2)}) %collective-permute-start.46) | collective-permute-done | bytes 4128 | tf_op jit(solution)/shard_map/ppermute | solution.py:22
  123.0 2.0 %collective-permute-start.50 = (f32[4,8,128]{2,1,0:T(8,128)S(1)}, f32[4,8,128]{2,1,0:T(8,128)S(1)}, u32[]{:S(2)}, u32[]{:S(2)}) collective-permute-start(f32[4,8,128]{2,1,0:T(8,128)S(1)} %pad_maximum_fusion.2), channel_id=1, source_target_pairs={{0,24},{1,25},{2,26},{3,27},{4,28},{5,29},{6,30},{7,31},{8,16},{9,... | collective-permute-start | bytes 49160 | tf_op jit(solution)/shard_map/ppermute | solution.py:22
  126.5 2.8 %collective-permute-done.48 = f32[4,8,128]{2,1,0:T(8,128)S(1)} collective-permute-done((f32[4,8,128]{2,1,0:T(8,128)S(1)}, f32[4,8,128]{2,1,0:T(8,128)S(1)}, u32[]{:S(2)}, u32[]{:S(2)}) %collective-permute-start.48) | collective-permute-done | bytes 16416 | tf_op jit(solution)/shard_map/ppermute | solution.py:22
  129.4 1.2 collective-permute-done.51.far_blocks_ref
  130.7 2.5 %step.5 = (f32[1,1,5,16,4,128]{5,4,3,2,1,0:T(4,128)}, f32[1,1,5,16,4,128]{5,4,3,2,1,0:T(4,128)}) custom-call(s32[2]{0:T(128)S(1)} %pad_add_fusion.info_ref, s32[1,1,4,5]{3,2,1,0:T(4,128)S(1)} %copy-done.7, f32[16,8,128]{2,1,0:T(8,128)S(1)} %constant_dynamic-update-slice_fusion.14.near_blocks_ref, f32[16,8,128]{2,1,0:T(8,128)S(1)} %collective-permute-done.51.far_blocks_ref, ...), custom_call_target="tpu_custom_call" | custom-call | tf_op jit(solution)/shard_map/step/pallas_call | solution.py:471
  (135 shorter events, 32.6 us)
Async XLA Ops:
  1.6 9.3 %collective-permute-start.1 = (f32[5,24,512]{2,1,0:T(8,128)S(1)}, f32[5,24,512]{2,1,0:T(8,128)S(1)}, u32[]{:S(2)}, u32[]{:S(2)}) collective-permute-start(f32[5,24,512]{2,1,0:T(8,128)S(1)} %slice_bitcast_fusion), channel_id=1, source_target_pairs={{0,1},{1,2},{2,3},{3,4},{4,5},{5,6},{6,7},{7,0},{8,9},{9,10},{10,1... | collective-permute-start | bytes 737288 | tf_op jit(solution)/shard_map/ppermute | solution.py:17
  3.6 7.1 %collective-permute-start = (s32[1,128]{1,0:T(1,128)S(1)}, s32[1,128]{1,0:T(1,128)S(1)}, u32[]{:S(2)}, u32[]{:S(2)}) collective-permute-start(s32[1,128]{1,0:T(1,128)S(1)} %pad_add_fusion.1), channel_id=1, source_target_pairs={{0,1},{1,2},{2,3},{3,4},{4,5},{5,6},{6,7},{7,0},{8,9},{9,10},{10,1... | collective-permute-start | bytes 1544 | tf_op jit(solution)/shard_map/ppermute | solution.py:17
  14.5 1.3 collective-permute-start.2
  15.9 16.9 %collective-permute-start.5 = (f32[16,768]{1,0:T(8,128)S(1)}, f32[16,768]{1,0:T(8,128)S(1)}, u32[]{:S(2)}, u32[]{:S(2)}) collective-permute-start(f32[16,768]{1,0:T(8,128)S(1)} %add.163), channel_id=1, source_target_pairs={{0,24},{1,25},{2,26},{3,27},{4,28},{5,29},{6,30},{7,31},{8,16},{9,... | collective-permute-start | bytes 147464 | tf_op jit(solution)/shard_map/ppermute | solution.py:22
  18.4 14.4 %collective-permute-start.4 = (f32[16,768]{1,0:T(8,128)S(1)}, f32[16,768]{1,0:T(8,128)S(1)}, u32[]{:S(2)}, u32[]{:S(2)}) collective-permute-start(f32[16,768]{1,0:T(8,128)S(1)} %add.163), channel_id=1, source_target_pairs={{0,16},{1,17},{2,18},{3,19},{4,20},{5,21},{6,22},{7,23},{8,24},{9,... | collective-permute-start | bytes 147464 | tf_op jit(solution)/shard_map/ppermute | solution.py:22
  18.9 13.9 %collective-permute-start.3 = (f32[16,768]{1,0:T(8,128)S(1)}, f32[16,768]{1,0:T(8,128)S(1)}, u32[]{:S(2)}, u32[]{:S(2)}) collective-permute-start(f32[16,768]{1,0:T(8,128)S(1)} %add.163), channel_id=1, source_target_pairs={{0,8},{1,9},{2,10},{3,11},{4,12},{5,13},{6,14},{7,15},{8,0},{9,1},... | collective-permute-start | bytes 147464 | tf_op jit(solution)/shard_map/ppermute | solution.py:22
  30.1 3.9 %collective-permute-start.6 = (f32[5,16,512]{2,1,0:T(8,128)S(1)}, f32[5,16,512]{2,1,0:T(8,128)S(1)}, u32[]{:S(2)}, u32[]{:S(2)}) collective-permute-start(f32[5,16,512]{2,1,0:T(8,128)S(1)} %get-tuple-element.84), channel_id=1, source_target_pairs={{0,7},{1,0},{2,1},{3,2},{4,3},{5,4},{6,5},{7,6},{8,15},{9,8},{10,9... | collective-permute-start | bytes 491528 | tf_op jit(solution)/shard_map/ppermute | solution.py:17
  34.0 6.4 %collective-permute-start.9 = (f32[16,768]{1,0:T(8,128)S(1)}, f32[16,768]{1,0:T(8,128)S(1)}, u32[]{:S(2)}, u32[]{:S(2)}) collective-permute-start(f32[16,768]{1,0:T(8,128)S(1)} %add_add_fusion.5), channel_id=1, source_target_pairs={{0,6},{1,7},{2,4},{3,5},{4,2},{5,3},{6,0},{7,1},{8,14},{9,15},{10,... | collective-permute-start | bytes 147464 | tf_op jit(solution)/shard_map/ppermute | solution.py:22
  35.9 6.4 %collective-permute-start.8 = (f32[16,768]{1,0:T(8,128)S(1)}, f32[16,768]{1,0:T(8,128)S(1)}, u32[]{:S(2)}, u32[]{:S(2)}) collective-permute-start(f32[16,768]{1,0:T(8,128)S(1)} %add_add_fusion.5), channel_id=1, source_target_pairs={{0,4},{1,5},{2,6},{3,7},{4,0},{5,1},{6,2},{7,3},{8,12},{9,13},{10,... | collective-permute-start | bytes 147464 | tf_op jit(solution)/shard_map/ppermute | solution.py:22
  36.1 6.3 %collective-permute-start.7 = (f32[16,768]{1,0:T(8,128)S(1)}, f32[16,768]{1,0:T(8,128)S(1)}, u32[]{:S(2)}, u32[]{:S(2)}) collective-permute-start(f32[16,768]{1,0:T(8,128)S(1)} %add_add_fusion.5), channel_id=1, source_target_pairs={{0,2},{1,3},{2,0},{3,1},{4,6},{5,7},{6,4},{7,5},{8,10},{9,11},{10,... | collective-permute-start | bytes 147464 | tf_op jit(solution)/shard_map/ppermute | solution.py:22
  42.5 16.9 %collective-permute-start.18 = (f32[5,16,512]{2,1,0:T(8,128)S(1)}, f32[5,16,512]{2,1,0:T(8,128)S(1)}, u32[]{:S(2)}, u32[]{:S(2)}) collective-permute-start(f32[5,16,512]{2,1,0:T(8,128)S(1)} %get-tuple-element.96), channel_id=1, source_target_pairs={{0,1},{1,2},{2,3},{3,4},{4,5},{5,6},{6,7},{7,0},{8,9},{9,10},{10,1... | collective-permute-start | bytes 491528 | tf_op jit(solution)/shard_map/ppermute | solution.py:17
  44.6 5.4 %collective-permute-start.13 = (f32[1,8,128]{2,1,0:T(8,128)S(1)}, f32[1,8,128]{2,1,0:T(8,128)S(1)}, u32[]{:S(2)}, u32[]{:S(2)}) collective-permute-start(f32[1,8,128]{2,1,0:T(8,128)S(1)} %coarse.3), channel_id=1, source_target_pairs={{0,6},{1,7},{2,4},{3,5},{4,2},{5,3},{6,0},{7,1},{8,14},{9,15},{10,... | collective-permute-start | bytes 12296 | tf_op jit(solution)/shard_map/ppermute | solution.py:22
  46.8 4.5 %collective-permute-start.12 = (f32[1,8,128]{2,1,0:T(8,128)S(1)}, f32[1,8,128]{2,1,0:T(8,128)S(1)}, u32[]{:S(2)}, u32[]{:S(2)}) collective-permute-start(f32[1,8,128]{2,1,0:T(8,128)S(1)} %coarse.3), channel_id=1, source_target_pairs={{0,4},{1,5},{2,6},{3,7},{4,0},{5,1},{6,2},{7,3},{8,12},{9,13},{10,... | collective-permute-start | bytes 12296 | tf_op jit(solution)/shard_map/ppermute | solution.py:22
  46.8 4.5 %collective-permute-start.11 = (f32[1,8,128]{2,1,0:T(8,128)S(1)}, f32[1,8,128]{2,1,0:T(8,128)S(1)}, u32[]{:S(2)}, u32[]{:S(2)}) collective-permute-start(f32[1,8,128]{2,1,0:T(8,128)S(1)} %coarse.3), channel_id=1, source_target_pairs={{0,2},{1,3},{2,0},{3,1},{4,6},{5,7},{6,4},{7,5},{8,10},{9,11},{10,... | collective-permute-start | bytes 12296 | tf_op jit(solution)/shard_map/ppermute | solution.py:22
  51.4 6.7 %collective-permute-start.16 = (f32[4,8,128]{2,1,0:T(8,128)S(1)}, f32[4,8,128]{2,1,0:T(8,128)S(1)}, u32[]{:S(2)}, u32[]{:S(2)}) collective-permute-start(f32[4,8,128]{2,1,0:T(8,128)S(1)} %pad_maximum_fusion), channel_id=1, source_target_pairs={{0,24},{1,25},{2,26},{3,27},{4,28},{5,29},{6,30},{7,31},{8,16},{9,... | collective-permute-start | bytes 49160 | tf_op jit(solution)/shard_map/ppermute | solution.py:22
  53.8 4.3 %collective-permute-start.15 = (f32[4,8,128]{2,1,0:T(8,128)S(1)}, f32[4,8,128]{2,1,0:T(8,128)S(1)}, u32[]{:S(2)}, u32[]{:S(2)}) collective-permute-start(f32[4,8,128]{2,1,0:T(8,128)S(1)} %pad_maximum_fusion), channel_id=1, source_target_pairs={{0,16},{1,17},{2,18},{3,19},{4,20},{5,21},{6,22},{7,23},{8,24},{9,... | collective-permute-start | bytes 49160 | tf_op jit(solution)/shard_map/ppermute | solution.py:22
  54.3 3.7 %collective-permute-start.14 = (f32[4,8,128]{2,1,0:T(8,128)S(1)}, f32[4,8,128]{2,1,0:T(8,128)S(1)}, u32[]{:S(2)}, u32[]{:S(2)}) collective-permute-start(f32[4,8,128]{2,1,0:T(8,128)S(1)} %pad_maximum_fusion), channel_id=1, source_target_pairs={{0,8},{1,9},{2,10},{3,11},{4,12},{5,13},{6,14},{7,15},{8,0},{9,1},... | collective-permute-start | bytes 49160 | tf_op jit(solution)/shard_map/ppermute | solution.py:22
  58.1 1.3 collective-permute-start.17
  63.1 5.7 %collective-permute-start.22 = (f32[16,768]{1,0:T(8,128)S(1)}, f32[16,768]{1,0:T(8,128)S(1)}, u32[]{:S(2)}, u32[]{:S(2)}) collective-permute-start(f32[16,768]{1,0:T(8,128)S(1)} %add.175), channel_id=1, source_target_pairs={{0,24},{1,25},{2,26},{3,27},{4,28},{5,29},{6,30},{7,31},{8,16},{9,... | collective-permute-start | bytes 147464 | tf_op jit(solution)/shard_map/ppermute | solution.py:22
  64.6 4.3 %collective-permute-start.21 = (f32[16,768]{1,0:T(8,128)S(1)}, f32[16,768]{1,0:T(8,128)S(1)}, u32[]{:S(2)}, u32[]{:S(2)}) collective-permute-start(f32[16,768]{1,0:T(8,128)S(1)} %add.175), channel_id=1, source_target_pairs={{0,16},{1,17},{2,18},{3,19},{4,20},{5,21},{6,22},{7,23},{8,24},{9,... | collective-permute-start | bytes 147464 | tf_op jit(solution)/shard_map/ppermute | solution.py:22
  65.1 4.1 %collective-permute-start.20 = (f32[16,768]{1,0:T(8,128)S(1)}, f32[16,768]{1,0:T(8,128)S(1)}, u32[]{:S(2)}, u32[]{:S(2)}) collective-permute-start(f32[16,768]{1,0:T(8,128)S(1)} %add.175), channel_id=1, source_target_pairs={{0,8},{1,9},{2,10},{3,11},{4,12},{5,13},{6,14},{7,15},{8,0},{9,1},... | collective-permute-start | bytes 147464 | tf_op jit(solution)/shard_map/ppermute | solution.py:22
  66.6 3.4 %collective-permute-start.23 = (f32[5,16,512]{2,1,0:T(8,128)S(1)}, f32[5,16,512]{2,1,0:T(8,128)S(1)}, u32[]{:S(2)}, u32[]{:S(2)}) collective-permute-start(f32[5,16,512]{2,1,0:T(8,128)S(1)} %get-tuple-element.109), channel_id=1, source_target_pairs={{0,7},{1,0},{2,1},{3,2},{4,3},{5,4},{6,5},{7,6},{8,15},{9,8},{10,9... | collective-permute-start | bytes 491528 | tf_op jit(solution)/shard_map/ppermute | solution.py:17
  70.0 6.4 %collective-permute-start.26 = (f32[16,768]{1,0:T(8,128)S(1)}, f32[16,768]{1,0:T(8,128)S(1)}, u32[]{:S(2)}, u32[]{:S(2)}) collective-permute-start(f32[16,768]{1,0:T(8,128)S(1)} %add_add_fusion.3), channel_id=1, source_target_pairs={{0,6},{1,7},{2,4},{3,5},{4,2},{5,3},{6,0},{7,1},{8,14},{9,15},{10,... | collective-permute-start | bytes 147464 | tf_op jit(solution)/shard_map/ppermute | solution.py:22
  71.9 6.6 %collective-permute-start.25 = (f32[16,768]{1,0:T(8,128)S(1)}, f32[16,768]{1,0:T(8,128)S(1)}, u32[]{:S(2)}, u32[]{:S(2)}) collective-permute-start(f32[16,768]{1,0:T(8,128)S(1)} %add_add_fusion.3), channel_id=1, source_target_pairs={{0,4},{1,5},{2,6},{3,7},{4,0},{5,1},{6,2},{7,3},{8,12},{9,13},{10,... | collective-permute-start | bytes 147464 | tf_op jit(solution)/shard_map/ppermute | solution.py:22
  72.2 6.2 %collective-permute-start.24 = (f32[16,768]{1,0:T(8,128)S(1)}, f32[16,768]{1,0:T(8,128)S(1)}, u32[]{:S(2)}, u32[]{:S(2)}) collective-permute-start(f32[16,768]{1,0:T(8,128)S(1)} %add_add_fusion.3), channel_id=1, source_target_pairs={{0,2},{1,3},{2,0},{3,1},{4,6},{5,7},{6,4},{7,5},{8,10},{9,11},{10,... | collective-permute-start | bytes 147464 | tf_op jit(solution)/shard_map/ppermute | solution.py:22
  78.6 16.2 %collective-permute-start.35 = (f32[5,16,512]{2,1,0:T(8,128)S(1)}, f32[5,16,512]{2,1,0:T(8,128)S(1)}, u32[]{:S(2)}, u32[]{:S(2)}) collective-permute-start(f32[5,16,512]{2,1,0:T(8,128)S(1)} %get-tuple-element.120), channel_id=1, source_target_pairs={{0,1},{1,2},{2,3},{3,4},{4,5},{5,6},{6,7},{7,0},{8,9},{9,10},{10,1... | collective-permute-start | bytes 491528 | tf_op jit(solution)/shard_map/ppermute | solution.py:17
  80.7 5.4 %collective-permute-start.30 = (f32[1,8,128]{2,1,0:T(8,128)S(1)}, f32[1,8,128]{2,1,0:T(8,128)S(1)}, u32[]{:S(2)}, u32[]{:S(2)}) collective-permute-start(f32[1,8,128]{2,1,0:T(8,128)S(1)} %coarse.4), channel_id=1, source_target_pairs={{0,6},{1,7},{2,4},{3,5},{4,2},{5,3},{6,0},{7,1},{8,14},{9,15},{10,... | collective-permute-start | bytes 12296 | tf_op jit(solution)/shard_map/ppermute | solution.py:22
  82.8 4.5 %collective-permute-start.29 = (f32[1,8,128]{2,1,0:T(8,128)S(1)}, f32[1,8,128]{2,1,0:T(8,128)S(1)}, u32[]{:S(2)}, u32[]{:S(2)}) collective-permute-start(f32[1,8,128]{2,1,0:T(8,128)S(1)} %coarse.4), channel_id=1, source_target_pairs={{0,4},{1,5},{2,6},{3,7},{4,0},{5,1},{6,2},{7,3},{8,12},{9,13},{10,... | collective-permute-start | bytes 12296 | tf_op jit(solution)/shard_map/ppermute | solution.py:22
  82.8 4.5 %collective-permute-start.28 = (f32[1,8,128]{2,1,0:T(8,128)S(1)}, f32[1,8,128]{2,1,0:T(8,128)S(1)}, u32[]{:S(2)}, u32[]{:S(2)}) collective-permute-start(f32[1,8,128]{2,1,0:T(8,128)S(1)} %coarse.4), channel_id=1, source_target_pairs={{0,2},{1,3},{2,0},{3,1},{4,6},{5,7},{6,4},{7,5},{8,10},{9,11},{10,... | collective-permute-start | bytes 12296 | tf_op jit(solution)/shard_map/ppermute | solution.py:22
  87.3 6.2 %collective-permute-start.33 = (f32[4,8,128]{2,1,0:T(8,128)S(1)}, f32[4,8,128]{2,1,0:T(8,128)S(1)}, u32[]{:S(2)}, u32[]{:S(2)}) collective-permute-start(f32[4,8,128]{2,1,0:T(8,128)S(1)} %pad_maximum_fusion.1), channel_id=1, source_target_pairs={{0,24},{1,25},{2,26},{3,27},{4,28},{5,29},{6,30},{7,31},{8,16},{9,... | collective-permute-start | bytes 49160 | tf_op jit(solution)/shard_map/ppermute | solution.py:22
  89.2 4.3 %collective-permute-start.32 = (f32[4,8,128]{2,1,0:T(8,128)S(1)}, f32[4,8,128]{2,1,0:T(8,128)S(1)}, u32[]{:S(2)}, u32[]{:S(2)}) collective-permute-start(f32[4,8,128]{2,1,0:T(8,128)S(1)} %pad_maximum_fusion.1), channel_id=1, source_target_pairs={{0,16},{1,17},{2,18},{3,19},{4,20},{5,21},{6,22},{7,23},{8,24},{9,... | collective-permute-start | bytes 49160 | tf_op jit(solution)/shard_map/ppermute | solution.py:22
  89.8 3.7 %collective-permute-start.31 = (f32[4,8,128]{2,1,0:T(8,128)S(1)}, f32[4,8,128]{2,1,0:T(8,128)S(1)}, u32[]{:S(2)}, u32[]{:S(2)}) collective-permute-start(f32[4,8,128]{2,1,0:T(8,128)S(1)} %pad_maximum_fusion.1), channel_id=1, source_target_pairs={{0,8},{1,9},{2,10},{3,11},{4,12},{5,13},{6,14},{7,15},{8,0},{9,1},... | collective-permute-start | bytes 49160 | tf_op jit(solution)/shard_map/ppermute | solution.py:22
  93.5 1.3 collective-permute-start.34
  98.5 5.7 %collective-permute-start.39 = (f32[16,768]{1,0:T(8,128)S(1)}, f32[16,768]{1,0:T(8,128)S(1)}, u32[]{:S(2)}, u32[]{:S(2)}) collective-permute-start(f32[16,768]{1,0:T(8,128)S(1)} %add.182), channel_id=1, source_target_pairs={{0,24},{1,25},{2,26},{3,27},{4,28},{5,29},{6,30},{7,31},{8,16},{9,... | collective-permute-start | bytes 147464 | tf_op jit(solution)/shard_map/ppermute | solution.py:22
  100.5 4.1 %collective-permute-start.38 = (f32[16,768]{1,0:T(8,128)S(1)}, f32[16,768]{1,0:T(8,128)S(1)}, u32[]{:S(2)}, u32[]{:S(2)}) collective-permute-start(f32[16,768]{1,0:T(8,128)S(1)} %add.182), channel_id=1, source_target_pairs={{0,16},{1,17},{2,18},{3,19},{4,20},{5,21},{6,22},{7,23},{8,24},{9,... | collective-permute-start | bytes 147464 | tf_op jit(solution)/shard_map/ppermute | solution.py:22
  101.0 4.1 %collective-permute-start.37 = (f32[16,768]{1,0:T(8,128)S(1)}, f32[16,768]{1,0:T(8,128)S(1)}, u32[]{:S(2)}, u32[]{:S(2)}) collective-permute-start(f32[16,768]{1,0:T(8,128)S(1)} %add.182), channel_id=1, source_target_pairs={{0,8},{1,9},{2,10},{3,11},{4,12},{5,13},{6,14},{7,15},{8,0},{9,1},... | collective-permute-start | bytes 147464 | tf_op jit(solution)/shard_map/ppermute | solution.py:22
  102.0 3.3 %collective-permute-start.40 = (f32[5,16,512]{2,1,0:T(8,128)S(1)}, f32[5,16,512]{2,1,0:T(8,128)S(1)}, u32[]{:S(2)}, u32[]{:S(2)}) collective-permute-start(f32[5,16,512]{2,1,0:T(8,128)S(1)} %get-tuple-element.131), channel_id=1, source_target_pairs={{0,7},{1,0},{2,1},{3,2},{4,3},{5,4},{6,5},{7,6},{8,15},{9,8},{10,9... | collective-permute-start | bytes 491528 | tf_op jit(solution)/shard_map/ppermute | solution.py:17
  105.4 6.4 %collective-permute-start.43 = (f32[16,768]{1,0:T(8,128)S(1)}, f32[16,768]{1,0:T(8,128)S(1)}, u32[]{:S(2)}, u32[]{:S(2)}) collective-permute-start(f32[16,768]{1,0:T(8,128)S(1)} %add_add_fusion.1), channel_id=1, source_target_pairs={{0,6},{1,7},{2,4},{3,5},{4,2},{5,3},{6,0},{7,1},{8,14},{9,15},{10,... | collective-permute-start | bytes 147464 | tf_op jit(solution)/shard_map/ppermute | solution.py:22
  107.3 6.5 %collective-permute-start.42 = (f32[16,768]{1,0:T(8,128)S(1)}, f32[16,768]{1,0:T(8,128)S(1)}, u32[]{:S(2)}, u32[]{:S(2)}) collective-permute-start(f32[16,768]{1,0:T(8,128)S(1)} %add_add_fusion.1), channel_id=1, source_target_pairs={{0,4},{1,5},{2,6},{3,7},{4,0},{5,1},{6,2},{7,3},{8,12},{9,13},{10,... | collective-permute-start | bytes 147464 | tf_op jit(solution)/shard_map/ppermute | solution.py:22
  108.2 5.7 %collective-permute-start.41 = (f32[16,768]{1,0:T(8,128)S(1)}, f32[16,768]{1,0:T(8,128)S(1)}, u32[]{:S(2)}, u32[]{:S(2)}) collective-permute-start(f32[16,768]{1,0:T(8,128)S(1)} %add_add_fusion.1), channel_id=1, source_target_pairs={{0,2},{1,3},{2,0},{3,1},{4,6},{5,7},{6,4},{7,5},{8,10},{9,11},{10,... | collective-permute-start | bytes 147464 | tf_op jit(solution)/shard_map/ppermute | solution.py:22
  114.0 16.6 %collective-permute-start.52 = (f32[5,16,512]{2,1,0:T(8,128)S(1)}, f32[5,16,512]{2,1,0:T(8,128)S(1)}, u32[]{:S(2)}, u32[]{:S(2)}) collective-permute-start(f32[5,16,512]{2,1,0:T(8,128)S(1)} %get-tuple-element.142), channel_id=1, source_target_pairs={{0,1},{1,2},{2,3},{3,4},{4,5},{5,6},{6,7},{7,0},{8,9},{9,10},{10,1... | collective-permute-start | bytes 491528 | tf_op jit(solution)/shard_map/ppermute | solution.py:17
  116.1 5.4 %collective-permute-start.47 = (f32[1,8,128]{2,1,0:T(8,128)S(1)}, f32[1,8,128]{2,1,0:T(8,128)S(1)}, u32[]{:S(2)}, u32[]{:S(2)}) collective-permute-start(f32[1,8,128]{2,1,0:T(8,128)S(1)} %coarse.5), channel_id=1, source_target_pairs={{0,6},{1,7},{2,4},{3,5},{4,2},{5,3},{6,0},{7,1},{8,14},{9,15},{10,... | collective-permute-start | bytes 12296 | tf_op jit(solution)/shard_map/ppermute | solution.py:22
  118.5 4.5 %collective-permute-start.46 = (f32[1,8,128]{2,1,0:T(8,128)S(1)}, f32[1,8,128]{2,1,0:T(8,128)S(1)}, u32[]{:S(2)}, u32[]{:S(2)}) collective-permute-start(f32[1,8,128]{2,1,0:T(8,128)S(1)} %coarse.5), channel_id=1, source_target_pairs={{0,4},{1,5},{2,6},{3,7},{4,0},{5,1},{6,2},{7,3},{8,12},{9,13},{10,... | collective-permute-start | bytes 12296 | tf_op jit(solution)/shard_map/ppermute | solution.py:22
  118.5 4.5 %collective-permute-start.45 = (f32[1,8,128]{2,1,0:T(8,128)S(1)}, f32[1,8,128]{2,1,0:T(8,128)S(1)}, u32[]{:S(2)}, u32[]{:S(2)}) collective-permute-start(f32[1,8,128]{2,1,0:T(8,128)S(1)} %coarse.5), channel_id=1, source_target_pairs={{0,2},{1,3},{2,0},{3,1},{4,6},{5,7},{6,4},{7,5},{8,10},{9,11},{10,... | collective-permute-start | bytes 12296 | tf_op jit(solution)/shard_map/ppermute | solution.py:22
  123.0 6.3 %collective-permute-start.50 = (f32[4,8,128]{2,1,0:T(8,128)S(1)}, f32[4,8,128]{2,1,0:T(8,128)S(1)}, u32[]{:S(2)}, u32[]{:S(2)}) collective-permute-start(f32[4,8,128]{2,1,0:T(8,128)S(1)} %pad_maximum_fusion.2), channel_id=1, source_target_pairs={{0,24},{1,25},{2,26},{3,27},{4,28},{5,29},{6,30},{7,31},{8,16},{9,... | collective-permute-start | bytes 49160 | tf_op jit(solution)/shard_map/ppermute | solution.py:22
  125.0 4.3 %collective-permute-start.49 = (f32[4,8,128]{2,1,0:T(8,128)S(1)}, f32[4,8,128]{2,1,0:T(8,128)S(1)}, u32[]{:S(2)}, u32[]{:S(2)}) collective-permute-start(f32[4,8,128]{2,1,0:T(8,128)S(1)} %pad_maximum_fusion.2), channel_id=1, source_target_pairs={{0,16},{1,17},{2,18},{3,19},{4,20},{5,21},{6,22},{7,23},{8,24},{9,... | collective-permute-start | bytes 49160 | tf_op jit(solution)/shard_map/ppermute | solution.py:22
  125.6 3.7 %collective-permute-start.48 = (f32[4,8,128]{2,1,0:T(8,128)S(1)}, f32[4,8,128]{2,1,0:T(8,128)S(1)}, u32[]{:S(2)}, u32[]{:S(2)}) collective-permute-start(f32[4,8,128]{2,1,0:T(8,128)S(1)} %pad_maximum_fusion.2), channel_id=1, source_target_pairs={{0,8},{1,9},{2,10},{3,11},{4,12},{5,13},{6,14},{7,15},{8,0},{9,1},... | collective-permute-start | bytes 49160 | tf_op jit(solution)/shard_map/ppermute | solution.py:22
  129.3 1.3 collective-permute-start.51
  (13 other events, 64.6 us)

commit v3 on v2

v3 whole, which is shorter than its diff:
```python
import functools
import jax
import jax.numpy as jnp
from jax import lax
from jax.experimental import pallas as pl
from jax.experimental.pallas import tpu as pltpu
from jax.sharding import PartitionSpec as P

ITERS = 3
BOTH = ("row", "col")
LANES = 128
BUFFERS = 6


def shifted(x, axis, by):
    devices = lax.axis_size(axis)
    return lax.ppermute(x, axis, [(i, (i + by) % devices) for i in range(devices)])


def swapped(x, bits):
    devices = lax.axis_size(BOTH)
    return lax.ppermute(x, BOTH, [(i, i ^ bits) for i in range(devices)])


def pieces(x, count):
    out = []
    for step in range(count):
        part = x.astype(jnp.bfloat16)
        out.append(part)
        if step + 1 < count:
            x = x - part.astype(jnp.float32)
    return out


def stacked(x, count):
    return jnp.concatenate(pieces(x, count), axis=0)


def matmul(a, b):
    return jnp.dot(a, b, preferred_element_type=jnp.float32)


def through_table(x, table):
    rows = x.shape[0]
    full = matmul(stacked(x, 3), table)
    return full[2 * rows :] + full[rows : 2 * rows] + full[:rows]


def slot_mask(slots, loads, corners):
    row = lax.broadcasted_iota(jnp.int32, (slots * loads, LANES), 0) // loads
    lane = lax.broadcasted_iota(jnp.int32, (slots * loads, LANES), 1) // corners
    return row == lane


def to_corners(values, columns, corners):
    slots, loads, n = values.shape
    rows = slots * loads
    full = matmul(stacked(values.reshape(rows, n), 2), columns)
    full = (full[rows:, :LANES] + full[:rows, LANES:]) + full[:rows, :LANES]
    kept = jnp.where(slot_mask(slots, loads, corners), full, 0.0)
    return jnp.sum(kept.reshape(slots, loads, LANES), axis=0)


def from_corners(answer, matrix, slots, corners):
    loads = answer.shape[0]
    rows = slots * loads
    spread = jnp.broadcast_to(answer[None], (slots, loads, LANES)).reshape(rows, LANES)
    spread = jnp.where(slot_mask(slots, loads, corners), spread, 0.0)
    both = stacked(spread, 2)
    full = matmul(jnp.concatenate([both, both], axis=1), matrix)
    return (full[rows:] + full[:rows]).reshape(slots, loads, full.shape[1])


def corner_rows(coupling, width):
    slots, corners, _ = coupling.shape
    parts = [coupling[s, :, :width] for s in range(slots)]
    if slots * corners < LANES:
        parts.append(jnp.zeros((LANES - slots * corners, width), jnp.float32))
    return jnp.concatenate(parts, axis=0)


def split_in_turn(flex_ref, part, large_ref, small_ref, buffer, sem):
    slots, iface = flex_ref.shape[2:4]
    depth = buffer.shape[1]
    per_slot = iface // 2 // depth
    chunks = slots * per_slot

    def chunk(c):
        first = pl.multiple_of(part * (iface // 2) + (c % per_slot) * depth, depth)
        return pltpu.make_async_copy(
            flex_ref.at[0, 0, c // per_slot, pl.ds(first, depth), :], buffer.at[c % BUFFERS], sem.at[c % BUFFERS]
        )

    def begin():
        for c in range(min(BUFFERS, chunks)):
            chunk(c).start()

    def one(c, carry):
        chunk(c).wait()
        rows = pl.ds(pl.multiple_of((c % per_slot) * depth, depth), depth)
        large, small = pieces(buffer[c % BUFFERS], 2)
        large_ref[c // per_slot, rows, :] = large
        small_ref[c // per_slot, rows, :] = small

        @pl.when(c + BUFFERS < chunks)
        def _():
            chunk(c + BUFFERS).start()

        return carry

    return begin, lambda: lax.fori_loop(0, chunks, one, 0)


def split_kernel(flex_ref, large_ref, small_ref, buffer, sem):
    begin, end = split_in_turn(flex_ref, 1, large_ref, small_ref, buffer, sem)
    begin()
    end()


def pack_kernel(coupling_ref, map_ref, counts_ref, out_ref, sem):
    slots, corners = map_ref.shape[2:]
    span = out_ref.shape[2] - LANES
    copy = pltpu.make_async_copy(coupling_ref.at[0, 0, :, :, pl.ds(span, span)], out_ref.at[:, :, pl.ds(0, span)], sem)
    copy.start()
    padded = jnp.concatenate([map_ref[0, 0].astype(jnp.float32), jnp.zeros((8 - slots, corners), jnp.float32)], axis=0)
    column = jnp.concatenate([padded, jnp.zeros((8, LANES - corners), jnp.float32)], axis=1).T
    lane = lax.broadcasted_iota(jnp.int32, (corners, LANES), 1)
    live = jnp.full((corners, LANES), counts_ref[0, 0], jnp.int32).astype(jnp.float32)
    for s in range(slots):
        out_ref[s, :, span:] = jnp.where(lane == 0, column[:corners, s : s + 1], live)
    copy.wait()


def prepare_kernel(
    info_ref, flex_ref, coupling_ref, dof_ref, right_ref, weight_ref, large_ref, small_ref, inverse_ref, dof_rows_ref, link_ref,
    link_t_ref, right_rows_ref, weight_rows_ref, buffer, coupling_buffer, dof_buffer, right_buffer, weight_buffer, flex_sem, sem,
):
    slots, links, width = dof_buffer.shape
    span = links * width
    begin, end = split_in_turn(flex_ref, 0, large_ref, small_ref, buffer, flex_sem)
    others = [
        pltpu.make_async_copy(dof_ref.at[0, 0], dof_buffer, sem.at[0]),
        pltpu.make_async_copy(coupling_ref.at[0, 0], coupling_buffer, sem.at[1]),
        pltpu.make_async_copy(right_ref.at[0, 0], right_buffer, sem.at[2]),
        pltpu.make_async_copy(weight_ref.at[0, 0], weight_buffer, sem.at[3]),
    ]
    for copy in others:
        copy.start()
    begin()
    others[0].wait()
    for j in range(slots):
        for k in range(links):
            at = slice(j * links + k, j * links + k + 1)
            met = dof_buffer[j, k : k + 1, :]
            hit = jnp.broadcast_to(met, (width, width)) == lax.broadcasted_iota(jnp.int32, (width, width), 0)
            place = jnp.where(hit, lax.broadcasted_iota(jnp.int32, (width, width), 1), 0).astype(jnp.float32)
            found = jnp.sum(place.T, axis=0, keepdims=True)
            inverse_ref[at, :] = found.astype(jnp.int32)
            dof_rows_ref[at, :] = met
    others[1].wait()
    link = corner_rows(coupling_buffer[...], span)
    link_ref[...] = stacked(link, 2)
    link_t_ref[...] = jnp.concatenate(pieces(link.T, 2), axis=1)
    others[2].wait()
    others[3].wait()
    for j in range(slots):
        for k in range(links):
            lanes = slice(k * width, (k + 1) * width)
            right_rows_ref[j, :, lanes] = right_buffer[j, :, k, :]
            weight_rows_ref[j : j + 1, lanes] = weight_buffer[j, k : k + 1, :]
    end()


def start_exchange(
    z, norm, partner_ref, inverse_ref, link_t_ref, prev_t_ref, scatter_ref, parity, corners, send_ref, mine_ref, other_ref
):
    slots, loads, span = z.shape
    links = span // LANES
    for j in range(slots):
        for k in range(links):
            block = z[j, :, k * LANES : (k + 1) * LANES]
            index = jnp.broadcast_to(inverse_ref[j * links + k][None], (loads, LANES))
            send_ref[partner_ref[0, 0, k, j], :, k * LANES : (k + 1) * LANES] = -jnp.take_along_axis(block, index, axis=1)
    own = to_corners(z, link_t_ref[...], corners)
    prev = to_corners(send_ref[...], prev_t_ref[...], corners)
    load = through_table(jnp.concatenate([own, prev], axis=1), scatter_ref[...])
    half = load.shape[1] // 2
    low, high = load[:, :half], load[:, half:]
    mine_ref[:, :half] = jnp.where(parity == 0, low, high)
    other_ref[:, :half] = jnp.where(parity == 0, high, low)
    spare = jnp.where(lax.broadcasted_iota(jnp.int32, (loads, LANES), 1) == 0, norm, 0.0)
    mine_ref[:, half:] = spare
    other_ref[:, half:] = spare


def local_norm(r, z):
    return jnp.sum(jnp.sum(r * z, axis=0), axis=1, keepdims=True)


def first_kernel(
    corners, info_ref, partner_ref, counts_ref, right_ref, weight_ref, inverse_ref, link_t_ref, map_ref, prev_coupling_ref,
    mask_ref, r_ref, z_ref, send_ref, mine_ref, other_ref, prev_t_ref, scatter_ref,
):
    slots, loads, span = r_ref.shape
    links = span // LANES
    live_prev = prev_coupling_ref[0, 0:1, span:][:, 1:2]
    for j in range(slots):
        live = jnp.where(j < counts_ref[0, 0], live_prev, 0.0)
        for k in range(links):
            met = jnp.full((1, LANES), partner_ref[0, 0, k, j], jnp.int32).astype(jnp.float32)
            mask_ref[j : j + 1, k * LANES : (k + 1) * LANES] = jnp.where(met < live, 1.0, 0.0)
    r = right_ref[...] * mask_ref[...][:, None, :]
    z = weight_ref[...][:, None, :] * r
    r_ref[...] = r
    z_ref[...] = z
    prev_t_ref[...] = jnp.concatenate(pieces(corner_rows(prev_coupling_ref[...], span).T, 2), axis=1)
    size = scatter_ref.shape[1]
    lane = lax.broadcasted_iota(jnp.int32, (corners, size), 1)
    padded = jnp.concatenate([map_ref[0, 0].astype(jnp.float32), jnp.zeros((8 - slots, corners), jnp.float32)], axis=0)
    column = jnp.concatenate([padded, jnp.zeros((8, LANES - corners), jnp.float32)], axis=1).T
    own = [column[:corners, s : s + 1] for s in range(slots)]
    prev = [prev_coupling_ref[s, :, span:][:, :1] for s in range(slots)]
    for side, columns in enumerate((own, prev)):
        parts = [(c.astype(jnp.int32) == lane).astype(jnp.float32) for c in columns]
        if slots * corners < LANES:
            parts.append(jnp.zeros((LANES - slots * corners, size), jnp.float32))
        scatter_ref[side * LANES : (side + 1) * LANES, :] = jnp.concatenate(parts, axis=0).astype(jnp.bfloat16)
    start_exchange(
        z, local_norm(r, z), partner_ref, inverse_ref, link_t_ref, prev_t_ref, scatter_ref, info_ref[0], corners,
        send_ref, mine_ref, other_ref,
    )


def table_kernel(rows, levels, info_ref, prev_coupling_ref, map_ref, *refs):
    *parts, prev_ref, pick_ref, coarse_ref, joined_ref = refs
    span = prev_ref.shape[1]
    prev_ref[...] = stacked(corner_rows(prev_coupling_ref[...], span), 2)
    slots, corners = map_ref.shape[2:]
    side_rows = len(parts) // 2
    per_level = rows * len(parts)
    lines = []
    own = [map_ref[0, 0, s : s + 1, :] for s in range(slots)]
    filled = jnp.zeros((LANES - corners, LANES), jnp.float32)
    prev = [jnp.concatenate([prev_coupling_ref[s, :, span:], filled], axis=0).T for s in range(slots)]
    prev = [turned[:1, :corners].astype(jnp.int32) for turned in prev]
    for line in (own, prev):
        if slots * corners < LANES:
            line.append(jnp.full((1, LANES - slots * corners), -1, jnp.int32))
        lines += line
    maps = jnp.concatenate(lines, axis=1)
    row = maps // (2 * rows * levels)
    rest = maps - row * (2 * rows * levels)
    level = rest // (2 * rows)
    within = rest - level * (2 * rows)
    place = jnp.bitwise_xor(level, info_ref[2]) * per_level + row * (2 * rows) + within
    place = jnp.where(maps >= 0, place, -1)
    pick_ref[...] = (place == lax.broadcasted_iota(jnp.int32, pick_ref.shape, 0)).astype(jnp.bfloat16)
    for core in range(2):
        for away in range(side_rows):
            at = jnp.bitwise_xor(info_ref[1], away) * (2 * rows) + jnp.bitwise_xor(info_ref[0], core) * rows
            joined_ref[pl.ds(pl.multiple_of(at, 8), rows), :] = parts[core * side_rows + away][...]
    coarse_ref[...] = jnp.concatenate(pieces(joined_ref[...].T, 2), axis=1)


def step_kernel(
    corners, levels, first, last, info_ref, partner_ref, own_ref, facing_ref, weight_ref, dof_ref,
    inverse_ref, mask_ref, link_ref, prev_ref, link_t_ref, prev_t_ref, scatter_ref, pick_ref, r_ref, z_ref, *refs,
):
    refs = list(refs)
    block_refs = refs[:levels]
    refs = refs[levels:]
    if not first:
        x_ref, p_ref, s_ref, past_ref = refs[:4]
        refs = refs[4:]
    x_out, r_out = refs[:2]
    far_ref = refs[-1]
    slots, loads, span = own_ref.shape
    links = span // LANES
    per_level = pick_ref.shape[0] // levels
    spare = block_refs[0][:, per_level:]
    norm = spare[:, 1:2]
    product = spare[:, :1]
    for ref in block_refs[1:]:
        product = product + ref[:, per_level:][:, :1]
    gathered = jnp.concatenate([ref[:, :per_level] for ref in block_refs], axis=1)
    picked = through_table(gathered, pick_ref[...])
    near = own_ref[...] + from_corners(picked[:, :LANES], link_ref[...], slots, corners)
    far_ref[...] = facing_ref[...] + from_corners(picked[:, LANES:], prev_ref[...], slots, corners)
    jumps = []
    for j in range(slots):
        parts = []
        for k in range(links):
            block = far_ref[partner_ref[0, 0, k, j], :, k * LANES : (k + 1) * LANES]
            index = jnp.broadcast_to(dof_ref[j * links + k][None], (loads, LANES))
            parts.append(jnp.take_along_axis(block, index, axis=1))
        jumps.append(jnp.concatenate(parts, axis=1)[None])
    image = (near - jnp.concatenate(jumps, axis=0)) * mask_ref[...][:, None, :]
    if first:
        alpha = norm / product
        p, s = z_ref[...], image
        x = alpha[None] * p
    else:
        ratio = norm / past_ref[:, :1]
        alpha = norm / (product - ratio * norm / past_ref[:, 1:2])
        p = z_ref[...] + ratio[None] * p_ref[...]
        s = image + ratio[None] * s_ref[...]
        x = x_ref[...] + alpha[None] * p
    r = r_ref[...] - alpha[None] * s
    if last:
        for j in range(slots):
            for k in range(links):
                x_out[0, 0, j, :, k, :] = x[j, :, k * LANES : (k + 1) * LANES]
                r_out[0, 0, j, :, k, :] = r[j, :, k * LANES : (k + 1) * LANES]
        return
    z_out, p_out, s_out, past_out, send_ref, mine_ref, other_ref = refs[2:9]
    x_out[...] = x
    r_out[...] = r
    z = weight_ref[...][:, None, :] * r
    z_out[...] = z
    p_out[...] = p
    s_out[...] = s
    lane = lax.broadcasted_iota(jnp.int32, past_out.shape, 1)
    past_out[...] = jnp.where(lane == 0, norm, alpha)
    start_exchange(
        z, local_norm(r, z), partner_ref, inverse_ref, link_t_ref, prev_t_ref, scatter_ref, info_ref[0], corners,
        send_ref, mine_ref, other_ref,
    )


def flex_product(values, large, small):
    loads = values.shape[0]
    full = matmul(stacked(values, 2), large)
    rest = matmul(values.astype(jnp.bfloat16), small)
    return (full[loads:] + rest) + full[:loads]


def flex_near_kernel(values_ref, large_ref, small_ref, out_ref):
    slots, _, width = values_ref.shape
    for s in range(slots):
        out_ref[s] = flex_product(values_ref[s], large_ref[s], small_ref[s])


def flex_far_kernel(values_ref, forces_ref, begun_ref, large_ref, small_ref, own_ref, facing_ref, energy_ref):
    slots, loads, width = values_ref.shape
    work = jnp.zeros((loads, 1), jnp.float32)
    for s in range(slots):
        answer = begun_ref[s] + flex_product(forces_ref[s], large_ref[s], small_ref[s])
        own, facing = answer[:, :width], answer[:, width:]
        own_ref[s] = own
        facing_ref[s] = facing
        work += jnp.sum(values_ref[s] * own + forces_ref[s] * facing, axis=1, keepdims=True)
    half = energy_ref.shape[1] - LANES
    energy_ref[:, :half] = jnp.zeros((loads, half), jnp.float32)
    energy_ref[:, half:] = jnp.where(lax.broadcasted_iota(jnp.int32, (loads, LANES), 1) == 1, work, 0.0)


def coarse_kernel(rows, levels, info_ref, mine_ref, other_ref, table_ref, out_ref):
    parity = info_ref[0]
    half = mine_ref.shape[1] - LANES
    mine, other = mine_ref[:, :half], other_ref[:, :half]
    low, high = jnp.where(parity == 0, mine, other), jnp.where(parity == 0, other, mine)
    load = jnp.concatenate([low, high], axis=1)
    loads, size = load.shape
    per_level = table_ref.shape[1] // 2
    full = matmul(stacked(load, 3), table_ref[...])

    def part(i, j):
        return full[i * loads : (i + 1) * loads, j * per_level : (j + 1) * per_level]

    answer = ((part(2, 0) + part(1, 1)) + (part(1, 0) + part(0, 1))) + part(0, 0)
    stretch = 2 * rows
    own = jnp.zeros((loads, per_level), jnp.float32)
    for level in range(levels):
        starts = range(level * stretch, size, levels * stretch)
        own = jnp.where(info_ref[2] == level, jnp.concatenate([load[:, a : a + stretch] for a in starts], axis=1), own)
    mine_spare, other_spare = mine_ref[:, half:], other_ref[:, half:]
    product = jnp.sum(answer * own, axis=1, keepdims=True) + (mine_spare[:, 1:2] + other_spare[:, 1:2])
    lane = lax.broadcasted_iota(jnp.int32, (loads, LANES), 1)
    out_ref[:, :per_level] = answer
    out_ref[:, per_level:] = jnp.where(lane == 0, product, jnp.where(lane == 1, mine_spare[:, :1], 0.0))


VMEM = pl.BlockSpec(memory_space=pltpu.VMEM)
SMEM = pl.BlockSpec(memory_space=pltpu.SMEM)
HBM = pl.BlockSpec(memory_space=pltpu.HBM)
LITTLE = pl.CostEstimate(flops=1024, bytes_accessed=1024, transcendentals=0)
PARAMS = pltpu.CompilerParams(vmem_limit_bytes=14 * 1024 * 1024)


def shape_of(*dims, dtype=jnp.float32):
    return pltpu.VMEM(dims, dtype)


def gathered_along(blocks, bits):
    if len(bits) == 2 and len(blocks) == 1:
        return blocks + [swapped(blocks[0], b) for b in (bits[0], bits[1], bits[0] + bits[1])]
    for bit in bits:
        blocks = blocks + [swapped(b, bit) for b in blocks]
    return blocks


def summed_along(total, bits):
    if len(bits) == 2:
        return sum([swapped(total, b) for b in (bits[0], bits[1], bits[0] + bits[1])], total)
    for bit in bits:
        total = total + swapped(total, bit)
    return total


def powers(start, stop):
    out = []
    while start < stop:
        out.append(start)
        start *= 2
    return out


def local(
    flexibility,
    coupling,
    coarse_inverse,
    precon_weight,
    right_side,
    counts,
    partner,
    dof_index,
    corner_map,
):
    devices, columns = lax.axis_size(BOTH), lax.axis_size("col")
    levels = columns // 2
    slots, iface = flexibility.shape[2:4]
    links, width = dof_index.shape[-2:]
    loads = right_side.shape[3]
    corners = corner_map.shape[-1]
    rows, coarse_size = coarse_inverse.shape
    span = links * width
    per_level = coarse_size // levels
    row_bits, level_bits = powers(columns, devices), powers(2, columns)
    at_col = lax.axis_index("col")
    info = jnp.stack([at_col % 2, lax.axis_index("row"), at_col // 2]).astype(jnp.int32)

    coupling = pltpu.with_memory_space_constraint(coupling, pltpu.HBM)
    to_next = pl.pallas_call(
        pack_kernel,
        out_shape=shape_of(slots, corners, span + LANES),
        in_specs=[HBM, VMEM, SMEM],
        out_specs=VMEM,
        scratch_shapes=[pltpu.SemaphoreType.DMA],
        compiler_params=PARAMS,
        cost_estimate=LITTLE,
        name="pack",
    )(coupling, corner_map, counts)
    prev_coupling = shifted(to_next, "col", 1)
    coarse_parts = gathered_along([coarse_inverse], row_bits)
    coarse_parts = coarse_parts + [swapped(part, 1) for part in coarse_parts]

    state = shape_of(slots, loads, span)
    small = shape_of(loads, LANES)
    half_load = shape_of(loads, coarse_size // 2 + LANES)
    out_state = jax.ShapeDtypeStruct(right_side.shape, jnp.float32)

    def table(*dims):
        return shape_of(*dims, dtype=jnp.bfloat16)

    depth = iface // 4
    half_pieces = (table(slots, span, iface), table(slots, span, iface))
    buffers = [pltpu.VMEM((BUFFERS, depth, iface), jnp.float32)]
    flex = pltpu.with_memory_space_constraint(flexibility, pltpu.HBM)
    in_place = [pltpu.with_memory_space_constraint(a, pltpu.HBM) for a in (dof_index, right_side, precon_weight)]
    near_large, near_small, inverse, dof, link, link_t, right, weight = pl.pallas_call(
        prepare_kernel,
        out_shape=half_pieces
        + (
            shape_of(slots * links, width, dtype=jnp.int32), shape_of(slots * links, width, dtype=jnp.int32),
            table(2 * LANES, span), table(span, 2 * LANES), state, shape_of(slots, span),
        ),
        in_specs=[SMEM] + [HBM] * 5,
        out_specs=[VMEM] * 8,
        scratch_shapes=buffers
        + [
            pltpu.VMEM(coupling.shape[2:], jnp.float32),
            pltpu.VMEM((slots, links, width), jnp.int32),
            pltpu.VMEM(right_side.shape[2:], jnp.float32),
            pltpu.VMEM((slots, links, width), jnp.float32),
            pltpu.SemaphoreType.DMA((BUFFERS,)),
            pltpu.SemaphoreType.DMA((4,)),
        ],
        compiler_params=PARAMS,
        cost_estimate=LITTLE,
        name="prepare",
    )(info, flex, coupling, *in_place)
    mask, r, z, send, mine, other, prev_t, scatter = pl.pallas_call(
        functools.partial(first_kernel, corners),
        out_shape=(
            shape_of(slots, span), state, state, state, half_load, half_load, table(span, 2 * LANES),
            table(2 * LANES, coarse_size),
        ),
        in_specs=[SMEM] * 3 + [VMEM] * 6,
        out_specs=[VMEM] * 8,
        compiler_params=PARAMS,
        cost_estimate=LITTLE,
        name="first",
    )(info, partner, counts, right, weight, inverse, link_t, corner_map, prev_coupling)

    def split_far(flex):
        return pl.pallas_call(
            split_kernel,
            out_shape=half_pieces,
            in_specs=[HBM],
            out_specs=[VMEM] * 2,
            scratch_shapes=buffers + [pltpu.SemaphoreType.DMA((BUFFERS,))],
            compiler_params=PARAMS,
            cost_estimate=LITTLE,
            name="split",
        )(pltpu.with_memory_space_constraint(flex, pltpu.HBM))

    def tables():
        return pl.pallas_call(
            functools.partial(table_kernel, rows, levels),
            out_shape=(table(2 * LANES, span), table(coarse_size, 2 * LANES), table(coarse_size, 2 * per_level)),
            in_specs=[SMEM] + [VMEM] * (2 + len(coarse_parts)),
            out_specs=[VMEM] * 3,
            scratch_shapes=[pltpu.VMEM((per_level, coarse_size), jnp.float32)],
            compiler_params=pltpu.CompilerParams(vmem_limit_bytes=max(14 * 1024 * 1024, 16 * per_level * coarse_size)),
            cost_estimate=LITTLE,
            name="tables",
        )(info, prev_coupling, corner_map, *coarse_parts)

    kept = ()
    for iteration in range(ITERS):
        first, last = iteration == 0, iteration + 1 == ITERS
        forces = shifted(send, "col", -1)
        total = mine + swapped(other, 1)
        total, held, flexibility = lax.optimization_barrier((total, z, flexibility))
        if first:
            far_large, far_small = split_far(flexibility)
        begun = pl.pallas_call(
            flex_near_kernel,
            out_shape=shape_of(slots, loads, iface),
            in_specs=[VMEM] * 3,
            out_specs=VMEM,
            compiler_params=PARAMS,
            cost_estimate=LITTLE,
            name="flex_near",
        )(held, near_large, near_small)
        total = summed_along(total, level_bits)
        own, facing, energy = pl.pallas_call(
            flex_far_kernel,
            out_shape=(state, state, half_load),
            in_specs=[VMEM] * 5,
            out_specs=[VMEM] * 3,
            compiler_params=PARAMS,
            cost_estimate=LITTLE,
            name="flex_far",
        )(held, forces, begun, far_large, far_small)
        total = summed_along(total + energy, row_bits)
        rest = swapped(total, 1)
        facing_prev = shifted(facing, "col", 1)
        if first:
            prev, pick, coarse_table = tables()
        block = pl.pallas_call(
            functools.partial(coarse_kernel, rows, levels),
            out_shape=shape_of(loads, per_level + LANES),
            in_specs=[SMEM] + [VMEM] * 3,
            out_specs=VMEM,
            compiler_params=PARAMS,
            cost_estimate=LITTLE,
            name="coarse",
        )(info, total, rest, coarse_table)
        blocks = gathered_along([block], level_bits)
        outs = (out_state, out_state) if last else (state,) * 5 + (small, state, half_load, half_load)
        results = pl.pallas_call(
            functools.partial(step_kernel, corners, levels, first, last),
            out_shape=outs,
            in_specs=[SMEM, SMEM] + [VMEM] * (14 + levels + len(kept)),
            out_specs=[VMEM] * len(outs),
            scratch_shapes=[pltpu.VMEM((slots, loads, span), jnp.float32)],
            compiler_params=PARAMS,
            cost_estimate=LITTLE,
            name="step",
        )(
            info, partner, own, facing_prev, weight, dof, inverse, mask, link, prev, link_t, prev_t,
            scatter, pick, r, z, *blocks, *kept,
        )
        if last:
            return results
        x, r, z, p, s, past, send, mine, other = results
        kept = (x, p, s, past)


def solution(mesh):
    in_specs = (
        P("row", "col", None, None, None),
        P("row", "col", None, None, None),
        P(("row", "col"), None),
        P("row", "col", None, None, None),
        P("row", "col", None, None, None, None),
        P("row", "col"),
        P("row", "col", None, None),
        P("row", "col", None, None, None),
        P("row", "col", None, None),
    )
    out_specs = (P("row", "col", None, None, None, None), P("row", "col", None, None, None, None))
    return jax.shard_map(local, mesh=mesh, in_specs=in_specs, out_specs=out_specs, check_vma=False)
```

time: 134 us -> 112 us (0.84)
  waiting for transfers between devices: 34.8 us -> 26.3 us
  local copies, waits for them, and re-layouts: 6.36 us -> 0.69 us
  starting transfers between devices: 55.2 us -> 49.7 us
    ppermute x45 -> x40, waiting for transfers between devices: 32.6 us -> 23.6 us  [swapped(): return lax.ppermute(x, BOTH, [(i, i ^ bits) for i in range(devices)])]
    unnamed x34 -> x5, local copies, waits for them, and re-layouts: 5.03 us -> 0.69 us
    ppermute x45 -> x40, starting transfers between devices: 48.7 us -> 45.1 us  [swapped(): return lax.ppermute(x, BOTH, [(i, i ^ bits) for i in range(devices)])]
    ppermute x8 -> x7, starting transfers between devices: 6.45 us -> 4.6 us  [shifted(): lax.ppermute(x, axis, [(i, (i + by) % devices) for i in range(devices)])]
    ppermute x8 -> x7, waiting for transfers between devices: 2.15 us -> 2.75 us  [shifted(): lax.ppermute(x, axis, [(i, (i + by) % devices) for i in range(devices)])]
    pallas_call x15 -> x16, Pallas kernels: 32.8 us -> 32.4 us  [the longest x3 6.01 us: local(): pl.pallas_call(functools.partial(step_kernel, corners, levels, first, las...]
  transfers between devices with their start and end apart: 53 -> 47, of which waited for: 31 -> 22; matrix products, arithmetic and copies ran while one was open for 1% -> 0% of each run, Pallas kernels for 19% -> 23%
where the time goes in v3:
time: 112 us
  starting transfers between devices  49.7 us (44%)
  Pallas kernels  33.8 us (30%)
  waiting for transfers between devices  26.3 us (23%)
  between operations  1.44 us (1%)
    ppermute x40, starting transfers between devices, swapped(): return lax.ppermute(x, BOTH, [(i, i ^ bits) for i in range(devices)])  45.1 us
    ppermute x40, waiting for transfers between devices, swapped(): return lax.ppermute(x, BOTH, [(i, i ^ bits) for i in range(devices)])  23.6 us
    pallas_call x3, Pallas kernels, local(): pl.pallas_call(functools.partial(step_kernel, corners, levels, first, las...  6.01 us
    pallas_call x1, Pallas kernels, local(): pl.pallas_call(prepare_kernel, out_shape=half_pieces + (shape_of(slots *...  5.75 us
    pallas_call x3, Pallas kernels, local(): pl.pallas_call(flex_far_kernel, out_shape=(state, state, half_load), in_s...  5.17 us
    pallas_call x3, Pallas kernels, local(): pl.pallas_call(flex_near_kernel, out_shape=shape_of(slots, loads, iface),...  4.84 us
    ppermute x7, starting transfers between devices, shifted(): lax.ppermute(x, axis, [(i, (i + by) % devices) for i in range(devices)])  4.6 us
    pallas_call x1, Pallas kernels, split_far(): pl.pallas_call(split_kernel, out_shape=half_pieces, in_specs=[HBM], out_s...  4.38 us
  transfers between devices with their start and end apart: 47, of which 22 were waited for; matrix products, arithmetic and copies ran while one was open for 0% of the time, Pallas kernels for 23%

profile of v3, /device:TPU:0, one launch (start us, length us, event | category | flops | bytes accessed | tf_op | source)
XLA Modules:
  0.0 112.2 jit_solution(17730553978979484469)
XLA Ops:
  3.5 5.8 %prepare.1 = (bf16[5,512,1024]{2,1,0:T(8,128)(2,1)S(1)}, bf16[5,512,1024]{2,1,0:T(8,128)(2,1)S(1)}, s32[20,128]{1,0:T(8,128)S(1)}, s32[20,128]{1,0:T(8,128)S(1)}...) custom-call(s32[3]{0:T(128)S(1)} %pad_add_fusion.info_ref, ...), custom_call_target="tpu_custom_call" | custom-call | flops 1024 | bytes 1024 | tf_op jit(solution)/shard_map/prepare/pallas_call | solution.py:470
  9.3 2.7 %collective-permute-done.prev_coupling_ref = f32[5,24,640]{2,1,0:T(8,128)S(1)} collective-permute-done((f32[5,24,640]{2,1,0:T(8,128)S(1)}, f32[5,24,640]{2,1,0:T(8,128)S(1)}, u32[]{:S(2)}, u32[]{:S(2)}) %collective-permute-start) | collective-permute-done | bytes 307232 | tf_op jit(solution)/shard_map/ppermute | solution.py:17
  12.0 1.4 %first.1 = (f32[5,512]{1,0:T(8,128)S(1)}, f32[5,16,512]{2,1,0:T(8,128)S(1)}, f32[5,16,512]{2,1,0:T(8,128)S(1)}, f32[5,16,512]{2,1,0:T(8,128)S(1)}, f32[16,896]{1...) custom-call(s32[3]{0:T(128)S(1)} %pad_add_fusion.info_ref, ...), custom_call_target="tpu_custom_call" | custom-call | flops 1024 | bytes 1024 | tf_op jit(solution)/shard_map/first/pallas_call | solution.py:492
  13.5 2.4 %collective-permute-start.2 = (f32[5,16,512]{2,1,0:T(8,128)S(1)}, f32[5,16,512]{2,1,0:T(8,128)S(1)}, u32[]{:S(2)}, u32[]{:S(2)}) collective-permute-start(f32[5,16,512]{2,1,0:T(8,128)S(1)} %get-tuple-element.65), channel_id=1, source_target_pairs={{0,7},{1,0},{2,1},{3,2},{4,3},{5,4},{6,5},{7,6},{8,15},{9,8},{10,9... | collective-permute-start | bytes 491528 | tf_op jit(solution)/shard_map/ppermute | solution.py:17
  15.9 1.3 %collective-permute-start.13 = (f32[16,896]{1,0:T(8,128)S(1)}, f32[16,896]{1,0:T(8,128)S(1)}, u32[]{:S(2)}, u32[]{:S(2)}) collective-permute-start(f32[16,896]{1,0:T(8,128)S(1)} %add.78), channel_id=1, source_target_pairs={{0,6},{1,7},{2,4},{3,5},{4,2},{5,3},{6,0},{7,1},{8,14},{9,15},{10,... | collective-permute-start | bytes 172040 | tf_op jit(solution)/shard_map/ppermute | solution.py:22
  17.2 2.4 %collective-permute-start.6 = (f32[48,1536]{1,0:T(8,128)S(1)}, f32[48,1536]{1,0:T(8,128)S(1)}, u32[]{:S(2)}, u32[]{:S(2)}) collective-permute-start(f32[48,1536]{1,0:T(8,128)S(1)} %copy-done), channel_id=1, source_target_pairs={{0,24},{1,25},{2,26},{3,27},{4,28},{5,29},{6,30},{7,31},{8,16},{9,... | collective-permute-start | bytes 884744 | tf_op jit(solution)/shard_map/ppermute | solution.py:22
  20.1 2.7 %collective-permute-start.11 = (f32[16,896]{1,0:T(8,128)S(1)}, f32[16,896]{1,0:T(8,128)S(1)}, u32[]{:S(2)}, u32[]{:S(2)}) collective-permute-start(f32[16,896]{1,0:T(8,128)S(1)} %add.78), channel_id=1, source_target_pairs={{0,2},{1,3},{2,0},{3,1},{4,6},{5,7},{6,4},{7,5},{8,10},{9,11},{10,... | collective-permute-start | bytes 172040 | tf_op jit(solution)/shard_map/ppermute | solution.py:22
  23.8 1.8 %collective-permute-start.4 = (f32[48,1536]{1,0:T(8,128)S(1)}, f32[48,1536]{1,0:T(8,128)S(1)}, u32[]{:S(2)}, u32[]{:S(2)}) collective-permute-start(f32[48,1536]{1,0:T(8,128)S(1)} %copy-done), channel_id=1, source_target_pairs={{0,8},{1,9},{2,10},{3,11},{4,12},{5,13},{6,14},{7,15},{8,0},{9,1},... | collective-permute-start | bytes 884744 | tf_op jit(solution)/shard_map/ppermute | solution.py:22
  25.6 4.4 %split.1 = (bf16[5,512,1024]{2,1,0:T(8,128)(2,1)S(1)}, bf16[5,512,1024]{2,1,0:T(8,128)(2,1)S(1)}) custom-call(f32[1,1,5,1024,1024]{4,3,2,1,0:T(8,128)} %flex_ref.2), custom_call_target="tpu_custom_call" | custom-call | flops 1024 | bytes 1024 | tf_op jit(solution)/shard_map/split/pallas_call | solution.py:506
  30.0 1.6 %flex_near.3.begun_ref = f32[5,16,1024]{2,1,0:T(8,128)S(1)} custom-call(f32[5,16,512]{2,1,0:T(8,128)S(1)} %get-tuple-element.64.values_ref.z_ref, bf16[5,512,1024]{2,1,0:T(8,128)(2,1)S(1)} %get-tuple-element.66.large_ref, bf16[5,512,1024]{2,1,0:T(8,128)(2,1)S(1)} %get-tuple-element.67.small_ref), custom_call_target="tpu_custom_call" | custom-call | flops 1024 | bytes 1024 | tf_op jit(solution)/shard_map/flex_near/pallas_call | solution.py:537
  31.6 1.7 %flex_far.3 = (f32[5,16,512]{2,1,0:T(8,128)S(1)}, f32[5,16,512]{2,1,0:T(8,128)S(1)}, f32[16,896]{1,0:T(8,128)S(1)}) custom-call(f32[5,16,512]{2,1,0:T(8,128)S(1)} %get-tuple-element.64.values_ref.z_ref, f32[5,16,512]{2,1,0:T(8,128)S(1)} %collective-permute-done.2.forces_ref, f32[5,16,1024]{2,1,0:T(8,128)S(1)} %flex_near.3.begun_ref, ...), custom_call_target="tpu_custom_call" | custom-call | flops 1024 | bytes 1024 | tf_op jit(solution)/shard_map/flex_far/pallas_call | solution.py:547
  35.1 1.9 %collective-permute-start.14 = (f32[16,896]{1,0:T(8,128)S(1)}, f32[16,896]{1,0:T(8,128)S(1)}, u32[]{:S(2)}, u32[]{:S(2)}) collective-permute-start(f32[16,896]{1,0:T(8,128)S(1)} %add_add_fusion.5), channel_id=1, source_target_pairs={{0,8},{1,9},{2,10},{3,11},{4,12},{5,13},{6,14},{7,15},{8,0},{9,1},... | collective-permute-start | bytes 172040 | tf_op jit(solution)/shard_map/ppermute | solution.py:22
  37.2 1.4 %collective-permute-done.16 = f32[16,896]{1,0:T(8,128)S(1)} collective-permute-done((f32[16,896]{1,0:T(8,128)S(1)}, f32[16,896]{1,0:T(8,128)S(1)}, u32[]{:S(2)}, u32[]{:S(2)}) %collective-permute-start.16) | collective-permute-done | bytes 57376 | tf_op jit(solution)/shard_map/ppermute | solution.py:22
  39.6 1.6 %collective-permute-start.17 = (f32[16,896]{1,0:T(8,128)S(1)}, f32[16,896]{1,0:T(8,128)S(1)}, u32[]{:S(2)}, u32[]{:S(2)}) collective-permute-start(f32[16,896]{1,0:T(8,128)S(1)} %add_add_fusion.4.mine_ref), channel_id=1, source_target_pairs={{0,1},{1,0},{2,3},{3,2},{4,5},{5,4},{6,7},{7,6},{8,9},{9,8},{10,11... | collective-permute-start | bytes 172040 | tf_op jit(solution)/shard_map/ppermute | solution.py:22
  41.1 1.7 %tables.1 = (bf16[256,512]{1,0:T(8,128)(2,1)S(1)}, bf16[1536,256]{1,0:T(8,128)(2,1)S(1)}, bf16[1536,768]{1,0:T(8,128)(2,1)S(1)}) custom-call(s32[3]{0:T(128)S(1)} %pad_add_fusion.info_ref, f32[5,24,640]{2,1,0:T(8,128)S(1)} %collective-permute-done.prev_coupling_ref, s32[1,1,5,24]{3,2,1,0:T(8,128)S(1)} %copy.12.map_ref, f32[48,1536]{1,0:T(8,128)S(1)} %copy-done, ...), custom_call_target="tpu_custom_call" | custom-call | flops 1024 | bytes 1024 | tf_op jit(solution)/shard_map/tables/pallas_call | solution.py:518
  42.9 1.2 %coarse.3.refs_0_ = f32[16,512]{1,0:T(8,128)S(1)} custom-call(s32[3]{0:T(128)S(1)} %pad_add_fusion.info_ref, f32[16,896]{1,0:T(8,128)S(1)} %add_add_fusion.4.mine_ref, f32[16,896]{1,0:T(8,128)S(1)} %collective-permute-done.17.other_ref, bf16[1536,768]{1,0:T(8,128)(2,1)S(1)} %get-tuple-element.83.table_ref), custom_call_target="tpu_custom_call" | custom-call | flops 1024 | bytes 1024 | tf_op jit(solution)/shard_map/coarse/pallas_call | solution.py:561
  44.1 2.7 %collective-permute-start.20 = (f32[16,512]{1,0:T(8,128)S(1)}, f32[16,512]{1,0:T(8,128)S(1)}, u32[]{:S(2)}, u32[]{:S(2)}) collective-permute-start(f32[16,512]{1,0:T(8,128)S(1)} %coarse.3.refs_0_), channel_id=1, source_target_pairs={{0,6},{1,7},{2,4},{3,5},{4,2},{5,3},{6,0},{7,1},{8,14},{9,15},{10,... | collective-permute-start | bytes 98312 | tf_op jit(solution)/shard_map/ppermute | solution.py:22
  46.8 1.4 %collective-permute-start.19 = (f32[16,512]{1,0:T(8,128)S(1)}, f32[16,512]{1,0:T(8,128)S(1)}, u32[]{:S(2)}, u32[]{:S(2)}) collective-permute-start(f32[16,512]{1,0:T(8,128)S(1)} %coarse.3.refs_0_), channel_id=1, source_target_pairs={{0,4},{1,5},{2,6},{3,7},{4,0},{5,1},{6,2},{7,3},{8,12},{9,13},{10,... | collective-permute-start | bytes 98312 | tf_op jit(solution)/shard_map/ppermute | solution.py:22
  48.5 1.3 %collective-permute-done.20.refs_3_ = f32[16,512]{1,0:T(8,128)S(1)} collective-permute-done((f32[16,512]{1,0:T(8,128)S(1)}, f32[16,512]{1,0:T(8,128)S(1)}, u32[]{:S(2)}, u32[]{:S(2)}) %collective-permute-start.20) | collective-permute-done | bytes 32800 | tf_op jit(solution)/shard_map/ppermute | solution.py:22
  49.8 2.1 %collective-permute-done.19.refs_2_ = f32[16,512]{1,0:T(8,128)S(1)} collective-permute-done((f32[16,512]{1,0:T(8,128)S(1)}, f32[16,512]{1,0:T(8,128)S(1)}, u32[]{:S(2)}, u32[]{:S(2)}) %collective-permute-start.19) | collective-permute-done | bytes 32800 | tf_op jit(solution)/shard_map/ppermute | solution.py:22
  52.2 1.9 %step.3 = (f32[5,16,512]{2,1,0:T(8,128)S(1)}, f32[5,16,512]{2,1,0:T(8,128)S(1)}, f32[5,16,512]{2,1,0:T(8,128)S(1)}, f32[5,16,512]{2,1,0:T(8,128)S(1)}, f32[5,16,...) custom-call(s32[3]{0:T(128)S(1)} %pad_add_fusion.info_ref, ...), custom_call_target="tpu_custom_call" | custom-call | flops 1024 | bytes 1024 | tf_op jit(solution)/shard_map/step/pallas_call | solution.py:572
  55.6 1.4 %collective-permute-start.26 = (f32[16,896]{1,0:T(8,128)S(1)}, f32[16,896]{1,0:T(8,128)S(1)}, u32[]{:S(2)}, u32[]{:S(2)}) collective-permute-start(f32[16,896]{1,0:T(8,128)S(1)} %add.86), channel_id=1, source_target_pairs={{0,6},{1,7},{2,4},{3,5},{4,2},{5,3},{6,0},{7,1},{8,14},{9,15},{10,... | collective-permute-start | bytes 172040 | tf_op jit(solution)/shard_map/ppermute | solution.py:22
  57.4 2.7 %collective-permute-start.24 = (f32[16,896]{1,0:T(8,128)S(1)}, f32[16,896]{1,0:T(8,128)S(1)}, u32[]{:S(2)}, u32[]{:S(2)}) collective-permute-start(f32[16,896]{1,0:T(8,128)S(1)} %add.86), channel_id=1, source_target_pairs={{0,2},{1,3},{2,0},{3,1},{4,6},{5,7},{6,4},{7,5},{8,10},{9,11},{10,... | collective-permute-start | bytes 172040 | tf_op jit(solution)/shard_map/ppermute | solution.py:22
  60.1 1.6 %flex_near.4.begun_ref = f32[5,16,1024]{2,1,0:T(8,128)S(1)} custom-call(f32[5,16,512]{2,1,0:T(8,128)S(1)} %get-tuple-element.87.values_ref.z_ref, bf16[5,512,1024]{2,1,0:T(8,128)(2,1)S(1)} %get-tuple-element.66.large_ref, bf16[5,512,1024]{2,1,0:T(8,128)(2,1)S(1)} %get-tuple-element.67.small_ref), custom_call_target="tpu_custom_call" | custom-call | flops 1024 | bytes 1024 | tf_op jit(solution)/shard_map/flex_near/pallas_call | solution.py:537
  61.7 1.7 %flex_far.4 = (f32[5,16,512]{2,1,0:T(8,128)S(1)}, f32[5,16,512]{2,1,0:T(8,128)S(1)}, f32[16,896]{1,0:T(8,128)S(1)}) custom-call(f32[5,16,512]{2,1,0:T(8,128)S(1)} %get-tuple-element.87.values_ref.z_ref, f32[5,16,512]{2,1,0:T(8,128)S(1)} %collective-permute-done.22.forces_ref, f32[5,16,1024]{2,1,0:T(8,128)S(1)} %flex_near.4.begun_ref, ...), custom_call_target="tpu_custom_call" | custom-call | flops 1024 | bytes 1024 | tf_op jit(solution)/shard_map/flex_far/pallas_call | solution.py:547
  64.1 1.3 %collective-permute-start.29 = (f32[16,896]{1,0:T(8,128)S(1)}, f32[16,896]{1,0:T(8,128)S(1)}, u32[]{:S(2)}, u32[]{:S(2)}) collective-permute-start(f32[16,896]{1,0:T(8,128)S(1)} %add_add_fusion.3), channel_id=1, source_target_pairs={{0,24},{1,25},{2,26},{3,27},{4,28},{5,29},{6,30},{7,31},{8,16},{9,... | collective-permute-start | bytes 172040 | tf_op jit(solution)/shard_map/ppermute | solution.py:22
  65.4 1.5 %collective-permute-start.28 = (f32[16,896]{1,0:T(8,128)S(1)}, f32[16,896]{1,0:T(8,128)S(1)}, u32[]{:S(2)}, u32[]{:S(2)}) collective-permute-start(f32[16,896]{1,0:T(8,128)S(1)} %add_add_fusion.3), channel_id=1, source_target_pairs={{0,16},{1,17},{2,18},{3,19},{4,20},{5,21},{6,22},{7,23},{8,24},{9,... | collective-permute-start | bytes 172040 | tf_op jit(solution)/shard_map/ppermute | solution.py:22
  67.7 1.9 %collective-permute-done.29 = f32[16,896]{1,0:T(8,128)S(1)} collective-permute-done((f32[16,896]{1,0:T(8,128)S(1)}, f32[16,896]{1,0:T(8,128)S(1)}, u32[]{:S(2)}, u32[]{:S(2)}) %collective-permute-start.29) | collective-permute-done | bytes 57376 | tf_op jit(solution)/shard_map/ppermute | solution.py:22
  71.2 1.2 %collective-permute-done.30.other_ref = f32[16,896]{1,0:T(8,128)S(1)} collective-permute-done((f32[16,896]{1,0:T(8,128)S(1)}, f32[16,896]{1,0:T(8,128)S(1)}, u32[]{:S(2)}, u32[]{:S(2)}) %collective-permute-start.30) | collective-permute-done | bytes 57376 | tf_op jit(solution)/shard_map/ppermute | solution.py:22
  73.7 2.4 %collective-permute-start.33 = (f32[16,512]{1,0:T(8,128)S(1)}, f32[16,512]{1,0:T(8,128)S(1)}, u32[]{:S(2)}, u32[]{:S(2)}) collective-permute-start(f32[16,512]{1,0:T(8,128)S(1)} %coarse.4.refs_0_), channel_id=1, source_target_pairs={{0,6},{1,7},{2,4},{3,5},{4,2},{5,3},{6,0},{7,1},{8,14},{9,15},{10,... | collective-permute-start | bytes 98312 | tf_op jit(solution)/shard_map/ppermute | solution.py:22
  76.1 2.0 %collective-permute-start.31 = (f32[16,512]{1,0:T(8,128)S(1)}, f32[16,512]{1,0:T(8,128)S(1)}, u32[]{:S(2)}, u32[]{:S(2)}) collective-permute-start(f32[16,512]{1,0:T(8,128)S(1)} %coarse.4.refs_0_), channel_id=1, source_target_pairs={{0,2},{1,3},{2,0},{3,1},{4,6},{5,7},{6,4},{7,5},{8,10},{9,11},{10,... | collective-permute-start | bytes 98312 | tf_op jit(solution)/shard_map/ppermute | solution.py:22
  78.1 1.3 %collective-permute-done.33.refs_3_ = f32[16,512]{1,0:T(8,128)S(1)} collective-permute-done((f32[16,512]{1,0:T(8,128)S(1)}, f32[16,512]{1,0:T(8,128)S(1)}, u32[]{:S(2)}, u32[]{:S(2)}) %collective-permute-start.33) | collective-permute-done | bytes 32800 | tf_op jit(solution)/shard_map/ppermute | solution.py:22
  79.4 1.5 %collective-permute-done.32.refs_2_ = f32[16,512]{1,0:T(8,128)S(1)} collective-permute-done((f32[16,512]{1,0:T(8,128)S(1)}, f32[16,512]{1,0:T(8,128)S(1)}, u32[]{:S(2)}, u32[]{:S(2)}) %collective-permute-start.32) | collective-permute-done | bytes 32800 | tf_op jit(solution)/shard_map/ppermute | solution.py:22
  80.9 1.9 %step.4 = (f32[5,16,512]{2,1,0:T(8,128)S(1)}, f32[5,16,512]{2,1,0:T(8,128)S(1)}, f32[5,16,512]{2,1,0:T(8,128)S(1)}, f32[5,16,512]{2,1,0:T(8,128)S(1)}, f32[5,16,...) custom-call(s32[3]{0:T(128)S(1)} %pad_add_fusion.info_ref, ...), custom_call_target="tpu_custom_call" | custom-call | flops 1024 | bytes 1024 | tf_op jit(solution)/shard_map/step/pallas_call | solution.py:572
  82.8 1.5 %collective-permute-start.35 = (f32[5,16,512]{2,1,0:T(8,128)S(1)}, f32[5,16,512]{2,1,0:T(8,128)S(1)}, u32[]{:S(2)}, u32[]{:S(2)}) collective-permute-start(f32[5,16,512]{2,1,0:T(8,128)S(1)} %get-tuple-element.102), channel_id=1, source_target_pairs={{0,7},{1,0},{2,1},{3,2},{4,3},{5,4},{6,5},{7,6},{8,15},{9,8},{10,9... | collective-permute-start | bytes 491528 | tf_op jit(solution)/shard_map/ppermute | solution.py:17
  84.3 1.2 %collective-permute-done.34 = f32[16,896]{1,0:T(8,128)S(1)} collective-permute-done((f32[16,896]{1,0:T(8,128)S(1)}, f32[16,896]{1,0:T(8,128)S(1)}, u32[]{:S(2)}, u32[]{:S(2)}) %collective-permute-start.34) | collective-permute-done | bytes 57376 | tf_op jit(solution)/shard_map/ppermute | solution.py:22
  86.9 3.1 %collective-permute-start.37 = (f32[16,896]{1,0:T(8,128)S(1)}, f32[16,896]{1,0:T(8,128)S(1)}, u32[]{:S(2)}, u32[]{:S(2)}) collective-permute-start(f32[16,896]{1,0:T(8,128)S(1)} %add.94), channel_id=1, source_target_pairs={{0,2},{1,3},{2,0},{3,1},{4,6},{5,7},{6,4},{7,5},{8,10},{9,11},{10,... | collective-permute-start | bytes 172040 | tf_op jit(solution)/shard_map/ppermute | solution.py:22
  90.0 1.6 %flex_near.5.begun_ref = f32[5,16,1024]{2,1,0:T(8,128)S(1)} custom-call(f32[5,16,512]{2,1,0:T(8,128)S(1)} %get-tuple-element.101.values_ref.z_ref, bf16[5,512,1024]{2,1,0:T(8,128)(2,1)S(1)} %get-tuple-element.66.large_ref, bf16[5,512,1024]{2,1,0:T(8,128)(2,1)S(1)} %get-tuple-element.67.small_ref), custom_call_target="tpu_custom_call" | custom-call | flops 1024 | bytes 1024 | tf_op jit(solution)/shard_map/flex_near/pallas_call | solution.py:537
  91.6 1.7 %flex_far.5 = (f32[5,16,512]{2,1,0:T(8,128)S(1)}, f32[5,16,512]{2,1,0:T(8,128)S(1)}, f32[16,896]{1,0:T(8,128)S(1)}) custom-call(f32[5,16,512]{2,1,0:T(8,128)S(1)} %get-tuple-element.101.values_ref.z_ref, f32[5,16,512]{2,1,0:T(8,128)S(1)} %collective-permute-done.35.forces_ref, f32[5,16,1024]{2,1,0:T(8,128)S(1)} %flex_near.5.begun_ref, ...), custom_call_target="tpu_custom_call" | custom-call | flops 1024 | bytes 1024 | tf_op jit(solution)/shard_map/flex_far/pallas_call | solution.py:547
  94.1 1.6 %collective-permute-start.41 = (f32[16,896]{1,0:T(8,128)S(1)}, f32[16,896]{1,0:T(8,128)S(1)}, u32[]{:S(2)}, u32[]{:S(2)}) collective-permute-start(f32[16,896]{1,0:T(8,128)S(1)} %add_add_fusion.1), channel_id=1, source_target_pairs={{0,16},{1,17},{2,18},{3,19},{4,20},{5,21},{6,22},{7,23},{8,24},{9,... | collective-permute-start | bytes 172040 | tf_op jit(solution)/shard_map/ppermute | solution.py:22
  95.7 1.5 %collective-permute-start.40 = (f32[16,896]{1,0:T(8,128)S(1)}, f32[16,896]{1,0:T(8,128)S(1)}, u32[]{:S(2)}, u32[]{:S(2)}) collective-permute-start(f32[16,896]{1,0:T(8,128)S(1)} %add_add_fusion.1), channel_id=1, source_target_pairs={{0,8},{1,9},{2,10},{3,11},{4,12},{5,13},{6,14},{7,15},{8,0},{9,1},... | collective-permute-start | bytes 172040 | tf_op jit(solution)/shard_map/ppermute | solution.py:22
  97.2 1.7 %collective-permute-done.42 = f32[16,896]{1,0:T(8,128)S(1)} collective-permute-done((f32[16,896]{1,0:T(8,128)S(1)}, f32[16,896]{1,0:T(8,128)S(1)}, u32[]{:S(2)}, u32[]{:S(2)}) %collective-permute-start.42) | collective-permute-done | bytes 57376 | tf_op jit(solution)/shard_map/ppermute | solution.py:22
  100.0 1.2 %collective-permute-done.43.other_ref = f32[16,896]{1,0:T(8,128)S(1)} collective-permute-done((f32[16,896]{1,0:T(8,128)S(1)}, f32[16,896]{1,0:T(8,128)S(1)}, u32[]{:S(2)}, u32[]{:S(2)}) %collective-permute-start.43) | collective-permute-done | bytes 57376 | tf_op jit(solution)/shard_map/ppermute | solution.py:22
  102.4 2.7 %collective-permute-start.46 = (f32[16,512]{1,0:T(8,128)S(1)}, f32[16,512]{1,0:T(8,128)S(1)}, u32[]{:S(2)}, u32[]{:S(2)}) collective-permute-start(f32[16,512]{1,0:T(8,128)S(1)} %coarse.5.refs_0_), channel_id=1, source_target_pairs={{0,6},{1,7},{2,4},{3,5},{4,2},{5,3},{6,0},{7,1},{8,14},{9,15},{10,... | collective-permute-start | bytes 98312 | tf_op jit(solution)/shard_map/ppermute | solution.py:22
  105.1 1.7 %collective-permute-start.44 = (f32[16,512]{1,0:T(8,128)S(1)}, f32[16,512]{1,0:T(8,128)S(1)}, u32[]{:S(2)}, u32[]{:S(2)}) collective-permute-start(f32[16,512]{1,0:T(8,128)S(1)} %coarse.5.refs_0_), channel_id=1, source_target_pairs={{0,2},{1,3},{2,0},{3,1},{4,6},{5,7},{6,4},{7,5},{8,10},{9,11},{10,... | collective-permute-start | bytes 98312 | tf_op jit(solution)/shard_map/ppermute | solution.py:22
  106.8 1.4 %collective-permute-done.46.refs_3_ = f32[16,512]{1,0:T(8,128)S(1)} collective-permute-done((f32[16,512]{1,0:T(8,128)S(1)}, f32[16,512]{1,0:T(8,128)S(1)}, u32[]{:S(2)}, u32[]{:S(2)}) %collective-permute-start.46) | collective-permute-done | bytes 32800 | tf_op jit(solution)/shard_map/ppermute | solution.py:22
  108.2 1.7 %collective-permute-done.45.refs_2_ = f32[16,512]{1,0:T(8,128)S(1)} collective-permute-done((f32[16,512]{1,0:T(8,128)S(1)}, f32[16,512]{1,0:T(8,128)S(1)}, u32[]{:S(2)}, u32[]{:S(2)}) %collective-permute-start.45) | collective-permute-done | bytes 32800 | tf_op jit(solution)/shard_map/ppermute | solution.py:22
  109.9 2.3 %step.5 = (f32[1,1,5,16,4,128]{5,4,3,2,1,0:T(4,128)}, f32[1,1,5,16,4,128]{5,4,3,2,1,0:T(4,128)}) custom-call(s32[3]{0:T(128)S(1)} %pad_add_fusion.info_ref, s32[1,1,4,5]{3,2,1,0:T(4,128)S(1)} %copy-done.1, f32[5,16,512]{2,1,0:T(8,128)S(1)} %get-tuple-element.103.own_ref, f32[5,16,512]{2,1,0:T(8,128)S(1)} %collective-permute-done.36.facing_ref, ...), custom_call_target="tpu_custom_call" | custom-call | flops 1024 | bytes 1024 | tf_op jit(solution)/shard_map/step/pallas_call | solution.py:572
  (78 shorter events, 17.7 us)
Async XLA Ops:
  2.9 9.1 %collective-permute-start = (f32[5,24,640]{2,1,0:T(8,128)S(1)}, f32[5,24,640]{2,1,0:T(8,128)S(1)}, u32[]{:S(2)}, u32[]{:S(2)}) collective-permute-start(f32[5,24,640]{2,1,0:T(8,128)S(1)} %pack.1), channel_id=1, source_target_pairs={{0,1},{1,2},{2,3},{3,4},{4,5},{5,6},{6,7},{7,0},{8,9},{9,10},{10,1... | collective-permute-start | bytes 921608 | tf_op jit(solution)/shard_map/ppermute | solution.py:17
  3.5 13.7 %copy-start = (f32[48,1536]{1,0:T(8,128)S(1)}, f32[48,1536]{1,0:T(8,128)}, u32[]{:S(2)}) copy-start(f32[48,1536]{1,0:T(8,128)} %refs_0_.1) | copy-start | bytes 884740
  13.4 2.5 %collective-permute-start.1 = (f32[16,896]{1,0:T(8,128)S(1)}, f32[16,896]{1,0:T(8,128)S(1)}, u32[]{:S(2)}, u32[]{:S(2)}) collective-permute-start(f32[16,896]{1,0:T(8,128)S(1)} %get-tuple-element.62), channel_id=1, source_target_pairs={{0,1},{1,0},{2,3},{3,2},{4,5},{5,4},{6,7},{7,6},{8,9},{9,8},{10,11... | collective-permute-start | bytes 172040 | tf_op jit(solution)/shard_map/ppermute | solution.py:22
  13.5 10.3 %collective-permute-start.2 = (f32[5,16,512]{2,1,0:T(8,128)S(1)}, f32[5,16,512]{2,1,0:T(8,128)S(1)}, u32[]{:S(2)}, u32[]{:S(2)}) collective-permute-start(f32[5,16,512]{2,1,0:T(8,128)S(1)} %get-tuple-element.65), channel_id=1, source_target_pairs={{0,7},{1,0},{2,1},{3,2},{4,3},{5,4},{6,5},{7,6},{8,15},{9,8},{10,9... | collective-permute-start | bytes 491528 | tf_op jit(solution)/shard_map/ppermute | solution.py:17
  15.9 6.9 %collective-permute-start.13 = (f32[16,896]{1,0:T(8,128)S(1)}, f32[16,896]{1,0:T(8,128)S(1)}, u32[]{:S(2)}, u32[]{:S(2)}) collective-permute-start(f32[16,896]{1,0:T(8,128)S(1)} %add.78), channel_id=1, source_target_pairs={{0,6},{1,7},{2,4},{3,5},{4,2},{5,3},{6,0},{7,1},{8,14},{9,15},{10,... | collective-permute-start | bytes 172040 | tf_op jit(solution)/shard_map/ppermute | solution.py:22
  17.2 17.9 %collective-permute-start.6 = (f32[48,1536]{1,0:T(8,128)S(1)}, f32[48,1536]{1,0:T(8,128)S(1)}, u32[]{:S(2)}, u32[]{:S(2)}) collective-permute-start(f32[48,1536]{1,0:T(8,128)S(1)} %copy-done), channel_id=1, source_target_pairs={{0,24},{1,25},{2,26},{3,27},{4,28},{5,29},{6,30},{7,31},{8,16},{9,... | collective-permute-start | bytes 884744 | tf_op jit(solution)/shard_map/ppermute | solution.py:22
  19.7 13.7 %collective-permute-start.12 = (f32[16,896]{1,0:T(8,128)S(1)}, f32[16,896]{1,0:T(8,128)S(1)}, u32[]{:S(2)}, u32[]{:S(2)}) collective-permute-start(f32[16,896]{1,0:T(8,128)S(1)} %add.78), channel_id=1, source_target_pairs={{0,4},{1,5},{2,6},{3,7},{4,0},{5,1},{6,2},{7,3},{8,12},{9,13},{10,... | collective-permute-start | bytes 172040 | tf_op jit(solution)/shard_map/ppermute | solution.py:22
  20.1 13.3 %collective-permute-start.11 = (f32[16,896]{1,0:T(8,128)S(1)}, f32[16,896]{1,0:T(8,128)S(1)}, u32[]{:S(2)}, u32[]{:S(2)}) collective-permute-start(f32[16,896]{1,0:T(8,128)S(1)} %add.78), channel_id=1, source_target_pairs={{0,2},{1,3},{2,0},{3,1},{4,6},{5,7},{6,4},{7,5},{8,10},{9,11},{10,... | collective-permute-start | bytes 172040 | tf_op jit(solution)/shard_map/ppermute | solution.py:22
  22.8 12.3 %collective-permute-start.5 = (f32[48,1536]{1,0:T(8,128)S(1)}, f32[48,1536]{1,0:T(8,128)S(1)}, u32[]{:S(2)}, u32[]{:S(2)}) collective-permute-start(f32[48,1536]{1,0:T(8,128)S(1)} %copy-done), channel_id=1, source_target_pairs={{0,16},{1,17},{2,18},{3,19},{4,20},{5,21},{6,22},{7,23},{8,24},{9,... | collective-permute-start | bytes 884744 | tf_op jit(solution)/shard_map/ppermute | solution.py:22
  23.8 13.2 %collective-permute-start.4 = (f32[48,1536]{1,0:T(8,128)S(1)}, f32[48,1536]{1,0:T(8,128)S(1)}, u32[]{:S(2)}, u32[]{:S(2)}) collective-permute-start(f32[48,1536]{1,0:T(8,128)S(1)} %copy-done), channel_id=1, source_target_pairs={{0,8},{1,9},{2,10},{3,11},{4,12},{5,13},{6,14},{7,15},{8,0},{9,1},... | collective-permute-start | bytes 884744 | tf_op jit(solution)/shard_map/ppermute | solution.py:22
  33.4 5.2 %collective-permute-start.16 = (f32[16,896]{1,0:T(8,128)S(1)}, f32[16,896]{1,0:T(8,128)S(1)}, u32[]{:S(2)}, u32[]{:S(2)}) collective-permute-start(f32[16,896]{1,0:T(8,128)S(1)} %add_add_fusion.5), channel_id=1, source_target_pairs={{0,24},{1,25},{2,26},{3,27},{4,28},{5,29},{6,30},{7,31},{8,16},{9,... | collective-permute-start | bytes 172040 | tf_op jit(solution)/shard_map/ppermute | solution.py:22
  34.1 4.8 %collective-permute-start.15 = (f32[16,896]{1,0:T(8,128)S(1)}, f32[16,896]{1,0:T(8,128)S(1)}, u32[]{:S(2)}, u32[]{:S(2)}) collective-permute-start(f32[16,896]{1,0:T(8,128)S(1)} %add_add_fusion.5), channel_id=1, source_target_pairs={{0,16},{1,17},{2,18},{3,19},{4,20},{5,21},{6,22},{7,23},{8,24},{9,... | collective-permute-start | bytes 172040 | tf_op jit(solution)/shard_map/ppermute | solution.py:22
  35.1 4.5 %collective-permute-start.7 = (f32[48,1536]{1,0:T(8,128)S(1)}, f32[48,1536]{1,0:T(8,128)S(1)}, u32[]{:S(2)}, u32[]{:S(2)}) collective-permute-start(f32[48,1536]{1,0:T(8,128)S(1)} %copy-done), channel_id=1, source_target_pairs={{0,1},{1,0},{2,3},{3,2},{4,5},{5,4},{6,7},{7,6},{8,9},{9,8},{10,11... | collective-permute-start | bytes 884744 | tf_op jit(solution)/shard_map/ppermute | solution.py:22
  35.1 4.4 %collective-permute-start.14 = (f32[16,896]{1,0:T(8,128)S(1)}, f32[16,896]{1,0:T(8,128)S(1)}, u32[]{:S(2)}, u32[]{:S(2)}) collective-permute-start(f32[16,896]{1,0:T(8,128)S(1)} %add_add_fusion.5), channel_id=1, source_target_pairs={{0,8},{1,9},{2,10},{3,11},{4,12},{5,13},{6,14},{7,15},{8,0},{9,1},... | collective-permute-start | bytes 172040 | tf_op jit(solution)/shard_map/ppermute | solution.py:22
  37.0 4.1 %collective-permute-start.10 = (f32[48,1536]{1,0:T(8,128)S(1)}, f32[48,1536]{1,0:T(8,128)S(1)}, u32[]{:S(2)}, u32[]{:S(2)}) collective-permute-start(f32[48,1536]{1,0:T(8,128)S(1)} %collective-permute-done.6.refs_3_), channel_id=1, source_target_pairs={{0,1},{1,0},{2,3},{3,2},{4,5},{5,4},{6,7},{7,6},{8,9},{9,8},{10,11... | collective-permute-start | bytes 884744 | tf_op jit(solution)/shard_map/ppermute | solution.py:22
  38.6 2.5 %collective-permute-start.9 = (f32[48,1536]{1,0:T(8,128)S(1)}, f32[48,1536]{1,0:T(8,128)S(1)}, u32[]{:S(2)}, u32[]{:S(2)}) collective-permute-start(f32[48,1536]{1,0:T(8,128)S(1)} %collective-permute-done.5.refs_2_), channel_id=1, source_target_pairs={{0,1},{1,0},{2,3},{3,2},{4,5},{5,4},{6,7},{7,6},{8,9},{9,8},{10,11... | collective-permute-start | bytes 884744 | tf_op jit(solution)/shard_map/ppermute | solution.py:22
  38.9 2.2 %collective-permute-start.8 = (f32[48,1536]{1,0:T(8,128)S(1)}, f32[48,1536]{1,0:T(8,128)S(1)}, u32[]{:S(2)}, u32[]{:S(2)}) collective-permute-start(f32[48,1536]{1,0:T(8,128)S(1)} %collective-permute-done.4.refs_1_), channel_id=1, source_target_pairs={{0,1},{1,0},{2,3},{3,2},{4,5},{5,4},{6,7},{7,6},{8,9},{9,8},{10,11... | collective-permute-start | bytes 884744 | tf_op jit(solution)/shard_map/ppermute | solution.py:22
  39.5 12.7 %collective-permute-start.3 = (f32[5,16,512]{2,1,0:T(8,128)S(1)}, f32[5,16,512]{2,1,0:T(8,128)S(1)}, u32[]{:S(2)}, u32[]{:S(2)}) collective-permute-start(f32[5,16,512]{2,1,0:T(8,128)S(1)} %get-tuple-element.72), channel_id=1, source_target_pairs={{0,1},{1,2},{2,3},{3,4},{4,5},{5,6},{6,7},{7,0},{8,9},{9,10},{10,1... | collective-permute-start | bytes 491528 | tf_op jit(solution)/shard_map/ppermute | solution.py:17
  39.6 3.3 %collective-permute-start.17 = (f32[16,896]{1,0:T(8,128)S(1)}, f32[16,896]{1,0:T(8,128)S(1)}, u32[]{:S(2)}, u32[]{:S(2)}) collective-permute-start(f32[16,896]{1,0:T(8,128)S(1)} %add_add_fusion.4.mine_ref), channel_id=1, source_target_pairs={{0,1},{1,0},{2,3},{3,2},{4,5},{5,4},{6,7},{7,6},{8,9},{9,8},{10,11... | collective-permute-start | bytes 172040 | tf_op jit(solution)/shard_map/ppermute | solution.py:22
  44.1 5.7 %collective-permute-start.20 = (f32[16,512]{1,0:T(8,128)S(1)}, f32[16,512]{1,0:T(8,128)S(1)}, u32[]{:S(2)}, u32[]{:S(2)}) collective-permute-start(f32[16,512]{1,0:T(8,128)S(1)} %coarse.3.refs_0_), channel_id=1, source_target_pairs={{0,6},{1,7},{2,4},{3,5},{4,2},{5,3},{6,0},{7,1},{8,14},{9,15},{10,... | collective-permute-start | bytes 98312 | tf_op jit(solution)/shard_map/ppermute | solution.py:22
  46.8 5.1 %collective-permute-start.19 = (f32[16,512]{1,0:T(8,128)S(1)}, f32[16,512]{1,0:T(8,128)S(1)}, u32[]{:S(2)}, u32[]{:S(2)}) collective-permute-start(f32[16,512]{1,0:T(8,128)S(1)} %coarse.3.refs_0_), channel_id=1, source_target_pairs={{0,4},{1,5},{2,6},{3,7},{4,0},{5,1},{6,2},{7,3},{8,12},{9,13},{10,... | collective-permute-start | bytes 98312 | tf_op jit(solution)/shard_map/ppermute | solution.py:22
  48.2 4.1 %collective-permute-start.18 = (f32[16,512]{1,0:T(8,128)S(1)}, f32[16,512]{1,0:T(8,128)S(1)}, u32[]{:S(2)}, u32[]{:S(2)}) collective-permute-start(f32[16,512]{1,0:T(8,128)S(1)} %coarse.3.refs_0_), channel_id=1, source_target_pairs={{0,2},{1,3},{2,0},{3,1},{4,6},{5,7},{6,4},{7,5},{8,10},{9,11},{10,... | collective-permute-start | bytes 98312 | tf_op jit(solution)/shard_map/ppermute | solution.py:22
  54.1 7.6 %collective-permute-start.22 = (f32[5,16,512]{2,1,0:T(8,128)S(1)}, f32[5,16,512]{2,1,0:T(8,128)S(1)}, u32[]{:S(2)}, u32[]{:S(2)}) collective-permute-start(f32[5,16,512]{2,1,0:T(8,128)S(1)} %get-tuple-element.88), channel_id=1, source_target_pairs={{0,7},{1,0},{2,1},{3,2},{4,3},{5,4},{6,5},{7,6},{8,15},{9,8},{10,9... | collective-permute-start | bytes 491528 | tf_op jit(solution)/shard_map/ppermute | solution.py:17
  54.3 1.4 %collective-permute-start.21 = (f32[16,896]{1,0:T(8,128)S(1)}, f32[16,896]{1,0:T(8,128)S(1)}, u32[]{:S(2)}, u32[]{:S(2)}) collective-permute-start(f32[16,896]{1,0:T(8,128)S(1)} %get-tuple-element.85), channel_id=1, source_target_pairs={{0,1},{1,0},{2,3},{3,2},{4,5},{5,4},{6,7},{7,6},{8,9},{9,8},{10,11... | collective-permute-start | bytes 172040 | tf_op jit(solution)/shard_map/ppermute | solution.py:22
  55.6 7.8 %collective-permute-start.26 = (f32[16,896]{1,0:T(8,128)S(1)}, f32[16,896]{1,0:T(8,128)S(1)}, u32[]{:S(2)}, u32[]{:S(2)}) collective-permute-start(f32[16,896]{1,0:T(8,128)S(1)} %add.86), channel_id=1, source_target_pairs={{0,6},{1,7},{2,4},{3,5},{4,2},{5,3},{6,0},{7,1},{8,14},{9,15},{10,... | collective-permute-start | bytes 172040 | tf_op jit(solution)/shard_map/ppermute | solution.py:22
  57.1 7.0 %collective-permute-start.25 = (f32[16,896]{1,0:T(8,128)S(1)}, f32[16,896]{1,0:T(8,128)S(1)}, u32[]{:S(2)}, u32[]{:S(2)}) collective-permute-start(f32[16,896]{1,0:T(8,128)S(1)} %add.86), channel_id=1, source_target_pairs={{0,4},{1,5},{2,6},{3,7},{4,0},{5,1},{6,2},{7,3},{8,12},{9,13},{10,... | collective-permute-start | bytes 172040 | tf_op jit(solution)/shard_map/ppermute | solution.py:22
  57.4 6.7 %collective-permute-start.24 = (f32[16,896]{1,0:T(8,128)S(1)}, f32[16,896]{1,0:T(8,128)S(1)}, u32[]{:S(2)}, u32[]{:S(2)}) collective-permute-start(f32[16,896]{1,0:T(8,128)S(1)} %add.86), channel_id=1, source_target_pairs={{0,2},{1,3},{2,0},{3,1},{4,6},{5,7},{6,4},{7,5},{8,10},{9,11},{10,... | collective-permute-start | bytes 172040 | tf_op jit(solution)/shard_map/ppermute | solution.py:22
  64.1 5.4 %collective-permute-start.29 = (f32[16,896]{1,0:T(8,128)S(1)}, f32[16,896]{1,0:T(8,128)S(1)}, u32[]{:S(2)}, u32[]{:S(2)}) collective-permute-start(f32[16,896]{1,0:T(8,128)S(1)} %add_add_fusion.3), channel_id=1, source_target_pairs={{0,24},{1,25},{2,26},{3,27},{4,28},{5,29},{6,30},{7,31},{8,16},{9,... | collective-permute-start | bytes 172040 | tf_op jit(solution)/shard_map/ppermute | solution.py:22
  65.4 4.7 %collective-permute-start.28 = (f32[16,896]{1,0:T(8,128)S(1)}, f32[16,896]{1,0:T(8,128)S(1)}, u32[]{:S(2)}, u32[]{:S(2)}) collective-permute-start(f32[16,896]{1,0:T(8,128)S(1)} %add_add_fusion.3), channel_id=1, source_target_pairs={{0,16},{1,17},{2,18},{3,19},{4,20},{5,21},{6,22},{7,23},{8,24},{9,... | collective-permute-start | bytes 172040 | tf_op jit(solution)/shard_map/ppermute | solution.py:22
  67.0 4.2 %collective-permute-start.27 = (f32[16,896]{1,0:T(8,128)S(1)}, f32[16,896]{1,0:T(8,128)S(1)}, u32[]{:S(2)}, u32[]{:S(2)}) collective-permute-start(f32[16,896]{1,0:T(8,128)S(1)} %add_add_fusion.3), channel_id=1, source_target_pairs={{0,8},{1,9},{2,10},{3,11},{4,12},{5,13},{6,14},{7,15},{8,0},{9,1},... | collective-permute-start | bytes 172040 | tf_op jit(solution)/shard_map/ppermute | solution.py:22
  67.6 13.2 %collective-permute-start.23 = (f32[5,16,512]{2,1,0:T(8,128)S(1)}, f32[5,16,512]{2,1,0:T(8,128)S(1)}, u32[]{:S(2)}, u32[]{:S(2)}) collective-permute-start(f32[5,16,512]{2,1,0:T(8,128)S(1)} %get-tuple-element.90), channel_id=1, source_target_pairs={{0,1},{1,2},{2,3},{3,4},{4,5},{5,6},{6,7},{7,0},{8,9},{9,10},{10,1... | collective-permute-start | bytes 491528 | tf_op jit(solution)/shard_map/ppermute | solution.py:17
  71.2 1.3 %collective-permute-start.30 = (f32[16,896]{1,0:T(8,128)S(1)}, f32[16,896]{1,0:T(8,128)S(1)}, u32[]{:S(2)}, u32[]{:S(2)}) collective-permute-start(f32[16,896]{1,0:T(8,128)S(1)} %add_add_fusion.2.mine_ref), channel_id=1, source_target_pairs={{0,1},{1,0},{2,3},{3,2},{4,5},{5,4},{6,7},{7,6},{8,9},{9,8},{10,11... | collective-permute-start | bytes 172040 | tf_op jit(solution)/shard_map/ppermute | solution.py:22
  73.7 5.7 %collective-permute-start.33 = (f32[16,512]{1,0:T(8,128)S(1)}, f32[16,512]{1,0:T(8,128)S(1)}, u32[]{:S(2)}, u32[]{:S(2)}) collective-permute-start(f32[16,512]{1,0:T(8,128)S(1)} %coarse.4.refs_0_), channel_id=1, source_target_pairs={{0,6},{1,7},{2,4},{3,5},{4,2},{5,3},{6,0},{7,1},{8,14},{9,15},{10,... | collective-permute-start | bytes 98312 | tf_op jit(solution)/shard_map/ppermute | solution.py:22
  76.1 4.8 %collective-permute-start.32 = (f32[16,512]{1,0:T(8,128)S(1)}, f32[16,512]{1,0:T(8,128)S(1)}, u32[]{:S(2)}, u32[]{:S(2)}) collective-permute-start(f32[16,512]{1,0:T(8,128)S(1)} %coarse.4.refs_0_), channel_id=1, source_target_pairs={{0,4},{1,5},{2,6},{3,7},{4,0},{5,1},{6,2},{7,3},{8,12},{9,13},{10,... | collective-permute-start | bytes 98312 | tf_op jit(solution)/shard_map/ppermute | solution.py:22
  76.1 4.8 %collective-permute-start.31 = (f32[16,512]{1,0:T(8,128)S(1)}, f32[16,512]{1,0:T(8,128)S(1)}, u32[]{:S(2)}, u32[]{:S(2)}) collective-permute-start(f32[16,512]{1,0:T(8,128)S(1)} %coarse.4.refs_0_), channel_id=1, source_target_pairs={{0,2},{1,3},{2,0},{3,1},{4,6},{5,7},{6,4},{7,5},{8,10},{9,11},{10,... | collective-permute-start | bytes 98312 | tf_op jit(solution)/shard_map/ppermute | solution.py:22
  82.8 8.8 %collective-permute-start.35 = (f32[5,16,512]{2,1,0:T(8,128)S(1)}, f32[5,16,512]{2,1,0:T(8,128)S(1)}, u32[]{:S(2)}, u32[]{:S(2)}) collective-permute-start(f32[5,16,512]{2,1,0:T(8,128)S(1)} %get-tuple-element.102), channel_id=1, source_target_pairs={{0,7},{1,0},{2,1},{3,2},{4,3},{5,4},{6,5},{7,6},{8,15},{9,8},{10,9... | collective-permute-start | bytes 491528 | tf_op jit(solution)/shard_map/ppermute | solution.py:17
  84.3 1.2 %collective-permute-start.34 = (f32[16,896]{1,0:T(8,128)S(1)}, f32[16,896]{1,0:T(8,128)S(1)}, u32[]{:S(2)}, u32[]{:S(2)}) collective-permute-start(f32[16,896]{1,0:T(8,128)S(1)} %get-tuple-element.99), channel_id=1, source_target_pairs={{0,1},{1,0},{2,3},{3,2},{4,5},{5,4},{6,7},{7,6},{8,9},{9,8},{10,11... | collective-permute-start | bytes 172040 | tf_op jit(solution)/shard_map/ppermute | solution.py:22
  85.5 7.8 %collective-permute-start.39 = (f32[16,896]{1,0:T(8,128)S(1)}, f32[16,896]{1,0:T(8,128)S(1)}, u32[]{:S(2)}, u32[]{:S(2)}) collective-permute-start(f32[16,896]{1,0:T(8,128)S(1)} %add.94), channel_id=1, source_target_pairs={{0,6},{1,7},{2,4},{3,5},{4,2},{5,3},{6,0},{7,1},{8,14},{9,15},{10,... | collective-permute-start | bytes 172040 | tf_op jit(solution)/shard_map/ppermute | solution.py:22
  86.4 7.2 %collective-permute-start.38 = (f32[16,896]{1,0:T(8,128)S(1)}, f32[16,896]{1,0:T(8,128)S(1)}, u32[]{:S(2)}, u32[]{:S(2)}) collective-permute-start(f32[16,896]{1,0:T(8,128)S(1)} %add.94), channel_id=1, source_target_pairs={{0,4},{1,5},{2,6},{3,7},{4,0},{5,1},{6,2},{7,3},{8,12},{9,13},{10,... | collective-permute-start | bytes 172040 | tf_op jit(solution)/shard_map/ppermute | solution.py:22
  86.9 6.7 %collective-permute-start.37 = (f32[16,896]{1,0:T(8,128)S(1)}, f32[16,896]{1,0:T(8,128)S(1)}, u32[]{:S(2)}, u32[]{:S(2)}) collective-permute-start(f32[16,896]{1,0:T(8,128)S(1)} %add.94), channel_id=1, source_target_pairs={{0,2},{1,3},{2,0},{3,1},{4,6},{5,7},{6,4},{7,5},{8,10},{9,11},{10,... | collective-permute-start | bytes 172040 | tf_op jit(solution)/shard_map/ppermute | solution.py:22
  93.6 5.3 %collective-permute-start.42 = (f32[16,896]{1,0:T(8,128)S(1)}, f32[16,896]{1,0:T(8,128)S(1)}, u32[]{:S(2)}, u32[]{:S(2)}) collective-permute-start(f32[16,896]{1,0:T(8,128)S(1)} %add_add_fusion.1), channel_id=1, source_target_pairs={{0,24},{1,25},{2,26},{3,27},{4,28},{5,29},{6,30},{7,31},{8,16},{9,... | collective-permute-start | bytes 172040 | tf_op jit(solution)/shard_map/ppermute | solution.py:22
  94.1 4.8 %collective-permute-start.41 = (f32[16,896]{1,0:T(8,128)S(1)}, f32[16,896]{1,0:T(8,128)S(1)}, u32[]{:S(2)}, u32[]{:S(2)}) collective-permute-start(f32[16,896]{1,0:T(8,128)S(1)} %add_add_fusion.1), channel_id=1, source_target_pairs={{0,16},{1,17},{2,18},{3,19},{4,20},{5,21},{6,22},{7,23},{8,24},{9,... | collective-permute-start | bytes 172040 | tf_op jit(solution)/shard_map/ppermute | solution.py:22
  95.7 4.2 %collective-permute-start.40 = (f32[16,896]{1,0:T(8,128)S(1)}, f32[16,896]{1,0:T(8,128)S(1)}, u32[]{:S(2)}, u32[]{:S(2)}) collective-permute-start(f32[16,896]{1,0:T(8,128)S(1)} %add_add_fusion.1), channel_id=1, source_target_pairs={{0,8},{1,9},{2,10},{3,11},{4,12},{5,13},{6,14},{7,15},{8,0},{9,1},... | collective-permute-start | bytes 172040 | tf_op jit(solution)/shard_map/ppermute | solution.py:22
  97.2 12.8 %collective-permute-start.36 = (f32[5,16,512]{2,1,0:T(8,128)S(1)}, f32[5,16,512]{2,1,0:T(8,128)S(1)}, u32[]{:S(2)}, u32[]{:S(2)}) collective-permute-start(f32[5,16,512]{2,1,0:T(8,128)S(1)} %get-tuple-element.104), channel_id=1, source_target_pairs={{0,1},{1,2},{2,3},{3,4},{4,5},{5,6},{6,7},{7,0},{8,9},{9,10},{10,1... | collective-permute-start | bytes 491528 | tf_op jit(solution)/shard_map/ppermute | solution.py:17
  99.9 1.3 %collective-permute-start.43 = (f32[16,896]{1,0:T(8,128)S(1)}, f32[16,896]{1,0:T(8,128)S(1)}, u32[]{:S(2)}, u32[]{:S(2)}) collective-permute-start(f32[16,896]{1,0:T(8,128)S(1)} %add_add_fusion.mine_ref), channel_id=1, source_target_pairs={{0,1},{1,0},{2,3},{3,2},{4,5},{5,4},{6,7},{7,6},{8,9},{9,8},{10,11... | collective-permute-start | bytes 172040 | tf_op jit(solution)/shard_map/ppermute | solution.py:22
  102.4 5.8 %collective-permute-start.46 = (f32[16,512]{1,0:T(8,128)S(1)}, f32[16,512]{1,0:T(8,128)S(1)}, u32[]{:S(2)}, u32[]{:S(2)}) collective-permute-start(f32[16,512]{1,0:T(8,128)S(1)} %coarse.5.refs_0_), channel_id=1, source_target_pairs={{0,6},{1,7},{2,4},{3,5},{4,2},{5,3},{6,0},{7,1},{8,14},{9,15},{10,... | collective-permute-start | bytes 98312 | tf_op jit(solution)/shard_map/ppermute | solution.py:22
  105.1 4.8 %collective-permute-start.45 = (f32[16,512]{1,0:T(8,128)S(1)}, f32[16,512]{1,0:T(8,128)S(1)}, u32[]{:S(2)}, u32[]{:S(2)}) collective-permute-start(f32[16,512]{1,0:T(8,128)S(1)} %coarse.5.refs_0_), channel_id=1, source_target_pairs={{0,4},{1,5},{2,6},{3,7},{4,0},{5,1},{6,2},{7,3},{8,12},{9,13},{10,... | collective-permute-start | bytes 98312 | tf_op jit(solution)/shard_map/ppermute | solution.py:22
  105.1 4.8 %collective-permute-start.44 = (f32[16,512]{1,0:T(8,128)S(1)}, f32[16,512]{1,0:T(8,128)S(1)}, u32[]{:S(2)}, u32[]{:S(2)}) collective-permute-start(f32[16,512]{1,0:T(8,128)S(1)} %coarse.5.refs_0_), channel_id=1, source_target_pairs={{0,2},{1,3},{2,0},{3,1},{4,6},{5,7},{6,4},{7,5},{8,10},{9,11},{10,... | collective-permute-start | bytes 98312 | tf_op jit(solution)/shard_map/ppermute | solution.py:22
  (1 other events, 8.5 us)

commit v4 on v3

--- a/solution.py
+++ b/solution.py
@@ -108,27 +108,36 @@
 
         return carry
 
-    return begin, lambda: lax.fori_loop(0, chunks, one, 0)
-
-
-def split_kernel(flex_ref, large_ref, small_ref, buffer, sem):
-    begin, end = split_in_turn(flex_ref, 1, large_ref, small_ref, buffer, sem)
-    begin()
-    end()
-
-
-def pack_kernel(coupling_ref, map_ref, counts_ref, out_ref, sem):
-    slots, corners = map_ref.shape[2:]
-    span = out_ref.shape[2] - LANES
-    copy = pltpu.make_async_copy(coupling_ref.at[0, 0, :, :, pl.ds(span, span)], out_ref.at[:, :, pl.ds(0, span)], sem)
-    copy.start()
-    padded = jnp.concatenate([map_ref[0, 0].astype(jnp.float32), jnp.zeros((8 - slots, corners), jnp.float32)], axis=0)
-    column = jnp.concatenate([padded, jnp.zeros((8, LANES - corners), jnp.float32)], axis=1).T
-    lane = lax.broadcasted_iota(jnp.int32, (corners, LANES), 1)
-    live = jnp.full((corners, LANES), counts_ref[0, 0], jnp.int32).astype(jnp.float32)
-    for s in range(slots):
-        out_ref[s, :, span:] = jnp.where(lane == 0, column[:corners, s : s + 1], live)
-    copy.wait()
+    return begin, lambda slot, slots: lax.fori_loop(slot * per_slot, (slot + slots) * per_slot, one, 0)
+
+
+def pack_kernel(coupling_ref, map_ref, counts_ref, out_ref, map_buffer, sem):
+    slots, corners = coupling_ref.shape[2:4]
+    span = out_ref.shape[1]
+    copies = [
+        pltpu.make_async_copy(
+            coupling_ref.at[0, 0, s, :, pl.ds(span, span)], out_ref.at[pl.ds(s * corners, corners), :], sem.at[s]
+        )
+        for s in range(slots)
+    ]
+    maps = pltpu.make_async_copy(map_ref, map_buffer, sem.at[slots])
+    maps.start()
+    for copy in copies:
+        copy.start()
+    maps.wait()
+    numbers = jnp.concatenate([map_buffer[s] for s in range(slots)], axis=0).astype(jnp.float32)
+    numbers = jnp.concatenate([numbers, jnp.zeros((slots, LANES - corners), jnp.float32)], axis=1)
+    live = jnp.full((slots, span - LANES), counts_ref[0, 0], jnp.int32).astype(jnp.float32)
+    rest = out_ref.shape[0] - slots * corners - slots
+    numbers = jnp.concatenate([jnp.concatenate([numbers, live], axis=1), jnp.zeros((rest, span), jnp.float32)], axis=0)
+    out_ref[slots * corners :, :] = numbers
+    for copy in copies:
+        copy.wait()
+
+
+def without_numbers(packed, used):
+    row = lax.broadcasted_iota(jnp.int32, packed.shape, 0)
+    return jnp.where(row < used, packed, 0.0)
 
 
 def prepare_kernel(
@@ -168,7 +177,27 @@
             lanes = slice(k * width, (k + 1) * width)
             right_rows_ref[j, :, lanes] = right_buffer[j, :, k, :]
             weight_rows_ref[j : j + 1, lanes] = weight_buffer[j, k : k + 1, :]
-    end()
+    end(0, slots)
+
+
+def beside(x):
+    half = x.shape[0] // 2
+    return jnp.concatenate([x[:half], x[half:]], axis=1)
+
+
+def stacked_again(x):
+    half = x.shape[1] // 2
+    return jnp.concatenate([x[:, :half], x[:, half:]], axis=0)
+
+
+def lane_pair(column, at):
+    half = column.shape[0] // 2
+    lane = lax.broadcasted_iota(jnp.int32, (half, LANES), 1)
+    return jnp.where(lane == at, column[:half], jnp.where(lane == at + 1, column[half:], 0.0))
+
+
+def column_of(tile, at):
+    return jnp.concatenate([tile[:, at : at + 1], tile[:, at + 1 : at + 2]], axis=0)
 
 
 def start_exchange(
@@ -185,12 +214,12 @@
     prev = to_corners(send_ref[...], prev_t_ref[...], corners)
     load = through_table(jnp.concatenate([own, prev], axis=1), scatter_ref[...])
     half = load.shape[1] // 2
-    low, high = load[:, :half], load[:, half:]
-    mine_ref[:, :half] = jnp.where(parity == 0, low, high)
-    other_ref[:, :half] = jnp.where(parity == 0, high, low)
-    spare = jnp.where(lax.broadcasted_iota(jnp.int32, (loads, LANES), 1) == 0, norm, 0.0)
-    mine_ref[:, half:] = spare
-    other_ref[:, half:] = spare
+    low, high = beside(load[:, :half]), beside(load[:, half:])
+    spare = lane_pair(norm, 0)
+    mine_ref[:, : 2 * half] = jnp.where(parity == 0, low, high)
+    other_ref[:, : 2 * half] = jnp.where(parity == 0, high, low)
+    mine_ref[:, 2 * half :] = spare
+    other_ref[:, 2 * half :] = spare
 
 
 def local_norm(r, z):
@@ -198,12 +227,13 @@
 
 
 def first_kernel(
-    corners, info_ref, partner_ref, counts_ref, right_ref, weight_ref, inverse_ref, link_t_ref, map_ref, prev_coupling_ref,
+    corners, info_ref, partner_ref, counts_ref, right_ref, weight_ref, inverse_ref, link_t_ref, map_ref, prev_ref,
     mask_ref, r_ref, z_ref, send_ref, mine_ref, other_ref, prev_t_ref, scatter_ref,
 ):
     slots, loads, span = r_ref.shape
     links = span // LANES
-    live_prev = prev_coupling_ref[0, 0:1, span:][:, 1:2]
+    used = slots * corners
+    live_prev = prev_ref[used : used + 1, LANES : LANES + 1]
     for j in range(slots):
         live = jnp.where(j < counts_ref[0, 0], live_prev, 0.0)
         for k in range(links):
@@ -213,13 +243,15 @@
     z = weight_ref[...][:, None, :] * r
     r_ref[...] = r
     z_ref[...] = z
-    prev_t_ref[...] = jnp.concatenate(pieces(corner_rows(prev_coupling_ref[...], span).T, 2), axis=1)
+    prev_t_ref[...] = jnp.concatenate(pieces(without_numbers(prev_ref[...], used).T, 2), axis=1)
     size = scatter_ref.shape[1]
     lane = lax.broadcasted_iota(jnp.int32, (corners, size), 1)
-    padded = jnp.concatenate([map_ref[0, 0].astype(jnp.float32), jnp.zeros((8 - slots, corners), jnp.float32)], axis=0)
-    column = jnp.concatenate([padded, jnp.zeros((8, LANES - corners), jnp.float32)], axis=1).T
-    own = [column[:corners, s : s + 1] for s in range(slots)]
-    prev = [prev_coupling_ref[s, :, span:][:, :1] for s in range(slots)]
+    own = jnp.concatenate([map_ref[j] for j in range(slots)], axis=0).astype(jnp.float32)
+    own = jnp.concatenate([own, jnp.zeros((slots, LANES - corners), jnp.float32)], axis=1)
+    both = jnp.concatenate([own, prev_ref[used : used + slots, :LANES]], axis=0)
+    both = jnp.concatenate([both, jnp.zeros((16 - 2 * slots, LANES), jnp.float32)], axis=0).T
+    own = [both[:corners, j : j + 1] for j in range(slots)]
+    prev = [both[:corners, slots + j : slots + j + 1] for j in range(slots)]
     for side, columns in enumerate((own, prev)):
         parts = [(c.astype(jnp.int32) == lane).astype(jnp.float32) for c in columns]
         if slots * corners < LANES:
@@ -231,18 +263,16 @@
     )
 
 
-def table_kernel(rows, levels, info_ref, prev_coupling_ref, map_ref, *refs):
+def table_kernel(rows, levels, info_ref, packed_ref, map_ref, *refs):
     *parts, prev_ref, pick_ref, coarse_ref, joined_ref = refs
-    span = prev_ref.shape[1]
-    prev_ref[...] = stacked(corner_rows(prev_coupling_ref[...], span), 2)
-    slots, corners = map_ref.shape[2:]
+    slots, _, corners = map_ref.shape
+    used = slots * corners
+    prev_ref[...] = stacked(without_numbers(packed_ref[...], used), 2)
     side_rows = len(parts) // 2
     per_level = rows * len(parts)
     lines = []
-    own = [map_ref[0, 0, s : s + 1, :] for s in range(slots)]
-    filled = jnp.zeros((LANES - corners, LANES), jnp.float32)
-    prev = [jnp.concatenate([prev_coupling_ref[s, :, span:], filled], axis=0).T for s in range(slots)]
-    prev = [turned[:1, :corners].astype(jnp.int32) for turned in prev]
+    own = [map_ref[s] for s in range(slots)]
+    prev = [packed_ref[used + s : used + s + 1, :corners].astype(jnp.int32) for s in range(slots)]
     for line in (own, prev):
         if slots * corners < LANES:
             line.append(jnp.full((1, LANES - slots * corners), -1, jnp.int32))
@@ -277,12 +307,12 @@
     slots, loads, span = own_ref.shape
     links = span // LANES
     per_level = pick_ref.shape[0] // levels
-    spare = block_refs[0][:, per_level:]
-    norm = spare[:, 1:2]
-    product = spare[:, :1]
+    spare = block_refs[0][:, 2 * per_level :]
+    norm = column_of(spare, 2)
     for ref in block_refs[1:]:
-        product = product + ref[:, per_level:][:, :1]
-    gathered = jnp.concatenate([ref[:, :per_level] for ref in block_refs], axis=1)
+        spare = spare + ref[:, 2 * per_level :]
+    product = column_of(spare, 0)
+    gathered = jnp.concatenate([stacked_again(ref[:, : 2 * per_level]) for ref in block_refs], axis=1)
     picked = through_table(gathered, pick_ref[...])
     near = own_ref[...] + from_corners(picked[:, :LANES], link_ref[...], slots, corners)
     far_ref[...] = facing_ref[...] + from_corners(picked[:, LANES:], prev_ref[...], slots, corners)
@@ -340,24 +370,48 @@
         out_ref[s] = flex_product(values_ref[s], large_ref[s], small_ref[s])
 
 
+def flex_far_slot(s, begun, values_ref, forces_ref, large_ref, small_ref, own_ref, facing_ref):
+    width = values_ref.shape[2]
+    answer = begun + flex_product(forces_ref[s], large_ref[s], small_ref[s])
+    own, facing = answer[:, :width], answer[:, width:]
+    own_ref[s] = own
+    facing_ref[s] = facing
+    return jnp.sum(values_ref[s] * own + forces_ref[s] * facing, axis=1, keepdims=True)
+
+
+def write_energy(work, energy_ref):
+    half = energy_ref.shape[1] - LANES
+    energy_ref[:, :half] = jnp.zeros((energy_ref.shape[0], half), jnp.float32)
+    energy_ref[:, half:] = lane_pair(work, 2)
+
+
 def flex_far_kernel(values_ref, forces_ref, begun_ref, large_ref, small_ref, own_ref, facing_ref, energy_ref):
-    slots, loads, width = values_ref.shape
+    slots, loads, _ = values_ref.shape
     work = jnp.zeros((loads, 1), jnp.float32)
     for s in range(slots):
-        answer = begun_ref[s] + flex_product(forces_ref[s], large_ref[s], small_ref[s])
-        own, facing = answer[:, :width], answer[:, width:]
-        own_ref[s] = own
-        facing_ref[s] = facing
-        work += jnp.sum(values_ref[s] * own + forces_ref[s] * facing, axis=1, keepdims=True)
-    half = energy_ref.shape[1] - LANES
-    energy_ref[:, :half] = jnp.zeros((loads, half), jnp.float32)
-    energy_ref[:, half:] = jnp.where(lax.broadcasted_iota(jnp.int32, (loads, LANES), 1) == 1, work, 0.0)
+        work += flex_far_slot(s, begun_ref[s], values_ref, forces_ref, large_ref, small_ref, own_ref, facing_ref)
+    write_energy(work, energy_ref)
+
+
+def flex_first_kernel(
+    values_ref, forces_ref, near_large_ref, near_small_ref, flex_ref, own_ref, facing_ref, energy_ref, large_ref, small_ref,
+    begun_ref, buffer, sem,
+):
+    slots, loads, _ = values_ref.shape
+    begin, end = split_in_turn(flex_ref, 1, large_ref, small_ref, buffer, sem)
+    begin()
+    flex_near_kernel(values_ref, near_large_ref, near_small_ref, begun_ref)
+    work = jnp.zeros((loads, 1), jnp.float32)
+    for s in range(slots):
+        end(s, 1)
+        work += flex_far_slot(s, begun_ref[s], values_ref, forces_ref, large_ref, small_ref, own_ref, facing_ref)
+    write_energy(work, energy_ref)
 
 
 def coarse_kernel(rows, levels, info_ref, mine_ref, other_ref, table_ref, out_ref):
     parity = info_ref[0]
     half = mine_ref.shape[1] - LANES
-    mine, other = mine_ref[:, :half], other_ref[:, :half]
+    mine, other = stacked_again(mine_ref[:, :half]), stacked_again(other_ref[:, :half])
     low, high = jnp.where(parity == 0, mine, other), jnp.where(parity == 0, other, mine)
     load = jnp.concatenate([low, high], axis=1)
     loads, size = load.shape
@@ -373,11 +427,10 @@
     for level in range(levels):
         starts = range(level * stretch, size, levels * stretch)
         own = jnp.where(info_ref[2] == level, jnp.concatenate([load[:, a : a + stretch] for a in starts], axis=1), own)
-    mine_spare, other_spare = mine_ref[:, half:], other_ref[:, half:]
-    product = jnp.sum(answer * own, axis=1, keepdims=True) + (mine_spare[:, 1:2] + other_spare[:, 1:2])
-    lane = lax.broadcasted_iota(jnp.int32, (loads, LANES), 1)
-    out_ref[:, :per_level] = answer
-    out_ref[:, per_level:] = jnp.where(lane == 0, product, jnp.where(lane == 1, mine_spare[:, :1], 0.0))
+    spare = mine_ref[:, half:]
+    product = jnp.sum(answer * own, axis=1, keepdims=True) + column_of(spare + other_ref[:, half:], 2)
+    out_ref[:, : 2 * per_level] = beside(answer)
+    out_ref[:, 2 * per_level :] = lane_pair(product, 0) + lane_pair(column_of(spare, 0), 2)
 
 
 VMEM = pl.BlockSpec(memory_space=pltpu.VMEM)
@@ -439,24 +492,27 @@
     at_col = lax.axis_index("col")
     info = jnp.stack([at_col % 2, lax.axis_index("row"), at_col // 2]).astype(jnp.int32)
 
+    own_map = corner_map.reshape(slots, 1, corners)
     coupling = pltpu.with_memory_space_constraint(coupling, pltpu.HBM)
     to_next = pl.pallas_call(
         pack_kernel,
-        out_shape=shape_of(slots, corners, span + LANES),
-        in_specs=[HBM, VMEM, SMEM],
+        out_shape=shape_of(LANES, span),
+        in_specs=[HBM, HBM, SMEM],
         out_specs=VMEM,
-        scratch_shapes=[pltpu.SemaphoreType.DMA],
+        scratch_shapes=[pltpu.VMEM((slots, 1, corners), jnp.int32), pltpu.SemaphoreType.DMA((slots + 1,))],
         compiler_params=PARAMS,
         cost_estimate=LITTLE,
         name="pack",
-    )(coupling, corner_map, counts)
+    )(coupling, pltpu.with_memory_space_constraint(own_map, pltpu.HBM), counts)
+    coarse_inverse, to_next = lax.optimization_barrier((coarse_inverse, to_next))
     prev_coupling = shifted(to_next, "col", 1)
     coarse_parts = gathered_along([coarse_inverse], row_bits)
+    prev_coupling, *coarse_parts[1:3] = lax.optimization_barrier((prev_coupling, *coarse_parts[1:3]))
     coarse_parts = coarse_parts + [swapped(part, 1) for part in coarse_parts]
 
     state = shape_of(slots, loads, span)
     small = shape_of(loads, LANES)
-    half_load = shape_of(loads, coarse_size // 2 + LANES)
+    half_load = shape_of(loads // 2, coarse_size + LANES)
     out_state = jax.ShapeDtypeStruct(right_side.shape, jnp.float32)
 
     def table(*dims):
@@ -500,19 +556,7 @@
         compiler_params=PARAMS,
         cost_estimate=LITTLE,
         name="first",
-    )(info, partner, counts, right, weight, inverse, link_t, corner_map, prev_coupling)
-
-    def split_far(flex):
-        return pl.pallas_call(
-            split_kernel,
-            out_shape=half_pieces,
-            in_specs=[HBM],
-            out_specs=[VMEM] * 2,
-            scratch_shapes=buffers + [pltpu.SemaphoreType.DMA((BUFFERS,))],
-            compiler_params=PARAMS,
-            cost_estimate=LITTLE,
-            name="split",
-        )(pltpu.with_memory_space_constraint(flex, pltpu.HBM))
+    )(info, partner, counts, right, weight, inverse, link_t, own_map, prev_coupling)
 
     def tables():
         return pl.pallas_call(
@@ -524,35 +568,45 @@
             compiler_params=pltpu.CompilerParams(vmem_limit_bytes=max(14 * 1024 * 1024, 16 * per_level * coarse_size)),
             cost_estimate=LITTLE,
             name="tables",
-        )(info, prev_coupling, corner_map, *coarse_parts)
+        )(info, prev_coupling, own_map, *coarse_parts)
 
     kept = ()
     for iteration in range(ITERS):
         first, last = iteration == 0, iteration + 1 == ITERS
         forces = shifted(send, "col", -1)
         total = mine + swapped(other, 1)
-        total, held, flexibility = lax.optimization_barrier((total, z, flexibility))
         if first:
-            far_large, far_small = split_far(flexibility)
-        begun = pl.pallas_call(
-            flex_near_kernel,
-            out_shape=shape_of(slots, loads, iface),
-            in_specs=[VMEM] * 3,
-            out_specs=VMEM,
-            compiler_params=PARAMS,
-            cost_estimate=LITTLE,
-            name="flex_near",
-        )(held, near_large, near_small)
-        total = summed_along(total, level_bits)
-        own, facing, energy = pl.pallas_call(
-            flex_far_kernel,
-            out_shape=(state, state, half_load),
-            in_specs=[VMEM] * 5,
-            out_specs=[VMEM] * 3,
-            compiler_params=PARAMS,
-            cost_estimate=LITTLE,
-            name="flex_far",
-        )(held, forces, begun, far_large, far_small)
+            total = summed_along(total, level_bits)
+            own, facing, energy, far_large, far_small = pl.pallas_call(
+                flex_first_kernel,
+                out_shape=(state, state, half_load) + half_pieces,
+                in_specs=[VMEM] * 4 + [HBM],
+                out_specs=[VMEM] * 5,
+                scratch_shapes=[pltpu.VMEM((slots, loads, iface), jnp.float32)] + buffers + [pltpu.SemaphoreType.DMA((BUFFERS,))],
+                compiler_params=PARAMS,
+                cost_estimate=LITTLE,
+                name="flex_first",
+            )(z, forces, near_large, near_small, flex)
+        else:
+            begun = pl.pallas_call(
+                flex_near_kernel,
+                out_shape=shape_of(slots, loads, iface),
+                in_specs=[VMEM] * 3,
+                out_specs=VMEM,
+                compiler_params=PARAMS,
+                cost_estimate=LITTLE,
+                name="flex_near",
+            )(z, near_large, near_small)
+            total = summed_along(total, level_bits)
+            own, facing, energy = pl.pallas_call(
+                flex_far_kernel,
+                out_shape=(state, state, half_load),
+                in_specs=[VMEM] * 5,
+                out_specs=[VMEM] * 3,
+                compiler_params=PARAMS,
+                cost_estimate=LITTLE,
+                name="flex_far",
+            )(z, forces, begun, far_large, far_small)
         total = summed_along(total + energy, row_bits)
         rest = swapped(total, 1)
         facing_prev = shifted(facing, "col", 1)
@@ -560,7 +614,7 @@
             prev, pick, coarse_table = tables()
         block = pl.pallas_call(
             functools.partial(coarse_kernel, rows, levels),
-            out_shape=shape_of(loads, per_level + LANES),
+            out_shape=shape_of(loads // 2, 2 * per_level + LANES),
             in_specs=[SMEM] + [VMEM] * 3,
             out_specs=VMEM,
             compiler_params=PARAMS,

time: 112 us -> 107 us (0.955)
  starting transfers between devices: 49.7 us -> 47.2 us
  Pallas kernels: 33.8 us -> 31.8 us
    pallas_call x3 -> x2, Pallas kernels: 5.17 us -> 3.45 us  [local(): pl.pallas_call(flex_far_kernel, out_shape=(state, state, half_load), in_s...]
    pallas_call x3 -> x2, Pallas kernels: 4.84 us -> 3.23 us  [local(): pl.pallas_call(flex_near_kernel, out_shape=shape_of(slots, loads, iface),...]
    ppermute x7, starting transfers between devices: 4.6 us -> 3.07 us  [shifted(): lax.ppermute(x, axis, [(i, (i + by) % devices) for i in range(devices)])]
    pallas_call x2, Pallas kernels: 5.34 us -> 6.65 us  [the longest x1 5.68 us: local(): pl.pallas_call(flex_first_kernel, out_shape=(state, state, half_load) + h...]
    ppermute x40, waiting for transfers between devices: 23.6 us -> 24.8 us  [swapped(): return lax.ppermute(x, BOTH, [(i, i ^ bits) for i in range(devices)])]
  transfers between devices with their start and end apart: 47 -> 47, of which waited for: 22 -> 24; matrix products, arithmetic and copies ran while one was open for 0% -> 0% of each run, Pallas kernels for 23% -> 22%
where the time goes in v4:
time: 107 us
  starting transfers between devices  47.2 us (44%)
  Pallas kernels  31.8 us (30%)
  waiting for transfers between devices  26.6 us (25%)
  between operations  1.46 us (1%)
    ppermute x40, starting transfers between devices, swapped(): return lax.ppermute(x, BOTH, [(i, i ^ bits) for i in range(devices)])  44.1 us
    ppermute x40, waiting for transfers between devices, swapped(): return lax.ppermute(x, BOTH, [(i, i ^ bits) for i in range(devices)])  24.8 us
    pallas_call x3, Pallas kernels, local(): pl.pallas_call(functools.partial(step_kernel, corners, levels, first, las...  6.03 us
    pallas_call x1, Pallas kernels, local(): pl.pallas_call(prepare_kernel, out_shape=half_pieces + (shape_of(slots *...  5.75 us
    pallas_call x1, Pallas kernels, local(): pl.pallas_call(flex_first_kernel, out_shape=(state, state, half_load) + h...  5.68 us
    pallas_call x3, Pallas kernels, local(): pl.pallas_call(functools.partial(coarse_kernel, rows, levels), out_shape=...  3.6 us
    pallas_call x2, Pallas kernels, local(): pl.pallas_call(flex_far_kernel, out_shape=(state, state, half_load), in_s...  3.45 us
    pallas_call x2, Pallas kernels, local(): pl.pallas_call(flex_near_kernel, out_shape=shape_of(slots, loads, iface),...  3.23 us
  transfers between devices with their start and end apart: 47, of which 24 were waited for; matrix products, arithmetic and copies ran while one was open for 0% of the time, Pallas kernels for 22%

profile of v4, /device:TPU:0, one launch (start us, length us, event | category | flops | bytes accessed | tf_op | source)
XLA Modules:
  0.0 107.2 jit_solution(9872089373622118539)
XLA Ops:
  2.2 3.0 %collective-permute-start.2 = (f32[48,1536]{1,0:T(8,128)}, f32[48,1536]{1,0:T(8,128)S(1)}, u32[]{:S(2)}, u32[]{:S(2)}) collective-permute-start(f32[48,1536]{1,0:T(8,128)} %refs_0_), channel_id=1, source_target_pairs={{0,16},{1,17},{2,18},{3,19},{4,20},{5,21},{6,22},{7,23},{8,24},{9,... | collective-permute-start | bytes 884744 | tf_op jit(solution)/shard_map/ppermute | solution.py:22
  5.3 1.5 %collective-permute-start.1 = (f32[48,1536]{1,0:T(8,128)}, f32[48,1536]{1,0:T(8,128)S(1)}, u32[]{:S(2)}, u32[]{:S(2)}) collective-permute-start(f32[48,1536]{1,0:T(8,128)} %refs_0_), channel_id=1, source_target_pairs={{0,8},{1,9},{2,10},{3,11},{4,12},{5,13},{6,14},{7,15},{8,0},{9,1},... | collective-permute-start | bytes 884744 | tf_op jit(solution)/shard_map/ppermute | solution.py:22
  6.9 5.8 %prepare.1 = (bf16[5,512,1024]{2,1,0:T(8,128)(2,1)S(1)}, bf16[5,512,1024]{2,1,0:T(8,128)(2,1)S(1)}, s32[20,128]{1,0:T(8,128)S(1)}, s32[20,128]{1,0:T(8,128)S(1)}...) custom-call(s32[3]{0:T(128)S(1)} %pad_add_fusion.info_ref, ...), custom_call_target="tpu_custom_call" | custom-call | flops 1024 | bytes 1024 | tf_op jit(solution)/shard_map/prepare/pallas_call | solution.py:526
  12.6 1.8 %collective-permute-done.prev_ref.packed_ref = f32[128,512]{1,0:T(8,128)S(1)} collective-permute-done((f32[128,512]{1,0:T(8,128)S(1)}, f32[128,512]{1,0:T(8,128)S(1)}, u32[]{:S(2)}, u32[]{:S(2)}) %collective-permute-start) | collective-permute-done | bytes 262176 | tf_op jit(solution)/shard_map/ppermute | solution.py:17
  14.4 1.4 %first.1 = (f32[5,512]{1,0:T(8,128)S(1)}, f32[5,16,512]{2,1,0:T(8,128)S(1)}, f32[5,16,512]{2,1,0:T(8,128)S(1)}, f32[5,16,512]{2,1,0:T(8,128)S(1)}, f32[8,1664]{1...) custom-call(s32[3]{0:T(128)S(1)} %pad_add_fusion.info_ref, ...), custom_call_target="tpu_custom_call" | custom-call | flops 1024 | bytes 1024 | tf_op jit(solution)/shard_map/first/pallas_call | solution.py:548
  15.8 1.9 %collective-permute-start.3 = (f32[5,16,512]{2,1,0:T(8,128)S(1)}, f32[5,16,512]{2,1,0:T(8,128)S(1)}, u32[]{:S(2)}, u32[]{:S(2)}) collective-permute-start(f32[5,16,512]{2,1,0:T(8,128)S(1)} %get-tuple-element.63), channel_id=1, source_target_pairs={{0,7},{1,0},{2,1},{3,2},{4,3},{5,4},{6,5},{7,6},{8,15},{9,8},{10,9... | collective-permute-start | bytes 491528 | tf_op jit(solution)/shard_map/ppermute | solution.py:17
  17.7 1.2 %collective-permute-done.10 = f32[8,1664]{1,0:T(8,128)S(1)} collective-permute-done((f32[8,1664]{1,0:T(8,128)S(1)}, f32[8,1664]{1,0:T(8,128)S(1)}, u32[]{:S(2)}, u32[]{:S(2)}) %collective-permute-start.10) | collective-permute-done | bytes 53280 | tf_op jit(solution)/shard_map/ppermute | solution.py:22
  18.9 1.9 %collective-permute-start.13 = (f32[8,1664]{1,0:T(8,128)S(1)}, f32[8,1664]{1,0:T(8,128)S(1)}, u32[]{:S(2)}, u32[]{:S(2)}) collective-permute-start(f32[8,1664]{1,0:T(8,128)S(1)} %add.78), channel_id=1, source_target_pairs={{0,6},{1,7},{2,4},{3,5},{4,2},{5,3},{6,0},{7,1},{8,14},{9,15},{10,... | collective-permute-start | bytes 159752 | tf_op jit(solution)/shard_map/ppermute | solution.py:22
  20.8 2.6 %collective-permute-start.11 = (f32[8,1664]{1,0:T(8,128)S(1)}, f32[8,1664]{1,0:T(8,128)S(1)}, u32[]{:S(2)}, u32[]{:S(2)}) collective-permute-start(f32[8,1664]{1,0:T(8,128)S(1)} %add.78), channel_id=1, source_target_pairs={{0,2},{1,3},{2,0},{3,1},{4,6},{5,7},{6,4},{7,5},{8,10},{9,11},{10,... | collective-permute-start | bytes 159752 | tf_op jit(solution)/shard_map/ppermute | solution.py:22
  23.4 1.1 %collective-permute-start.5 = (f32[48,1536]{1,0:T(8,128)S(1)}, f32[48,1536]{1,0:T(8,128)S(1)}, u32[]{:S(2)}, u32[]{:S(2)}) collective-permute-start(f32[48,1536]{1,0:T(8,128)S(1)} %copy-done), channel_id=1, source_target_pairs={{0,24},{1,25},{2,26},{3,27},{4,28},{5,29},{6,30},{7,31},{8,16},{9,... | collective-permute-start | bytes 884744 | tf_op jit(solution)/shard_map/ppermute | solution.py:22
  24.5 5.7 %flex_first.1 = (f32[5,16,512]{2,1,0:T(8,128)S(1)}, f32[5,16,512]{2,1,0:T(8,128)S(1)}, f32[8,1664]{1,0:T(8,128)S(1)}, bf16[5,512,1024]{2,1,0:T(8,128)(2,1)S(1)}, bf16[5,512,1024]{2,1,0:T(8,128)(2,1)S(1)}) custom-call(f32[5,16,512]{2,1,0:T(8,128)S(1)} %get-tuple-element.62.values_ref.z_ref, f32[5,16,512]{2,1,0:T(8,128)S(1)} %collective-permute-done.3.forces_ref, ...), custom_call_target="tpu_custom_call" | custom-call | flops 1024 | bytes 1024 | tf_op jit(solution)/shard_map/flex_first/pallas_call | solution.py:580
  30.2 1.8 %collective-permute-start.16 = (f32[8,1664]{1,0:T(8,128)S(1)}, f32[8,1664]{1,0:T(8,128)S(1)}, u32[]{:S(2)}, u32[]{:S(2)}) collective-permute-start(f32[8,1664]{1,0:T(8,128)S(1)} %add_add_fusion.5), channel_id=1, source_target_pairs={{0,24},{1,25},{2,26},{3,27},{4,28},{5,29},{6,30},{7,31},{8,16},{9,... | collective-permute-start | bytes 159752 | tf_op jit(solution)/shard_map/ppermute | solution.py:22
  32.6 1.2 %collective-permute-start.14 = (f32[8,1664]{1,0:T(8,128)S(1)}, f32[8,1664]{1,0:T(8,128)S(1)}, u32[]{:S(2)}, u32[]{:S(2)}) collective-permute-start(f32[8,1664]{1,0:T(8,128)S(1)} %add_add_fusion.5), channel_id=1, source_target_pairs={{0,8},{1,9},{2,10},{3,11},{4,12},{5,13},{6,14},{7,15},{8,0},{9,1},... | collective-permute-start | bytes 159752 | tf_op jit(solution)/shard_map/ppermute | solution.py:22
  34.3 1.4 %collective-permute-done.16 = f32[8,1664]{1,0:T(8,128)S(1)} collective-permute-done((f32[8,1664]{1,0:T(8,128)S(1)}, f32[8,1664]{1,0:T(8,128)S(1)}, u32[]{:S(2)}, u32[]{:S(2)}) %collective-permute-start.16) | collective-permute-done | bytes 53280 | tf_op jit(solution)/shard_map/ppermute | solution.py:22
  37.9 1.7 %tables.1 = (bf16[256,512]{1,0:T(8,128)(2,1)S(1)}, bf16[1536,256]{1,0:T(8,128)(2,1)S(1)}, bf16[1536,768]{1,0:T(8,128)(2,1)S(1)}) custom-call(s32[3]{0:T(128)S(1)} %pad_add_fusion.info_ref, f32[128,512]{1,0:T(8,128)S(1)} %collective-permute-done.prev_ref.packed_ref, s32[5,1,24]{2,1,0:T(1,128)S(1)} %bitcast.6, f32[48,1536]{1,0:T(8,128)S(1)} %copy-done, ...), custom_call_target="tpu_custom_call" | custom-call | flops 1024 | bytes 1024 | tf_op jit(solution)/shard_map/tables/pallas_call | solution.py:562
  39.6 1.2 %coarse.3.refs_0_ = f32[8,896]{1,0:T(8,128)S(1)} custom-call(s32[3]{0:T(128)S(1)} %pad_add_fusion.info_ref, f32[8,1664]{1,0:T(8,128)S(1)} %add_add_fusion.4.mine_ref, f32[8,1664]{1,0:T(8,128)S(1)} %collective-permute-done.17.other_ref, bf16[1536,768]{1,0:T(8,128)(2,1)S(1)} %get-tuple-element.81.table_ref), custom_call_target="tpu_custom_call" | custom-call | flops 1024 | bytes 1024 | tf_op jit(solution)/shard_map/coarse/pallas_call | solution.py:615
  40.8 2.9 %collective-permute-start.20 = (f32[8,896]{1,0:T(8,128)S(1)}, f32[8,896]{1,0:T(8,128)S(1)}, u32[]{:S(2)}, u32[]{:S(2)}) collective-permute-start(f32[8,896]{1,0:T(8,128)S(1)} %coarse.3.refs_0_), channel_id=1, source_target_pairs={{0,6},{1,7},{2,4},{3,5},{4,2},{5,3},{6,0},{7,1},{8,14},{9,15},{10,... | collective-permute-start | bytes 86024 | tf_op jit(solution)/shard_map/ppermute | solution.py:22
  43.7 1.5 %collective-permute-start.18 = (f32[8,896]{1,0:T(8,128)S(1)}, f32[8,896]{1,0:T(8,128)S(1)}, u32[]{:S(2)}, u32[]{:S(2)}) collective-permute-start(f32[8,896]{1,0:T(8,128)S(1)} %coarse.3.refs_0_), channel_id=1, source_target_pairs={{0,2},{1,3},{2,0},{3,1},{4,6},{5,7},{6,4},{7,5},{8,10},{9,11},{10,... | collective-permute-start | bytes 86024 | tf_op jit(solution)/shard_map/ppermute | solution.py:22
  45.2 1.4 %collective-permute-done.20.refs_3_ = f32[8,896]{1,0:T(8,128)S(1)} collective-permute-done((f32[8,896]{1,0:T(8,128)S(1)}, f32[8,896]{1,0:T(8,128)S(1)}, u32[]{:S(2)}, u32[]{:S(2)}) %collective-permute-start.20) | collective-permute-done | bytes 28704 | tf_op jit(solution)/shard_map/ppermute | solution.py:22
  46.6 1.9 %collective-permute-done.19.refs_2_ = f32[8,896]{1,0:T(8,128)S(1)} collective-permute-done((f32[8,896]{1,0:T(8,128)S(1)}, f32[8,896]{1,0:T(8,128)S(1)}, u32[]{:S(2)}, u32[]{:S(2)}) %collective-permute-start.19) | collective-permute-done | bytes 28704 | tf_op jit(solution)/shard_map/ppermute | solution.py:22
  48.5 1.9 %step.3 = (f32[5,16,512]{2,1,0:T(8,128)S(1)}, f32[5,16,512]{2,1,0:T(8,128)S(1)}, f32[5,16,512]{2,1,0:T(8,128)S(1)}, f32[5,16,512]{2,1,0:T(8,128)S(1)}, f32[5,16,...) custom-call(s32[3]{0:T(128)S(1)} %pad_add_fusion.info_ref, ...), custom_call_target="tpu_custom_call" | custom-call | flops 1024 | bytes 1024 | tf_op jit(solution)/shard_map/step/pallas_call | solution.py:626
  52.1 1.6 %collective-permute-start.26 = (f32[8,1664]{1,0:T(8,128)S(1)}, f32[8,1664]{1,0:T(8,128)S(1)}, u32[]{:S(2)}, u32[]{:S(2)}) collective-permute-start(f32[8,1664]{1,0:T(8,128)S(1)} %add.86), channel_id=1, source_target_pairs={{0,6},{1,7},{2,4},{3,5},{4,2},{5,3},{6,0},{7,1},{8,14},{9,15},{10,... | collective-permute-start | bytes 159752 | tf_op jit(solution)/shard_map/ppermute | solution.py:22
  54.3 2.3 %collective-permute-start.24 = (f32[8,1664]{1,0:T(8,128)S(1)}, f32[8,1664]{1,0:T(8,128)S(1)}, u32[]{:S(2)}, u32[]{:S(2)}) collective-permute-start(f32[8,1664]{1,0:T(8,128)S(1)} %add.86), channel_id=1, source_target_pairs={{0,2},{1,3},{2,0},{3,1},{4,6},{5,7},{6,4},{7,5},{8,10},{9,11},{10,... | collective-permute-start | bytes 159752 | tf_op jit(solution)/shard_map/ppermute | solution.py:22
  56.5 1.6 %flex_near.2.begun_ref = f32[5,16,1024]{2,1,0:T(8,128)S(1)} custom-call(f32[5,16,512]{2,1,0:T(8,128)S(1)} %get-tuple-element.82.values_ref.z_ref, bf16[5,512,1024]{2,1,0:T(8,128)(2,1)S(1)} %get-tuple-element.64.near_large_ref.large_ref, bf16[5,512,1024]{2,1,0:T(8,128)(2,1)S(1)} %get-tuple-element.65.near_small_ref.small_ref), custom_call_target="tpu_custom_call" | custom-call | flops 1024 | bytes 1024 | tf_op jit(solution)/shard_map/flex_near/pallas_call | solution.py:591
  58.2 1.7 %flex_far.2 = (f32[5,16,512]{2,1,0:T(8,128)S(1)}, f32[5,16,512]{2,1,0:T(8,128)S(1)}, f32[8,1664]{1,0:T(8,128)S(1)}) custom-call(f32[5,16,512]{2,1,0:T(8,128)S(1)} %get-tuple-element.82.values_ref.z_ref, f32[5,16,512]{2,1,0:T(8,128)S(1)} %collective-permute-done.21.forces_ref, f32[5,16,1024]{2,1,0:T(8,128)S(1)} %flex_near.2.begun_ref, ...), custom_call_target="tpu_custom_call" | custom-call | flops 1024 | bytes 1024 | tf_op jit(solution)/shard_map/flex_far/pallas_call | solution.py:601
  60.5 2.1 %collective-permute-start.29 = (f32[8,1664]{1,0:T(8,128)S(1)}, f32[8,1664]{1,0:T(8,128)S(1)}, u32[]{:S(2)}, u32[]{:S(2)}) collective-permute-start(f32[8,1664]{1,0:T(8,128)S(1)} %add_add_fusion.3), channel_id=1, source_target_pairs={{0,24},{1,25},{2,26},{3,27},{4,28},{5,29},{6,30},{7,31},{8,16},{9,... | collective-permute-start | bytes 159752 | tf_op jit(solution)/shard_map/ppermute | solution.py:22
  64.1 1.6 %collective-permute-done.29 = f32[8,1664]{1,0:T(8,128)S(1)} collective-permute-done((f32[8,1664]{1,0:T(8,128)S(1)}, f32[8,1664]{1,0:T(8,128)S(1)}, u32[]{:S(2)}, u32[]{:S(2)}) %collective-permute-start.29) | collective-permute-done | bytes 53280 | tf_op jit(solution)/shard_map/ppermute | solution.py:22
  67.5 1.2 %collective-permute-done.30.other_ref = f32[8,1664]{1,0:T(8,128)S(1)} collective-permute-done((f32[8,1664]{1,0:T(8,128)S(1)}, f32[8,1664]{1,0:T(8,128)S(1)}, u32[]{:S(2)}, u32[]{:S(2)}) %collective-permute-start.30) | collective-permute-done | bytes 53280 | tf_op jit(solution)/shard_map/ppermute | solution.py:22
  68.7 1.2 %coarse.4.refs_0_ = f32[8,896]{1,0:T(8,128)S(1)} custom-call(s32[3]{0:T(128)S(1)} %pad_add_fusion.info_ref, f32[8,1664]{1,0:T(8,128)S(1)} %add_add_fusion.2.mine_ref, f32[8,1664]{1,0:T(8,128)S(1)} %collective-permute-done.30.other_ref, bf16[1536,768]{1,0:T(8,128)(2,1)S(1)} %get-tuple-element.81.table_ref), custom_call_target="tpu_custom_call" | custom-call | flops 1024 | bytes 1024 | tf_op jit(solution)/shard_map/coarse/pallas_call | solution.py:615
  69.9 2.1 %collective-permute-start.33 = (f32[8,896]{1,0:T(8,128)S(1)}, f32[8,896]{1,0:T(8,128)S(1)}, u32[]{:S(2)}, u32[]{:S(2)}) collective-permute-start(f32[8,896]{1,0:T(8,128)S(1)} %coarse.4.refs_0_), channel_id=1, source_target_pairs={{0,6},{1,7},{2,4},{3,5},{4,2},{5,3},{6,0},{7,1},{8,14},{9,15},{10,... | collective-permute-start | bytes 86024 | tf_op jit(solution)/shard_map/ppermute | solution.py:22
  72.0 2.4 %collective-permute-start.31 = (f32[8,896]{1,0:T(8,128)S(1)}, f32[8,896]{1,0:T(8,128)S(1)}, u32[]{:S(2)}, u32[]{:S(2)}) collective-permute-start(f32[8,896]{1,0:T(8,128)S(1)} %coarse.4.refs_0_), channel_id=1, source_target_pairs={{0,2},{1,3},{2,0},{3,1},{4,6},{5,7},{6,4},{7,5},{8,10},{9,11},{10,... | collective-permute-start | bytes 86024 | tf_op jit(solution)/shard_map/ppermute | solution.py:22
  74.3 1.3 %collective-permute-done.33.refs_3_ = f32[8,896]{1,0:T(8,128)S(1)} collective-permute-done((f32[8,896]{1,0:T(8,128)S(1)}, f32[8,896]{1,0:T(8,128)S(1)}, u32[]{:S(2)}, u32[]{:S(2)}) %collective-permute-start.33) | collective-permute-done | bytes 28704 | tf_op jit(solution)/shard_map/ppermute | solution.py:22
  76.8 1.9 %step.4 = (f32[5,16,512]{2,1,0:T(8,128)S(1)}, f32[5,16,512]{2,1,0:T(8,128)S(1)}, f32[5,16,512]{2,1,0:T(8,128)S(1)}, f32[5,16,512]{2,1,0:T(8,128)S(1)}, f32[5,16,...) custom-call(s32[3]{0:T(128)S(1)} %pad_add_fusion.info_ref, ...), custom_call_target="tpu_custom_call" | custom-call | flops 1024 | bytes 1024 | tf_op jit(solution)/shard_map/step/pallas_call | solution.py:626
  79.5 1.2 %collective-permute-done.36 = f32[8,1664]{1,0:T(8,128)S(1)} collective-permute-done((f32[8,1664]{1,0:T(8,128)S(1)}, f32[8,1664]{1,0:T(8,128)S(1)}, u32[]{:S(2)}, u32[]{:S(2)}) %collective-permute-start.36) | collective-permute-done | bytes 53280 | tf_op jit(solution)/shard_map/ppermute | solution.py:22
  80.7 1.3 %collective-permute-start.39 = (f32[8,1664]{1,0:T(8,128)S(1)}, f32[8,1664]{1,0:T(8,128)S(1)}, u32[]{:S(2)}, u32[]{:S(2)}) collective-permute-start(f32[8,1664]{1,0:T(8,128)S(1)} %add.94), channel_id=1, source_target_pairs={{0,6},{1,7},{2,4},{3,5},{4,2},{5,3},{6,0},{7,1},{8,14},{9,15},{10,... | collective-permute-start | bytes 159752 | tf_op jit(solution)/shard_map/ppermute | solution.py:22
  83.2 2.0 %collective-permute-start.37 = (f32[8,1664]{1,0:T(8,128)S(1)}, f32[8,1664]{1,0:T(8,128)S(1)}, u32[]{:S(2)}, u32[]{:S(2)}) collective-permute-start(f32[8,1664]{1,0:T(8,128)S(1)} %add.94), channel_id=1, source_target_pairs={{0,2},{1,3},{2,0},{3,1},{4,6},{5,7},{6,4},{7,5},{8,10},{9,11},{10,... | collective-permute-start | bytes 159752 | tf_op jit(solution)/shard_map/ppermute | solution.py:22
  85.1 1.6 %flex_near.3.begun_ref = f32[5,16,1024]{2,1,0:T(8,128)S(1)} custom-call(f32[5,16,512]{2,1,0:T(8,128)S(1)} %get-tuple-element.96.values_ref.z_ref, bf16[5,512,1024]{2,1,0:T(8,128)(2,1)S(1)} %get-tuple-element.64.near_large_ref.large_ref, bf16[5,512,1024]{2,1,0:T(8,128)(2,1)S(1)} %get-tuple-element.65.near_small_ref.small_ref), custom_call_target="tpu_custom_call" | custom-call | flops 1024 | bytes 1024 | tf_op jit(solution)/shard_map/flex_near/pallas_call | solution.py:591
  86.8 1.7 %flex_far.3 = (f32[5,16,512]{2,1,0:T(8,128)S(1)}, f32[5,16,512]{2,1,0:T(8,128)S(1)}, f32[8,1664]{1,0:T(8,128)S(1)}) custom-call(f32[5,16,512]{2,1,0:T(8,128)S(1)} %get-tuple-element.96.values_ref.z_ref, f32[5,16,512]{2,1,0:T(8,128)S(1)} %collective-permute-done.34.forces_ref, f32[5,16,1024]{2,1,0:T(8,128)S(1)} %flex_near.3.begun_ref, ...), custom_call_target="tpu_custom_call" | custom-call | flops 1024 | bytes 1024 | tf_op jit(solution)/shard_map/flex_far/pallas_call | solution.py:601
  88.7 1.8 %collective-permute-start.42 = (f32[8,1664]{1,0:T(8,128)S(1)}, f32[8,1664]{1,0:T(8,128)S(1)}, u32[]{:S(2)}, u32[]{:S(2)}) collective-permute-start(f32[8,1664]{1,0:T(8,128)S(1)} %add_add_fusion.1), channel_id=1, source_target_pairs={{0,24},{1,25},{2,26},{3,27},{4,28},{5,29},{6,30},{7,31},{8,16},{9,... | collective-permute-start | bytes 159752 | tf_op jit(solution)/shard_map/ppermute | solution.py:22
  91.1 1.2 %collective-permute-start.40 = (f32[8,1664]{1,0:T(8,128)S(1)}, f32[8,1664]{1,0:T(8,128)S(1)}, u32[]{:S(2)}, u32[]{:S(2)}) collective-permute-start(f32[8,1664]{1,0:T(8,128)S(1)} %add_add_fusion.1), channel_id=1, source_target_pairs={{0,8},{1,9},{2,10},{3,11},{4,12},{5,13},{6,14},{7,15},{8,0},{9,1},... | collective-permute-start | bytes 159752 | tf_op jit(solution)/shard_map/ppermute | solution.py:22
  92.3 1.6 %collective-permute-done.42 = f32[8,1664]{1,0:T(8,128)S(1)} collective-permute-done((f32[8,1664]{1,0:T(8,128)S(1)}, f32[8,1664]{1,0:T(8,128)S(1)}, u32[]{:S(2)}, u32[]{:S(2)}) %collective-permute-start.42) | collective-permute-done | bytes 53280 | tf_op jit(solution)/shard_map/ppermute | solution.py:22
  95.3 1.2 %collective-permute-done.43.other_ref = f32[8,1664]{1,0:T(8,128)S(1)} collective-permute-done((f32[8,1664]{1,0:T(8,128)S(1)}, f32[8,1664]{1,0:T(8,128)S(1)}, u32[]{:S(2)}, u32[]{:S(2)}) %collective-permute-start.43) | collective-permute-done | bytes 53280 | tf_op jit(solution)/shard_map/ppermute | solution.py:22
  96.5 1.2 %coarse.5.refs_0_ = f32[8,896]{1,0:T(8,128)S(1)} custom-call(s32[3]{0:T(128)S(1)} %pad_add_fusion.info_ref, f32[8,1664]{1,0:T(8,128)S(1)} %add_add_fusion.mine_ref, f32[8,1664]{1,0:T(8,128)S(1)} %collective-permute-done.43.other_ref, bf16[1536,768]{1,0:T(8,128)(2,1)S(1)} %get-tuple-element.81.table_ref), custom_call_target="tpu_custom_call" | custom-call | flops 1024 | bytes 1024 | tf_op jit(solution)/shard_map/coarse/pallas_call | solution.py:615
  97.7 2.5 %collective-permute-start.46 = (f32[8,896]{1,0:T(8,128)S(1)}, f32[8,896]{1,0:T(8,128)S(1)}, u32[]{:S(2)}, u32[]{:S(2)}) collective-permute-start(f32[8,896]{1,0:T(8,128)S(1)} %coarse.5.refs_0_), channel_id=1, source_target_pairs={{0,6},{1,7},{2,4},{3,5},{4,2},{5,3},{6,0},{7,1},{8,14},{9,15},{10,... | collective-permute-start | bytes 86024 | tf_op jit(solution)/shard_map/ppermute | solution.py:22
  100.2 2.0 %collective-permute-start.44 = (f32[8,896]{1,0:T(8,128)S(1)}, f32[8,896]{1,0:T(8,128)S(1)}, u32[]{:S(2)}, u32[]{:S(2)}) collective-permute-start(f32[8,896]{1,0:T(8,128)S(1)} %coarse.5.refs_0_), channel_id=1, source_target_pairs={{0,2},{1,3},{2,0},{3,1},{4,6},{5,7},{6,4},{7,5},{8,10},{9,11},{10,... | collective-permute-start | bytes 86024 | tf_op jit(solution)/shard_map/ppermute | solution.py:22
  102.2 1.3 %collective-permute-done.46.refs_3_ = f32[8,896]{1,0:T(8,128)S(1)} collective-permute-done((f32[8,896]{1,0:T(8,128)S(1)}, f32[8,896]{1,0:T(8,128)S(1)}, u32[]{:S(2)}, u32[]{:S(2)}) %collective-permute-start.46) | collective-permute-done | bytes 28704 | tf_op jit(solution)/shard_map/ppermute | solution.py:22
  103.4 1.5 %collective-permute-done.45.refs_2_ = f32[8,896]{1,0:T(8,128)S(1)} collective-permute-done((f32[8,896]{1,0:T(8,128)S(1)}, f32[8,896]{1,0:T(8,128)S(1)}, u32[]{:S(2)}, u32[]{:S(2)}) %collective-permute-start.45) | collective-permute-done | bytes 28704 | tf_op jit(solution)/shard_map/ppermute | solution.py:22
  105.0 2.3 %step.5 = (f32[1,1,5,16,4,128]{5,4,3,2,1,0:T(4,128)}, f32[1,1,5,16,4,128]{5,4,3,2,1,0:T(4,128)}) custom-call(s32[3]{0:T(128)S(1)} %pad_add_fusion.info_ref, s32[1,1,4,5]{3,2,1,0:T(4,128)S(1)} %copy-done.1, f32[5,16,512]{2,1,0:T(8,128)S(1)} %get-tuple-element.98.own_ref, f32[5,16,512]{2,1,0:T(8,128)S(1)} %collective-permute-done.35.facing_ref, ...), custom_call_target="tpu_custom_call" | custom-call | flops 1024 | bytes 1024 | tf_op jit(solution)/shard_map/step/pallas_call | solution.py:626
  (77 shorter events, 15.5 us)
Async XLA Ops:
  2.2 12.1 %collective-permute-start.2 = (f32[48,1536]{1,0:T(8,128)}, f32[48,1536]{1,0:T(8,128)S(1)}, u32[]{:S(2)}, u32[]{:S(2)}) collective-permute-start(f32[48,1536]{1,0:T(8,128)} %refs_0_), channel_id=1, source_target_pairs={{0,16},{1,17},{2,18},{3,19},{4,20},{5,21},{6,22},{7,23},{8,24},{9,... | collective-permute-start | bytes 884744 | tf_op jit(solution)/shard_map/ppermute | solution.py:22
  5.3 9.1 %collective-permute-start.1 = (f32[48,1536]{1,0:T(8,128)}, f32[48,1536]{1,0:T(8,128)S(1)}, u32[]{:S(2)}, u32[]{:S(2)}) collective-permute-start(f32[48,1536]{1,0:T(8,128)} %refs_0_), channel_id=1, source_target_pairs={{0,8},{1,9},{2,10},{3,11},{4,12},{5,13},{6,14},{7,15},{8,0},{9,1},... | collective-permute-start | bytes 884744 | tf_op jit(solution)/shard_map/ppermute | solution.py:22
  6.8 7.6 %collective-permute-start = (f32[128,512]{1,0:T(8,128)S(1)}, f32[128,512]{1,0:T(8,128)S(1)}, u32[]{:S(2)}, u32[]{:S(2)}) collective-permute-start(f32[128,512]{1,0:T(8,128)S(1)} %pack.1), channel_id=1, source_target_pairs={{0,1},{1,2},{2,3},{3,4},{4,5},{5,6},{6,7},{7,0},{8,9},{9,10},{10,1... | collective-permute-start | bytes 786440 | tf_op jit(solution)/shard_map/ppermute | solution.py:17
  6.9 16.5 %copy-start = (f32[48,1536]{1,0:T(8,128)S(1)}, f32[48,1536]{1,0:T(8,128)}, u32[]{:S(2)}) copy-start(f32[48,1536]{1,0:T(8,128)} %refs_0_) | copy-start | bytes 884740
  15.8 8.7 %collective-permute-start.3 = (f32[5,16,512]{2,1,0:T(8,128)S(1)}, f32[5,16,512]{2,1,0:T(8,128)S(1)}, u32[]{:S(2)}, u32[]{:S(2)}) collective-permute-start(f32[5,16,512]{2,1,0:T(8,128)S(1)} %get-tuple-element.63), channel_id=1, source_target_pairs={{0,7},{1,0},{2,1},{3,2},{4,3},{5,4},{6,5},{7,6},{8,15},{9,8},{10,9... | collective-permute-start | bytes 491528 | tf_op jit(solution)/shard_map/ppermute | solution.py:17
  17.7 1.2 %collective-permute-start.10 = (f32[8,1664]{1,0:T(8,128)S(1)}, f32[8,1664]{1,0:T(8,128)S(1)}, u32[]{:S(2)}, u32[]{:S(2)}) collective-permute-start(f32[8,1664]{1,0:T(8,128)S(1)} %get-tuple-element.79), channel_id=1, source_target_pairs={{0,1},{1,0},{2,3},{3,2},{4,5},{5,4},{6,7},{7,6},{8,9},{9,8},{10,11... | collective-permute-start | bytes 159752 | tf_op jit(solution)/shard_map/ppermute | solution.py:22
  18.9 11.3 %collective-permute-start.13 = (f32[8,1664]{1,0:T(8,128)S(1)}, f32[8,1664]{1,0:T(8,128)S(1)}, u32[]{:S(2)}, u32[]{:S(2)}) collective-permute-start(f32[8,1664]{1,0:T(8,128)S(1)} %add.78), channel_id=1, source_target_pairs={{0,6},{1,7},{2,4},{3,5},{4,2},{5,3},{6,0},{7,1},{8,14},{9,15},{10,... | collective-permute-start | bytes 159752 | tf_op jit(solution)/shard_map/ppermute | solution.py:22
  20.8 9.4 %collective-permute-start.12 = (f32[8,1664]{1,0:T(8,128)S(1)}, f32[8,1664]{1,0:T(8,128)S(1)}, u32[]{:S(2)}, u32[]{:S(2)}) collective-permute-start(f32[8,1664]{1,0:T(8,128)S(1)} %add.78), channel_id=1, source_target_pairs={{0,4},{1,5},{2,6},{3,7},{4,0},{5,1},{6,2},{7,3},{8,12},{9,13},{10,... | collective-permute-start | bytes 159752 | tf_op jit(solution)/shard_map/ppermute | solution.py:22
  20.8 9.4 %collective-permute-start.11 = (f32[8,1664]{1,0:T(8,128)S(1)}, f32[8,1664]{1,0:T(8,128)S(1)}, u32[]{:S(2)}, u32[]{:S(2)}) collective-permute-start(f32[8,1664]{1,0:T(8,128)S(1)} %add.78), channel_id=1, source_target_pairs={{0,2},{1,3},{2,0},{3,1},{4,6},{5,7},{6,4},{7,5},{8,10},{9,11},{10,... | collective-permute-start | bytes 159752 | tf_op jit(solution)/shard_map/ppermute | solution.py:22
  23.4 10.5 %collective-permute-start.5 = (f32[48,1536]{1,0:T(8,128)S(1)}, f32[48,1536]{1,0:T(8,128)S(1)}, u32[]{:S(2)}, u32[]{:S(2)}) collective-permute-start(f32[48,1536]{1,0:T(8,128)S(1)} %copy-done), channel_id=1, source_target_pairs={{0,24},{1,25},{2,26},{3,27},{4,28},{5,29},{6,30},{7,31},{8,16},{9,... | collective-permute-start | bytes 884744 | tf_op jit(solution)/shard_map/ppermute | solution.py:22
  30.2 5.5 %collective-permute-start.16 = (f32[8,1664]{1,0:T(8,128)S(1)}, f32[8,1664]{1,0:T(8,128)S(1)}, u32[]{:S(2)}, u32[]{:S(2)}) collective-permute-start(f32[8,1664]{1,0:T(8,128)S(1)} %add_add_fusion.5), channel_id=1, source_target_pairs={{0,24},{1,25},{2,26},{3,27},{4,28},{5,29},{6,30},{7,31},{8,16},{9,... | collective-permute-start | bytes 159752 | tf_op jit(solution)/shard_map/ppermute | solution.py:22
  32.1 4.2 %collective-permute-start.15 = (f32[8,1664]{1,0:T(8,128)S(1)}, f32[8,1664]{1,0:T(8,128)S(1)}, u32[]{:S(2)}, u32[]{:S(2)}) collective-permute-start(f32[8,1664]{1,0:T(8,128)S(1)} %add_add_fusion.5), channel_id=1, source_target_pairs={{0,16},{1,17},{2,18},{3,19},{4,20},{5,21},{6,22},{7,23},{8,24},{9,... | collective-permute-start | bytes 159752 | tf_op jit(solution)/shard_map/ppermute | solution.py:22
  32.6 4.1 %collective-permute-start.14 = (f32[8,1664]{1,0:T(8,128)S(1)}, f32[8,1664]{1,0:T(8,128)S(1)}, u32[]{:S(2)}, u32[]{:S(2)}) collective-permute-start(f32[8,1664]{1,0:T(8,128)S(1)} %add_add_fusion.5), channel_id=1, source_target_pairs={{0,8},{1,9},{2,10},{3,11},{4,12},{5,13},{6,14},{7,15},{8,0},{9,1},... | collective-permute-start | bytes 159752 | tf_op jit(solution)/shard_map/ppermute | solution.py:22
  33.8 3.0 %collective-permute-start.6 = (f32[48,1536]{1,0:T(8,128)S(1)}, f32[48,1536]{1,0:T(8,128)S(1)}, u32[]{:S(2)}, u32[]{:S(2)}) collective-permute-start(f32[48,1536]{1,0:T(8,128)S(1)} %copy-done), channel_id=1, source_target_pairs={{0,1},{1,0},{2,3},{3,2},{4,5},{5,4},{6,7},{7,6},{8,9},{9,8},{10,11... | collective-permute-start | bytes 884744 | tf_op jit(solution)/shard_map/ppermute | solution.py:22
  33.8 4.1 %collective-permute-start.7 = (f32[48,1536]{1,0:T(8,128)S(1)}, f32[48,1536]{1,0:T(8,128)S(1)}, u32[]{:S(2)}, u32[]{:S(2)}) collective-permute-start(f32[48,1536]{1,0:T(8,128)S(1)} %collective-permute-done.1.refs_1_), channel_id=1, source_target_pairs={{0,1},{1,0},{2,3},{3,2},{4,5},{5,4},{6,7},{7,6},{8,9},{9,8},{10,11... | collective-permute-start | bytes 884744 | tf_op jit(solution)/shard_map/ppermute | solution.py:22
  35.7 2.2 %collective-permute-start.8 = (f32[48,1536]{1,0:T(8,128)S(1)}, f32[48,1536]{1,0:T(8,128)S(1)}, u32[]{:S(2)}, u32[]{:S(2)}) collective-permute-start(f32[48,1536]{1,0:T(8,128)S(1)} %collective-permute-done.2.refs_2_), channel_id=1, source_target_pairs={{0,1},{1,0},{2,3},{3,2},{4,5},{5,4},{6,7},{7,6},{8,9},{9,8},{10,11... | collective-permute-start | bytes 884744 | tf_op jit(solution)/shard_map/ppermute | solution.py:22
  36.3 1.6 %collective-permute-start.9 = (f32[48,1536]{1,0:T(8,128)S(1)}, f32[48,1536]{1,0:T(8,128)S(1)}, u32[]{:S(2)}, u32[]{:S(2)}) collective-permute-start(f32[48,1536]{1,0:T(8,128)S(1)} %collective-permute-done.5.refs_3_), channel_id=1, source_target_pairs={{0,1},{1,0},{2,3},{3,2},{4,5},{5,4},{6,7},{7,6},{8,9},{9,8},{10,11... | collective-permute-start | bytes 884744 | tf_op jit(solution)/shard_map/ppermute | solution.py:22
  36.7 11.7 %collective-permute-start.4 = (f32[5,16,512]{2,1,0:T(8,128)S(1)}, f32[5,16,512]{2,1,0:T(8,128)S(1)}, u32[]{:S(2)}, u32[]{:S(2)}) collective-permute-start(f32[5,16,512]{2,1,0:T(8,128)S(1)} %get-tuple-element.67), channel_id=1, source_target_pairs={{0,1},{1,2},{2,3},{3,4},{4,5},{5,6},{6,7},{7,0},{8,9},{9,10},{10,1... | collective-permute-start | bytes 491528 | tf_op jit(solution)/shard_map/ppermute | solution.py:17
  36.8 2.7 %collective-permute-start.17 = (f32[8,1664]{1,0:T(8,128)S(1)}, f32[8,1664]{1,0:T(8,128)S(1)}, u32[]{:S(2)}, u32[]{:S(2)}) collective-permute-start(f32[8,1664]{1,0:T(8,128)S(1)} %add_add_fusion.4.mine_ref), channel_id=1, source_target_pairs={{0,1},{1,0},{2,3},{3,2},{4,5},{5,4},{6,7},{7,6},{8,9},{9,8},{10,11... | collective-permute-start | bytes 159752 | tf_op jit(solution)/shard_map/ppermute | solution.py:22
  40.8 5.8 %collective-permute-start.20 = (f32[8,896]{1,0:T(8,128)S(1)}, f32[8,896]{1,0:T(8,128)S(1)}, u32[]{:S(2)}, u32[]{:S(2)}) collective-permute-start(f32[8,896]{1,0:T(8,128)S(1)} %coarse.3.refs_0_), channel_id=1, source_target_pairs={{0,6},{1,7},{2,4},{3,5},{4,2},{5,3},{6,0},{7,1},{8,14},{9,15},{10,... | collective-permute-start | bytes 86024 | tf_op jit(solution)/shard_map/ppermute | solution.py:22
  43.7 4.8 %collective-permute-start.19 = (f32[8,896]{1,0:T(8,128)S(1)}, f32[8,896]{1,0:T(8,128)S(1)}, u32[]{:S(2)}, u32[]{:S(2)}) collective-permute-start(f32[8,896]{1,0:T(8,128)S(1)} %coarse.3.refs_0_), channel_id=1, source_target_pairs={{0,4},{1,5},{2,6},{3,7},{4,0},{5,1},{6,2},{7,3},{8,12},{9,13},{10,... | collective-permute-start | bytes 86024 | tf_op jit(solution)/shard_map/ppermute | solution.py:22
  43.7 4.8 %collective-permute-start.18 = (f32[8,896]{1,0:T(8,128)S(1)}, f32[8,896]{1,0:T(8,128)S(1)}, u32[]{:S(2)}, u32[]{:S(2)}) collective-permute-start(f32[8,896]{1,0:T(8,128)S(1)} %coarse.3.refs_0_), channel_id=1, source_target_pairs={{0,2},{1,3},{2,0},{3,1},{4,6},{5,7},{6,4},{7,5},{8,10},{9,11},{10,... | collective-permute-start | bytes 86024 | tf_op jit(solution)/shard_map/ppermute | solution.py:22
  50.4 7.8 %collective-permute-start.21 = (f32[5,16,512]{2,1,0:T(8,128)S(1)}, f32[5,16,512]{2,1,0:T(8,128)S(1)}, u32[]{:S(2)}, u32[]{:S(2)}) collective-permute-start(f32[5,16,512]{2,1,0:T(8,128)S(1)} %get-tuple-element.83), channel_id=1, source_target_pairs={{0,7},{1,0},{2,1},{3,2},{4,3},{5,4},{6,5},{7,6},{8,15},{9,8},{10,9... | collective-permute-start | bytes 491528 | tf_op jit(solution)/shard_map/ppermute | solution.py:17
  50.7 1.4 %collective-permute-start.23 = (f32[8,1664]{1,0:T(8,128)S(1)}, f32[8,1664]{1,0:T(8,128)S(1)}, u32[]{:S(2)}, u32[]{:S(2)}) collective-permute-start(f32[8,1664]{1,0:T(8,128)S(1)} %get-tuple-element.90), channel_id=1, source_target_pairs={{0,1},{1,0},{2,3},{3,2},{4,5},{5,4},{6,7},{7,6},{8,9},{9,8},{10,11... | collective-permute-start | bytes 159752 | tf_op jit(solution)/shard_map/ppermute | solution.py:22
  52.1 7.8 %collective-permute-start.26 = (f32[8,1664]{1,0:T(8,128)S(1)}, f32[8,1664]{1,0:T(8,128)S(1)}, u32[]{:S(2)}, u32[]{:S(2)}) collective-permute-start(f32[8,1664]{1,0:T(8,128)S(1)} %add.86), channel_id=1, source_target_pairs={{0,6},{1,7},{2,4},{3,5},{4,2},{5,3},{6,0},{7,1},{8,14},{9,15},{10,... | collective-permute-start | bytes 159752 | tf_op jit(solution)/shard_map/ppermute | solution.py:22
  53.7 6.8 %collective-permute-start.25 = (f32[8,1664]{1,0:T(8,128)S(1)}, f32[8,1664]{1,0:T(8,128)S(1)}, u32[]{:S(2)}, u32[]{:S(2)}) collective-permute-start(f32[8,1664]{1,0:T(8,128)S(1)} %add.86), channel_id=1, source_target_pairs={{0,4},{1,5},{2,6},{3,7},{4,0},{5,1},{6,2},{7,3},{8,12},{9,13},{10,... | collective-permute-start | bytes 159752 | tf_op jit(solution)/shard_map/ppermute | solution.py:22
  54.3 6.2 %collective-permute-start.24 = (f32[8,1664]{1,0:T(8,128)S(1)}, f32[8,1664]{1,0:T(8,128)S(1)}, u32[]{:S(2)}, u32[]{:S(2)}) collective-permute-start(f32[8,1664]{1,0:T(8,128)S(1)} %add.86), channel_id=1, source_target_pairs={{0,2},{1,3},{2,0},{3,1},{4,6},{5,7},{6,4},{7,5},{8,10},{9,11},{10,... | collective-permute-start | bytes 159752 | tf_op jit(solution)/shard_map/ppermute | solution.py:22
  60.5 5.2 %collective-permute-start.29 = (f32[8,1664]{1,0:T(8,128)S(1)}, f32[8,1664]{1,0:T(8,128)S(1)}, u32[]{:S(2)}, u32[]{:S(2)}) collective-permute-start(f32[8,1664]{1,0:T(8,128)S(1)} %add_add_fusion.3), channel_id=1, source_target_pairs={{0,24},{1,25},{2,26},{3,27},{4,28},{5,29},{6,30},{7,31},{8,16},{9,... | collective-permute-start | bytes 159752 | tf_op jit(solution)/shard_map/ppermute | solution.py:22
  62.6 4.1 %collective-permute-start.28 = (f32[8,1664]{1,0:T(8,128)S(1)}, f32[8,1664]{1,0:T(8,128)S(1)}, u32[]{:S(2)}, u32[]{:S(2)}) collective-permute-start(f32[8,1664]{1,0:T(8,128)S(1)} %add_add_fusion.3), channel_id=1, source_target_pairs={{0,16},{1,17},{2,18},{3,19},{4,20},{5,21},{6,22},{7,23},{8,24},{9,... | collective-permute-start | bytes 159752 | tf_op jit(solution)/shard_map/ppermute | solution.py:22
  63.2 4.1 %collective-permute-start.27 = (f32[8,1664]{1,0:T(8,128)S(1)}, f32[8,1664]{1,0:T(8,128)S(1)}, u32[]{:S(2)}, u32[]{:S(2)}) collective-permute-start(f32[8,1664]{1,0:T(8,128)S(1)} %add_add_fusion.3), channel_id=1, source_target_pairs={{0,8},{1,9},{2,10},{3,11},{4,12},{5,13},{6,14},{7,15},{8,0},{9,1},... | collective-permute-start | bytes 159752 | tf_op jit(solution)/shard_map/ppermute | solution.py:22
  64.1 12.7 %collective-permute-start.22 = (f32[5,16,512]{2,1,0:T(8,128)S(1)}, f32[5,16,512]{2,1,0:T(8,128)S(1)}, u32[]{:S(2)}, u32[]{:S(2)}) collective-permute-start(f32[5,16,512]{2,1,0:T(8,128)S(1)} %get-tuple-element.87), channel_id=1, source_target_pairs={{0,1},{1,2},{2,3},{3,4},{4,5},{5,6},{6,7},{7,0},{8,9},{9,10},{10,1... | collective-permute-start | bytes 491528 | tf_op jit(solution)/shard_map/ppermute | solution.py:17
  67.4 1.3 %collective-permute-start.30 = (f32[8,1664]{1,0:T(8,128)S(1)}, f32[8,1664]{1,0:T(8,128)S(1)}, u32[]{:S(2)}, u32[]{:S(2)}) collective-permute-start(f32[8,1664]{1,0:T(8,128)S(1)} %add_add_fusion.2.mine_ref), channel_id=1, source_target_pairs={{0,1},{1,0},{2,3},{3,2},{4,5},{5,4},{6,7},{7,6},{8,9},{9,8},{10,11... | collective-permute-start | bytes 159752 | tf_op jit(solution)/shard_map/ppermute | solution.py:22
  69.9 5.7 %collective-permute-start.33 = (f32[8,896]{1,0:T(8,128)S(1)}, f32[8,896]{1,0:T(8,128)S(1)}, u32[]{:S(2)}, u32[]{:S(2)}) collective-permute-start(f32[8,896]{1,0:T(8,128)S(1)} %coarse.4.refs_0_), channel_id=1, source_target_pairs={{0,6},{1,7},{2,4},{3,5},{4,2},{5,3},{6,0},{7,1},{8,14},{9,15},{10,... | collective-permute-start | bytes 86024 | tf_op jit(solution)/shard_map/ppermute | solution.py:22
  72.0 4.8 %collective-permute-start.32 = (f32[8,896]{1,0:T(8,128)S(1)}, f32[8,896]{1,0:T(8,128)S(1)}, u32[]{:S(2)}, u32[]{:S(2)}) collective-permute-start(f32[8,896]{1,0:T(8,128)S(1)} %coarse.4.refs_0_), channel_id=1, source_target_pairs={{0,4},{1,5},{2,6},{3,7},{4,0},{5,1},{6,2},{7,3},{8,12},{9,13},{10,... | collective-permute-start | bytes 86024 | tf_op jit(solution)/shard_map/ppermute | solution.py:22
  72.0 4.8 %collective-permute-start.31 = (f32[8,896]{1,0:T(8,128)S(1)}, f32[8,896]{1,0:T(8,128)S(1)}, u32[]{:S(2)}, u32[]{:S(2)}) collective-permute-start(f32[8,896]{1,0:T(8,128)S(1)} %coarse.4.refs_0_), channel_id=1, source_target_pairs={{0,2},{1,3},{2,0},{3,1},{4,6},{5,7},{6,4},{7,5},{8,10},{9,11},{10,... | collective-permute-start | bytes 86024 | tf_op jit(solution)/shard_map/ppermute | solution.py:22
  78.6 8.1 %collective-permute-start.34 = (f32[5,16,512]{2,1,0:T(8,128)S(1)}, f32[5,16,512]{2,1,0:T(8,128)S(1)}, u32[]{:S(2)}, u32[]{:S(2)}) collective-permute-start(f32[5,16,512]{2,1,0:T(8,128)S(1)} %get-tuple-element.97), channel_id=1, source_target_pairs={{0,7},{1,0},{2,1},{3,2},{4,3},{5,4},{6,5},{7,6},{8,15},{9,8},{10,9... | collective-permute-start | bytes 491528 | tf_op jit(solution)/shard_map/ppermute | solution.py:17
  79.4 1.2 %collective-permute-start.36 = (f32[8,1664]{1,0:T(8,128)S(1)}, f32[8,1664]{1,0:T(8,128)S(1)}, u32[]{:S(2)}, u32[]{:S(2)}) collective-permute-start(f32[8,1664]{1,0:T(8,128)S(1)} %get-tuple-element.102), channel_id=1, source_target_pairs={{0,1},{1,0},{2,3},{3,2},{4,5},{5,4},{6,7},{7,6},{8,9},{9,8},{10,11... | collective-permute-start | bytes 159752 | tf_op jit(solution)/shard_map/ppermute | solution.py:22
  80.7 7.8 %collective-permute-start.39 = (f32[8,1664]{1,0:T(8,128)S(1)}, f32[8,1664]{1,0:T(8,128)S(1)}, u32[]{:S(2)}, u32[]{:S(2)}) collective-permute-start(f32[8,1664]{1,0:T(8,128)S(1)} %add.94), channel_id=1, source_target_pairs={{0,6},{1,7},{2,4},{3,5},{4,2},{5,3},{6,0},{7,1},{8,14},{9,15},{10,... | collective-permute-start | bytes 159752 | tf_op jit(solution)/shard_map/ppermute | solution.py:22
  82.0 6.6 %collective-permute-start.38 = (f32[8,1664]{1,0:T(8,128)S(1)}, f32[8,1664]{1,0:T(8,128)S(1)}, u32[]{:S(2)}, u32[]{:S(2)}) collective-permute-start(f32[8,1664]{1,0:T(8,128)S(1)} %add.94), channel_id=1, source_target_pairs={{0,4},{1,5},{2,6},{3,7},{4,0},{5,1},{6,2},{7,3},{8,12},{9,13},{10,... | collective-permute-start | bytes 159752 | tf_op jit(solution)/shard_map/ppermute | solution.py:22
  83.2 5.5 %collective-permute-start.37 = (f32[8,1664]{1,0:T(8,128)S(1)}, f32[8,1664]{1,0:T(8,128)S(1)}, u32[]{:S(2)}, u32[]{:S(2)}) collective-permute-start(f32[8,1664]{1,0:T(8,128)S(1)} %add.94), channel_id=1, source_target_pairs={{0,2},{1,3},{2,0},{3,1},{4,6},{5,7},{6,4},{7,5},{8,10},{9,11},{10,... | collective-permute-start | bytes 159752 | tf_op jit(solution)/shard_map/ppermute | solution.py:22
  88.7 5.2 %collective-permute-start.42 = (f32[8,1664]{1,0:T(8,128)S(1)}, f32[8,1664]{1,0:T(8,128)S(1)}, u32[]{:S(2)}, u32[]{:S(2)}) collective-permute-start(f32[8,1664]{1,0:T(8,128)S(1)} %add_add_fusion.1), channel_id=1, source_target_pairs={{0,24},{1,25},{2,26},{3,27},{4,28},{5,29},{6,30},{7,31},{8,16},{9,... | collective-permute-start | bytes 159752 | tf_op jit(solution)/shard_map/ppermute | solution.py:22
  90.6 4.1 %collective-permute-start.41 = (f32[8,1664]{1,0:T(8,128)S(1)}, f32[8,1664]{1,0:T(8,128)S(1)}, u32[]{:S(2)}, u32[]{:S(2)}) collective-permute-start(f32[8,1664]{1,0:T(8,128)S(1)} %add_add_fusion.1), channel_id=1, source_target_pairs={{0,16},{1,17},{2,18},{3,19},{4,20},{5,21},{6,22},{7,23},{8,24},{9,... | collective-permute-start | bytes 159752 | tf_op jit(solution)/shard_map/ppermute | solution.py:22
  91.1 4.1 %collective-permute-start.40 = (f32[8,1664]{1,0:T(8,128)S(1)}, f32[8,1664]{1,0:T(8,128)S(1)}, u32[]{:S(2)}, u32[]{:S(2)}) collective-permute-start(f32[8,1664]{1,0:T(8,128)S(1)} %add_add_fusion.1), channel_id=1, source_target_pairs={{0,8},{1,9},{2,10},{3,11},{4,12},{5,13},{6,14},{7,15},{8,0},{9,1},... | collective-permute-start | bytes 159752 | tf_op jit(solution)/shard_map/ppermute | solution.py:22
  92.3 12.7 %collective-permute-start.35 = (f32[5,16,512]{2,1,0:T(8,128)S(1)}, f32[5,16,512]{2,1,0:T(8,128)S(1)}, u32[]{:S(2)}, u32[]{:S(2)}) collective-permute-start(f32[5,16,512]{2,1,0:T(8,128)S(1)} %get-tuple-element.99), channel_id=1, source_target_pairs={{0,1},{1,2},{2,3},{3,4},{4,5},{5,6},{6,7},{7,0},{8,9},{9,10},{10,1... | collective-permute-start | bytes 491528 | tf_op jit(solution)/shard_map/ppermute | solution.py:17
  95.2 1.3 %collective-permute-start.43 = (f32[8,1664]{1,0:T(8,128)S(1)}, f32[8,1664]{1,0:T(8,128)S(1)}, u32[]{:S(2)}, u32[]{:S(2)}) collective-permute-start(f32[8,1664]{1,0:T(8,128)S(1)} %add_add_fusion.mine_ref), channel_id=1, source_target_pairs={{0,1},{1,0},{2,3},{3,2},{4,5},{5,4},{6,7},{7,6},{8,9},{9,8},{10,11... | collective-permute-start | bytes 159752 | tf_op jit(solution)/shard_map/ppermute | solution.py:22
  97.7 5.7 %collective-permute-start.46 = (f32[8,896]{1,0:T(8,128)S(1)}, f32[8,896]{1,0:T(8,128)S(1)}, u32[]{:S(2)}, u32[]{:S(2)}) collective-permute-start(f32[8,896]{1,0:T(8,128)S(1)} %coarse.5.refs_0_), channel_id=1, source_target_pairs={{0,6},{1,7},{2,4},{3,5},{4,2},{5,3},{6,0},{7,1},{8,14},{9,15},{10,... | collective-permute-start | bytes 86024 | tf_op jit(solution)/shard_map/ppermute | solution.py:22
  100.2 4.8 %collective-permute-start.45 = (f32[8,896]{1,0:T(8,128)S(1)}, f32[8,896]{1,0:T(8,128)S(1)}, u32[]{:S(2)}, u32[]{:S(2)}) collective-permute-start(f32[8,896]{1,0:T(8,128)S(1)} %coarse.5.refs_0_), channel_id=1, source_target_pairs={{0,4},{1,5},{2,6},{3,7},{4,0},{5,1},{6,2},{7,3},{8,12},{9,13},{10,... | collective-permute-start | bytes 86024 | tf_op jit(solution)/shard_map/ppermute | solution.py:22
  100.2 4.8 %collective-permute-start.44 = (f32[8,896]{1,0:T(8,128)S(1)}, f32[8,896]{1,0:T(8,128)S(1)}, u32[]{:S(2)}, u32[]{:S(2)}) collective-permute-start(f32[8,896]{1,0:T(8,128)S(1)} %coarse.5.refs_0_), channel_id=1, source_target_pairs={{0,2},{1,3},{2,0},{3,1},{4,6},{5,7},{6,4},{7,5},{8,10},{9,11},{10,... | collective-permute-start | bytes 86024 | tf_op jit(solution)/shard_map/ppermute | solution.py:22
  (2 other events, 15.1 us)

commit v5 on v4

--- a/solution.py
+++ b/solution.py
@@ -226,8 +226,15 @@
     return jnp.sum(jnp.sum(r * z, axis=0), axis=1, keepdims=True)
 
 
+def by_level(numbers, rows, levels):
+    row = numbers // (2 * rows * levels)
+    rest = numbers - row * (2 * rows * levels)
+    level = rest // (2 * rows)
+    return level, row * (2 * rows) + rest - level * (2 * rows)
+
+
 def first_kernel(
-    corners, info_ref, partner_ref, counts_ref, right_ref, weight_ref, inverse_ref, link_t_ref, map_ref, prev_ref,
+    corners, rows, levels, info_ref, partner_ref, counts_ref, right_ref, weight_ref, inverse_ref, link_t_ref, map_ref, prev_ref,
     mask_ref, r_ref, z_ref, send_ref, mine_ref, other_ref, prev_t_ref, scatter_ref,
 ):
     slots, loads, span = r_ref.shape
@@ -249,7 +256,9 @@
     own = jnp.concatenate([map_ref[j] for j in range(slots)], axis=0).astype(jnp.float32)
     own = jnp.concatenate([own, jnp.zeros((slots, LANES - corners), jnp.float32)], axis=1)
     both = jnp.concatenate([own, prev_ref[used : used + slots, :LANES]], axis=0)
-    both = jnp.concatenate([both, jnp.zeros((16 - 2 * slots, LANES), jnp.float32)], axis=0).T
+    both = jnp.concatenate([both, jnp.zeros((16 - 2 * slots, LANES), jnp.float32)], axis=0)
+    level, within = by_level(both.astype(jnp.int32), rows, levels)
+    both = (level * (size // levels) + within).astype(jnp.float32).T
     own = [both[:corners, j : j + 1] for j in range(slots)]
     prev = [both[:corners, slots + j : slots + j + 1] for j in range(slots)]
     for side, columns in enumerate((own, prev)):
@@ -278,18 +287,21 @@
             line.append(jnp.full((1, LANES - slots * corners), -1, jnp.int32))
         lines += line
     maps = jnp.concatenate(lines, axis=1)
-    row = maps // (2 * rows * levels)
-    rest = maps - row * (2 * rows * levels)
-    level = rest // (2 * rows)
-    within = rest - level * (2 * rows)
-    place = jnp.bitwise_xor(level, info_ref[2]) * per_level + row * (2 * rows) + within
+    level, within = by_level(maps, rows, levels)
+    place = jnp.bitwise_xor(level, info_ref[2]) * per_level + within
     place = jnp.where(maps >= 0, place, -1)
     pick_ref[...] = (place == lax.broadcasted_iota(jnp.int32, pick_ref.shape, 0)).astype(jnp.bfloat16)
     for core in range(2):
         for away in range(side_rows):
             at = jnp.bitwise_xor(info_ref[1], away) * (2 * rows) + jnp.bitwise_xor(info_ref[0], core) * rows
             joined_ref[pl.ds(pl.multiple_of(at, 8), rows), :] = parts[core * side_rows + away][...]
-    coarse_ref[...] = jnp.concatenate(pieces(joined_ref[...].T, 2), axis=1)
+    turned = jnp.concatenate(pieces(joined_ref[...].T, 2), axis=1)
+    stretch = 2 * rows
+    for at in range(side_rows):
+        for level in range(levels):
+            source = (at * levels + level) * stretch
+            target = level * per_level + at * stretch
+            coarse_ref[target : target + stretch, :] = turned[source : source + stretch]
 
 
 def step_kernel(
@@ -422,11 +434,9 @@
         return full[i * loads : (i + 1) * loads, j * per_level : (j + 1) * per_level]
 
     answer = ((part(2, 0) + part(1, 1)) + (part(1, 0) + part(0, 1))) + part(0, 0)
-    stretch = 2 * rows
-    own = jnp.zeros((loads, per_level), jnp.float32)
-    for level in range(levels):
-        starts = range(level * stretch, size, levels * stretch)
-        own = jnp.where(info_ref[2] == level, jnp.concatenate([load[:, a : a + stretch] for a in starts], axis=1), own)
+    own = load[:, :per_level]
+    for level in range(1, levels):
+        own = jnp.where(info_ref[2] == level, load[:, level * per_level : (level + 1) * per_level], own)
     spare = mine_ref[:, half:]
     product = jnp.sum(answer * own, axis=1, keepdims=True) + column_of(spare + other_ref[:, half:], 2)
     out_ref[:, : 2 * per_level] = beside(answer)
@@ -507,8 +517,6 @@
     coarse_inverse, to_next = lax.optimization_barrier((coarse_inverse, to_next))
     prev_coupling = shifted(to_next, "col", 1)
     coarse_parts = gathered_along([coarse_inverse], row_bits)
-    prev_coupling, *coarse_parts[1:3] = lax.optimization_barrier((prev_coupling, *coarse_parts[1:3]))
-    coarse_parts = coarse_parts + [swapped(part, 1) for part in coarse_parts]
 
     state = shape_of(slots, loads, span)
     small = shape_of(loads, LANES)
@@ -546,7 +554,7 @@
         name="prepare",
     )(info, flex, coupling, *in_place)
     mask, r, z, send, mine, other, prev_t, scatter = pl.pallas_call(
-        functools.partial(first_kernel, corners),
+        functools.partial(first_kernel, corners, rows, levels),
         out_shape=(
             shape_of(slots, span), state, state, state, half_load, half_load, table(span, 2 * LANES),
             table(2 * LANES, coarse_size),
@@ -574,6 +582,9 @@
     for iteration in range(ITERS):
         first, last = iteration == 0, iteration + 1 == ITERS
         forces = shifted(send, "col", -1)
+        if first:
+            forces, *coarse_parts[1:] = lax.optimization_barrier((forces, *coarse_parts[1:]))
+            coarse_parts += [swapped(part, 1) for part in coarse_parts]
         total = mine + swapped(other, 1)
         if first:
             total = summed_along(total, level_bits)

time: 107 us -> 107 us (level)
    ppermute x7, waiting for transfers between devices: 1.77 us -> 0.02 us  [shifted(): lax.ppermute(x, axis, [(i, (i + by) % devices) for i in range(devices)])]
    ppermute x40, starting transfers between devices: 44.1 us -> 42.6 us  [swapped(): return lax.ppermute(x, BOTH, [(i, i ^ bits) for i in range(devices)])]
    ppermute x7, starting transfers between devices: 3.07 us -> 4.51 us  [shifted(): lax.ppermute(x, axis, [(i, (i + by) % devices) for i in range(devices)])]
  transfers between devices with their start and end apart: 47 -> 47, of which waited for: 24 -> 24; matrix products, arithmetic and copies ran while one was open for 0% -> 0% of each run, Pallas kernels for 22% -> 23%
where the time goes in v5:
time: 107 us; the launch traced here: 106 us
  starting transfers between devices  47.1 us (44%)
  Pallas kernels  31.8 us (30%)
  waiting for transfers between devices  25.8 us (24%)
  between operations  1.47 us (1%)
    ppermute x40, starting transfers between devices, swapped(): return lax.ppermute(x, BOTH, [(i, i ^ bits) for i in range(devices)])  42.6 us
    ppermute x40, waiting for transfers between devices, swapped(): return lax.ppermute(x, BOTH, [(i, i ^ bits) for i in range(devices)])  25.7 us
    pallas_call x3, Pallas kernels, local(): pl.pallas_call(functools.partial(step_kernel, corners, levels, first, las...  6.03 us
    pallas_call x1, Pallas kernels, local(): pl.pallas_call(prepare_kernel, out_shape=half_pieces + (shape_of(slots *...  5.75 us
    pallas_call x1, Pallas kernels, local(): pl.pallas_call(flex_first_kernel, out_shape=(state, state, half_load) + h...  5.69 us
    ppermute x7, starting transfers between devices, shifted(): lax.ppermute(x, axis, [(i, (i + by) % devices) for i in range(devices)])  4.51 us
    pallas_call x3, Pallas kernels, local(): pl.pallas_call(functools.partial(coarse_kernel, rows, levels), out_shape=...  3.63 us
    pallas_call x2, Pallas kernels, local(): pl.pallas_call(flex_far_kernel, out_shape=(state, state, half_load), in_s...  3.45 us
  transfers between devices with their start and end apart: 47, of which 24 were waited for; matrix products, arithmetic and copies ran while one was open for 0% of the time, Pallas kernels for 23%

profile of v5, /device:TPU:0, one launch (start us, length us, event | category | flops | bytes accessed | tf_op | source)
XLA Modules:
  0.0 106.3 jit_solution(12394089681692059057)
XLA Ops:
  2.8 3.5 %collective-permute-start.4 = (f32[48,1536]{1,0:T(8,128)}, f32[48,1536]{1,0:T(8,128)S(1)}, u32[]{:S(2)}, u32[]{:S(2)}) collective-permute-start(f32[48,1536]{1,0:T(8,128)} %refs_0_), channel_id=1, source_target_pairs={{0,24},{1,25},{2,26},{3,27},{4,28},{5,29},{6,30},{7,31},{8,16},{9,... | collective-permute-start | bytes 884744 | tf_op jit(solution)/shard_map/ppermute | solution.py:22
  7.0 5.8 %prepare.1 = (bf16[5,512,1024]{2,1,0:T(8,128)(2,1)S(1)}, bf16[5,512,1024]{2,1,0:T(8,128)(2,1)S(1)}, s32[20,128]{1,0:T(8,128)S(1)}, s32[20,128]{1,0:T(8,128)S(1)}...) custom-call(s32[3]{0:T(128)S(1)} %pad_add_fusion.info_ref, ...), custom_call_target="tpu_custom_call" | custom-call | flops 1024 | bytes 1024 | tf_op jit(solution)/shard_map/prepare/pallas_call | solution.py:534
  12.8 1.4 %first.1 = (f32[5,512]{1,0:T(8,128)S(1)}, f32[5,16,512]{2,1,0:T(8,128)S(1)}, f32[5,16,512]{2,1,0:T(8,128)S(1)}, f32[5,16,512]{2,1,0:T(8,128)S(1)}, f32[8,1664]{1...) custom-call(s32[3]{0:T(128)S(1)} %pad_add_fusion.info_ref, ...), custom_call_target="tpu_custom_call" | custom-call | flops 1024 | bytes 1024 | tf_op jit(solution)/shard_map/first/pallas_call | solution.py:556
  14.2 2.9 %collective-permute-start.1 = (f32[5,16,512]{2,1,0:T(8,128)S(1)}, f32[5,16,512]{2,1,0:T(8,128)S(1)}, u32[]{:S(2)}, u32[]{:S(2)}) collective-permute-start(f32[5,16,512]{2,1,0:T(8,128)S(1)} %get-tuple-element.62), channel_id=1, source_target_pairs={{0,7},{1,0},{2,1},{3,2},{4,3},{5,4},{6,5},{7,6},{8,15},{9,8},{10,9... | collective-permute-start | bytes 491528 | tf_op jit(solution)/shard_map/ppermute | solution.py:17
  17.1 1.2 %collective-permute-done.10 = f32[8,1664]{1,0:T(8,128)S(1)} collective-permute-done((f32[8,1664]{1,0:T(8,128)S(1)}, f32[8,1664]{1,0:T(8,128)S(1)}, u32[]{:S(2)}, u32[]{:S(2)}) %collective-permute-start.10) | collective-permute-done | bytes 53280 | tf_op jit(solution)/shard_map/ppermute | solution.py:22
  18.3 2.1 %collective-permute-start.13 = (f32[8,1664]{1,0:T(8,128)S(1)}, f32[8,1664]{1,0:T(8,128)S(1)}, u32[]{:S(2)}, u32[]{:S(2)}) collective-permute-start(f32[8,1664]{1,0:T(8,128)S(1)} %add.78), channel_id=1, source_target_pairs={{0,6},{1,7},{2,4},{3,5},{4,2},{5,3},{6,0},{7,1},{8,14},{9,15},{10,... | collective-permute-start | bytes 159752 | tf_op jit(solution)/shard_map/ppermute | solution.py:22
  20.6 2.1 %collective-permute-start.11 = (f32[8,1664]{1,0:T(8,128)S(1)}, f32[8,1664]{1,0:T(8,128)S(1)}, u32[]{:S(2)}, u32[]{:S(2)}) collective-permute-start(f32[8,1664]{1,0:T(8,128)S(1)} %add.78), channel_id=1, source_target_pairs={{0,2},{1,3},{2,0},{3,1},{4,6},{5,7},{6,4},{7,5},{8,10},{9,11},{10,... | collective-permute-start | bytes 159752 | tf_op jit(solution)/shard_map/ppermute | solution.py:22
  22.8 5.7 %flex_first.1 = (f32[5,16,512]{2,1,0:T(8,128)S(1)}, f32[5,16,512]{2,1,0:T(8,128)S(1)}, f32[8,1664]{1,0:T(8,128)S(1)}, bf16[5,512,1024]{2,1,0:T(8,128)(2,1)S(1)}, bf16[5,512,1024]{2,1,0:T(8,128)(2,1)S(1)}) custom-call(f32[5,16,512]{2,1,0:T(8,128)S(1)} %get-tuple-element.61.values_ref.z_ref, f32[5,16,512]{2,1,0:T(8,128)S(1)} %collective-permute-done.1.forces_ref, ...), custom_call_target="tpu_custom_call" | custom-call | flops 1024 | bytes 1024 | tf_op jit(solution)/shard_map/flex_first/pallas_call | solution.py:591
  28.5 2.7 %collective-permute-start.16 = (f32[8,1664]{1,0:T(8,128)S(1)}, f32[8,1664]{1,0:T(8,128)S(1)}, u32[]{:S(2)}, u32[]{:S(2)}) collective-permute-start(f32[8,1664]{1,0:T(8,128)S(1)} %add_add_fusion.5), channel_id=1, source_target_pairs={{0,24},{1,25},{2,26},{3,27},{4,28},{5,29},{6,30},{7,31},{8,16},{9,... | collective-permute-start | bytes 159752 | tf_op jit(solution)/shard_map/ppermute | solution.py:22
  32.6 1.1 %collective-permute-done.16 = f32[8,1664]{1,0:T(8,128)S(1)} collective-permute-done((f32[8,1664]{1,0:T(8,128)S(1)}, f32[8,1664]{1,0:T(8,128)S(1)}, u32[]{:S(2)}, u32[]{:S(2)}) %collective-permute-start.16) | collective-permute-done | bytes 53280 | tf_op jit(solution)/shard_map/ppermute | solution.py:22
  33.7 1.6 %collective-permute-done.15 = f32[8,1664]{1,0:T(8,128)S(1)} collective-permute-done((f32[8,1664]{1,0:T(8,128)S(1)}, f32[8,1664]{1,0:T(8,128)S(1)}, u32[]{:S(2)}, u32[]{:S(2)}) %collective-permute-start.15) | collective-permute-done | bytes 53280 | tf_op jit(solution)/shard_map/ppermute | solution.py:22
  37.0 1.7 %tables.1 = (bf16[256,512]{1,0:T(8,128)(2,1)S(1)}, bf16[1536,256]{1,0:T(8,128)(2,1)S(1)}, bf16[1536,768]{1,0:T(8,128)(2,1)S(1)}) custom-call(s32[3]{0:T(128)S(1)} %pad_add_fusion.info_ref, f32[128,512]{1,0:T(8,128)S(1)} %collective-permute-done.prev_ref.packed_ref, s32[5,1,24]{2,1,0:T(1,128)S(1)} %bitcast.6, f32[48,1536]{1,0:T(8,128)S(1)} %copy-done, ...), custom_call_target="tpu_custom_call" | custom-call | flops 1024 | bytes 1024 | tf_op jit(solution)/shard_map/tables/pallas_call | solution.py:570
  38.6 1.2 %coarse.3.refs_0_ = f32[8,896]{1,0:T(8,128)S(1)} custom-call(s32[3]{0:T(128)S(1)} %pad_add_fusion.info_ref, f32[8,1664]{1,0:T(8,128)S(1)} %add_add_fusion.4.mine_ref, f32[8,1664]{1,0:T(8,128)S(1)} %collective-permute-done.17.other_ref, bf16[1536,768]{1,0:T(8,128)(2,1)S(1)} %get-tuple-element.83.table_ref), custom_call_target="tpu_custom_call" | custom-call | flops 1024 | bytes 1024 | tf_op jit(solution)/shard_map/coarse/pallas_call | solution.py:626
  39.8 3.0 %collective-permute-start.20 = (f32[8,896]{1,0:T(8,128)S(1)}, f32[8,896]{1,0:T(8,128)S(1)}, u32[]{:S(2)}, u32[]{:S(2)}) collective-permute-start(f32[8,896]{1,0:T(8,128)S(1)} %coarse.3.refs_0_), channel_id=1, source_target_pairs={{0,6},{1,7},{2,4},{3,5},{4,2},{5,3},{6,0},{7,1},{8,14},{9,15},{10,... | collective-permute-start | bytes 86024 | tf_op jit(solution)/shard_map/ppermute | solution.py:22
  42.8 1.4 %collective-permute-start.18 = (f32[8,896]{1,0:T(8,128)S(1)}, f32[8,896]{1,0:T(8,128)S(1)}, u32[]{:S(2)}, u32[]{:S(2)}) collective-permute-start(f32[8,896]{1,0:T(8,128)S(1)} %coarse.3.refs_0_), channel_id=1, source_target_pairs={{0,2},{1,3},{2,0},{3,1},{4,6},{5,7},{6,4},{7,5},{8,10},{9,11},{10,... | collective-permute-start | bytes 86024 | tf_op jit(solution)/shard_map/ppermute | solution.py:22
  44.3 1.5 %collective-permute-done.20.refs_3_ = f32[8,896]{1,0:T(8,128)S(1)} collective-permute-done((f32[8,896]{1,0:T(8,128)S(1)}, f32[8,896]{1,0:T(8,128)S(1)}, u32[]{:S(2)}, u32[]{:S(2)}) %collective-permute-start.20) | collective-permute-done | bytes 28704 | tf_op jit(solution)/shard_map/ppermute | solution.py:22
  45.7 1.9 %collective-permute-done.19.refs_2_ = f32[8,896]{1,0:T(8,128)S(1)} collective-permute-done((f32[8,896]{1,0:T(8,128)S(1)}, f32[8,896]{1,0:T(8,128)S(1)}, u32[]{:S(2)}, u32[]{:S(2)}) %collective-permute-start.19) | collective-permute-done | bytes 28704 | tf_op jit(solution)/shard_map/ppermute | solution.py:22
  47.6 1.9 %step.3 = (f32[5,16,512]{2,1,0:T(8,128)S(1)}, f32[5,16,512]{2,1,0:T(8,128)S(1)}, f32[5,16,512]{2,1,0:T(8,128)S(1)}, f32[5,16,512]{2,1,0:T(8,128)S(1)}, f32[5,16,...) custom-call(s32[3]{0:T(128)S(1)} %pad_add_fusion.info_ref, ...), custom_call_target="tpu_custom_call" | custom-call | flops 1024 | bytes 1024 | tf_op jit(solution)/shard_map/step/pallas_call | solution.py:637
  51.2 1.5 %collective-permute-start.26 = (f32[8,1664]{1,0:T(8,128)S(1)}, f32[8,1664]{1,0:T(8,128)S(1)}, u32[]{:S(2)}, u32[]{:S(2)}) collective-permute-start(f32[8,1664]{1,0:T(8,128)S(1)} %add.86), channel_id=1, source_target_pairs={{0,6},{1,7},{2,4},{3,5},{4,2},{5,3},{6,0},{7,1},{8,14},{9,15},{10,... | collective-permute-start | bytes 159752 | tf_op jit(solution)/shard_map/ppermute | solution.py:22
  53.4 2.3 %collective-permute-start.24 = (f32[8,1664]{1,0:T(8,128)S(1)}, f32[8,1664]{1,0:T(8,128)S(1)}, u32[]{:S(2)}, u32[]{:S(2)}) collective-permute-start(f32[8,1664]{1,0:T(8,128)S(1)} %add.86), channel_id=1, source_target_pairs={{0,2},{1,3},{2,0},{3,1},{4,6},{5,7},{6,4},{7,5},{8,10},{9,11},{10,... | collective-permute-start | bytes 159752 | tf_op jit(solution)/shard_map/ppermute | solution.py:22
  55.7 1.6 %flex_near.2.begun_ref = f32[5,16,1024]{2,1,0:T(8,128)S(1)} custom-call(f32[5,16,512]{2,1,0:T(8,128)S(1)} %get-tuple-element.84.values_ref.z_ref, bf16[5,512,1024]{2,1,0:T(8,128)(2,1)S(1)} %get-tuple-element.65.near_large_ref.large_ref, bf16[5,512,1024]{2,1,0:T(8,128)(2,1)S(1)} %get-tuple-element.66.near_small_ref.small_ref), custom_call_target="tpu_custom_call" | custom-call | flops 1024 | bytes 1024 | tf_op jit(solution)/shard_map/flex_near/pallas_call | solution.py:602
  57.3 1.7 %flex_far.2 = (f32[5,16,512]{2,1,0:T(8,128)S(1)}, f32[5,16,512]{2,1,0:T(8,128)S(1)}, f32[8,1664]{1,0:T(8,128)S(1)}) custom-call(f32[5,16,512]{2,1,0:T(8,128)S(1)} %get-tuple-element.84.values_ref.z_ref, f32[5,16,512]{2,1,0:T(8,128)S(1)} %collective-permute-done.21.forces_ref, f32[5,16,1024]{2,1,0:T(8,128)S(1)} %flex_near.2.begun_ref, ...), custom_call_target="tpu_custom_call" | custom-call | flops 1024 | bytes 1024 | tf_op jit(solution)/shard_map/flex_far/pallas_call | solution.py:612
  59.6 1.6 %collective-permute-start.29 = (f32[8,1664]{1,0:T(8,128)S(1)}, f32[8,1664]{1,0:T(8,128)S(1)}, u32[]{:S(2)}, u32[]{:S(2)}) collective-permute-start(f32[8,1664]{1,0:T(8,128)S(1)} %add_add_fusion.3), channel_id=1, source_target_pairs={{0,24},{1,25},{2,26},{3,27},{4,28},{5,29},{6,30},{7,31},{8,16},{9,... | collective-permute-start | bytes 159752 | tf_op jit(solution)/shard_map/ppermute | solution.py:22
  61.6 1.6 %collective-permute-start.27 = (f32[8,1664]{1,0:T(8,128)S(1)}, f32[8,1664]{1,0:T(8,128)S(1)}, u32[]{:S(2)}, u32[]{:S(2)}) collective-permute-start(f32[8,1664]{1,0:T(8,128)S(1)} %add_add_fusion.3), channel_id=1, source_target_pairs={{0,8},{1,9},{2,10},{3,11},{4,12},{5,13},{6,14},{7,15},{8,0},{9,1},... | collective-permute-start | bytes 159752 | tf_op jit(solution)/shard_map/ppermute | solution.py:22
  63.2 1.6 %collective-permute-done.29 = f32[8,1664]{1,0:T(8,128)S(1)} collective-permute-done((f32[8,1664]{1,0:T(8,128)S(1)}, f32[8,1664]{1,0:T(8,128)S(1)}, u32[]{:S(2)}, u32[]{:S(2)}) %collective-permute-start.29) | collective-permute-done | bytes 53280 | tf_op jit(solution)/shard_map/ppermute | solution.py:22
  65.8 1.2 %collective-permute-done.30.other_ref = f32[8,1664]{1,0:T(8,128)S(1)} collective-permute-done((f32[8,1664]{1,0:T(8,128)S(1)}, f32[8,1664]{1,0:T(8,128)S(1)}, u32[]{:S(2)}, u32[]{:S(2)}) %collective-permute-start.30) | collective-permute-done | bytes 53280 | tf_op jit(solution)/shard_map/ppermute | solution.py:22
  67.0 1.2 %coarse.4.refs_0_ = f32[8,896]{1,0:T(8,128)S(1)} custom-call(s32[3]{0:T(128)S(1)} %pad_add_fusion.info_ref, f32[8,1664]{1,0:T(8,128)S(1)} %add_add_fusion.2.mine_ref, f32[8,1664]{1,0:T(8,128)S(1)} %collective-permute-done.30.other_ref, bf16[1536,768]{1,0:T(8,128)(2,1)S(1)} %get-tuple-element.83.table_ref), custom_call_target="tpu_custom_call" | custom-call | flops 1024 | bytes 1024 | tf_op jit(solution)/shard_map/coarse/pallas_call | solution.py:626
  68.2 2.1 %collective-permute-start.33 = (f32[8,896]{1,0:T(8,128)S(1)}, f32[8,896]{1,0:T(8,128)S(1)}, u32[]{:S(2)}, u32[]{:S(2)}) collective-permute-start(f32[8,896]{1,0:T(8,128)S(1)} %coarse.4.refs_0_), channel_id=1, source_target_pairs={{0,6},{1,7},{2,4},{3,5},{4,2},{5,3},{6,0},{7,1},{8,14},{9,15},{10,... | collective-permute-start | bytes 86024 | tf_op jit(solution)/shard_map/ppermute | solution.py:22
  70.4 2.3 %collective-permute-start.31 = (f32[8,896]{1,0:T(8,128)S(1)}, f32[8,896]{1,0:T(8,128)S(1)}, u32[]{:S(2)}, u32[]{:S(2)}) collective-permute-start(f32[8,896]{1,0:T(8,128)S(1)} %coarse.4.refs_0_), channel_id=1, source_target_pairs={{0,2},{1,3},{2,0},{3,1},{4,6},{5,7},{6,4},{7,5},{8,10},{9,11},{10,... | collective-permute-start | bytes 86024 | tf_op jit(solution)/shard_map/ppermute | solution.py:22
  72.6 1.3 %collective-permute-done.33.refs_3_ = f32[8,896]{1,0:T(8,128)S(1)} collective-permute-done((f32[8,896]{1,0:T(8,128)S(1)}, f32[8,896]{1,0:T(8,128)S(1)}, u32[]{:S(2)}, u32[]{:S(2)}) %collective-permute-start.33) | collective-permute-done | bytes 28704 | tf_op jit(solution)/shard_map/ppermute | solution.py:22
  73.9 1.2 %collective-permute-done.32.refs_2_ = f32[8,896]{1,0:T(8,128)S(1)} collective-permute-done((f32[8,896]{1,0:T(8,128)S(1)}, f32[8,896]{1,0:T(8,128)S(1)}, u32[]{:S(2)}, u32[]{:S(2)}) %collective-permute-start.32) | collective-permute-done | bytes 28704 | tf_op jit(solution)/shard_map/ppermute | solution.py:22
  75.1 1.9 %step.4 = (f32[5,16,512]{2,1,0:T(8,128)S(1)}, f32[5,16,512]{2,1,0:T(8,128)S(1)}, f32[5,16,512]{2,1,0:T(8,128)S(1)}, f32[5,16,512]{2,1,0:T(8,128)S(1)}, f32[5,16,...) custom-call(s32[3]{0:T(128)S(1)} %pad_add_fusion.info_ref, ...), custom_call_target="tpu_custom_call" | custom-call | flops 1024 | bytes 1024 | tf_op jit(solution)/shard_map/step/pallas_call | solution.py:637
  77.8 1.2 %collective-permute-done.36 = f32[8,1664]{1,0:T(8,128)S(1)} collective-permute-done((f32[8,1664]{1,0:T(8,128)S(1)}, f32[8,1664]{1,0:T(8,128)S(1)}, u32[]{:S(2)}, u32[]{:S(2)}) %collective-permute-start.36) | collective-permute-done | bytes 53280 | tf_op jit(solution)/shard_map/ppermute | solution.py:22
  79.1 1.4 %collective-permute-start.39 = (f32[8,1664]{1,0:T(8,128)S(1)}, f32[8,1664]{1,0:T(8,128)S(1)}, u32[]{:S(2)}, u32[]{:S(2)}) collective-permute-start(f32[8,1664]{1,0:T(8,128)S(1)} %add.94), channel_id=1, source_target_pairs={{0,6},{1,7},{2,4},{3,5},{4,2},{5,3},{6,0},{7,1},{8,14},{9,15},{10,... | collective-permute-start | bytes 159752 | tf_op jit(solution)/shard_map/ppermute | solution.py:22
  80.5 1.0 collective-permute-start.38
  81.5 2.1 %collective-permute-start.37 = (f32[8,1664]{1,0:T(8,128)S(1)}, f32[8,1664]{1,0:T(8,128)S(1)}, u32[]{:S(2)}, u32[]{:S(2)}) collective-permute-start(f32[8,1664]{1,0:T(8,128)S(1)} %add.94), channel_id=1, source_target_pairs={{0,2},{1,3},{2,0},{3,1},{4,6},{5,7},{6,4},{7,5},{8,10},{9,11},{10,... | collective-permute-start | bytes 159752 | tf_op jit(solution)/shard_map/ppermute | solution.py:22
  83.5 1.6 %flex_near.3.begun_ref = f32[5,16,1024]{2,1,0:T(8,128)S(1)} custom-call(f32[5,16,512]{2,1,0:T(8,128)S(1)} %get-tuple-element.98.values_ref.z_ref, bf16[5,512,1024]{2,1,0:T(8,128)(2,1)S(1)} %get-tuple-element.65.near_large_ref.large_ref, bf16[5,512,1024]{2,1,0:T(8,128)(2,1)S(1)} %get-tuple-element.66.near_small_ref.small_ref), custom_call_target="tpu_custom_call" | custom-call | flops 1024 | bytes 1024 | tf_op jit(solution)/shard_map/flex_near/pallas_call | solution.py:602
  85.2 1.7 %flex_far.3 = (f32[5,16,512]{2,1,0:T(8,128)S(1)}, f32[5,16,512]{2,1,0:T(8,128)S(1)}, f32[8,1664]{1,0:T(8,128)S(1)}) custom-call(f32[5,16,512]{2,1,0:T(8,128)S(1)} %get-tuple-element.98.values_ref.z_ref, f32[5,16,512]{2,1,0:T(8,128)S(1)} %collective-permute-done.34.forces_ref, f32[5,16,1024]{2,1,0:T(8,128)S(1)} %flex_near.3.begun_ref, ...), custom_call_target="tpu_custom_call" | custom-call | flops 1024 | bytes 1024 | tf_op jit(solution)/shard_map/flex_far/pallas_call | solution.py:612
  87.1 2.6 %collective-permute-start.42 = (f32[8,1664]{1,0:T(8,128)S(1)}, f32[8,1664]{1,0:T(8,128)S(1)}, u32[]{:S(2)}, u32[]{:S(2)}) collective-permute-start(f32[8,1664]{1,0:T(8,128)S(1)} %add_add_fusion.1), channel_id=1, source_target_pairs={{0,24},{1,25},{2,26},{3,27},{4,28},{5,29},{6,30},{7,31},{8,16},{9,... | collective-permute-start | bytes 159752 | tf_op jit(solution)/shard_map/ppermute | solution.py:22
  90.7 1.6 %collective-permute-done.42 = f32[8,1664]{1,0:T(8,128)S(1)} collective-permute-done((f32[8,1664]{1,0:T(8,128)S(1)}, f32[8,1664]{1,0:T(8,128)S(1)}, u32[]{:S(2)}, u32[]{:S(2)}) %collective-permute-start.42) | collective-permute-done | bytes 53280 | tf_op jit(solution)/shard_map/ppermute | solution.py:22
  92.2 1.6 %collective-permute-done.41 = f32[8,1664]{1,0:T(8,128)S(1)} collective-permute-done((f32[8,1664]{1,0:T(8,128)S(1)}, f32[8,1664]{1,0:T(8,128)S(1)}, u32[]{:S(2)}, u32[]{:S(2)}) %collective-permute-start.41) | collective-permute-done | bytes 53280 | tf_op jit(solution)/shard_map/ppermute | solution.py:22
  94.4 1.2 %collective-permute-done.43.other_ref = f32[8,1664]{1,0:T(8,128)S(1)} collective-permute-done((f32[8,1664]{1,0:T(8,128)S(1)}, f32[8,1664]{1,0:T(8,128)S(1)}, u32[]{:S(2)}, u32[]{:S(2)}) %collective-permute-start.43) | collective-permute-done | bytes 53280 | tf_op jit(solution)/shard_map/ppermute | solution.py:22
  95.6 1.2 %coarse.5.refs_0_ = f32[8,896]{1,0:T(8,128)S(1)} custom-call(s32[3]{0:T(128)S(1)} %pad_add_fusion.info_ref, f32[8,1664]{1,0:T(8,128)S(1)} %add_add_fusion.mine_ref, f32[8,1664]{1,0:T(8,128)S(1)} %collective-permute-done.43.other_ref, bf16[1536,768]{1,0:T(8,128)(2,1)S(1)} %get-tuple-element.83.table_ref), custom_call_target="tpu_custom_call" | custom-call | flops 1024 | bytes 1024 | tf_op jit(solution)/shard_map/coarse/pallas_call | solution.py:626
  96.8 2.4 %collective-permute-start.46 = (f32[8,896]{1,0:T(8,128)S(1)}, f32[8,896]{1,0:T(8,128)S(1)}, u32[]{:S(2)}, u32[]{:S(2)}) collective-permute-start(f32[8,896]{1,0:T(8,128)S(1)} %coarse.5.refs_0_), channel_id=1, source_target_pairs={{0,6},{1,7},{2,4},{3,5},{4,2},{5,3},{6,0},{7,1},{8,14},{9,15},{10,... | collective-permute-start | bytes 86024 | tf_op jit(solution)/shard_map/ppermute | solution.py:22
  99.3 2.0 %collective-permute-start.44 = (f32[8,896]{1,0:T(8,128)S(1)}, f32[8,896]{1,0:T(8,128)S(1)}, u32[]{:S(2)}, u32[]{:S(2)}) collective-permute-start(f32[8,896]{1,0:T(8,128)S(1)} %coarse.5.refs_0_), channel_id=1, source_target_pairs={{0,2},{1,3},{2,0},{3,1},{4,6},{5,7},{6,4},{7,5},{8,10},{9,11},{10,... | collective-permute-start | bytes 86024 | tf_op jit(solution)/shard_map/ppermute | solution.py:22
  101.2 1.3 %collective-permute-done.46.refs_3_ = f32[8,896]{1,0:T(8,128)S(1)} collective-permute-done((f32[8,896]{1,0:T(8,128)S(1)}, f32[8,896]{1,0:T(8,128)S(1)}, u32[]{:S(2)}, u32[]{:S(2)}) %collective-permute-start.46) | collective-permute-done | bytes 28704 | tf_op jit(solution)/shard_map/ppermute | solution.py:22
  102.5 1.5 %collective-permute-done.45.refs_2_ = f32[8,896]{1,0:T(8,128)S(1)} collective-permute-done((f32[8,896]{1,0:T(8,128)S(1)}, f32[8,896]{1,0:T(8,128)S(1)}, u32[]{:S(2)}, u32[]{:S(2)}) %collective-permute-start.45) | collective-permute-done | bytes 28704 | tf_op jit(solution)/shard_map/ppermute | solution.py:22
  104.1 2.3 %step.5 = (f32[1,1,5,16,4,128]{5,4,3,2,1,0:T(4,128)}, f32[1,1,5,16,4,128]{5,4,3,2,1,0:T(4,128)}) custom-call(s32[3]{0:T(128)S(1)} %pad_add_fusion.info_ref, s32[1,1,4,5]{3,2,1,0:T(4,128)S(1)} %copy-done.1, f32[5,16,512]{2,1,0:T(8,128)S(1)} %get-tuple-element.100.own_ref, f32[5,16,512]{2,1,0:T(8,128)S(1)} %collective-permute-done.35.facing_ref, ...), custom_call_target="tpu_custom_call" | custom-call | flops 1024 | bytes 1024 | tf_op jit(solution)/shard_map/step/pallas_call | solution.py:637
  (77 shorter events, 12.4 us)
Async XLA Ops:
  2.2 10.5 %collective-permute-start = (f32[128,512]{1,0:T(8,128)S(1)}, f32[128,512]{1,0:T(8,128)S(1)}, u32[]{:S(2)}, u32[]{:S(2)}) collective-permute-start(f32[128,512]{1,0:T(8,128)S(1)} %pack.1), channel_id=1, source_target_pairs={{0,1},{1,2},{2,3},{3,4},{4,5},{5,6},{6,7},{7,0},{8,9},{9,10},{10,1... | collective-permute-start | bytes 786440 | tf_op jit(solution)/shard_map/ppermute | solution.py:17
  2.8 17.6 %collective-permute-start.4 = (f32[48,1536]{1,0:T(8,128)}, f32[48,1536]{1,0:T(8,128)S(1)}, u32[]{:S(2)}, u32[]{:S(2)}) collective-permute-start(f32[48,1536]{1,0:T(8,128)} %refs_0_), channel_id=1, source_target_pairs={{0,24},{1,25},{2,26},{3,27},{4,28},{5,29},{6,30},{7,31},{8,16},{9,... | collective-permute-start | bytes 884744 | tf_op jit(solution)/shard_map/ppermute | solution.py:22
  6.3 14.4 %collective-permute-start.3 = (f32[48,1536]{1,0:T(8,128)}, f32[48,1536]{1,0:T(8,128)S(1)}, u32[]{:S(2)}, u32[]{:S(2)}) collective-permute-start(f32[48,1536]{1,0:T(8,128)} %refs_0_), channel_id=1, source_target_pairs={{0,16},{1,17},{2,18},{3,19},{4,20},{5,21},{6,22},{7,23},{8,24},{9,... | collective-permute-start | bytes 884744 | tf_op jit(solution)/shard_map/ppermute | solution.py:22
  6.8 16.0 %collective-permute-start.2 = (f32[48,1536]{1,0:T(8,128)}, f32[48,1536]{1,0:T(8,128)S(1)}, u32[]{:S(2)}, u32[]{:S(2)}) collective-permute-start(f32[48,1536]{1,0:T(8,128)} %refs_0_), channel_id=1, source_target_pairs={{0,8},{1,9},{2,10},{3,11},{4,12},{5,13},{6,14},{7,15},{8,0},{9,1},... | collective-permute-start | bytes 884744 | tf_op jit(solution)/shard_map/ppermute | solution.py:22
  14.2 8.6 %collective-permute-start.1 = (f32[5,16,512]{2,1,0:T(8,128)S(1)}, f32[5,16,512]{2,1,0:T(8,128)S(1)}, u32[]{:S(2)}, u32[]{:S(2)}) collective-permute-start(f32[5,16,512]{2,1,0:T(8,128)S(1)} %get-tuple-element.62), channel_id=1, source_target_pairs={{0,7},{1,0},{2,1},{3,2},{4,3},{5,4},{6,5},{7,6},{8,15},{9,8},{10,9... | collective-permute-start | bytes 491528 | tf_op jit(solution)/shard_map/ppermute | solution.py:17
  17.1 1.2 %collective-permute-start.10 = (f32[8,1664]{1,0:T(8,128)S(1)}, f32[8,1664]{1,0:T(8,128)S(1)}, u32[]{:S(2)}, u32[]{:S(2)}) collective-permute-start(f32[8,1664]{1,0:T(8,128)S(1)} %get-tuple-element.81), channel_id=1, source_target_pairs={{0,1},{1,0},{2,3},{3,2},{4,5},{5,4},{6,7},{7,6},{8,9},{9,8},{10,11... | collective-permute-start | bytes 159752 | tf_op jit(solution)/shard_map/ppermute | solution.py:22
  18.3 10.2 %collective-permute-start.13 = (f32[8,1664]{1,0:T(8,128)S(1)}, f32[8,1664]{1,0:T(8,128)S(1)}, u32[]{:S(2)}, u32[]{:S(2)}) collective-permute-start(f32[8,1664]{1,0:T(8,128)S(1)} %add.78), channel_id=1, source_target_pairs={{0,6},{1,7},{2,4},{3,5},{4,2},{5,3},{6,0},{7,1},{8,14},{9,15},{10,... | collective-permute-start | bytes 159752 | tf_op jit(solution)/shard_map/ppermute | solution.py:22
  20.4 8.1 %collective-permute-start.12 = (f32[8,1664]{1,0:T(8,128)S(1)}, f32[8,1664]{1,0:T(8,128)S(1)}, u32[]{:S(2)}, u32[]{:S(2)}) collective-permute-start(f32[8,1664]{1,0:T(8,128)S(1)} %add.78), channel_id=1, source_target_pairs={{0,4},{1,5},{2,6},{3,7},{4,0},{5,1},{6,2},{7,3},{8,12},{9,13},{10,... | collective-permute-start | bytes 159752 | tf_op jit(solution)/shard_map/ppermute | solution.py:22
  20.6 7.9 %collective-permute-start.11 = (f32[8,1664]{1,0:T(8,128)S(1)}, f32[8,1664]{1,0:T(8,128)S(1)}, u32[]{:S(2)}, u32[]{:S(2)}) collective-permute-start(f32[8,1664]{1,0:T(8,128)S(1)} %add.78), channel_id=1, source_target_pairs={{0,2},{1,3},{2,0},{3,1},{4,6},{5,7},{6,4},{7,5},{8,10},{9,11},{10,... | collective-permute-start | bytes 159752 | tf_op jit(solution)/shard_map/ppermute | solution.py:22
  22.8 9.3 %copy-start = (f32[48,1536]{1,0:T(8,128)S(1)}, f32[48,1536]{1,0:T(8,128)}, u32[]{:S(2)}) copy-start(f32[48,1536]{1,0:T(8,128)} %refs_0_) | copy-start | bytes 884740
  28.5 5.2 %collective-permute-start.16 = (f32[8,1664]{1,0:T(8,128)S(1)}, f32[8,1664]{1,0:T(8,128)S(1)}, u32[]{:S(2)}, u32[]{:S(2)}) collective-permute-start(f32[8,1664]{1,0:T(8,128)S(1)} %add_add_fusion.5), channel_id=1, source_target_pairs={{0,24},{1,25},{2,26},{3,27},{4,28},{5,29},{6,30},{7,31},{8,16},{9,... | collective-permute-start | bytes 159752 | tf_op jit(solution)/shard_map/ppermute | solution.py:22
  31.2 4.1 %collective-permute-start.15 = (f32[8,1664]{1,0:T(8,128)S(1)}, f32[8,1664]{1,0:T(8,128)S(1)}, u32[]{:S(2)}, u32[]{:S(2)}) collective-permute-start(f32[8,1664]{1,0:T(8,128)S(1)} %add_add_fusion.5), channel_id=1, source_target_pairs={{0,16},{1,17},{2,18},{3,19},{4,20},{5,21},{6,22},{7,23},{8,24},{9,... | collective-permute-start | bytes 159752 | tf_op jit(solution)/shard_map/ppermute | solution.py:22
  31.7 4.1 %collective-permute-start.14 = (f32[8,1664]{1,0:T(8,128)S(1)}, f32[8,1664]{1,0:T(8,128)S(1)}, u32[]{:S(2)}, u32[]{:S(2)}) collective-permute-start(f32[8,1664]{1,0:T(8,128)S(1)} %add_add_fusion.5), channel_id=1, source_target_pairs={{0,8},{1,9},{2,10},{3,11},{4,12},{5,13},{6,14},{7,15},{8,0},{9,1},... | collective-permute-start | bytes 159752 | tf_op jit(solution)/shard_map/ppermute | solution.py:22
  32.1 3.8 %collective-permute-start.6 = (f32[48,1536]{1,0:T(8,128)S(1)}, f32[48,1536]{1,0:T(8,128)S(1)}, u32[]{:S(2)}, u32[]{:S(2)}) collective-permute-start(f32[48,1536]{1,0:T(8,128)S(1)} %copy-done), channel_id=1, source_target_pairs={{0,1},{1,0},{2,3},{3,2},{4,5},{5,4},{6,7},{7,6},{8,9},{9,8},{10,11... | collective-permute-start | bytes 884744 | tf_op jit(solution)/shard_map/ppermute | solution.py:22
  32.1 4.2 %collective-permute-start.7 = (f32[48,1536]{1,0:T(8,128)S(1)}, f32[48,1536]{1,0:T(8,128)S(1)}, u32[]{:S(2)}, u32[]{:S(2)}) collective-permute-start(f32[48,1536]{1,0:T(8,128)S(1)} %collective-permute-done.2.refs_1_), channel_id=1, source_target_pairs={{0,1},{1,0},{2,3},{3,2},{4,5},{5,4},{6,7},{7,6},{8,9},{9,8},{10,11... | collective-permute-start | bytes 884744 | tf_op jit(solution)/shard_map/ppermute | solution.py:22
  33.7 2.5 %collective-permute-start.8 = (f32[48,1536]{1,0:T(8,128)S(1)}, f32[48,1536]{1,0:T(8,128)S(1)}, u32[]{:S(2)}, u32[]{:S(2)}) collective-permute-start(f32[48,1536]{1,0:T(8,128)S(1)} %collective-permute-done.3.refs_2_), channel_id=1, source_target_pairs={{0,1},{1,0},{2,3},{3,2},{4,5},{5,4},{6,7},{7,6},{8,9},{9,8},{10,11... | collective-permute-start | bytes 884744 | tf_op jit(solution)/shard_map/ppermute | solution.py:22
  35.4 1.6 %collective-permute-start.9 = (f32[48,1536]{1,0:T(8,128)S(1)}, f32[48,1536]{1,0:T(8,128)S(1)}, u32[]{:S(2)}, u32[]{:S(2)}) collective-permute-start(f32[48,1536]{1,0:T(8,128)S(1)} %collective-permute-done.4.refs_3_), channel_id=1, source_target_pairs={{0,1},{1,0},{2,3},{3,2},{4,5},{5,4},{6,7},{7,6},{8,9},{9,8},{10,11... | collective-permute-start | bytes 884744 | tf_op jit(solution)/shard_map/ppermute | solution.py:22
  35.9 8.4 %collective-permute-start.5 = (f32[5,16,512]{2,1,0:T(8,128)S(1)}, f32[5,16,512]{2,1,0:T(8,128)S(1)}, u32[]{:S(2)}, u32[]{:S(2)}) collective-permute-start(f32[5,16,512]{2,1,0:T(8,128)S(1)} %get-tuple-element.68), channel_id=1, source_target_pairs={{0,1},{1,2},{2,3},{3,4},{4,5},{5,6},{6,7},{7,0},{8,9},{9,10},{10,1... | collective-permute-start | bytes 491528 | tf_op jit(solution)/shard_map/ppermute | solution.py:17
  35.9 2.7 %collective-permute-start.17 = (f32[8,1664]{1,0:T(8,128)S(1)}, f32[8,1664]{1,0:T(8,128)S(1)}, u32[]{:S(2)}, u32[]{:S(2)}) collective-permute-start(f32[8,1664]{1,0:T(8,128)S(1)} %add_add_fusion.4.mine_ref), channel_id=1, source_target_pairs={{0,1},{1,0},{2,3},{3,2},{4,5},{5,4},{6,7},{7,6},{8,9},{9,8},{10,11... | collective-permute-start | bytes 159752 | tf_op jit(solution)/shard_map/ppermute | solution.py:22
  39.8 5.9 %collective-permute-start.20 = (f32[8,896]{1,0:T(8,128)S(1)}, f32[8,896]{1,0:T(8,128)S(1)}, u32[]{:S(2)}, u32[]{:S(2)}) collective-permute-start(f32[8,896]{1,0:T(8,128)S(1)} %coarse.3.refs_0_), channel_id=1, source_target_pairs={{0,6},{1,7},{2,4},{3,5},{4,2},{5,3},{6,0},{7,1},{8,14},{9,15},{10,... | collective-permute-start | bytes 86024 | tf_op jit(solution)/shard_map/ppermute | solution.py:22
  42.8 4.8 %collective-permute-start.19 = (f32[8,896]{1,0:T(8,128)S(1)}, f32[8,896]{1,0:T(8,128)S(1)}, u32[]{:S(2)}, u32[]{:S(2)}) collective-permute-start(f32[8,896]{1,0:T(8,128)S(1)} %coarse.3.refs_0_), channel_id=1, source_target_pairs={{0,4},{1,5},{2,6},{3,7},{4,0},{5,1},{6,2},{7,3},{8,12},{9,13},{10,... | collective-permute-start | bytes 86024 | tf_op jit(solution)/shard_map/ppermute | solution.py:22
  42.8 4.8 %collective-permute-start.18 = (f32[8,896]{1,0:T(8,128)S(1)}, f32[8,896]{1,0:T(8,128)S(1)}, u32[]{:S(2)}, u32[]{:S(2)}) collective-permute-start(f32[8,896]{1,0:T(8,128)S(1)} %coarse.3.refs_0_), channel_id=1, source_target_pairs={{0,2},{1,3},{2,0},{3,1},{4,6},{5,7},{6,4},{7,5},{8,10},{9,11},{10,... | collective-permute-start | bytes 86024 | tf_op jit(solution)/shard_map/ppermute | solution.py:22
  49.5 7.8 %collective-permute-start.21 = (f32[5,16,512]{2,1,0:T(8,128)S(1)}, f32[5,16,512]{2,1,0:T(8,128)S(1)}, u32[]{:S(2)}, u32[]{:S(2)}) collective-permute-start(f32[5,16,512]{2,1,0:T(8,128)S(1)} %get-tuple-element.85), channel_id=1, source_target_pairs={{0,7},{1,0},{2,1},{3,2},{4,3},{5,4},{6,5},{7,6},{8,15},{9,8},{10,9... | collective-permute-start | bytes 491528 | tf_op jit(solution)/shard_map/ppermute | solution.py:17
  49.8 1.4 %collective-permute-start.23 = (f32[8,1664]{1,0:T(8,128)S(1)}, f32[8,1664]{1,0:T(8,128)S(1)}, u32[]{:S(2)}, u32[]{:S(2)}) collective-permute-start(f32[8,1664]{1,0:T(8,128)S(1)} %get-tuple-element.92), channel_id=1, source_target_pairs={{0,1},{1,0},{2,3},{3,2},{4,5},{5,4},{6,7},{7,6},{8,9},{9,8},{10,11... | collective-permute-start | bytes 159752 | tf_op jit(solution)/shard_map/ppermute | solution.py:22
  51.2 7.8 %collective-permute-start.26 = (f32[8,1664]{1,0:T(8,128)S(1)}, f32[8,1664]{1,0:T(8,128)S(1)}, u32[]{:S(2)}, u32[]{:S(2)}) collective-permute-start(f32[8,1664]{1,0:T(8,128)S(1)} %add.86), channel_id=1, source_target_pairs={{0,6},{1,7},{2,4},{3,5},{4,2},{5,3},{6,0},{7,1},{8,14},{9,15},{10,... | collective-permute-start | bytes 159752 | tf_op jit(solution)/shard_map/ppermute | solution.py:22
  52.8 6.9 %collective-permute-start.25 = (f32[8,1664]{1,0:T(8,128)S(1)}, f32[8,1664]{1,0:T(8,128)S(1)}, u32[]{:S(2)}, u32[]{:S(2)}) collective-permute-start(f32[8,1664]{1,0:T(8,128)S(1)} %add.86), channel_id=1, source_target_pairs={{0,4},{1,5},{2,6},{3,7},{4,0},{5,1},{6,2},{7,3},{8,12},{9,13},{10,... | collective-permute-start | bytes 159752 | tf_op jit(solution)/shard_map/ppermute | solution.py:22
  53.4 6.2 %collective-permute-start.24 = (f32[8,1664]{1,0:T(8,128)S(1)}, f32[8,1664]{1,0:T(8,128)S(1)}, u32[]{:S(2)}, u32[]{:S(2)}) collective-permute-start(f32[8,1664]{1,0:T(8,128)S(1)} %add.86), channel_id=1, source_target_pairs={{0,2},{1,3},{2,0},{3,1},{4,6},{5,7},{6,4},{7,5},{8,10},{9,11},{10,... | collective-permute-start | bytes 159752 | tf_op jit(solution)/shard_map/ppermute | solution.py:22
  59.6 5.2 %collective-permute-start.29 = (f32[8,1664]{1,0:T(8,128)S(1)}, f32[8,1664]{1,0:T(8,128)S(1)}, u32[]{:S(2)}, u32[]{:S(2)}) collective-permute-start(f32[8,1664]{1,0:T(8,128)S(1)} %add_add_fusion.3), channel_id=1, source_target_pairs={{0,24},{1,25},{2,26},{3,27},{4,28},{5,29},{6,30},{7,31},{8,16},{9,... | collective-permute-start | bytes 159752 | tf_op jit(solution)/shard_map/ppermute | solution.py:22
  61.2 4.3 %collective-permute-start.28 = (f32[8,1664]{1,0:T(8,128)S(1)}, f32[8,1664]{1,0:T(8,128)S(1)}, u32[]{:S(2)}, u32[]{:S(2)}) collective-permute-start(f32[8,1664]{1,0:T(8,128)S(1)} %add_add_fusion.3), channel_id=1, source_target_pairs={{0,16},{1,17},{2,18},{3,19},{4,20},{5,21},{6,22},{7,23},{8,24},{9,... | collective-permute-start | bytes 159752 | tf_op jit(solution)/shard_map/ppermute | solution.py:22
  61.6 4.1 %collective-permute-start.27 = (f32[8,1664]{1,0:T(8,128)S(1)}, f32[8,1664]{1,0:T(8,128)S(1)}, u32[]{:S(2)}, u32[]{:S(2)}) collective-permute-start(f32[8,1664]{1,0:T(8,128)S(1)} %add_add_fusion.3), channel_id=1, source_target_pairs={{0,8},{1,9},{2,10},{3,11},{4,12},{5,13},{6,14},{7,15},{8,0},{9,1},... | collective-permute-start | bytes 159752 | tf_op jit(solution)/shard_map/ppermute | solution.py:22
  63.2 11.9 %collective-permute-start.22 = (f32[5,16,512]{2,1,0:T(8,128)S(1)}, f32[5,16,512]{2,1,0:T(8,128)S(1)}, u32[]{:S(2)}, u32[]{:S(2)}) collective-permute-start(f32[5,16,512]{2,1,0:T(8,128)S(1)} %get-tuple-element.89), channel_id=1, source_target_pairs={{0,1},{1,2},{2,3},{3,4},{4,5},{5,6},{6,7},{7,0},{8,9},{9,10},{10,1... | collective-permute-start | bytes 491528 | tf_op jit(solution)/shard_map/ppermute | solution.py:17
  65.7 1.3 %collective-permute-start.30 = (f32[8,1664]{1,0:T(8,128)S(1)}, f32[8,1664]{1,0:T(8,128)S(1)}, u32[]{:S(2)}, u32[]{:S(2)}) collective-permute-start(f32[8,1664]{1,0:T(8,128)S(1)} %add_add_fusion.2.mine_ref), channel_id=1, source_target_pairs={{0,1},{1,0},{2,3},{3,2},{4,5},{5,4},{6,7},{7,6},{8,9},{9,8},{10,11... | collective-permute-start | bytes 159752 | tf_op jit(solution)/shard_map/ppermute | solution.py:22
  68.2 5.7 %collective-permute-start.33 = (f32[8,896]{1,0:T(8,128)S(1)}, f32[8,896]{1,0:T(8,128)S(1)}, u32[]{:S(2)}, u32[]{:S(2)}) collective-permute-start(f32[8,896]{1,0:T(8,128)S(1)} %coarse.4.refs_0_), channel_id=1, source_target_pairs={{0,6},{1,7},{2,4},{3,5},{4,2},{5,3},{6,0},{7,1},{8,14},{9,15},{10,... | collective-permute-start | bytes 86024 | tf_op jit(solution)/shard_map/ppermute | solution.py:22
  70.3 4.8 %collective-permute-start.32 = (f32[8,896]{1,0:T(8,128)S(1)}, f32[8,896]{1,0:T(8,128)S(1)}, u32[]{:S(2)}, u32[]{:S(2)}) collective-permute-start(f32[8,896]{1,0:T(8,128)S(1)} %coarse.4.refs_0_), channel_id=1, source_target_pairs={{0,4},{1,5},{2,6},{3,7},{4,0},{5,1},{6,2},{7,3},{8,12},{9,13},{10,... | collective-permute-start | bytes 86024 | tf_op jit(solution)/shard_map/ppermute | solution.py:22
  70.4 4.8 %collective-permute-start.31 = (f32[8,896]{1,0:T(8,128)S(1)}, f32[8,896]{1,0:T(8,128)S(1)}, u32[]{:S(2)}, u32[]{:S(2)}) collective-permute-start(f32[8,896]{1,0:T(8,128)S(1)} %coarse.4.refs_0_), channel_id=1, source_target_pairs={{0,2},{1,3},{2,0},{3,1},{4,6},{5,7},{6,4},{7,5},{8,10},{9,11},{10,... | collective-permute-start | bytes 86024 | tf_op jit(solution)/shard_map/ppermute | solution.py:22
  77.0 8.1 %collective-permute-start.34 = (f32[5,16,512]{2,1,0:T(8,128)S(1)}, f32[5,16,512]{2,1,0:T(8,128)S(1)}, u32[]{:S(2)}, u32[]{:S(2)}) collective-permute-start(f32[5,16,512]{2,1,0:T(8,128)S(1)} %get-tuple-element.99), channel_id=1, source_target_pairs={{0,7},{1,0},{2,1},{3,2},{4,3},{5,4},{6,5},{7,6},{8,15},{9,8},{10,9... | collective-permute-start | bytes 491528 | tf_op jit(solution)/shard_map/ppermute | solution.py:17
  77.8 1.2 %collective-permute-start.36 = (f32[8,1664]{1,0:T(8,128)S(1)}, f32[8,1664]{1,0:T(8,128)S(1)}, u32[]{:S(2)}, u32[]{:S(2)}) collective-permute-start(f32[8,1664]{1,0:T(8,128)S(1)} %get-tuple-element.104), channel_id=1, source_target_pairs={{0,1},{1,0},{2,3},{3,2},{4,5},{5,4},{6,7},{7,6},{8,9},{9,8},{10,11... | collective-permute-start | bytes 159752 | tf_op jit(solution)/shard_map/ppermute | solution.py:22
  79.1 7.8 %collective-permute-start.39 = (f32[8,1664]{1,0:T(8,128)S(1)}, f32[8,1664]{1,0:T(8,128)S(1)}, u32[]{:S(2)}, u32[]{:S(2)}) collective-permute-start(f32[8,1664]{1,0:T(8,128)S(1)} %add.94), channel_id=1, source_target_pairs={{0,6},{1,7},{2,4},{3,5},{4,2},{5,3},{6,0},{7,1},{8,14},{9,15},{10,... | collective-permute-start | bytes 159752 | tf_op jit(solution)/shard_map/ppermute | solution.py:22
  80.5 6.6 %collective-permute-start.38 = (f32[8,1664]{1,0:T(8,128)S(1)}, f32[8,1664]{1,0:T(8,128)S(1)}, u32[]{:S(2)}, u32[]{:S(2)}) collective-permute-start(f32[8,1664]{1,0:T(8,128)S(1)} %add.94), channel_id=1, source_target_pairs={{0,4},{1,5},{2,6},{3,7},{4,0},{5,1},{6,2},{7,3},{8,12},{9,13},{10,... | collective-permute-start | bytes 159752 | tf_op jit(solution)/shard_map/ppermute | solution.py:22
  81.5 5.6 %collective-permute-start.37 = (f32[8,1664]{1,0:T(8,128)S(1)}, f32[8,1664]{1,0:T(8,128)S(1)}, u32[]{:S(2)}, u32[]{:S(2)}) collective-permute-start(f32[8,1664]{1,0:T(8,128)S(1)} %add.94), channel_id=1, source_target_pairs={{0,2},{1,3},{2,0},{3,1},{4,6},{5,7},{6,4},{7,5},{8,10},{9,11},{10,... | collective-permute-start | bytes 159752 | tf_op jit(solution)/shard_map/ppermute | solution.py:22
  87.1 5.1 %collective-permute-start.42 = (f32[8,1664]{1,0:T(8,128)S(1)}, f32[8,1664]{1,0:T(8,128)S(1)}, u32[]{:S(2)}, u32[]{:S(2)}) collective-permute-start(f32[8,1664]{1,0:T(8,128)S(1)} %add_add_fusion.1), channel_id=1, source_target_pairs={{0,24},{1,25},{2,26},{3,27},{4,28},{5,29},{6,30},{7,31},{8,16},{9,... | collective-permute-start | bytes 159752 | tf_op jit(solution)/shard_map/ppermute | solution.py:22
  89.7 4.1 %collective-permute-start.41 = (f32[8,1664]{1,0:T(8,128)S(1)}, f32[8,1664]{1,0:T(8,128)S(1)}, u32[]{:S(2)}, u32[]{:S(2)}) collective-permute-start(f32[8,1664]{1,0:T(8,128)S(1)} %add_add_fusion.1), channel_id=1, source_target_pairs={{0,16},{1,17},{2,18},{3,19},{4,20},{5,21},{6,22},{7,23},{8,24},{9,... | collective-permute-start | bytes 159752 | tf_op jit(solution)/shard_map/ppermute | solution.py:22
  90.2 4.1 %collective-permute-start.40 = (f32[8,1664]{1,0:T(8,128)S(1)}, f32[8,1664]{1,0:T(8,128)S(1)}, u32[]{:S(2)}, u32[]{:S(2)}) collective-permute-start(f32[8,1664]{1,0:T(8,128)S(1)} %add_add_fusion.1), channel_id=1, source_target_pairs={{0,8},{1,9},{2,10},{3,11},{4,12},{5,13},{6,14},{7,15},{8,0},{9,1},... | collective-permute-start | bytes 159752 | tf_op jit(solution)/shard_map/ppermute | solution.py:22
  90.7 13.4 %collective-permute-start.35 = (f32[5,16,512]{2,1,0:T(8,128)S(1)}, f32[5,16,512]{2,1,0:T(8,128)S(1)}, u32[]{:S(2)}, u32[]{:S(2)}) collective-permute-start(f32[5,16,512]{2,1,0:T(8,128)S(1)} %get-tuple-element.101), channel_id=1, source_target_pairs={{0,1},{1,2},{2,3},{3,4},{4,5},{5,6},{6,7},{7,0},{8,9},{9,10},{10,1... | collective-permute-start | bytes 491528 | tf_op jit(solution)/shard_map/ppermute | solution.py:17
  94.3 1.3 %collective-permute-start.43 = (f32[8,1664]{1,0:T(8,128)S(1)}, f32[8,1664]{1,0:T(8,128)S(1)}, u32[]{:S(2)}, u32[]{:S(2)}) collective-permute-start(f32[8,1664]{1,0:T(8,128)S(1)} %add_add_fusion.mine_ref), channel_id=1, source_target_pairs={{0,1},{1,0},{2,3},{3,2},{4,5},{5,4},{6,7},{7,6},{8,9},{9,8},{10,11... | collective-permute-start | bytes 159752 | tf_op jit(solution)/shard_map/ppermute | solution.py:22
  96.8 5.7 %collective-permute-start.46 = (f32[8,896]{1,0:T(8,128)S(1)}, f32[8,896]{1,0:T(8,128)S(1)}, u32[]{:S(2)}, u32[]{:S(2)}) collective-permute-start(f32[8,896]{1,0:T(8,128)S(1)} %coarse.5.refs_0_), channel_id=1, source_target_pairs={{0,6},{1,7},{2,4},{3,5},{4,2},{5,3},{6,0},{7,1},{8,14},{9,15},{10,... | collective-permute-start | bytes 86024 | tf_op jit(solution)/shard_map/ppermute | solution.py:22
  99.3 4.8 %collective-permute-start.45 = (f32[8,896]{1,0:T(8,128)S(1)}, f32[8,896]{1,0:T(8,128)S(1)}, u32[]{:S(2)}, u32[]{:S(2)}) collective-permute-start(f32[8,896]{1,0:T(8,128)S(1)} %coarse.5.refs_0_), channel_id=1, source_target_pairs={{0,4},{1,5},{2,6},{3,7},{4,0},{5,1},{6,2},{7,3},{8,12},{9,13},{10,... | collective-permute-start | bytes 86024 | tf_op jit(solution)/shard_map/ppermute | solution.py:22
  99.3 4.8 %collective-permute-start.44 = (f32[8,896]{1,0:T(8,128)S(1)}, f32[8,896]{1,0:T(8,128)S(1)}, u32[]{:S(2)}, u32[]{:S(2)}) collective-permute-start(f32[8,896]{1,0:T(8,128)S(1)} %coarse.5.refs_0_), channel_id=1, source_target_pairs={{0,2},{1,3},{2,0},{3,1},{4,6},{5,7},{6,4},{7,5},{8,10},{9,11},{10,... | collective-permute-start | bytes 86024 | tf_op jit(solution)/shard_map/ppermute | solution.py:22
  (2 other events, 11.6 us)

commit v6 on v5

--- a/solution.py
+++ b/solution.py
@@ -166,10 +166,12 @@
             found = jnp.sum(place.T, axis=0, keepdims=True)
             inverse_ref[at, :] = found.astype(jnp.int32)
             dof_rows_ref[at, :] = met
+    end(0, 2)
     others[1].wait()
     link = corner_rows(coupling_buffer[...], span)
     link_ref[...] = stacked(link, 2)
     link_t_ref[...] = jnp.concatenate(pieces(link.T, 2), axis=1)
+    end(2, 1)
     others[2].wait()
     others[3].wait()
     for j in range(slots):
@@ -177,7 +179,7 @@
             lanes = slice(k * width, (k + 1) * width)
             right_rows_ref[j, :, lanes] = right_buffer[j, :, k, :]
             weight_rows_ref[j : j + 1, lanes] = weight_buffer[j, k : k + 1, :]
-    end(0, slots)
+    end(3, slots - 3)
 
 
 def beside(x):
@@ -397,11 +399,14 @@
     energy_ref[:, half:] = lane_pair(work, 2)
 
 
-def flex_far_kernel(values_ref, forces_ref, begun_ref, large_ref, small_ref, own_ref, facing_ref, energy_ref):
+def flex_kernel(
+    values_ref, forces_ref, near_large_ref, near_small_ref, large_ref, small_ref, own_ref, facing_ref, energy_ref
+):
     slots, loads, _ = values_ref.shape
     work = jnp.zeros((loads, 1), jnp.float32)
     for s in range(slots):
-        work += flex_far_slot(s, begun_ref[s], values_ref, forces_ref, large_ref, small_ref, own_ref, facing_ref)
+        begun = flex_product(values_ref[s], near_large_ref[s], near_small_ref[s])
+        work += flex_far_slot(s, begun, values_ref, forces_ref, large_ref, small_ref, own_ref, facing_ref)
     write_energy(work, energy_ref)
 
 
@@ -599,25 +604,16 @@
                 name="flex_first",
             )(z, forces, near_large, near_small, flex)
         else:
-            begun = pl.pallas_call(
-                flex_near_kernel,
-                out_shape=shape_of(slots, loads, iface),
-                in_specs=[VMEM] * 3,
-                out_specs=VMEM,
-                compiler_params=PARAMS,
-                cost_estimate=LITTLE,
-                name="flex_near",
-            )(z, near_large, near_small)
             total = summed_along(total, level_bits)
             own, facing, energy = pl.pallas_call(
-                flex_far_kernel,
+                flex_kernel,
                 out_shape=(state, state, half_load),
-                in_specs=[VMEM] * 5,
+                in_specs=[VMEM] * 6,
                 out_specs=[VMEM] * 3,
                 compiler_params=PARAMS,
                 cost_estimate=LITTLE,
-                name="flex_far",
-            )(z, forces, begun, far_large, far_small)
+                name="flex",
+            )(z, forces, near_large, near_small, far_large, far_small)
         total = summed_along(total + energy, row_bits)
         rest = swapped(total, 1)
         facing_prev = shifted(facing, "col", 1)

time: 107 us -> 106 us (level)
    pallas_call x4 -> x2, Pallas kernels: 6.68 us -> 6.43 us  [local(): pl.pallas_call(flex_kernel, out_shape=(state, state, half_load), in_specs...]
where the time goes in v6:
time: 106 us
  starting transfers between devices  47.3 us (45%)
  Pallas kernels  31 us (29%)
  waiting for transfers between devices  26.1 us (25%)
  between operations  1.48 us (1%)
    ppermute x40, starting transfers between devices, swapped(): return lax.ppermute(x, BOTH, [(i, i ^ bits) for i in range(devices)])  42.8 us
    ppermute x40, waiting for transfers between devices, swapped(): return lax.ppermute(x, BOTH, [(i, i ^ bits) for i in range(devices)])  26.1 us
    pallas_call x2, Pallas kernels, local(): pl.pallas_call(flex_kernel, out_shape=(state, state, half_load), in_specs...  6.43 us
    pallas_call x3, Pallas kernels, local(): pl.pallas_call(functools.partial(step_kernel, corners, levels, first, las...  6.02 us
    pallas_call x1, Pallas kernels, local(): pl.pallas_call(flex_first_kernel, out_shape=(state, state, half_load) + h...  5.7 us
    pallas_call x1, Pallas kernels, local(): pl.pallas_call(prepare_kernel, out_shape=half_pieces + (shape_of(slots *...  5.18 us
    ppermute x7, starting transfers between devices, shifted(): lax.ppermute(x, axis, [(i, (i + by) % devices) for i in range(devices)])  4.43 us
    pallas_call x3, Pallas kernels, local(): pl.pallas_call(functools.partial(coarse_kernel, rows, levels), out_shape=...  3.63 us
  transfers between devices with their start and end apart: 47, of which 24 were waited for; matrix products, arithmetic and copies ran while one was open for 0% of the time, Pallas kernels for 23%

profile of v6, /device:TPU:0, one launch (start us, length us, event | category | flops | bytes accessed | tf_op | source)
XLA Modules:
  0.0 106.0 jit_solution(13908251501167780227)
XLA Ops:
  1.3 1.0 pack.1
  2.8 3.5 %collective-permute-start.4 = (f32[48,1536]{1,0:T(8,128)}, f32[48,1536]{1,0:T(8,128)S(1)}, u32[]{:S(2)}, u32[]{:S(2)}) collective-permute-start(f32[48,1536]{1,0:T(8,128)} %refs_0_), channel_id=1, source_target_pairs={{0,24},{1,25},{2,26},{3,27},{4,28},{5,29},{6,30},{7,31},{8,16},{9,... | collective-permute-start | bytes 884744 | tf_op jit(solution)/shard_map/ppermute | solution.py:22
  7.0 5.2 %prepare.1 = (bf16[5,512,1024]{2,1,0:T(8,128)(2,1)S(1)}, bf16[5,512,1024]{2,1,0:T(8,128)(2,1)S(1)}, s32[20,128]{1,0:T(8,128)S(1)}, s32[20,128]{1,0:T(8,128)S(1)}...) custom-call(s32[3]{0:T(128)S(1)} %pad_add_fusion.info_ref, ...), custom_call_target="tpu_custom_call" | custom-call | flops 1024 | bytes 1024 | tf_op jit(solution)/shard_map/prepare/pallas_call | solution.py:539
  12.2 1.4 %first.1 = (f32[5,512]{1,0:T(8,128)S(1)}, f32[5,16,512]{2,1,0:T(8,128)S(1)}, f32[5,16,512]{2,1,0:T(8,128)S(1)}, f32[5,16,512]{2,1,0:T(8,128)S(1)}, f32[8,1664]{1...) custom-call(s32[3]{0:T(128)S(1)} %pad_add_fusion.info_ref, ...), custom_call_target="tpu_custom_call" | custom-call | flops 1024 | bytes 1024 | tf_op jit(solution)/shard_map/first/pallas_call | solution.py:561
  13.6 2.9 %collective-permute-start.1 = (f32[5,16,512]{2,1,0:T(8,128)S(1)}, f32[5,16,512]{2,1,0:T(8,128)S(1)}, u32[]{:S(2)}, u32[]{:S(2)}) collective-permute-start(f32[5,16,512]{2,1,0:T(8,128)S(1)} %get-tuple-element.62), channel_id=1, source_target_pairs={{0,7},{1,0},{2,1},{3,2},{4,3},{5,4},{6,5},{7,6},{8,15},{9,8},{10,9... | collective-permute-start | bytes 491528 | tf_op jit(solution)/shard_map/ppermute | solution.py:17
  16.5 1.2 %collective-permute-done.10 = f32[8,1664]{1,0:T(8,128)S(1)} collective-permute-done((f32[8,1664]{1,0:T(8,128)S(1)}, f32[8,1664]{1,0:T(8,128)S(1)}, u32[]{:S(2)}, u32[]{:S(2)}) %collective-permute-start.10) | collective-permute-done | bytes 53280 | tf_op jit(solution)/shard_map/ppermute | solution.py:22
  17.7 2.1 %collective-permute-start.13 = (f32[8,1664]{1,0:T(8,128)S(1)}, f32[8,1664]{1,0:T(8,128)S(1)}, u32[]{:S(2)}, u32[]{:S(2)}) collective-permute-start(f32[8,1664]{1,0:T(8,128)S(1)} %add.78), channel_id=1, source_target_pairs={{0,6},{1,7},{2,4},{3,5},{4,2},{5,3},{6,0},{7,1},{8,14},{9,15},{10,... | collective-permute-start | bytes 159752 | tf_op jit(solution)/shard_map/ppermute | solution.py:22
  20.6 2.0 %collective-permute-start.11 = (f32[8,1664]{1,0:T(8,128)S(1)}, f32[8,1664]{1,0:T(8,128)S(1)}, u32[]{:S(2)}, u32[]{:S(2)}) collective-permute-start(f32[8,1664]{1,0:T(8,128)S(1)} %add.78), channel_id=1, source_target_pairs={{0,2},{1,3},{2,0},{3,1},{4,6},{5,7},{6,4},{7,5},{8,10},{9,11},{10,... | collective-permute-start | bytes 159752 | tf_op jit(solution)/shard_map/ppermute | solution.py:22
  22.7 5.7 %flex_first.1 = (f32[5,16,512]{2,1,0:T(8,128)S(1)}, f32[5,16,512]{2,1,0:T(8,128)S(1)}, f32[8,1664]{1,0:T(8,128)S(1)}, bf16[5,512,1024]{2,1,0:T(8,128)(2,1)S(1)}, bf16[5,512,1024]{2,1,0:T(8,128)(2,1)S(1)}) custom-call(f32[5,16,512]{2,1,0:T(8,128)S(1)} %get-tuple-element.61.values_ref.z_ref, f32[5,16,512]{2,1,0:T(8,128)S(1)} %collective-permute-done.1.forces_ref, ...), custom_call_target="tpu_custom_call" | custom-call | flops 1024 | bytes 1024 | tf_op jit(solution)/shard_map/flex_first/pallas_call | solution.py:596
  28.5 2.2 %collective-permute-start.16 = (f32[8,1664]{1,0:T(8,128)S(1)}, f32[8,1664]{1,0:T(8,128)S(1)}, u32[]{:S(2)}, u32[]{:S(2)}) collective-permute-start(f32[8,1664]{1,0:T(8,128)S(1)} %add_add_fusion.5), channel_id=1, source_target_pairs={{0,24},{1,25},{2,26},{3,27},{4,28},{5,29},{6,30},{7,31},{8,16},{9,... | collective-permute-start | bytes 159752 | tf_op jit(solution)/shard_map/ppermute | solution.py:22
  32.5 1.1 %collective-permute-done.16 = f32[8,1664]{1,0:T(8,128)S(1)} collective-permute-done((f32[8,1664]{1,0:T(8,128)S(1)}, f32[8,1664]{1,0:T(8,128)S(1)}, u32[]{:S(2)}, u32[]{:S(2)}) %collective-permute-start.16) | collective-permute-done | bytes 53280 | tf_op jit(solution)/shard_map/ppermute | solution.py:22
  33.7 1.2 %collective-permute-done.15 = f32[8,1664]{1,0:T(8,128)S(1)} collective-permute-done((f32[8,1664]{1,0:T(8,128)S(1)}, f32[8,1664]{1,0:T(8,128)S(1)}, u32[]{:S(2)}, u32[]{:S(2)}) %collective-permute-start.15) | collective-permute-done | bytes 53280 | tf_op jit(solution)/shard_map/ppermute | solution.py:22
  36.4 1.7 %tables.1 = (bf16[256,512]{1,0:T(8,128)(2,1)S(1)}, bf16[1536,256]{1,0:T(8,128)(2,1)S(1)}, bf16[1536,768]{1,0:T(8,128)(2,1)S(1)}) custom-call(s32[3]{0:T(128)S(1)} %pad_add_fusion.info_ref, f32[128,512]{1,0:T(8,128)S(1)} %collective-permute-done.prev_ref.packed_ref, s32[5,1,24]{2,1,0:T(1,128)S(1)} %bitcast.6, f32[48,1536]{1,0:T(8,128)S(1)} %copy-done, ...), custom_call_target="tpu_custom_call" | custom-call | flops 1024 | bytes 1024 | tf_op jit(solution)/shard_map/tables/pallas_call | solution.py:575
  38.1 1.2 %coarse.3.refs_0_ = f32[8,896]{1,0:T(8,128)S(1)} custom-call(s32[3]{0:T(128)S(1)} %pad_add_fusion.info_ref, f32[8,1664]{1,0:T(8,128)S(1)} %add_add_fusion.4.mine_ref, f32[8,1664]{1,0:T(8,128)S(1)} %collective-permute-done.17.other_ref, bf16[1536,768]{1,0:T(8,128)(2,1)S(1)} %get-tuple-element.83.table_ref), custom_call_target="tpu_custom_call" | custom-call | flops 1024 | bytes 1024 | tf_op jit(solution)/shard_map/coarse/pallas_call | solution.py:622
  39.3 3.3 %collective-permute-start.20 = (f32[8,896]{1,0:T(8,128)S(1)}, f32[8,896]{1,0:T(8,128)S(1)}, u32[]{:S(2)}, u32[]{:S(2)}) collective-permute-start(f32[8,896]{1,0:T(8,128)S(1)} %coarse.3.refs_0_), channel_id=1, source_target_pairs={{0,6},{1,7},{2,4},{3,5},{4,2},{5,3},{6,0},{7,1},{8,14},{9,15},{10,... | collective-permute-start | bytes 86024 | tf_op jit(solution)/shard_map/ppermute | solution.py:22
  42.7 1.0 collective-permute-start.18
  43.7 1.3 %collective-permute-done.20.refs_3_ = f32[8,896]{1,0:T(8,128)S(1)} collective-permute-done((f32[8,896]{1,0:T(8,128)S(1)}, f32[8,896]{1,0:T(8,128)S(1)}, u32[]{:S(2)}, u32[]{:S(2)}) %collective-permute-start.20) | collective-permute-done | bytes 28704 | tf_op jit(solution)/shard_map/ppermute | solution.py:22
  45.0 2.4 %collective-permute-done.19.refs_2_ = f32[8,896]{1,0:T(8,128)S(1)} collective-permute-done((f32[8,896]{1,0:T(8,128)S(1)}, f32[8,896]{1,0:T(8,128)S(1)}, u32[]{:S(2)}, u32[]{:S(2)}) %collective-permute-start.19) | collective-permute-done | bytes 28704 | tf_op jit(solution)/shard_map/ppermute | solution.py:22
  47.3 1.9 %step.3 = (f32[5,16,512]{2,1,0:T(8,128)S(1)}, f32[5,16,512]{2,1,0:T(8,128)S(1)}, f32[5,16,512]{2,1,0:T(8,128)S(1)}, f32[5,16,512]{2,1,0:T(8,128)S(1)}, f32[5,16,...) custom-call(s32[3]{0:T(128)S(1)} %pad_add_fusion.info_ref, ...), custom_call_target="tpu_custom_call" | custom-call | flops 1024 | bytes 1024 | tf_op jit(solution)/shard_map/step/pallas_call | solution.py:633
  50.0 1.0 collective-permute-done.23
  50.9 1.5 %collective-permute-start.26 = (f32[8,1664]{1,0:T(8,128)S(1)}, f32[8,1664]{1,0:T(8,128)S(1)}, u32[]{:S(2)}, u32[]{:S(2)}) collective-permute-start(f32[8,1664]{1,0:T(8,128)S(1)} %add.86), channel_id=1, source_target_pairs={{0,6},{1,7},{2,4},{3,5},{4,2},{5,3},{6,0},{7,1},{8,14},{9,15},{10,... | collective-permute-start | bytes 159752 | tf_op jit(solution)/shard_map/ppermute | solution.py:22
  53.1 2.3 %collective-permute-start.24 = (f32[8,1664]{1,0:T(8,128)S(1)}, f32[8,1664]{1,0:T(8,128)S(1)}, u32[]{:S(2)}, u32[]{:S(2)}) collective-permute-start(f32[8,1664]{1,0:T(8,128)S(1)} %add.86), channel_id=1, source_target_pairs={{0,2},{1,3},{2,0},{3,1},{4,6},{5,7},{6,4},{7,5},{8,10},{9,11},{10,... | collective-permute-start | bytes 159752 | tf_op jit(solution)/shard_map/ppermute | solution.py:22
  55.4 3.2 %flex.2 = (f32[5,16,512]{2,1,0:T(8,128)S(1)}, f32[5,16,512]{2,1,0:T(8,128)S(1)}, f32[8,1664]{1,0:T(8,128)S(1)}) custom-call(f32[5,16,512]{2,1,0:T(8,128)S(1)} %get-tuple-element.84.values_ref.z_ref, f32[5,16,512]{2,1,0:T(8,128)S(1)} %collective-permute-done.21.forces_ref, bf16[5,512,1024]{2,1,0:T(8,128)(2,1)S(1)} %get-tuple-element.65.near_large_ref, ...), custom_call_target="tpu_custom_call" | custom-call | flops 1024 | bytes 1024 | tf_op jit(solution)/shard_map/flex/pallas_call | solution.py:608
  59.4 1.6 %collective-permute-start.29 = (f32[8,1664]{1,0:T(8,128)S(1)}, f32[8,1664]{1,0:T(8,128)S(1)}, u32[]{:S(2)}, u32[]{:S(2)}) collective-permute-start(f32[8,1664]{1,0:T(8,128)S(1)} %add_add_fusion.3), channel_id=1, source_target_pairs={{0,24},{1,25},{2,26},{3,27},{4,28},{5,29},{6,30},{7,31},{8,16},{9,... | collective-permute-start | bytes 159752 | tf_op jit(solution)/shard_map/ppermute | solution.py:22
  61.4 1.5 %collective-permute-start.27 = (f32[8,1664]{1,0:T(8,128)S(1)}, f32[8,1664]{1,0:T(8,128)S(1)}, u32[]{:S(2)}, u32[]{:S(2)}) collective-permute-start(f32[8,1664]{1,0:T(8,128)S(1)} %add_add_fusion.3), channel_id=1, source_target_pairs={{0,8},{1,9},{2,10},{3,11},{4,12},{5,13},{6,14},{7,15},{8,0},{9,1},... | collective-permute-start | bytes 159752 | tf_op jit(solution)/shard_map/ppermute | solution.py:22
  62.9 1.6 %collective-permute-done.29 = f32[8,1664]{1,0:T(8,128)S(1)} collective-permute-done((f32[8,1664]{1,0:T(8,128)S(1)}, f32[8,1664]{1,0:T(8,128)S(1)}, u32[]{:S(2)}, u32[]{:S(2)}) %collective-permute-start.29) | collective-permute-done | bytes 53280 | tf_op jit(solution)/shard_map/ppermute | solution.py:22
  65.7 1.2 %collective-permute-done.30.other_ref = f32[8,1664]{1,0:T(8,128)S(1)} collective-permute-done((f32[8,1664]{1,0:T(8,128)S(1)}, f32[8,1664]{1,0:T(8,128)S(1)}, u32[]{:S(2)}, u32[]{:S(2)}) %collective-permute-start.30) | collective-permute-done | bytes 53280 | tf_op jit(solution)/shard_map/ppermute | solution.py:22
  66.9 1.2 %coarse.4.refs_0_ = f32[8,896]{1,0:T(8,128)S(1)} custom-call(s32[3]{0:T(128)S(1)} %pad_add_fusion.info_ref, f32[8,1664]{1,0:T(8,128)S(1)} %add_add_fusion.2.mine_ref, f32[8,1664]{1,0:T(8,128)S(1)} %collective-permute-done.30.other_ref, bf16[1536,768]{1,0:T(8,128)(2,1)S(1)} %get-tuple-element.83.table_ref), custom_call_target="tpu_custom_call" | custom-call | flops 1024 | bytes 1024 | tf_op jit(solution)/shard_map/coarse/pallas_call | solution.py:622
  68.1 2.0 %collective-permute-start.33 = (f32[8,896]{1,0:T(8,128)S(1)}, f32[8,896]{1,0:T(8,128)S(1)}, u32[]{:S(2)}, u32[]{:S(2)}) collective-permute-start(f32[8,896]{1,0:T(8,128)S(1)} %coarse.4.refs_0_), channel_id=1, source_target_pairs={{0,6},{1,7},{2,4},{3,5},{4,2},{5,3},{6,0},{7,1},{8,14},{9,15},{10,... | collective-permute-start | bytes 86024 | tf_op jit(solution)/shard_map/ppermute | solution.py:22
  70.1 2.4 %collective-permute-start.31 = (f32[8,896]{1,0:T(8,128)S(1)}, f32[8,896]{1,0:T(8,128)S(1)}, u32[]{:S(2)}, u32[]{:S(2)}) collective-permute-start(f32[8,896]{1,0:T(8,128)S(1)} %coarse.4.refs_0_), channel_id=1, source_target_pairs={{0,2},{1,3},{2,0},{3,1},{4,6},{5,7},{6,4},{7,5},{8,10},{9,11},{10,... | collective-permute-start | bytes 86024 | tf_op jit(solution)/shard_map/ppermute | solution.py:22
  72.5 1.3 %collective-permute-done.33.refs_3_ = f32[8,896]{1,0:T(8,128)S(1)} collective-permute-done((f32[8,896]{1,0:T(8,128)S(1)}, f32[8,896]{1,0:T(8,128)S(1)}, u32[]{:S(2)}, u32[]{:S(2)}) %collective-permute-start.33) | collective-permute-done | bytes 28704 | tf_op jit(solution)/shard_map/ppermute | solution.py:22
  73.8 1.1 %collective-permute-done.32.refs_2_ = f32[8,896]{1,0:T(8,128)S(1)} collective-permute-done((f32[8,896]{1,0:T(8,128)S(1)}, f32[8,896]{1,0:T(8,128)S(1)}, u32[]{:S(2)}, u32[]{:S(2)}) %collective-permute-start.32) | collective-permute-done | bytes 28704 | tf_op jit(solution)/shard_map/ppermute | solution.py:22
  74.9 1.9 %step.4 = (f32[5,16,512]{2,1,0:T(8,128)S(1)}, f32[5,16,512]{2,1,0:T(8,128)S(1)}, f32[5,16,512]{2,1,0:T(8,128)S(1)}, f32[5,16,512]{2,1,0:T(8,128)S(1)}, f32[5,16,...) custom-call(s32[3]{0:T(128)S(1)} %pad_add_fusion.info_ref, ...), custom_call_target="tpu_custom_call" | custom-call | flops 1024 | bytes 1024 | tf_op jit(solution)/shard_map/step/pallas_call | solution.py:633
  77.6 1.2 %collective-permute-done.36 = f32[8,1664]{1,0:T(8,128)S(1)} collective-permute-done((f32[8,1664]{1,0:T(8,128)S(1)}, f32[8,1664]{1,0:T(8,128)S(1)}, u32[]{:S(2)}, u32[]{:S(2)}) %collective-permute-start.36) | collective-permute-done | bytes 53280 | tf_op jit(solution)/shard_map/ppermute | solution.py:22
  78.8 1.3 %collective-permute-start.39 = (f32[8,1664]{1,0:T(8,128)S(1)}, f32[8,1664]{1,0:T(8,128)S(1)}, u32[]{:S(2)}, u32[]{:S(2)}) collective-permute-start(f32[8,1664]{1,0:T(8,128)S(1)} %add.94), channel_id=1, source_target_pairs={{0,6},{1,7},{2,4},{3,5},{4,2},{5,3},{6,0},{7,1},{8,14},{9,15},{10,... | collective-permute-start | bytes 159752 | tf_op jit(solution)/shard_map/ppermute | solution.py:22
  80.2 1.1 %collective-permute-start.38 = (f32[8,1664]{1,0:T(8,128)S(1)}, f32[8,1664]{1,0:T(8,128)S(1)}, u32[]{:S(2)}, u32[]{:S(2)}) collective-permute-start(f32[8,1664]{1,0:T(8,128)S(1)} %add.94), channel_id=1, source_target_pairs={{0,4},{1,5},{2,6},{3,7},{4,0},{5,1},{6,2},{7,3},{8,12},{9,13},{10,... | collective-permute-start | bytes 159752 | tf_op jit(solution)/shard_map/ppermute | solution.py:22
  81.3 2.0 %collective-permute-start.37 = (f32[8,1664]{1,0:T(8,128)S(1)}, f32[8,1664]{1,0:T(8,128)S(1)}, u32[]{:S(2)}, u32[]{:S(2)}) collective-permute-start(f32[8,1664]{1,0:T(8,128)S(1)} %add.94), channel_id=1, source_target_pairs={{0,2},{1,3},{2,0},{3,1},{4,6},{5,7},{6,4},{7,5},{8,10},{9,11},{10,... | collective-permute-start | bytes 159752 | tf_op jit(solution)/shard_map/ppermute | solution.py:22
  83.3 3.2 %flex.3 = (f32[5,16,512]{2,1,0:T(8,128)S(1)}, f32[5,16,512]{2,1,0:T(8,128)S(1)}, f32[8,1664]{1,0:T(8,128)S(1)}) custom-call(f32[5,16,512]{2,1,0:T(8,128)S(1)} %get-tuple-element.98.values_ref.z_ref, f32[5,16,512]{2,1,0:T(8,128)S(1)} %collective-permute-done.34.forces_ref, bf16[5,512,1024]{2,1,0:T(8,128)(2,1)S(1)} %get-tuple-element.65.near_large_ref, ...), custom_call_target="tpu_custom_call" | custom-call | flops 1024 | bytes 1024 | tf_op jit(solution)/shard_map/flex/pallas_call | solution.py:608
  86.9 2.2 %collective-permute-start.42 = (f32[8,1664]{1,0:T(8,128)S(1)}, f32[8,1664]{1,0:T(8,128)S(1)}, u32[]{:S(2)}, u32[]{:S(2)}) collective-permute-start(f32[8,1664]{1,0:T(8,128)S(1)} %add_add_fusion.1), channel_id=1, source_target_pairs={{0,24},{1,25},{2,26},{3,27},{4,28},{5,29},{6,30},{7,31},{8,16},{9,... | collective-permute-start | bytes 159752 | tf_op jit(solution)/shard_map/ppermute | solution.py:22
  90.4 1.6 %collective-permute-done.42 = f32[8,1664]{1,0:T(8,128)S(1)} collective-permute-done((f32[8,1664]{1,0:T(8,128)S(1)}, f32[8,1664]{1,0:T(8,128)S(1)}, u32[]{:S(2)}, u32[]{:S(2)}) %collective-permute-start.42) | collective-permute-done | bytes 53280 | tf_op jit(solution)/shard_map/ppermute | solution.py:22
  92.0 1.2 %collective-permute-done.41 = f32[8,1664]{1,0:T(8,128)S(1)} collective-permute-done((f32[8,1664]{1,0:T(8,128)S(1)}, f32[8,1664]{1,0:T(8,128)S(1)}, u32[]{:S(2)}, u32[]{:S(2)}) %collective-permute-start.41) | collective-permute-done | bytes 53280 | tf_op jit(solution)/shard_map/ppermute | solution.py:22
  94.1 1.2 %collective-permute-done.43.other_ref = f32[8,1664]{1,0:T(8,128)S(1)} collective-permute-done((f32[8,1664]{1,0:T(8,128)S(1)}, f32[8,1664]{1,0:T(8,128)S(1)}, u32[]{:S(2)}, u32[]{:S(2)}) %collective-permute-start.43) | collective-permute-done | bytes 53280 | tf_op jit(solution)/shard_map/ppermute | solution.py:22
  95.3 1.2 %coarse.5.refs_0_ = f32[8,896]{1,0:T(8,128)S(1)} custom-call(s32[3]{0:T(128)S(1)} %pad_add_fusion.info_ref, f32[8,1664]{1,0:T(8,128)S(1)} %add_add_fusion.mine_ref, f32[8,1664]{1,0:T(8,128)S(1)} %collective-permute-done.43.other_ref, bf16[1536,768]{1,0:T(8,128)(2,1)S(1)} %get-tuple-element.83.table_ref), custom_call_target="tpu_custom_call" | custom-call | flops 1024 | bytes 1024 | tf_op jit(solution)/shard_map/coarse/pallas_call | solution.py:622
  96.6 2.5 %collective-permute-start.46 = (f32[8,896]{1,0:T(8,128)S(1)}, f32[8,896]{1,0:T(8,128)S(1)}, u32[]{:S(2)}, u32[]{:S(2)}) collective-permute-start(f32[8,896]{1,0:T(8,128)S(1)} %coarse.5.refs_0_), channel_id=1, source_target_pairs={{0,6},{1,7},{2,4},{3,5},{4,2},{5,3},{6,0},{7,1},{8,14},{9,15},{10,... | collective-permute-start | bytes 86024 | tf_op jit(solution)/shard_map/ppermute | solution.py:22
  99.0 1.9 %collective-permute-start.44 = (f32[8,896]{1,0:T(8,128)S(1)}, f32[8,896]{1,0:T(8,128)S(1)}, u32[]{:S(2)}, u32[]{:S(2)}) collective-permute-start(f32[8,896]{1,0:T(8,128)S(1)} %coarse.5.refs_0_), channel_id=1, source_target_pairs={{0,2},{1,3},{2,0},{3,1},{4,6},{5,7},{6,4},{7,5},{8,10},{9,11},{10,... | collective-permute-start | bytes 86024 | tf_op jit(solution)/shard_map/ppermute | solution.py:22
  101.0 1.3 %collective-permute-done.46.refs_3_ = f32[8,896]{1,0:T(8,128)S(1)} collective-permute-done((f32[8,896]{1,0:T(8,128)S(1)}, f32[8,896]{1,0:T(8,128)S(1)}, u32[]{:S(2)}, u32[]{:S(2)}) %collective-permute-start.46) | collective-permute-done | bytes 28704 | tf_op jit(solution)/shard_map/ppermute | solution.py:22
  102.2 1.5 %collective-permute-done.45.refs_2_ = f32[8,896]{1,0:T(8,128)S(1)} collective-permute-done((f32[8,896]{1,0:T(8,128)S(1)}, f32[8,896]{1,0:T(8,128)S(1)}, u32[]{:S(2)}, u32[]{:S(2)}) %collective-permute-start.45) | collective-permute-done | bytes 28704 | tf_op jit(solution)/shard_map/ppermute | solution.py:22
  103.8 2.3 %step.5 = (f32[1,1,5,16,4,128]{5,4,3,2,1,0:T(4,128)}, f32[1,1,5,16,4,128]{5,4,3,2,1,0:T(4,128)}) custom-call(s32[3]{0:T(128)S(1)} %pad_add_fusion.info_ref, s32[1,1,4,5]{3,2,1,0:T(4,128)S(1)} %copy-done.1, f32[5,16,512]{2,1,0:T(8,128)S(1)} %get-tuple-element.100.own_ref, f32[5,16,512]{2,1,0:T(8,128)S(1)} %collective-permute-done.35.facing_ref, ...), custom_call_target="tpu_custom_call" | custom-call | flops 1024 | bytes 1024 | tf_op jit(solution)/shard_map/step/pallas_call | solution.py:633
  (75 shorter events, 12.8 us)
Async XLA Ops:
  2.2 9.9 %collective-permute-start = (f32[128,512]{1,0:T(8,128)S(1)}, f32[128,512]{1,0:T(8,128)S(1)}, u32[]{:S(2)}, u32[]{:S(2)}) collective-permute-start(f32[128,512]{1,0:T(8,128)S(1)} %pack.1), channel_id=1, source_target_pairs={{0,1},{1,2},{2,3},{3,4},{4,5},{5,6},{6,7},{7,0},{8,9},{9,10},{10,1... | collective-permute-start | bytes 786440 | tf_op jit(solution)/shard_map/ppermute | solution.py:17
  2.8 17.1 %collective-permute-start.4 = (f32[48,1536]{1,0:T(8,128)}, f32[48,1536]{1,0:T(8,128)S(1)}, u32[]{:S(2)}, u32[]{:S(2)}) collective-permute-start(f32[48,1536]{1,0:T(8,128)} %refs_0_), channel_id=1, source_target_pairs={{0,24},{1,25},{2,26},{3,27},{4,28},{5,29},{6,30},{7,31},{8,16},{9,... | collective-permute-start | bytes 884744 | tf_op jit(solution)/shard_map/ppermute | solution.py:22
  6.3 14.4 %collective-permute-start.3 = (f32[48,1536]{1,0:T(8,128)}, f32[48,1536]{1,0:T(8,128)S(1)}, u32[]{:S(2)}, u32[]{:S(2)}) collective-permute-start(f32[48,1536]{1,0:T(8,128)} %refs_0_), channel_id=1, source_target_pairs={{0,16},{1,17},{2,18},{3,19},{4,20},{5,21},{6,22},{7,23},{8,24},{9,... | collective-permute-start | bytes 884744 | tf_op jit(solution)/shard_map/ppermute | solution.py:22
  6.8 15.9 %collective-permute-start.2 = (f32[48,1536]{1,0:T(8,128)}, f32[48,1536]{1,0:T(8,128)S(1)}, u32[]{:S(2)}, u32[]{:S(2)}) collective-permute-start(f32[48,1536]{1,0:T(8,128)} %refs_0_), channel_id=1, source_target_pairs={{0,8},{1,9},{2,10},{3,11},{4,12},{5,13},{6,14},{7,15},{8,0},{9,1},... | collective-permute-start | bytes 884744 | tf_op jit(solution)/shard_map/ppermute | solution.py:22
  13.6 9.1 %collective-permute-start.1 = (f32[5,16,512]{2,1,0:T(8,128)S(1)}, f32[5,16,512]{2,1,0:T(8,128)S(1)}, u32[]{:S(2)}, u32[]{:S(2)}) collective-permute-start(f32[5,16,512]{2,1,0:T(8,128)S(1)} %get-tuple-element.62), channel_id=1, source_target_pairs={{0,7},{1,0},{2,1},{3,2},{4,3},{5,4},{6,5},{7,6},{8,15},{9,8},{10,9... | collective-permute-start | bytes 491528 | tf_op jit(solution)/shard_map/ppermute | solution.py:17
  16.5 1.2 %collective-permute-start.10 = (f32[8,1664]{1,0:T(8,128)S(1)}, f32[8,1664]{1,0:T(8,128)S(1)}, u32[]{:S(2)}, u32[]{:S(2)}) collective-permute-start(f32[8,1664]{1,0:T(8,128)S(1)} %get-tuple-element.81), channel_id=1, source_target_pairs={{0,1},{1,0},{2,3},{3,2},{4,5},{5,4},{6,7},{7,6},{8,9},{9,8},{10,11... | collective-permute-start | bytes 159752 | tf_op jit(solution)/shard_map/ppermute | solution.py:22
  17.7 10.7 %collective-permute-start.13 = (f32[8,1664]{1,0:T(8,128)S(1)}, f32[8,1664]{1,0:T(8,128)S(1)}, u32[]{:S(2)}, u32[]{:S(2)}) collective-permute-start(f32[8,1664]{1,0:T(8,128)S(1)} %add.78), channel_id=1, source_target_pairs={{0,6},{1,7},{2,4},{3,5},{4,2},{5,3},{6,0},{7,1},{8,14},{9,15},{10,... | collective-permute-start | bytes 159752 | tf_op jit(solution)/shard_map/ppermute | solution.py:22
  19.8 8.6 %collective-permute-start.12 = (f32[8,1664]{1,0:T(8,128)S(1)}, f32[8,1664]{1,0:T(8,128)S(1)}, u32[]{:S(2)}, u32[]{:S(2)}) collective-permute-start(f32[8,1664]{1,0:T(8,128)S(1)} %add.78), channel_id=1, source_target_pairs={{0,4},{1,5},{2,6},{3,7},{4,0},{5,1},{6,2},{7,3},{8,12},{9,13},{10,... | collective-permute-start | bytes 159752 | tf_op jit(solution)/shard_map/ppermute | solution.py:22
  20.6 7.8 %collective-permute-start.11 = (f32[8,1664]{1,0:T(8,128)S(1)}, f32[8,1664]{1,0:T(8,128)S(1)}, u32[]{:S(2)}, u32[]{:S(2)}) collective-permute-start(f32[8,1664]{1,0:T(8,128)S(1)} %add.78), channel_id=1, source_target_pairs={{0,2},{1,3},{2,0},{3,1},{4,6},{5,7},{6,4},{7,5},{8,10},{9,11},{10,... | collective-permute-start | bytes 159752 | tf_op jit(solution)/shard_map/ppermute | solution.py:22
  22.7 9.3 %copy-start = (f32[48,1536]{1,0:T(8,128)S(1)}, f32[48,1536]{1,0:T(8,128)}, u32[]{:S(2)}) copy-start(f32[48,1536]{1,0:T(8,128)} %refs_0_) | copy-start | bytes 884740
  28.5 5.2 %collective-permute-start.16 = (f32[8,1664]{1,0:T(8,128)S(1)}, f32[8,1664]{1,0:T(8,128)S(1)}, u32[]{:S(2)}, u32[]{:S(2)}) collective-permute-start(f32[8,1664]{1,0:T(8,128)S(1)} %add_add_fusion.5), channel_id=1, source_target_pairs={{0,24},{1,25},{2,26},{3,27},{4,28},{5,29},{6,30},{7,31},{8,16},{9,... | collective-permute-start | bytes 159752 | tf_op jit(solution)/shard_map/ppermute | solution.py:22
  30.7 4.1 %collective-permute-start.15 = (f32[8,1664]{1,0:T(8,128)S(1)}, f32[8,1664]{1,0:T(8,128)S(1)}, u32[]{:S(2)}, u32[]{:S(2)}) collective-permute-start(f32[8,1664]{1,0:T(8,128)S(1)} %add_add_fusion.5), channel_id=1, source_target_pairs={{0,16},{1,17},{2,18},{3,19},{4,20},{5,21},{6,22},{7,23},{8,24},{9,... | collective-permute-start | bytes 159752 | tf_op jit(solution)/shard_map/ppermute | solution.py:22
  31.5 4.1 %collective-permute-start.14 = (f32[8,1664]{1,0:T(8,128)S(1)}, f32[8,1664]{1,0:T(8,128)S(1)}, u32[]{:S(2)}, u32[]{:S(2)}) collective-permute-start(f32[8,1664]{1,0:T(8,128)S(1)} %add_add_fusion.5), channel_id=1, source_target_pairs={{0,8},{1,9},{2,10},{3,11},{4,12},{5,13},{6,14},{7,15},{8,0},{9,1},... | collective-permute-start | bytes 159752 | tf_op jit(solution)/shard_map/ppermute | solution.py:22
  32.0 3.6 %collective-permute-start.6 = (f32[48,1536]{1,0:T(8,128)S(1)}, f32[48,1536]{1,0:T(8,128)S(1)}, u32[]{:S(2)}, u32[]{:S(2)}) collective-permute-start(f32[48,1536]{1,0:T(8,128)S(1)} %copy-done), channel_id=1, source_target_pairs={{0,1},{1,0},{2,3},{3,2},{4,5},{5,4},{6,7},{7,6},{8,9},{9,8},{10,11... | collective-permute-start | bytes 884744 | tf_op jit(solution)/shard_map/ppermute | solution.py:22
  32.0 4.3 %collective-permute-start.7 = (f32[48,1536]{1,0:T(8,128)S(1)}, f32[48,1536]{1,0:T(8,128)S(1)}, u32[]{:S(2)}, u32[]{:S(2)}) collective-permute-start(f32[48,1536]{1,0:T(8,128)S(1)} %collective-permute-done.2.refs_1_), channel_id=1, source_target_pairs={{0,1},{1,0},{2,3},{3,2},{4,5},{5,4},{6,7},{7,6},{8,9},{9,8},{10,11... | collective-permute-start | bytes 884744 | tf_op jit(solution)/shard_map/ppermute | solution.py:22
  33.7 2.6 %collective-permute-start.8 = (f32[48,1536]{1,0:T(8,128)S(1)}, f32[48,1536]{1,0:T(8,128)S(1)}, u32[]{:S(2)}, u32[]{:S(2)}) collective-permute-start(f32[48,1536]{1,0:T(8,128)S(1)} %collective-permute-done.3.refs_2_), channel_id=1, source_target_pairs={{0,1},{1,0},{2,3},{3,2},{4,5},{5,4},{6,7},{7,6},{8,9},{9,8},{10,11... | collective-permute-start | bytes 884744 | tf_op jit(solution)/shard_map/ppermute | solution.py:22
  34.8 1.6 %collective-permute-start.9 = (f32[48,1536]{1,0:T(8,128)S(1)}, f32[48,1536]{1,0:T(8,128)S(1)}, u32[]{:S(2)}, u32[]{:S(2)}) collective-permute-start(f32[48,1536]{1,0:T(8,128)S(1)} %collective-permute-done.4.refs_3_), channel_id=1, source_target_pairs={{0,1},{1,0},{2,3},{3,2},{4,5},{5,4},{6,7},{7,6},{8,9},{9,8},{10,11... | collective-permute-start | bytes 884744 | tf_op jit(solution)/shard_map/ppermute | solution.py:22
  35.6 8.1 %collective-permute-start.5 = (f32[5,16,512]{2,1,0:T(8,128)S(1)}, f32[5,16,512]{2,1,0:T(8,128)S(1)}, u32[]{:S(2)}, u32[]{:S(2)}) collective-permute-start(f32[5,16,512]{2,1,0:T(8,128)S(1)} %get-tuple-element.68), channel_id=1, source_target_pairs={{0,1},{1,2},{2,3},{3,4},{4,5},{5,6},{6,7},{7,0},{8,9},{9,10},{10,1... | collective-permute-start | bytes 491528 | tf_op jit(solution)/shard_map/ppermute | solution.py:17
  35.6 2.4 %collective-permute-start.17 = (f32[8,1664]{1,0:T(8,128)S(1)}, f32[8,1664]{1,0:T(8,128)S(1)}, u32[]{:S(2)}, u32[]{:S(2)}) collective-permute-start(f32[8,1664]{1,0:T(8,128)S(1)} %add_add_fusion.4.mine_ref), channel_id=1, source_target_pairs={{0,1},{1,0},{2,3},{3,2},{4,5},{5,4},{6,7},{7,6},{8,9},{9,8},{10,11... | collective-permute-start | bytes 159752 | tf_op jit(solution)/shard_map/ppermute | solution.py:22
  39.3 5.7 %collective-permute-start.20 = (f32[8,896]{1,0:T(8,128)S(1)}, f32[8,896]{1,0:T(8,128)S(1)}, u32[]{:S(2)}, u32[]{:S(2)}) collective-permute-start(f32[8,896]{1,0:T(8,128)S(1)} %coarse.3.refs_0_), channel_id=1, source_target_pairs={{0,6},{1,7},{2,4},{3,5},{4,2},{5,3},{6,0},{7,1},{8,14},{9,15},{10,... | collective-permute-start | bytes 86024 | tf_op jit(solution)/shard_map/ppermute | solution.py:22
  42.6 4.8 %collective-permute-start.19 = (f32[8,896]{1,0:T(8,128)S(1)}, f32[8,896]{1,0:T(8,128)S(1)}, u32[]{:S(2)}, u32[]{:S(2)}) collective-permute-start(f32[8,896]{1,0:T(8,128)S(1)} %coarse.3.refs_0_), channel_id=1, source_target_pairs={{0,4},{1,5},{2,6},{3,7},{4,0},{5,1},{6,2},{7,3},{8,12},{9,13},{10,... | collective-permute-start | bytes 86024 | tf_op jit(solution)/shard_map/ppermute | solution.py:22
  42.7 4.7 %collective-permute-start.18 = (f32[8,896]{1,0:T(8,128)S(1)}, f32[8,896]{1,0:T(8,128)S(1)}, u32[]{:S(2)}, u32[]{:S(2)}) collective-permute-start(f32[8,896]{1,0:T(8,128)S(1)} %coarse.3.refs_0_), channel_id=1, source_target_pairs={{0,2},{1,3},{2,0},{3,1},{4,6},{5,7},{6,4},{7,5},{8,10},{9,11},{10,... | collective-permute-start | bytes 86024 | tf_op jit(solution)/shard_map/ppermute | solution.py:22
  49.2 6.2 %collective-permute-start.21 = (f32[5,16,512]{2,1,0:T(8,128)S(1)}, f32[5,16,512]{2,1,0:T(8,128)S(1)}, u32[]{:S(2)}, u32[]{:S(2)}) collective-permute-start(f32[5,16,512]{2,1,0:T(8,128)S(1)} %get-tuple-element.85), channel_id=1, source_target_pairs={{0,7},{1,0},{2,1},{3,2},{4,3},{5,4},{6,5},{7,6},{8,15},{9,8},{10,9... | collective-permute-start | bytes 491528 | tf_op jit(solution)/shard_map/ppermute | solution.py:17
  49.5 1.5 %collective-permute-start.23 = (f32[8,1664]{1,0:T(8,128)S(1)}, f32[8,1664]{1,0:T(8,128)S(1)}, u32[]{:S(2)}, u32[]{:S(2)}) collective-permute-start(f32[8,1664]{1,0:T(8,128)S(1)} %get-tuple-element.92), channel_id=1, source_target_pairs={{0,1},{1,0},{2,3},{3,2},{4,5},{5,4},{6,7},{7,6},{8,9},{9,8},{10,11... | collective-permute-start | bytes 159752 | tf_op jit(solution)/shard_map/ppermute | solution.py:22
  50.9 7.7 %collective-permute-start.26 = (f32[8,1664]{1,0:T(8,128)S(1)}, f32[8,1664]{1,0:T(8,128)S(1)}, u32[]{:S(2)}, u32[]{:S(2)}) collective-permute-start(f32[8,1664]{1,0:T(8,128)S(1)} %add.86), channel_id=1, source_target_pairs={{0,6},{1,7},{2,4},{3,5},{4,2},{5,3},{6,0},{7,1},{8,14},{9,15},{10,... | collective-permute-start | bytes 159752 | tf_op jit(solution)/shard_map/ppermute | solution.py:22
  52.5 6.9 %collective-permute-start.25 = (f32[8,1664]{1,0:T(8,128)S(1)}, f32[8,1664]{1,0:T(8,128)S(1)}, u32[]{:S(2)}, u32[]{:S(2)}) collective-permute-start(f32[8,1664]{1,0:T(8,128)S(1)} %add.86), channel_id=1, source_target_pairs={{0,4},{1,5},{2,6},{3,7},{4,0},{5,1},{6,2},{7,3},{8,12},{9,13},{10,... | collective-permute-start | bytes 159752 | tf_op jit(solution)/shard_map/ppermute | solution.py:22
  53.1 6.2 %collective-permute-start.24 = (f32[8,1664]{1,0:T(8,128)S(1)}, f32[8,1664]{1,0:T(8,128)S(1)}, u32[]{:S(2)}, u32[]{:S(2)}) collective-permute-start(f32[8,1664]{1,0:T(8,128)S(1)} %add.86), channel_id=1, source_target_pairs={{0,2},{1,3},{2,0},{3,1},{4,6},{5,7},{6,4},{7,5},{8,10},{9,11},{10,... | collective-permute-start | bytes 159752 | tf_op jit(solution)/shard_map/ppermute | solution.py:22
  59.4 5.2 %collective-permute-start.29 = (f32[8,1664]{1,0:T(8,128)S(1)}, f32[8,1664]{1,0:T(8,128)S(1)}, u32[]{:S(2)}, u32[]{:S(2)}) collective-permute-start(f32[8,1664]{1,0:T(8,128)S(1)} %add_add_fusion.3), channel_id=1, source_target_pairs={{0,24},{1,25},{2,26},{3,27},{4,28},{5,29},{6,30},{7,31},{8,16},{9,... | collective-permute-start | bytes 159752 | tf_op jit(solution)/shard_map/ppermute | solution.py:22
  60.9 4.3 %collective-permute-start.28 = (f32[8,1664]{1,0:T(8,128)S(1)}, f32[8,1664]{1,0:T(8,128)S(1)}, u32[]{:S(2)}, u32[]{:S(2)}) collective-permute-start(f32[8,1664]{1,0:T(8,128)S(1)} %add_add_fusion.3), channel_id=1, source_target_pairs={{0,16},{1,17},{2,18},{3,19},{4,20},{5,21},{6,22},{7,23},{8,24},{9,... | collective-permute-start | bytes 159752 | tf_op jit(solution)/shard_map/ppermute | solution.py:22
  61.4 4.1 %collective-permute-start.27 = (f32[8,1664]{1,0:T(8,128)S(1)}, f32[8,1664]{1,0:T(8,128)S(1)}, u32[]{:S(2)}, u32[]{:S(2)}) collective-permute-start(f32[8,1664]{1,0:T(8,128)S(1)} %add_add_fusion.3), channel_id=1, source_target_pairs={{0,8},{1,9},{2,10},{3,11},{4,12},{5,13},{6,14},{7,15},{8,0},{9,1},... | collective-permute-start | bytes 159752 | tf_op jit(solution)/shard_map/ppermute | solution.py:22
  62.9 12.0 %collective-permute-start.22 = (f32[5,16,512]{2,1,0:T(8,128)S(1)}, f32[5,16,512]{2,1,0:T(8,128)S(1)}, u32[]{:S(2)}, u32[]{:S(2)}) collective-permute-start(f32[5,16,512]{2,1,0:T(8,128)S(1)} %get-tuple-element.89), channel_id=1, source_target_pairs={{0,1},{1,2},{2,3},{3,4},{4,5},{5,6},{6,7},{7,0},{8,9},{9,10},{10,1... | collective-permute-start | bytes 491528 | tf_op jit(solution)/shard_map/ppermute | solution.py:17
  65.6 1.3 %collective-permute-start.30 = (f32[8,1664]{1,0:T(8,128)S(1)}, f32[8,1664]{1,0:T(8,128)S(1)}, u32[]{:S(2)}, u32[]{:S(2)}) collective-permute-start(f32[8,1664]{1,0:T(8,128)S(1)} %add_add_fusion.2.mine_ref), channel_id=1, source_target_pairs={{0,1},{1,0},{2,3},{3,2},{4,5},{5,4},{6,7},{7,6},{8,9},{9,8},{10,11... | collective-permute-start | bytes 159752 | tf_op jit(solution)/shard_map/ppermute | solution.py:22
  68.1 5.7 %collective-permute-start.33 = (f32[8,896]{1,0:T(8,128)S(1)}, f32[8,896]{1,0:T(8,128)S(1)}, u32[]{:S(2)}, u32[]{:S(2)}) collective-permute-start(f32[8,896]{1,0:T(8,128)S(1)} %coarse.4.refs_0_), channel_id=1, source_target_pairs={{0,6},{1,7},{2,4},{3,5},{4,2},{5,3},{6,0},{7,1},{8,14},{9,15},{10,... | collective-permute-start | bytes 86024 | tf_op jit(solution)/shard_map/ppermute | solution.py:22
  70.1 4.8 %collective-permute-start.32 = (f32[8,896]{1,0:T(8,128)S(1)}, f32[8,896]{1,0:T(8,128)S(1)}, u32[]{:S(2)}, u32[]{:S(2)}) collective-permute-start(f32[8,896]{1,0:T(8,128)S(1)} %coarse.4.refs_0_), channel_id=1, source_target_pairs={{0,4},{1,5},{2,6},{3,7},{4,0},{5,1},{6,2},{7,3},{8,12},{9,13},{10,... | collective-permute-start | bytes 86024 | tf_op jit(solution)/shard_map/ppermute | solution.py:22
  70.1 4.8 %collective-permute-start.31 = (f32[8,896]{1,0:T(8,128)S(1)}, f32[8,896]{1,0:T(8,128)S(1)}, u32[]{:S(2)}, u32[]{:S(2)}) collective-permute-start(f32[8,896]{1,0:T(8,128)S(1)} %coarse.4.refs_0_), channel_id=1, source_target_pairs={{0,2},{1,3},{2,0},{3,1},{4,6},{5,7},{6,4},{7,5},{8,10},{9,11},{10,... | collective-permute-start | bytes 86024 | tf_op jit(solution)/shard_map/ppermute | solution.py:22
  76.8 6.5 %collective-permute-start.34 = (f32[5,16,512]{2,1,0:T(8,128)S(1)}, f32[5,16,512]{2,1,0:T(8,128)S(1)}, u32[]{:S(2)}, u32[]{:S(2)}) collective-permute-start(f32[5,16,512]{2,1,0:T(8,128)S(1)} %get-tuple-element.99), channel_id=1, source_target_pairs={{0,7},{1,0},{2,1},{3,2},{4,3},{5,4},{6,5},{7,6},{8,15},{9,8},{10,9... | collective-permute-start | bytes 491528 | tf_op jit(solution)/shard_map/ppermute | solution.py:17
  77.6 1.2 %collective-permute-start.36 = (f32[8,1664]{1,0:T(8,128)S(1)}, f32[8,1664]{1,0:T(8,128)S(1)}, u32[]{:S(2)}, u32[]{:S(2)}) collective-permute-start(f32[8,1664]{1,0:T(8,128)S(1)} %get-tuple-element.104), channel_id=1, source_target_pairs={{0,1},{1,0},{2,3},{3,2},{4,5},{5,4},{6,7},{7,6},{8,9},{9,8},{10,11... | collective-permute-start | bytes 159752 | tf_op jit(solution)/shard_map/ppermute | solution.py:22
  78.8 7.7 %collective-permute-start.39 = (f32[8,1664]{1,0:T(8,128)S(1)}, f32[8,1664]{1,0:T(8,128)S(1)}, u32[]{:S(2)}, u32[]{:S(2)}) collective-permute-start(f32[8,1664]{1,0:T(8,128)S(1)} %add.94), channel_id=1, source_target_pairs={{0,6},{1,7},{2,4},{3,5},{4,2},{5,3},{6,0},{7,1},{8,14},{9,15},{10,... | collective-permute-start | bytes 159752 | tf_op jit(solution)/shard_map/ppermute | solution.py:22
  80.2 6.7 %collective-permute-start.38 = (f32[8,1664]{1,0:T(8,128)S(1)}, f32[8,1664]{1,0:T(8,128)S(1)}, u32[]{:S(2)}, u32[]{:S(2)}) collective-permute-start(f32[8,1664]{1,0:T(8,128)S(1)} %add.94), channel_id=1, source_target_pairs={{0,4},{1,5},{2,6},{3,7},{4,0},{5,1},{6,2},{7,3},{8,12},{9,13},{10,... | collective-permute-start | bytes 159752 | tf_op jit(solution)/shard_map/ppermute | solution.py:22
  81.3 5.5 %collective-permute-start.37 = (f32[8,1664]{1,0:T(8,128)S(1)}, f32[8,1664]{1,0:T(8,128)S(1)}, u32[]{:S(2)}, u32[]{:S(2)}) collective-permute-start(f32[8,1664]{1,0:T(8,128)S(1)} %add.94), channel_id=1, source_target_pairs={{0,2},{1,3},{2,0},{3,1},{4,6},{5,7},{6,4},{7,5},{8,10},{9,11},{10,... | collective-permute-start | bytes 159752 | tf_op jit(solution)/shard_map/ppermute | solution.py:22
  86.9 5.2 %collective-permute-start.42 = (f32[8,1664]{1,0:T(8,128)S(1)}, f32[8,1664]{1,0:T(8,128)S(1)}, u32[]{:S(2)}, u32[]{:S(2)}) collective-permute-start(f32[8,1664]{1,0:T(8,128)S(1)} %add_add_fusion.1), channel_id=1, source_target_pairs={{0,24},{1,25},{2,26},{3,27},{4,28},{5,29},{6,30},{7,31},{8,16},{9,... | collective-permute-start | bytes 159752 | tf_op jit(solution)/shard_map/ppermute | solution.py:22
  89.1 4.1 %collective-permute-start.41 = (f32[8,1664]{1,0:T(8,128)S(1)}, f32[8,1664]{1,0:T(8,128)S(1)}, u32[]{:S(2)}, u32[]{:S(2)}) collective-permute-start(f32[8,1664]{1,0:T(8,128)S(1)} %add_add_fusion.1), channel_id=1, source_target_pairs={{0,16},{1,17},{2,18},{3,19},{4,20},{5,21},{6,22},{7,23},{8,24},{9,... | collective-permute-start | bytes 159752 | tf_op jit(solution)/shard_map/ppermute | solution.py:22
  89.9 4.1 %collective-permute-start.40 = (f32[8,1664]{1,0:T(8,128)S(1)}, f32[8,1664]{1,0:T(8,128)S(1)}, u32[]{:S(2)}, u32[]{:S(2)}) collective-permute-start(f32[8,1664]{1,0:T(8,128)S(1)} %add_add_fusion.1), channel_id=1, source_target_pairs={{0,8},{1,9},{2,10},{3,11},{4,12},{5,13},{6,14},{7,15},{8,0},{9,1},... | collective-permute-start | bytes 159752 | tf_op jit(solution)/shard_map/ppermute | solution.py:22
  90.4 13.3 %collective-permute-start.35 = (f32[5,16,512]{2,1,0:T(8,128)S(1)}, f32[5,16,512]{2,1,0:T(8,128)S(1)}, u32[]{:S(2)}, u32[]{:S(2)}) collective-permute-start(f32[5,16,512]{2,1,0:T(8,128)S(1)} %get-tuple-element.101), channel_id=1, source_target_pairs={{0,1},{1,2},{2,3},{3,4},{4,5},{5,6},{6,7},{7,0},{8,9},{9,10},{10,1... | collective-permute-start | bytes 491528 | tf_op jit(solution)/shard_map/ppermute | solution.py:17
  94.0 1.3 %collective-permute-start.43 = (f32[8,1664]{1,0:T(8,128)S(1)}, f32[8,1664]{1,0:T(8,128)S(1)}, u32[]{:S(2)}, u32[]{:S(2)}) collective-permute-start(f32[8,1664]{1,0:T(8,128)S(1)} %add_add_fusion.mine_ref), channel_id=1, source_target_pairs={{0,1},{1,0},{2,3},{3,2},{4,5},{5,4},{6,7},{7,6},{8,9},{9,8},{10,11... | collective-permute-start | bytes 159752 | tf_op jit(solution)/shard_map/ppermute | solution.py:22
  96.6 5.7 %collective-permute-start.46 = (f32[8,896]{1,0:T(8,128)S(1)}, f32[8,896]{1,0:T(8,128)S(1)}, u32[]{:S(2)}, u32[]{:S(2)}) collective-permute-start(f32[8,896]{1,0:T(8,128)S(1)} %coarse.5.refs_0_), channel_id=1, source_target_pairs={{0,6},{1,7},{2,4},{3,5},{4,2},{5,3},{6,0},{7,1},{8,14},{9,15},{10,... | collective-permute-start | bytes 86024 | tf_op jit(solution)/shard_map/ppermute | solution.py:22
  99.0 4.8 %collective-permute-start.45 = (f32[8,896]{1,0:T(8,128)S(1)}, f32[8,896]{1,0:T(8,128)S(1)}, u32[]{:S(2)}, u32[]{:S(2)}) collective-permute-start(f32[8,896]{1,0:T(8,128)S(1)} %coarse.5.refs_0_), channel_id=1, source_target_pairs={{0,4},{1,5},{2,6},{3,7},{4,0},{5,1},{6,2},{7,3},{8,12},{9,13},{10,... | collective-permute-start | bytes 86024 | tf_op jit(solution)/shard_map/ppermute | solution.py:22
  99.0 4.8 %collective-permute-start.44 = (f32[8,896]{1,0:T(8,128)S(1)}, f32[8,896]{1,0:T(8,128)S(1)}, u32[]{:S(2)}, u32[]{:S(2)}) collective-permute-start(f32[8,896]{1,0:T(8,128)S(1)} %coarse.5.refs_0_), channel_id=1, source_target_pairs={{0,2},{1,3},{2,0},{3,1},{4,6},{5,7},{6,4},{7,5},{8,10},{9,11},{10,... | collective-permute-start | bytes 86024 | tf_op jit(solution)/shard_map/ppermute | solution.py:22
  (2 other events, 10.4 us)

commit v7 on v6

--- a/solution.py
+++ b/solution.py
@@ -42,8 +42,8 @@
 
 def through_table(x, table):
     rows = x.shape[0]
-    full = matmul(stacked(x, 3), table)
-    return full[2 * rows :] + full[rows : 2 * rows] + full[:rows]
+    full = matmul(stacked(x, 2), table)
+    return full[rows:] + full[:rows]
 
 
 def slot_mask(slots, loads, corners):
@@ -433,12 +433,12 @@
     load = jnp.concatenate([low, high], axis=1)
     loads, size = load.shape
     per_level = table_ref.shape[1] // 2
-    full = matmul(stacked(load, 3), table_ref[...])
+    full = matmul(stacked(load, 2), table_ref[...])
 
     def part(i, j):
         return full[i * loads : (i + 1) * loads, j * per_level : (j + 1) * per_level]
 
-    answer = ((part(2, 0) + part(1, 1)) + (part(1, 0) + part(0, 1))) + part(0, 0)
+    answer = (part(1, 1) + (part(1, 0) + part(0, 1))) + part(0, 0)
     own = load[:, :per_level]
     for level in range(1, levels):
         own = jnp.where(info_ref[2] == level, load[:, level * per_level : (level + 1) * per_level], own)

time: 106 us -> 106 us (level)
  no operation moved by 1% of the time
where the time goes in v7:
time: 106 us
  starting transfers between devices  47.3 us (45%)
  Pallas kernels  30.9 us (29%)
  waiting for transfers between devices  26.1 us (25%)
  between operations  1.48 us (1%)
    ppermute x40, starting transfers between devices, swapped(): return lax.ppermute(x, BOTH, [(i, i ^ bits) for i in range(devices)])  42.9 us
    ppermute x40, waiting for transfers between devices, swapped(): return lax.ppermute(x, BOTH, [(i, i ^ bits) for i in range(devices)])  26.1 us
    pallas_call x2, Pallas kernels, local(): pl.pallas_call(flex_kernel, out_shape=(state, state, half_load), in_specs...  6.43 us
    pallas_call x3, Pallas kernels, local(): pl.pallas_call(functools.partial(step_kernel, corners, levels, first, las...  6 us
    pallas_call x1, Pallas kernels, local(): pl.pallas_call(flex_first_kernel, out_shape=(state, state, half_load) + h...  5.7 us
    pallas_call x1, Pallas kernels, local(): pl.pallas_call(prepare_kernel, out_shape=half_pieces + (shape_of(slots *...  5.18 us
    ppermute x7, starting transfers between devices, shifted(): lax.ppermute(x, axis, [(i, (i + by) % devices) for i in range(devices)])  4.43 us
    pallas_call x3, Pallas kernels, local(): pl.pallas_call(functools.partial(coarse_kernel, rows, levels), out_shape=...  3.6 us
  transfers between devices with their start and end apart: 47, of which 24 were waited for; matrix products, arithmetic and copies ran while one was open for 0% of the time, Pallas kernels for 23%

profile of v7, /device:TPU:0, one launch (start us, length us, event | category | flops | bytes accessed | tf_op | source)
XLA Modules:
  0.0 106.0 jit_solution(9465685083054767608)
XLA Ops:
  1.3 1.0 pack.1
  2.8 3.5 %collective-permute-start.4 = (f32[48,1536]{1,0:T(8,128)}, f32[48,1536]{1,0:T(8,128)S(1)}, u32[]{:S(2)}, u32[]{:S(2)}) collective-permute-start(f32[48,1536]{1,0:T(8,128)} %refs_0_), channel_id=1, source_target_pairs={{0,24},{1,25},{2,26},{3,27},{4,28},{5,29},{6,30},{7,31},{8,16},{9,... | collective-permute-start | bytes 884744 | tf_op jit(solution)/shard_map/ppermute | solution.py:22
  7.0 5.2 %prepare.1 = (bf16[5,512,1024]{2,1,0:T(8,128)(2,1)S(1)}, bf16[5,512,1024]{2,1,0:T(8,128)(2,1)S(1)}, s32[20,128]{1,0:T(8,128)S(1)}, s32[20,128]{1,0:T(8,128)S(1)}...) custom-call(s32[3]{0:T(128)S(1)} %pad_add_fusion.info_ref, ...), custom_call_target="tpu_custom_call" | custom-call | flops 1024 | bytes 1024 | tf_op jit(solution)/shard_map/prepare/pallas_call | solution.py:539
  12.2 1.4 %first.1 = (f32[5,512]{1,0:T(8,128)S(1)}, f32[5,16,512]{2,1,0:T(8,128)S(1)}, f32[5,16,512]{2,1,0:T(8,128)S(1)}, f32[5,16,512]{2,1,0:T(8,128)S(1)}, f32[8,1664]{1...) custom-call(s32[3]{0:T(128)S(1)} %pad_add_fusion.info_ref, ...), custom_call_target="tpu_custom_call" | custom-call | flops 1024 | bytes 1024 | tf_op jit(solution)/shard_map/first/pallas_call | solution.py:561
  13.6 2.9 %collective-permute-start.1 = (f32[5,16,512]{2,1,0:T(8,128)S(1)}, f32[5,16,512]{2,1,0:T(8,128)S(1)}, u32[]{:S(2)}, u32[]{:S(2)}) collective-permute-start(f32[5,16,512]{2,1,0:T(8,128)S(1)} %get-tuple-element.62), channel_id=1, source_target_pairs={{0,7},{1,0},{2,1},{3,2},{4,3},{5,4},{6,5},{7,6},{8,15},{9,8},{10,9... | collective-permute-start | bytes 491528 | tf_op jit(solution)/shard_map/ppermute | solution.py:17
  16.5 1.2 %collective-permute-done.10 = f32[8,1664]{1,0:T(8,128)S(1)} collective-permute-done((f32[8,1664]{1,0:T(8,128)S(1)}, f32[8,1664]{1,0:T(8,128)S(1)}, u32[]{:S(2)}, u32[]{:S(2)}) %collective-permute-start.10) | collective-permute-done | bytes 53280 | tf_op jit(solution)/shard_map/ppermute | solution.py:22
  17.7 2.1 %collective-permute-start.13 = (f32[8,1664]{1,0:T(8,128)S(1)}, f32[8,1664]{1,0:T(8,128)S(1)}, u32[]{:S(2)}, u32[]{:S(2)}) collective-permute-start(f32[8,1664]{1,0:T(8,128)S(1)} %add.78), channel_id=1, source_target_pairs={{0,6},{1,7},{2,4},{3,5},{4,2},{5,3},{6,0},{7,1},{8,14},{9,15},{10,... | collective-permute-start | bytes 159752 | tf_op jit(solution)/shard_map/ppermute | solution.py:22
  20.6 2.0 %collective-permute-start.11 = (f32[8,1664]{1,0:T(8,128)S(1)}, f32[8,1664]{1,0:T(8,128)S(1)}, u32[]{:S(2)}, u32[]{:S(2)}) collective-permute-start(f32[8,1664]{1,0:T(8,128)S(1)} %add.78), channel_id=1, source_target_pairs={{0,2},{1,3},{2,0},{3,1},{4,6},{5,7},{6,4},{7,5},{8,10},{9,11},{10,... | collective-permute-start | bytes 159752 | tf_op jit(solution)/shard_map/ppermute | solution.py:22
  22.7 5.7 %flex_first.1 = (f32[5,16,512]{2,1,0:T(8,128)S(1)}, f32[5,16,512]{2,1,0:T(8,128)S(1)}, f32[8,1664]{1,0:T(8,128)S(1)}, bf16[5,512,1024]{2,1,0:T(8,128)(2,1)S(1)}, bf16[5,512,1024]{2,1,0:T(8,128)(2,1)S(1)}) custom-call(f32[5,16,512]{2,1,0:T(8,128)S(1)} %get-tuple-element.61.values_ref.z_ref, f32[5,16,512]{2,1,0:T(8,128)S(1)} %collective-permute-done.1.forces_ref, ...), custom_call_target="tpu_custom_call" | custom-call | flops 1024 | bytes 1024 | tf_op jit(solution)/shard_map/flex_first/pallas_call | solution.py:596
  28.5 2.2 %collective-permute-start.16 = (f32[8,1664]{1,0:T(8,128)S(1)}, f32[8,1664]{1,0:T(8,128)S(1)}, u32[]{:S(2)}, u32[]{:S(2)}) collective-permute-start(f32[8,1664]{1,0:T(8,128)S(1)} %add_add_fusion.5), channel_id=1, source_target_pairs={{0,24},{1,25},{2,26},{3,27},{4,28},{5,29},{6,30},{7,31},{8,16},{9,... | collective-permute-start | bytes 159752 | tf_op jit(solution)/shard_map/ppermute | solution.py:22
  32.5 1.1 %collective-permute-done.16 = f32[8,1664]{1,0:T(8,128)S(1)} collective-permute-done((f32[8,1664]{1,0:T(8,128)S(1)}, f32[8,1664]{1,0:T(8,128)S(1)}, u32[]{:S(2)}, u32[]{:S(2)}) %collective-permute-start.16) | collective-permute-done | bytes 53280 | tf_op jit(solution)/shard_map/ppermute | solution.py:22
  33.7 1.1 %collective-permute-done.15 = f32[8,1664]{1,0:T(8,128)S(1)} collective-permute-done((f32[8,1664]{1,0:T(8,128)S(1)}, f32[8,1664]{1,0:T(8,128)S(1)}, u32[]{:S(2)}, u32[]{:S(2)}) %collective-permute-start.15) | collective-permute-done | bytes 53280 | tf_op jit(solution)/shard_map/ppermute | solution.py:22
  36.4 1.7 %tables.1 = (bf16[256,512]{1,0:T(8,128)(2,1)S(1)}, bf16[1536,256]{1,0:T(8,128)(2,1)S(1)}, bf16[1536,768]{1,0:T(8,128)(2,1)S(1)}) custom-call(s32[3]{0:T(128)S(1)} %pad_add_fusion.info_ref, f32[128,512]{1,0:T(8,128)S(1)} %collective-permute-done.prev_ref.packed_ref, s32[5,1,24]{2,1,0:T(1,128)S(1)} %bitcast.6, f32[48,1536]{1,0:T(8,128)S(1)} %copy-done, ...), custom_call_target="tpu_custom_call" | custom-call | flops 1024 | bytes 1024 | tf_op jit(solution)/shard_map/tables/pallas_call | solution.py:575
  38.1 1.2 %coarse.3.refs_0_ = f32[8,896]{1,0:T(8,128)S(1)} custom-call(s32[3]{0:T(128)S(1)} %pad_add_fusion.info_ref, f32[8,1664]{1,0:T(8,128)S(1)} %add_add_fusion.4.mine_ref, f32[8,1664]{1,0:T(8,128)S(1)} %collective-permute-done.17.other_ref, bf16[1536,768]{1,0:T(8,128)(2,1)S(1)} %get-tuple-element.83.table_ref), custom_call_target="tpu_custom_call" | custom-call | flops 1024 | bytes 1024 | tf_op jit(solution)/shard_map/coarse/pallas_call | solution.py:622
  39.3 3.3 %collective-permute-start.20 = (f32[8,896]{1,0:T(8,128)S(1)}, f32[8,896]{1,0:T(8,128)S(1)}, u32[]{:S(2)}, u32[]{:S(2)}) collective-permute-start(f32[8,896]{1,0:T(8,128)S(1)} %coarse.3.refs_0_), channel_id=1, source_target_pairs={{0,6},{1,7},{2,4},{3,5},{4,2},{5,3},{6,0},{7,1},{8,14},{9,15},{10,... | collective-permute-start | bytes 86024 | tf_op jit(solution)/shard_map/ppermute | solution.py:22
  42.7 1.0 collective-permute-start.18
  43.7 1.3 %collective-permute-done.20.refs_3_ = f32[8,896]{1,0:T(8,128)S(1)} collective-permute-done((f32[8,896]{1,0:T(8,128)S(1)}, f32[8,896]{1,0:T(8,128)S(1)}, u32[]{:S(2)}, u32[]{:S(2)}) %collective-permute-start.20) | collective-permute-done | bytes 28704 | tf_op jit(solution)/shard_map/ppermute | solution.py:22
  45.0 2.4 %collective-permute-done.19.refs_2_ = f32[8,896]{1,0:T(8,128)S(1)} collective-permute-done((f32[8,896]{1,0:T(8,128)S(1)}, f32[8,896]{1,0:T(8,128)S(1)}, u32[]{:S(2)}, u32[]{:S(2)}) %collective-permute-start.19) | collective-permute-done | bytes 28704 | tf_op jit(solution)/shard_map/ppermute | solution.py:22
  47.3 1.9 %step.3 = (f32[5,16,512]{2,1,0:T(8,128)S(1)}, f32[5,16,512]{2,1,0:T(8,128)S(1)}, f32[5,16,512]{2,1,0:T(8,128)S(1)}, f32[5,16,512]{2,1,0:T(8,128)S(1)}, f32[5,16,...) custom-call(s32[3]{0:T(128)S(1)} %pad_add_fusion.info_ref, ...), custom_call_target="tpu_custom_call" | custom-call | flops 1024 | bytes 1024 | tf_op jit(solution)/shard_map/step/pallas_call | solution.py:633
  50.0 1.0 collective-permute-done.23
  50.9 1.5 %collective-permute-start.26 = (f32[8,1664]{1,0:T(8,128)S(1)}, f32[8,1664]{1,0:T(8,128)S(1)}, u32[]{:S(2)}, u32[]{:S(2)}) collective-permute-start(f32[8,1664]{1,0:T(8,128)S(1)} %add.86), channel_id=1, source_target_pairs={{0,6},{1,7},{2,4},{3,5},{4,2},{5,3},{6,0},{7,1},{8,14},{9,15},{10,... | collective-permute-start | bytes 159752 | tf_op jit(solution)/shard_map/ppermute | solution.py:22
  53.1 2.3 %collective-permute-start.24 = (f32[8,1664]{1,0:T(8,128)S(1)}, f32[8,1664]{1,0:T(8,128)S(1)}, u32[]{:S(2)}, u32[]{:S(2)}) collective-permute-start(f32[8,1664]{1,0:T(8,128)S(1)} %add.86), channel_id=1, source_target_pairs={{0,2},{1,3},{2,0},{3,1},{4,6},{5,7},{6,4},{7,5},{8,10},{9,11},{10,... | collective-permute-start | bytes 159752 | tf_op jit(solution)/shard_map/ppermute | solution.py:22
  55.4 3.2 %flex.2 = (f32[5,16,512]{2,1,0:T(8,128)S(1)}, f32[5,16,512]{2,1,0:T(8,128)S(1)}, f32[8,1664]{1,0:T(8,128)S(1)}) custom-call(f32[5,16,512]{2,1,0:T(8,128)S(1)} %get-tuple-element.84.values_ref.z_ref, f32[5,16,512]{2,1,0:T(8,128)S(1)} %collective-permute-done.21.forces_ref, bf16[5,512,1024]{2,1,0:T(8,128)(2,1)S(1)} %get-tuple-element.65.near_large_ref, ...), custom_call_target="tpu_custom_call" | custom-call | flops 1024 | bytes 1024 | tf_op jit(solution)/shard_map/flex/pallas_call | solution.py:608
  59.4 1.6 %collective-permute-start.29 = (f32[8,1664]{1,0:T(8,128)S(1)}, f32[8,1664]{1,0:T(8,128)S(1)}, u32[]{:S(2)}, u32[]{:S(2)}) collective-permute-start(f32[8,1664]{1,0:T(8,128)S(1)} %add_add_fusion.3), channel_id=1, source_target_pairs={{0,24},{1,25},{2,26},{3,27},{4,28},{5,29},{6,30},{7,31},{8,16},{9,... | collective-permute-start | bytes 159752 | tf_op jit(solution)/shard_map/ppermute | solution.py:22
  61.4 1.5 %collective-permute-start.27 = (f32[8,1664]{1,0:T(8,128)S(1)}, f32[8,1664]{1,0:T(8,128)S(1)}, u32[]{:S(2)}, u32[]{:S(2)}) collective-permute-start(f32[8,1664]{1,0:T(8,128)S(1)} %add_add_fusion.3), channel_id=1, source_target_pairs={{0,8},{1,9},{2,10},{3,11},{4,12},{5,13},{6,14},{7,15},{8,0},{9,1},... | collective-permute-start | bytes 159752 | tf_op jit(solution)/shard_map/ppermute | solution.py:22
  62.9 1.6 %collective-permute-done.29 = f32[8,1664]{1,0:T(8,128)S(1)} collective-permute-done((f32[8,1664]{1,0:T(8,128)S(1)}, f32[8,1664]{1,0:T(8,128)S(1)}, u32[]{:S(2)}, u32[]{:S(2)}) %collective-permute-start.29) | collective-permute-done | bytes 53280 | tf_op jit(solution)/shard_map/ppermute | solution.py:22
  65.7 1.2 %collective-permute-done.30.other_ref = f32[8,1664]{1,0:T(8,128)S(1)} collective-permute-done((f32[8,1664]{1,0:T(8,128)S(1)}, f32[8,1664]{1,0:T(8,128)S(1)}, u32[]{:S(2)}, u32[]{:S(2)}) %collective-permute-start.30) | collective-permute-done | bytes 53280 | tf_op jit(solution)/shard_map/ppermute | solution.py:22
  66.9 1.2 %coarse.4.refs_0_ = f32[8,896]{1,0:T(8,128)S(1)} custom-call(s32[3]{0:T(128)S(1)} %pad_add_fusion.info_ref, f32[8,1664]{1,0:T(8,128)S(1)} %add_add_fusion.2.mine_ref, f32[8,1664]{1,0:T(8,128)S(1)} %collective-permute-done.30.other_ref, bf16[1536,768]{1,0:T(8,128)(2,1)S(1)} %get-tuple-element.83.table_ref), custom_call_target="tpu_custom_call" | custom-call | flops 1024 | bytes 1024 | tf_op jit(solution)/shard_map/coarse/pallas_call | solution.py:622
  68.1 2.0 %collective-permute-start.33 = (f32[8,896]{1,0:T(8,128)S(1)}, f32[8,896]{1,0:T(8,128)S(1)}, u32[]{:S(2)}, u32[]{:S(2)}) collective-permute-start(f32[8,896]{1,0:T(8,128)S(1)} %coarse.4.refs_0_), channel_id=1, source_target_pairs={{0,6},{1,7},{2,4},{3,5},{4,2},{5,3},{6,0},{7,1},{8,14},{9,15},{10,... | collective-permute-start | bytes 86024 | tf_op jit(solution)/shard_map/ppermute | solution.py:22
  70.1 2.4 %collective-permute-start.31 = (f32[8,896]{1,0:T(8,128)S(1)}, f32[8,896]{1,0:T(8,128)S(1)}, u32[]{:S(2)}, u32[]{:S(2)}) collective-permute-start(f32[8,896]{1,0:T(8,128)S(1)} %coarse.4.refs_0_), channel_id=1, source_target_pairs={{0,2},{1,3},{2,0},{3,1},{4,6},{5,7},{6,4},{7,5},{8,10},{9,11},{10,... | collective-permute-start | bytes 86024 | tf_op jit(solution)/shard_map/ppermute | solution.py:22
  72.5 1.3 %collective-permute-done.33.refs_3_ = f32[8,896]{1,0:T(8,128)S(1)} collective-permute-done((f32[8,896]{1,0:T(8,128)S(1)}, f32[8,896]{1,0:T(8,128)S(1)}, u32[]{:S(2)}, u32[]{:S(2)}) %collective-permute-start.33) | collective-permute-done | bytes 28704 | tf_op jit(solution)/shard_map/ppermute | solution.py:22
  73.8 1.1 %collective-permute-done.32.refs_2_ = f32[8,896]{1,0:T(8,128)S(1)} collective-permute-done((f32[8,896]{1,0:T(8,128)S(1)}, f32[8,896]{1,0:T(8,128)S(1)}, u32[]{:S(2)}, u32[]{:S(2)}) %collective-permute-start.32) | collective-permute-done | bytes 28704 | tf_op jit(solution)/shard_map/ppermute | solution.py:22
  74.9 1.9 %step.4 = (f32[5,16,512]{2,1,0:T(8,128)S(1)}, f32[5,16,512]{2,1,0:T(8,128)S(1)}, f32[5,16,512]{2,1,0:T(8,128)S(1)}, f32[5,16,512]{2,1,0:T(8,128)S(1)}, f32[5,16,...) custom-call(s32[3]{0:T(128)S(1)} %pad_add_fusion.info_ref, ...), custom_call_target="tpu_custom_call" | custom-call | flops 1024 | bytes 1024 | tf_op jit(solution)/shard_map/step/pallas_call | solution.py:633
  77.6 1.2 %collective-permute-done.36 = f32[8,1664]{1,0:T(8,128)S(1)} collective-permute-done((f32[8,1664]{1,0:T(8,128)S(1)}, f32[8,1664]{1,0:T(8,128)S(1)}, u32[]{:S(2)}, u32[]{:S(2)}) %collective-permute-start.36) | collective-permute-done | bytes 53280 | tf_op jit(solution)/shard_map/ppermute | solution.py:22
  78.8 1.3 %collective-permute-start.39 = (f32[8,1664]{1,0:T(8,128)S(1)}, f32[8,1664]{1,0:T(8,128)S(1)}, u32[]{:S(2)}, u32[]{:S(2)}) collective-permute-start(f32[8,1664]{1,0:T(8,128)S(1)} %add.94), channel_id=1, source_target_pairs={{0,6},{1,7},{2,4},{3,5},{4,2},{5,3},{6,0},{7,1},{8,14},{9,15},{10,... | collective-permute-start | bytes 159752 | tf_op jit(solution)/shard_map/ppermute | solution.py:22
  80.2 1.1 %collective-permute-start.38 = (f32[8,1664]{1,0:T(8,128)S(1)}, f32[8,1664]{1,0:T(8,128)S(1)}, u32[]{:S(2)}, u32[]{:S(2)}) collective-permute-start(f32[8,1664]{1,0:T(8,128)S(1)} %add.94), channel_id=1, source_target_pairs={{0,4},{1,5},{2,6},{3,7},{4,0},{5,1},{6,2},{7,3},{8,12},{9,13},{10,... | collective-permute-start | bytes 159752 | tf_op jit(solution)/shard_map/ppermute | solution.py:22
  81.3 2.0 %collective-permute-start.37 = (f32[8,1664]{1,0:T(8,128)S(1)}, f32[8,1664]{1,0:T(8,128)S(1)}, u32[]{:S(2)}, u32[]{:S(2)}) collective-permute-start(f32[8,1664]{1,0:T(8,128)S(1)} %add.94), channel_id=1, source_target_pairs={{0,2},{1,3},{2,0},{3,1},{4,6},{5,7},{6,4},{7,5},{8,10},{9,11},{10,... | collective-permute-start | bytes 159752 | tf_op jit(solution)/shard_map/ppermute | solution.py:22
  83.3 3.2 %flex.3 = (f32[5,16,512]{2,1,0:T(8,128)S(1)}, f32[5,16,512]{2,1,0:T(8,128)S(1)}, f32[8,1664]{1,0:T(8,128)S(1)}) custom-call(f32[5,16,512]{2,1,0:T(8,128)S(1)} %get-tuple-element.98.values_ref.z_ref, f32[5,16,512]{2,1,0:T(8,128)S(1)} %collective-permute-done.34.forces_ref, bf16[5,512,1024]{2,1,0:T(8,128)(2,1)S(1)} %get-tuple-element.65.near_large_ref, ...), custom_call_target="tpu_custom_call" | custom-call | flops 1024 | bytes 1024 | tf_op jit(solution)/shard_map/flex/pallas_call | solution.py:608
  86.9 2.2 %collective-permute-start.42 = (f32[8,1664]{1,0:T(8,128)S(1)}, f32[8,1664]{1,0:T(8,128)S(1)}, u32[]{:S(2)}, u32[]{:S(2)}) collective-permute-start(f32[8,1664]{1,0:T(8,128)S(1)} %add_add_fusion.1), channel_id=1, source_target_pairs={{0,24},{1,25},{2,26},{3,27},{4,28},{5,29},{6,30},{7,31},{8,16},{9,... | collective-permute-start | bytes 159752 | tf_op jit(solution)/shard_map/ppermute | solution.py:22
  90.4 1.6 %collective-permute-done.42 = f32[8,1664]{1,0:T(8,128)S(1)} collective-permute-done((f32[8,1664]{1,0:T(8,128)S(1)}, f32[8,1664]{1,0:T(8,128)S(1)}, u32[]{:S(2)}, u32[]{:S(2)}) %collective-permute-start.42) | collective-permute-done | bytes 53280 | tf_op jit(solution)/shard_map/ppermute | solution.py:22
  92.0 1.2 %collective-permute-done.41 = f32[8,1664]{1,0:T(8,128)S(1)} collective-permute-done((f32[8,1664]{1,0:T(8,128)S(1)}, f32[8,1664]{1,0:T(8,128)S(1)}, u32[]{:S(2)}, u32[]{:S(2)}) %collective-permute-start.41) | collective-permute-done | bytes 53280 | tf_op jit(solution)/shard_map/ppermute | solution.py:22
  94.1 1.2 %collective-permute-done.43.other_ref = f32[8,1664]{1,0:T(8,128)S(1)} collective-permute-done((f32[8,1664]{1,0:T(8,128)S(1)}, f32[8,1664]{1,0:T(8,128)S(1)}, u32[]{:S(2)}, u32[]{:S(2)}) %collective-permute-start.43) | collective-permute-done | bytes 53280 | tf_op jit(solution)/shard_map/ppermute | solution.py:22
  95.3 1.2 %coarse.5.refs_0_ = f32[8,896]{1,0:T(8,128)S(1)} custom-call(s32[3]{0:T(128)S(1)} %pad_add_fusion.info_ref, f32[8,1664]{1,0:T(8,128)S(1)} %add_add_fusion.mine_ref, f32[8,1664]{1,0:T(8,128)S(1)} %collective-permute-done.43.other_ref, bf16[1536,768]{1,0:T(8,128)(2,1)S(1)} %get-tuple-element.83.table_ref), custom_call_target="tpu_custom_call" | custom-call | flops 1024 | bytes 1024 | tf_op jit(solution)/shard_map/coarse/pallas_call | solution.py:622
  96.5 2.5 %collective-permute-start.46 = (f32[8,896]{1,0:T(8,128)S(1)}, f32[8,896]{1,0:T(8,128)S(1)}, u32[]{:S(2)}, u32[]{:S(2)}) collective-permute-start(f32[8,896]{1,0:T(8,128)S(1)} %coarse.5.refs_0_), channel_id=1, source_target_pairs={{0,6},{1,7},{2,4},{3,5},{4,2},{5,3},{6,0},{7,1},{8,14},{9,15},{10,... | collective-permute-start | bytes 86024 | tf_op jit(solution)/shard_map/ppermute | solution.py:22
  99.0 2.0 %collective-permute-start.44 = (f32[8,896]{1,0:T(8,128)S(1)}, f32[8,896]{1,0:T(8,128)S(1)}, u32[]{:S(2)}, u32[]{:S(2)}) collective-permute-start(f32[8,896]{1,0:T(8,128)S(1)} %coarse.5.refs_0_), channel_id=1, source_target_pairs={{0,2},{1,3},{2,0},{3,1},{4,6},{5,7},{6,4},{7,5},{8,10},{9,11},{10,... | collective-permute-start | bytes 86024 | tf_op jit(solution)/shard_map/ppermute | solution.py:22
  100.9 1.3 %collective-permute-done.46.refs_3_ = f32[8,896]{1,0:T(8,128)S(1)} collective-permute-done((f32[8,896]{1,0:T(8,128)S(1)}, f32[8,896]{1,0:T(8,128)S(1)}, u32[]{:S(2)}, u32[]{:S(2)}) %collective-permute-start.46) | collective-permute-done | bytes 28704 | tf_op jit(solution)/shard_map/ppermute | solution.py:22
  102.2 1.5 %collective-permute-done.45.refs_2_ = f32[8,896]{1,0:T(8,128)S(1)} collective-permute-done((f32[8,896]{1,0:T(8,128)S(1)}, f32[8,896]{1,0:T(8,128)S(1)}, u32[]{:S(2)}, u32[]{:S(2)}) %collective-permute-start.45) | collective-permute-done | bytes 28704 | tf_op jit(solution)/shard_map/ppermute | solution.py:22
  103.8 2.2 %step.5 = (f32[1,1,5,16,4,128]{5,4,3,2,1,0:T(4,128)}, f32[1,1,5,16,4,128]{5,4,3,2,1,0:T(4,128)}) custom-call(s32[3]{0:T(128)S(1)} %pad_add_fusion.info_ref, s32[1,1,4,5]{3,2,1,0:T(4,128)S(1)} %copy-done.1, f32[5,16,512]{2,1,0:T(8,128)S(1)} %get-tuple-element.100.own_ref, f32[5,16,512]{2,1,0:T(8,128)S(1)} %collective-permute-done.35.facing_ref, ...), custom_call_target="tpu_custom_call" | custom-call | flops 1024 | bytes 1024 | tf_op jit(solution)/shard_map/step/pallas_call | solution.py:633
  (75 shorter events, 12.9 us)
Async XLA Ops:
  2.2 9.9 %collective-permute-start = (f32[128,512]{1,0:T(8,128)S(1)}, f32[128,512]{1,0:T(8,128)S(1)}, u32[]{:S(2)}, u32[]{:S(2)}) collective-permute-start(f32[128,512]{1,0:T(8,128)S(1)} %pack.1), channel_id=1, source_target_pairs={{0,1},{1,2},{2,3},{3,4},{4,5},{5,6},{6,7},{7,0},{8,9},{9,10},{10,1... | collective-permute-start | bytes 786440 | tf_op jit(solution)/shard_map/ppermute | solution.py:17
  2.8 17.0 %collective-permute-start.4 = (f32[48,1536]{1,0:T(8,128)}, f32[48,1536]{1,0:T(8,128)S(1)}, u32[]{:S(2)}, u32[]{:S(2)}) collective-permute-start(f32[48,1536]{1,0:T(8,128)} %refs_0_), channel_id=1, source_target_pairs={{0,24},{1,25},{2,26},{3,27},{4,28},{5,29},{6,30},{7,31},{8,16},{9,... | collective-permute-start | bytes 884744 | tf_op jit(solution)/shard_map/ppermute | solution.py:22
  6.3 14.4 %collective-permute-start.3 = (f32[48,1536]{1,0:T(8,128)}, f32[48,1536]{1,0:T(8,128)S(1)}, u32[]{:S(2)}, u32[]{:S(2)}) collective-permute-start(f32[48,1536]{1,0:T(8,128)} %refs_0_), channel_id=1, source_target_pairs={{0,16},{1,17},{2,18},{3,19},{4,20},{5,21},{6,22},{7,23},{8,24},{9,... | collective-permute-start | bytes 884744 | tf_op jit(solution)/shard_map/ppermute | solution.py:22
  6.8 15.9 %collective-permute-start.2 = (f32[48,1536]{1,0:T(8,128)}, f32[48,1536]{1,0:T(8,128)S(1)}, u32[]{:S(2)}, u32[]{:S(2)}) collective-permute-start(f32[48,1536]{1,0:T(8,128)} %refs_0_), channel_id=1, source_target_pairs={{0,8},{1,9},{2,10},{3,11},{4,12},{5,13},{6,14},{7,15},{8,0},{9,1},... | collective-permute-start | bytes 884744 | tf_op jit(solution)/shard_map/ppermute | solution.py:22
  13.6 9.1 %collective-permute-start.1 = (f32[5,16,512]{2,1,0:T(8,128)S(1)}, f32[5,16,512]{2,1,0:T(8,128)S(1)}, u32[]{:S(2)}, u32[]{:S(2)}) collective-permute-start(f32[5,16,512]{2,1,0:T(8,128)S(1)} %get-tuple-element.62), channel_id=1, source_target_pairs={{0,7},{1,0},{2,1},{3,2},{4,3},{5,4},{6,5},{7,6},{8,15},{9,8},{10,9... | collective-permute-start | bytes 491528 | tf_op jit(solution)/shard_map/ppermute | solution.py:17
  16.5 1.2 %collective-permute-start.10 = (f32[8,1664]{1,0:T(8,128)S(1)}, f32[8,1664]{1,0:T(8,128)S(1)}, u32[]{:S(2)}, u32[]{:S(2)}) collective-permute-start(f32[8,1664]{1,0:T(8,128)S(1)} %get-tuple-element.81), channel_id=1, source_target_pairs={{0,1},{1,0},{2,3},{3,2},{4,5},{5,4},{6,7},{7,6},{8,9},{9,8},{10,11... | collective-permute-start | bytes 159752 | tf_op jit(solution)/shard_map/ppermute | solution.py:22
  17.7 10.7 %collective-permute-start.13 = (f32[8,1664]{1,0:T(8,128)S(1)}, f32[8,1664]{1,0:T(8,128)S(1)}, u32[]{:S(2)}, u32[]{:S(2)}) collective-permute-start(f32[8,1664]{1,0:T(8,128)S(1)} %add.78), channel_id=1, source_target_pairs={{0,6},{1,7},{2,4},{3,5},{4,2},{5,3},{6,0},{7,1},{8,14},{9,15},{10,... | collective-permute-start | bytes 159752 | tf_op jit(solution)/shard_map/ppermute | solution.py:22
  19.8 8.6 %collective-permute-start.12 = (f32[8,1664]{1,0:T(8,128)S(1)}, f32[8,1664]{1,0:T(8,128)S(1)}, u32[]{:S(2)}, u32[]{:S(2)}) collective-permute-start(f32[8,1664]{1,0:T(8,128)S(1)} %add.78), channel_id=1, source_target_pairs={{0,4},{1,5},{2,6},{3,7},{4,0},{5,1},{6,2},{7,3},{8,12},{9,13},{10,... | collective-permute-start | bytes 159752 | tf_op jit(solution)/shard_map/ppermute | solution.py:22
  20.6 7.8 %collective-permute-start.11 = (f32[8,1664]{1,0:T(8,128)S(1)}, f32[8,1664]{1,0:T(8,128)S(1)}, u32[]{:S(2)}, u32[]{:S(2)}) collective-permute-start(f32[8,1664]{1,0:T(8,128)S(1)} %add.78), channel_id=1, source_target_pairs={{0,2},{1,3},{2,0},{3,1},{4,6},{5,7},{6,4},{7,5},{8,10},{9,11},{10,... | collective-permute-start | bytes 159752 | tf_op jit(solution)/shard_map/ppermute | solution.py:22
  22.7 9.3 %copy-start = (f32[48,1536]{1,0:T(8,128)S(1)}, f32[48,1536]{1,0:T(8,128)}, u32[]{:S(2)}) copy-start(f32[48,1536]{1,0:T(8,128)} %refs_0_) | copy-start | bytes 884740
  28.5 5.2 %collective-permute-start.16 = (f32[8,1664]{1,0:T(8,128)S(1)}, f32[8,1664]{1,0:T(8,128)S(1)}, u32[]{:S(2)}, u32[]{:S(2)}) collective-permute-start(f32[8,1664]{1,0:T(8,128)S(1)} %add_add_fusion.5), channel_id=1, source_target_pairs={{0,24},{1,25},{2,26},{3,27},{4,28},{5,29},{6,30},{7,31},{8,16},{9,... | collective-permute-start | bytes 159752 | tf_op jit(solution)/shard_map/ppermute | solution.py:22
  30.7 4.1 %collective-permute-start.15 = (f32[8,1664]{1,0:T(8,128)S(1)}, f32[8,1664]{1,0:T(8,128)S(1)}, u32[]{:S(2)}, u32[]{:S(2)}) collective-permute-start(f32[8,1664]{1,0:T(8,128)S(1)} %add_add_fusion.5), channel_id=1, source_target_pairs={{0,16},{1,17},{2,18},{3,19},{4,20},{5,21},{6,22},{7,23},{8,24},{9,... | collective-permute-start | bytes 159752 | tf_op jit(solution)/shard_map/ppermute | solution.py:22
  31.5 4.1 %collective-permute-start.14 = (f32[8,1664]{1,0:T(8,128)S(1)}, f32[8,1664]{1,0:T(8,128)S(1)}, u32[]{:S(2)}, u32[]{:S(2)}) collective-permute-start(f32[8,1664]{1,0:T(8,128)S(1)} %add_add_fusion.5), channel_id=1, source_target_pairs={{0,8},{1,9},{2,10},{3,11},{4,12},{5,13},{6,14},{7,15},{8,0},{9,1},... | collective-permute-start | bytes 159752 | tf_op jit(solution)/shard_map/ppermute | solution.py:22
  32.0 3.6 %collective-permute-start.6 = (f32[48,1536]{1,0:T(8,128)S(1)}, f32[48,1536]{1,0:T(8,128)S(1)}, u32[]{:S(2)}, u32[]{:S(2)}) collective-permute-start(f32[48,1536]{1,0:T(8,128)S(1)} %copy-done), channel_id=1, source_target_pairs={{0,1},{1,0},{2,3},{3,2},{4,5},{5,4},{6,7},{7,6},{8,9},{9,8},{10,11... | collective-permute-start | bytes 884744 | tf_op jit(solution)/shard_map/ppermute | solution.py:22
  32.0 4.3 %collective-permute-start.7 = (f32[48,1536]{1,0:T(8,128)S(1)}, f32[48,1536]{1,0:T(8,128)S(1)}, u32[]{:S(2)}, u32[]{:S(2)}) collective-permute-start(f32[48,1536]{1,0:T(8,128)S(1)} %collective-permute-done.2.refs_1_), channel_id=1, source_target_pairs={{0,1},{1,0},{2,3},{3,2},{4,5},{5,4},{6,7},{7,6},{8,9},{9,8},{10,11... | collective-permute-start | bytes 884744 | tf_op jit(solution)/shard_map/ppermute | solution.py:22
  33.7 2.6 %collective-permute-start.8 = (f32[48,1536]{1,0:T(8,128)S(1)}, f32[48,1536]{1,0:T(8,128)S(1)}, u32[]{:S(2)}, u32[]{:S(2)}) collective-permute-start(f32[48,1536]{1,0:T(8,128)S(1)} %collective-permute-done.3.refs_2_), channel_id=1, source_target_pairs={{0,1},{1,0},{2,3},{3,2},{4,5},{5,4},{6,7},{7,6},{8,9},{9,8},{10,11... | collective-permute-start | bytes 884744 | tf_op jit(solution)/shard_map/ppermute | solution.py:22
  34.8 1.6 %collective-permute-start.9 = (f32[48,1536]{1,0:T(8,128)S(1)}, f32[48,1536]{1,0:T(8,128)S(1)}, u32[]{:S(2)}, u32[]{:S(2)}) collective-permute-start(f32[48,1536]{1,0:T(8,128)S(1)} %collective-permute-done.4.refs_3_), channel_id=1, source_target_pairs={{0,1},{1,0},{2,3},{3,2},{4,5},{5,4},{6,7},{7,6},{8,9},{9,8},{10,11... | collective-permute-start | bytes 884744 | tf_op jit(solution)/shard_map/ppermute | solution.py:22
  35.6 8.1 %collective-permute-start.5 = (f32[5,16,512]{2,1,0:T(8,128)S(1)}, f32[5,16,512]{2,1,0:T(8,128)S(1)}, u32[]{:S(2)}, u32[]{:S(2)}) collective-permute-start(f32[5,16,512]{2,1,0:T(8,128)S(1)} %get-tuple-element.68), channel_id=1, source_target_pairs={{0,1},{1,2},{2,3},{3,4},{4,5},{5,6},{6,7},{7,0},{8,9},{9,10},{10,1... | collective-permute-start | bytes 491528 | tf_op jit(solution)/shard_map/ppermute | solution.py:17
  35.6 2.4 %collective-permute-start.17 = (f32[8,1664]{1,0:T(8,128)S(1)}, f32[8,1664]{1,0:T(8,128)S(1)}, u32[]{:S(2)}, u32[]{:S(2)}) collective-permute-start(f32[8,1664]{1,0:T(8,128)S(1)} %add_add_fusion.4.mine_ref), channel_id=1, source_target_pairs={{0,1},{1,0},{2,3},{3,2},{4,5},{5,4},{6,7},{7,6},{8,9},{9,8},{10,11... | collective-permute-start | bytes 159752 | tf_op jit(solution)/shard_map/ppermute | solution.py:22
  39.3 5.7 %collective-permute-start.20 = (f32[8,896]{1,0:T(8,128)S(1)}, f32[8,896]{1,0:T(8,128)S(1)}, u32[]{:S(2)}, u32[]{:S(2)}) collective-permute-start(f32[8,896]{1,0:T(8,128)S(1)} %coarse.3.refs_0_), channel_id=1, source_target_pairs={{0,6},{1,7},{2,4},{3,5},{4,2},{5,3},{6,0},{7,1},{8,14},{9,15},{10,... | collective-permute-start | bytes 86024 | tf_op jit(solution)/shard_map/ppermute | solution.py:22
  42.6 4.8 %collective-permute-start.19 = (f32[8,896]{1,0:T(8,128)S(1)}, f32[8,896]{1,0:T(8,128)S(1)}, u32[]{:S(2)}, u32[]{:S(2)}) collective-permute-start(f32[8,896]{1,0:T(8,128)S(1)} %coarse.3.refs_0_), channel_id=1, source_target_pairs={{0,4},{1,5},{2,6},{3,7},{4,0},{5,1},{6,2},{7,3},{8,12},{9,13},{10,... | collective-permute-start | bytes 86024 | tf_op jit(solution)/shard_map/ppermute | solution.py:22
  42.7 4.7 %collective-permute-start.18 = (f32[8,896]{1,0:T(8,128)S(1)}, f32[8,896]{1,0:T(8,128)S(1)}, u32[]{:S(2)}, u32[]{:S(2)}) collective-permute-start(f32[8,896]{1,0:T(8,128)S(1)} %coarse.3.refs_0_), channel_id=1, source_target_pairs={{0,2},{1,3},{2,0},{3,1},{4,6},{5,7},{6,4},{7,5},{8,10},{9,11},{10,... | collective-permute-start | bytes 86024 | tf_op jit(solution)/shard_map/ppermute | solution.py:22
  49.2 6.2 %collective-permute-start.21 = (f32[5,16,512]{2,1,0:T(8,128)S(1)}, f32[5,16,512]{2,1,0:T(8,128)S(1)}, u32[]{:S(2)}, u32[]{:S(2)}) collective-permute-start(f32[5,16,512]{2,1,0:T(8,128)S(1)} %get-tuple-element.85), channel_id=1, source_target_pairs={{0,7},{1,0},{2,1},{3,2},{4,3},{5,4},{6,5},{7,6},{8,15},{9,8},{10,9... | collective-permute-start | bytes 491528 | tf_op jit(solution)/shard_map/ppermute | solution.py:17
  49.5 1.5 %collective-permute-start.23 = (f32[8,1664]{1,0:T(8,128)S(1)}, f32[8,1664]{1,0:T(8,128)S(1)}, u32[]{:S(2)}, u32[]{:S(2)}) collective-permute-start(f32[8,1664]{1,0:T(8,128)S(1)} %get-tuple-element.92), channel_id=1, source_target_pairs={{0,1},{1,0},{2,3},{3,2},{4,5},{5,4},{6,7},{7,6},{8,9},{9,8},{10,11... | collective-permute-start | bytes 159752 | tf_op jit(solution)/shard_map/ppermute | solution.py:22
  50.9 7.7 %collective-permute-start.26 = (f32[8,1664]{1,0:T(8,128)S(1)}, f32[8,1664]{1,0:T(8,128)S(1)}, u32[]{:S(2)}, u32[]{:S(2)}) collective-permute-start(f32[8,1664]{1,0:T(8,128)S(1)} %add.86), channel_id=1, source_target_pairs={{0,6},{1,7},{2,4},{3,5},{4,2},{5,3},{6,0},{7,1},{8,14},{9,15},{10,... | collective-permute-start | bytes 159752 | tf_op jit(solution)/shard_map/ppermute | solution.py:22
  52.5 6.9 %collective-permute-start.25 = (f32[8,1664]{1,0:T(8,128)S(1)}, f32[8,1664]{1,0:T(8,128)S(1)}, u32[]{:S(2)}, u32[]{:S(2)}) collective-permute-start(f32[8,1664]{1,0:T(8,128)S(1)} %add.86), channel_id=1, source_target_pairs={{0,4},{1,5},{2,6},{3,7},{4,0},{5,1},{6,2},{7,3},{8,12},{9,13},{10,... | collective-permute-start | bytes 159752 | tf_op jit(solution)/shard_map/ppermute | solution.py:22
  53.1 6.2 %collective-permute-start.24 = (f32[8,1664]{1,0:T(8,128)S(1)}, f32[8,1664]{1,0:T(8,128)S(1)}, u32[]{:S(2)}, u32[]{:S(2)}) collective-permute-start(f32[8,1664]{1,0:T(8,128)S(1)} %add.86), channel_id=1, source_target_pairs={{0,2},{1,3},{2,0},{3,1},{4,6},{5,7},{6,4},{7,5},{8,10},{9,11},{10,... | collective-permute-start | bytes 159752 | tf_op jit(solution)/shard_map/ppermute | solution.py:22
  59.4 5.2 %collective-permute-start.29 = (f32[8,1664]{1,0:T(8,128)S(1)}, f32[8,1664]{1,0:T(8,128)S(1)}, u32[]{:S(2)}, u32[]{:S(2)}) collective-permute-start(f32[8,1664]{1,0:T(8,128)S(1)} %add_add_fusion.3), channel_id=1, source_target_pairs={{0,24},{1,25},{2,26},{3,27},{4,28},{5,29},{6,30},{7,31},{8,16},{9,... | collective-permute-start | bytes 159752 | tf_op jit(solution)/shard_map/ppermute | solution.py:22
  60.9 4.3 %collective-permute-start.28 = (f32[8,1664]{1,0:T(8,128)S(1)}, f32[8,1664]{1,0:T(8,128)S(1)}, u32[]{:S(2)}, u32[]{:S(2)}) collective-permute-start(f32[8,1664]{1,0:T(8,128)S(1)} %add_add_fusion.3), channel_id=1, source_target_pairs={{0,16},{1,17},{2,18},{3,19},{4,20},{5,21},{6,22},{7,23},{8,24},{9,... | collective-permute-start | bytes 159752 | tf_op jit(solution)/shard_map/ppermute | solution.py:22
  61.4 4.1 %collective-permute-start.27 = (f32[8,1664]{1,0:T(8,128)S(1)}, f32[8,1664]{1,0:T(8,128)S(1)}, u32[]{:S(2)}, u32[]{:S(2)}) collective-permute-start(f32[8,1664]{1,0:T(8,128)S(1)} %add_add_fusion.3), channel_id=1, source_target_pairs={{0,8},{1,9},{2,10},{3,11},{4,12},{5,13},{6,14},{7,15},{8,0},{9,1},... | collective-permute-start | bytes 159752 | tf_op jit(solution)/shard_map/ppermute | solution.py:22
  62.9 12.0 %collective-permute-start.22 = (f32[5,16,512]{2,1,0:T(8,128)S(1)}, f32[5,16,512]{2,1,0:T(8,128)S(1)}, u32[]{:S(2)}, u32[]{:S(2)}) collective-permute-start(f32[5,16,512]{2,1,0:T(8,128)S(1)} %get-tuple-element.89), channel_id=1, source_target_pairs={{0,1},{1,2},{2,3},{3,4},{4,5},{5,6},{6,7},{7,0},{8,9},{9,10},{10,1... | collective-permute-start | bytes 491528 | tf_op jit(solution)/shard_map/ppermute | solution.py:17
  65.6 1.3 %collective-permute-start.30 = (f32[8,1664]{1,0:T(8,128)S(1)}, f32[8,1664]{1,0:T(8,128)S(1)}, u32[]{:S(2)}, u32[]{:S(2)}) collective-permute-start(f32[8,1664]{1,0:T(8,128)S(1)} %add_add_fusion.2.mine_ref), channel_id=1, source_target_pairs={{0,1},{1,0},{2,3},{3,2},{4,5},{5,4},{6,7},{7,6},{8,9},{9,8},{10,11... | collective-permute-start | bytes 159752 | tf_op jit(solution)/shard_map/ppermute | solution.py:22
  68.1 5.7 %collective-permute-start.33 = (f32[8,896]{1,0:T(8,128)S(1)}, f32[8,896]{1,0:T(8,128)S(1)}, u32[]{:S(2)}, u32[]{:S(2)}) collective-permute-start(f32[8,896]{1,0:T(8,128)S(1)} %coarse.4.refs_0_), channel_id=1, source_target_pairs={{0,6},{1,7},{2,4},{3,5},{4,2},{5,3},{6,0},{7,1},{8,14},{9,15},{10,... | collective-permute-start | bytes 86024 | tf_op jit(solution)/shard_map/ppermute | solution.py:22
  70.1 4.8 %collective-permute-start.32 = (f32[8,896]{1,0:T(8,128)S(1)}, f32[8,896]{1,0:T(8,128)S(1)}, u32[]{:S(2)}, u32[]{:S(2)}) collective-permute-start(f32[8,896]{1,0:T(8,128)S(1)} %coarse.4.refs_0_), channel_id=1, source_target_pairs={{0,4},{1,5},{2,6},{3,7},{4,0},{5,1},{6,2},{7,3},{8,12},{9,13},{10,... | collective-permute-start | bytes 86024 | tf_op jit(solution)/shard_map/ppermute | solution.py:22
  70.1 4.8 %collective-permute-start.31 = (f32[8,896]{1,0:T(8,128)S(1)}, f32[8,896]{1,0:T(8,128)S(1)}, u32[]{:S(2)}, u32[]{:S(2)}) collective-permute-start(f32[8,896]{1,0:T(8,128)S(1)} %coarse.4.refs_0_), channel_id=1, source_target_pairs={{0,2},{1,3},{2,0},{3,1},{4,6},{5,7},{6,4},{7,5},{8,10},{9,11},{10,... | collective-permute-start | bytes 86024 | tf_op jit(solution)/shard_map/ppermute | solution.py:22
  76.8 6.5 %collective-permute-start.34 = (f32[5,16,512]{2,1,0:T(8,128)S(1)}, f32[5,16,512]{2,1,0:T(8,128)S(1)}, u32[]{:S(2)}, u32[]{:S(2)}) collective-permute-start(f32[5,16,512]{2,1,0:T(8,128)S(1)} %get-tuple-element.99), channel_id=1, source_target_pairs={{0,7},{1,0},{2,1},{3,2},{4,3},{5,4},{6,5},{7,6},{8,15},{9,8},{10,9... | collective-permute-start | bytes 491528 | tf_op jit(solution)/shard_map/ppermute | solution.py:17
  77.6 1.2 %collective-permute-start.36 = (f32[8,1664]{1,0:T(8,128)S(1)}, f32[8,1664]{1,0:T(8,128)S(1)}, u32[]{:S(2)}, u32[]{:S(2)}) collective-permute-start(f32[8,1664]{1,0:T(8,128)S(1)} %get-tuple-element.104), channel_id=1, source_target_pairs={{0,1},{1,0},{2,3},{3,2},{4,5},{5,4},{6,7},{7,6},{8,9},{9,8},{10,11... | collective-permute-start | bytes 159752 | tf_op jit(solution)/shard_map/ppermute | solution.py:22
  78.8 7.7 %collective-permute-start.39 = (f32[8,1664]{1,0:T(8,128)S(1)}, f32[8,1664]{1,0:T(8,128)S(1)}, u32[]{:S(2)}, u32[]{:S(2)}) collective-permute-start(f32[8,1664]{1,0:T(8,128)S(1)} %add.94), channel_id=1, source_target_pairs={{0,6},{1,7},{2,4},{3,5},{4,2},{5,3},{6,0},{7,1},{8,14},{9,15},{10,... | collective-permute-start | bytes 159752 | tf_op jit(solution)/shard_map/ppermute | solution.py:22
  80.2 6.7 %collective-permute-start.38 = (f32[8,1664]{1,0:T(8,128)S(1)}, f32[8,1664]{1,0:T(8,128)S(1)}, u32[]{:S(2)}, u32[]{:S(2)}) collective-permute-start(f32[8,1664]{1,0:T(8,128)S(1)} %add.94), channel_id=1, source_target_pairs={{0,4},{1,5},{2,6},{3,7},{4,0},{5,1},{6,2},{7,3},{8,12},{9,13},{10,... | collective-permute-start | bytes 159752 | tf_op jit(solution)/shard_map/ppermute | solution.py:22
  81.3 5.5 %collective-permute-start.37 = (f32[8,1664]{1,0:T(8,128)S(1)}, f32[8,1664]{1,0:T(8,128)S(1)}, u32[]{:S(2)}, u32[]{:S(2)}) collective-permute-start(f32[8,1664]{1,0:T(8,128)S(1)} %add.94), channel_id=1, source_target_pairs={{0,2},{1,3},{2,0},{3,1},{4,6},{5,7},{6,4},{7,5},{8,10},{9,11},{10,... | collective-permute-start | bytes 159752 | tf_op jit(solution)/shard_map/ppermute | solution.py:22
  86.9 5.2 %collective-permute-start.42 = (f32[8,1664]{1,0:T(8,128)S(1)}, f32[8,1664]{1,0:T(8,128)S(1)}, u32[]{:S(2)}, u32[]{:S(2)}) collective-permute-start(f32[8,1664]{1,0:T(8,128)S(1)} %add_add_fusion.1), channel_id=1, source_target_pairs={{0,24},{1,25},{2,26},{3,27},{4,28},{5,29},{6,30},{7,31},{8,16},{9,... | collective-permute-start | bytes 159752 | tf_op jit(solution)/shard_map/ppermute | solution.py:22
  89.1 4.1 %collective-permute-start.41 = (f32[8,1664]{1,0:T(8,128)S(1)}, f32[8,1664]{1,0:T(8,128)S(1)}, u32[]{:S(2)}, u32[]{:S(2)}) collective-permute-start(f32[8,1664]{1,0:T(8,128)S(1)} %add_add_fusion.1), channel_id=1, source_target_pairs={{0,16},{1,17},{2,18},{3,19},{4,20},{5,21},{6,22},{7,23},{8,24},{9,... | collective-permute-start | bytes 159752 | tf_op jit(solution)/shard_map/ppermute | solution.py:22
  89.9 4.1 %collective-permute-start.40 = (f32[8,1664]{1,0:T(8,128)S(1)}, f32[8,1664]{1,0:T(8,128)S(1)}, u32[]{:S(2)}, u32[]{:S(2)}) collective-permute-start(f32[8,1664]{1,0:T(8,128)S(1)} %add_add_fusion.1), channel_id=1, source_target_pairs={{0,8},{1,9},{2,10},{3,11},{4,12},{5,13},{6,14},{7,15},{8,0},{9,1},... | collective-permute-start | bytes 159752 | tf_op jit(solution)/shard_map/ppermute | solution.py:22
  90.4 13.3 %collective-permute-start.35 = (f32[5,16,512]{2,1,0:T(8,128)S(1)}, f32[5,16,512]{2,1,0:T(8,128)S(1)}, u32[]{:S(2)}, u32[]{:S(2)}) collective-permute-start(f32[5,16,512]{2,1,0:T(8,128)S(1)} %get-tuple-element.101), channel_id=1, source_target_pairs={{0,1},{1,2},{2,3},{3,4},{4,5},{5,6},{6,7},{7,0},{8,9},{9,10},{10,1... | collective-permute-start | bytes 491528 | tf_op jit(solution)/shard_map/ppermute | solution.py:17
  94.0 1.3 %collective-permute-start.43 = (f32[8,1664]{1,0:T(8,128)S(1)}, f32[8,1664]{1,0:T(8,128)S(1)}, u32[]{:S(2)}, u32[]{:S(2)}) collective-permute-start(f32[8,1664]{1,0:T(8,128)S(1)} %add_add_fusion.mine_ref), channel_id=1, source_target_pairs={{0,1},{1,0},{2,3},{3,2},{4,5},{5,4},{6,7},{7,6},{8,9},{9,8},{10,11... | collective-permute-start | bytes 159752 | tf_op jit(solution)/shard_map/ppermute | solution.py:22
  96.5 5.7 %collective-permute-start.46 = (f32[8,896]{1,0:T(8,128)S(1)}, f32[8,896]{1,0:T(8,128)S(1)}, u32[]{:S(2)}, u32[]{:S(2)}) collective-permute-start(f32[8,896]{1,0:T(8,128)S(1)} %coarse.5.refs_0_), channel_id=1, source_target_pairs={{0,6},{1,7},{2,4},{3,5},{4,2},{5,3},{6,0},{7,1},{8,14},{9,15},{10,... | collective-permute-start | bytes 86024 | tf_op jit(solution)/shard_map/ppermute | solution.py:22
  99.0 4.8 %collective-permute-start.45 = (f32[8,896]{1,0:T(8,128)S(1)}, f32[8,896]{1,0:T(8,128)S(1)}, u32[]{:S(2)}, u32[]{:S(2)}) collective-permute-start(f32[8,896]{1,0:T(8,128)S(1)} %coarse.5.refs_0_), channel_id=1, source_target_pairs={{0,4},{1,5},{2,6},{3,7},{4,0},{5,1},{6,2},{7,3},{8,12},{9,13},{10,... | collective-permute-start | bytes 86024 | tf_op jit(solution)/shard_map/ppermute | solution.py:22
  99.0 4.8 %collective-permute-start.44 = (f32[8,896]{1,0:T(8,128)S(1)}, f32[8,896]{1,0:T(8,128)S(1)}, u32[]{:S(2)}, u32[]{:S(2)}) collective-permute-start(f32[8,896]{1,0:T(8,128)S(1)} %coarse.5.refs_0_), channel_id=1, source_target_pairs={{0,2},{1,3},{2,0},{3,1},{4,6},{5,7},{6,4},{7,5},{8,10},{9,11},{10,... | collective-permute-start | bytes 86024 | tf_op jit(solution)/shard_map/ppermute | solution.py:22
  (2 other events, 10.4 us)
